TPU v7x, 32 devices: a whole 2x2x4 slice. The times are simulated.
32 devices in a mesh: pipe: 4 (over x, core), seq: 8 (over z, y).
Axes of the slice: x: 2, y: 2, z: 4, core: 2. Of those that a mesh axis runs over, the one named last changes fastest.
Arguments:
- saved_inputs: bfloat16 [4, 2, 2048, 1536], P('pipe', None, 'seq'), may hold values from -54 to 54
- arrived_grad: bfloat16 [4, 2048, 1536], P('pipe', 'seq'), may hold values from -6 to 6
- loss_grad: bfloat16 [1, 2048, 1536], P(None, 'seq'), may hold values from -6 to 6
- norm_gain: float32 [4, 1536], P('pipe'), may hold values from 0.25 to 1.75
- w_gate: bfloat16 [4, 384, 1536], P('pipe'), may hold values from -0.3125 to 0.3125
- w_value: bfloat16 [4, 384, 1536], P('pipe'), may hold values from -0.3125 to 0.3125
- w_out: bfloat16 [4, 384, 1536], P('pipe'), may hold values from -0.3125 to 0.3125
- r_factor: bfloat16 [4, 2048, 256], P('pipe', 'seq'), may hold values from -0.375 to 0.375
- l_factor: bfloat16 [4, 256, 64], P('pipe', 'seq'), may hold values from -2 to 2
Outputs:
- sent_grad: bfloat16 [4, 2, 2048, 1536], P('pipe', None, 'seq')
All inputs are finite; a program needn't handle non-finite values.
Results may differ from a plain program's by a relative error of at most 0.008.
Values may be sent and summed in bfloat16 or wider, within the bound.
No kernel may reach another device: no remote copies, remote signals or barrier semaphores. Data moves between devices by JAX's collectives and lax.ppermute only.
A program may use at most 128 MiB of HBM per device.

v0:
```python
import functools

import jax
import jax.numpy as jnp
from jax import lax
from jax.experimental import pallas as pl
from jax.experimental.pallas import tpu as pltpu
from jax.sharding import PartitionSpec as P

TICKS = 2
EPSILON = 1e-05
F32 = jnp.float32
BF16 = jnp.bfloat16
def params(mebibytes=32):
    return pltpu.CompilerParams(
        dimension_semantics=("arbitrary",), vmem_limit_bytes=mebibytes * 1024 * 1024
    )


def dot(a, b, over=((1,), (0,))):
    return lax.dot_general(a, b, (over, ((), ())), preferred_element_type=F32)


def rows_of(slot, size):
    owner = lax.axis_index("seq") ^ slot
    return pl.ds(pl.multiple_of(owner * size, size), size)


def inverse_rms(x_ref):
    x = x_ref[...].astype(F32)
    return lax.rsqrt(jnp.mean(x * x, axis=-1, keepdims=True) + EPSILON)


def columns(j, width):
    return pl.ds(pl.multiple_of(j * width, 128), width)


def split(outs, wide_ref):
    for slot, out in enumerate(outs):
        out[...] = wide_ref[rows_of(slot, out.shape[0]), :].astype(BF16)


def normed_block(j, x_ref, gain_ref, q_ref, width):
    @pl.when(j == 0)
    def _():
        q_ref[...] = inverse_rms(x_ref)

    x = x_ref[:, columns(j, width)].astype(F32)
    return (x * q_ref[...] * gain_ref[...]).astype(BF16)


def first_of(normed, w_ref, r_ref):
    return dot(r_ref[...], dot(normed, w_ref[...]).astype(BF16))


def grads_of(normed, grad, w_gate_ref, w_out_ref, factor_ref):
    gate = dot(normed, w_gate_ref[...])
    inner = dot(grad, w_out_ref[...], ((1,), (1,)))
    sigmoid = jax.nn.sigmoid(gate)
    factor_ref[...] = inner * sigmoid * (1.0 + gate * (1.0 - sigmoid))
    return inner * gate * sigmoid


def first_kernel(count, x_ref, gain_ref, w_ref, r_ref, *refs):
    outs, (q_ref, wide_ref) = refs[:count], refs[count:]
    normed = normed_block(pl.program_id(0), x_ref, gain_ref, q_ref, w_ref.shape[1])
    wide_ref[...] = first_of(normed, w_ref, r_ref)
    split(outs, wide_ref)


def pick_gradient(refs):
    if len(refs) == 1:
        return refs[0][...]
    last = lax.axis_index("pipe") == lax.axis_size("pipe") - 1
    return jnp.where(last, refs[1][...], refs[0][...])


def grad_kernel(count, sources, x_ref, gain_ref, w_gate_ref, w_out_ref, *refs):
    grads, refs = refs[:sources], refs[sources:]
    outs, (factor_ref, q_ref, wide_ref) = refs[:count], refs[count:]
    normed = normed_block(pl.program_id(0), x_ref, gain_ref, q_ref, w_gate_ref.shape[1])
    wide_ref[...] = grads_of(normed, pick_gradient(grads), w_gate_ref, w_out_ref, factor_ref)
    split(outs, wide_ref)


def matrix_kernel(count, l_ref, out_ref):
    size = l_ref.shape[0]
    wide = count * size
    bits = count.bit_length() - 1
    me = lax.axis_index("seq")
    iota = functools.partial(lax.broadcasted_iota, jnp.int32)

    shape = (count, size, count * count)
    tall = jnp.broadcast_to(l_ref[...].astype(F32)[None], shape)
    tall = jnp.where(iota(shape, 2) >> bits == iota(shape, 0) ^ me, tall, 0.0)
    tall = tall.reshape(wide, count * count).astype(BF16)

    shape = (count * count, wide)
    source = (iota(shape, 1) >> (size.bit_length() - 1)) ^ me
    spread = dot(tall, jnp.where(iota(shape, 0) & (count - 1) == source, 1.0, 0.0).astype(BF16))

    row, column = iota((wide, wide), 0) & (size - 1), iota((wide, wide), 1) & (size - 1)
    out_ref[...] = jnp.where(row == column, spread, 0.0).astype(BF16)


def stacked_slots(ins):
    if ins[0].shape[0] % 16 == 0:
        return jnp.concatenate([part[...] for part in ins], axis=0)
    return jnp.concatenate([part[...].astype(F32) for part in ins], axis=0).astype(BF16)


def spread_slots(outs, value):
    size = outs[0].shape[0]
    for slot, out in enumerate(outs):
        out[...] = value[slot * size : (slot + 1) * size].astype(BF16)


def joined(ins, wide_ref):
    for slot, part in enumerate(ins):
        wide_ref[rows_of(slot, part.shape[0]), :] = part[...].astype(wide_ref.dtype)
    return wide_ref[...]


def mix_kernel(count, transposed, m_ref, *refs):
    ins, outs = refs[:count], refs[count:]
    over = ((0,), (0,)) if transposed else ((1,), (0,))
    spread_slots(outs, dot(m_ref[...], stacked_slots(ins), over))


def back_kernel(count, w_gate_ref, factor_ref, *refs):
    mixed, (out_ref, wide_ref) = refs[:count], refs[count:]
    gate_grad = (factor_ref[...] * joined(mixed, wide_ref).astype(F32)).astype(BF16)
    out_ref[...] = dot(gate_grad, w_gate_ref[...], ((1,), (1,)))


def finish(j, back, folded, grads, outs, x_ref, gain_ref, w_value_ref, r_ref, e_ref, sum_ref):
    at = columns(j, w_value_ref.shape[1])
    value_grad = dot(r_ref[...], folded.astype(BF16), ((0,), (0,))).astype(BF16)
    e = (back + dot(value_grad, w_value_ref[...], ((1,), (1,)))) * gain_ref[...]
    e_ref[:, at] = e
    part = jnp.sum(e * x_ref[:, at].astype(F32), axis=-1, keepdims=True)

    @pl.when(j == 0)
    def _():
        sum_ref[...] = part

    @pl.when(j > 0)
    def _():
        sum_ref[...] += part

    @pl.when(j == pl.num_programs(0) - 1)
    def _():
        x = x_ref[...].astype(F32)
        q = inverse_rms(x_ref)
        mean = sum_ref[...] / x.shape[1]
        result = pick_gradient(grads).astype(F32) + q * e_ref[...] - q * q * q * x * mean
        for out in outs:
            out[...] = result.astype(BF16)


def result_kernel(count, sources, x_ref, gain_ref, w_value_ref, r_ref, back_ref, *refs):
    folded, refs = refs[:count], refs[count:]
    grads, refs = refs[:sources], refs[sources:]
    outs, (wide_ref, e_ref, sum_ref) = refs[sources - 1 : -3], refs[-3:]
    finish(
        pl.program_id(0), back_ref[...], joined(folded, wide_ref), grads, outs,
        x_ref, gain_ref, w_value_ref, r_ref, e_ref, sum_ref,
    )


class Exchange:
    def __init__(self, parts):
        self.parts = list(parts)
        self.got = {0: parts[0]}

    def send(self, slots, after=()):
        for slot in slots:
            pairs = [(i, i ^ slot) for i in range(len(self.parts))]
            self.got[slot] = lax.ppermute(tied(self.parts[slot], after), "seq", pairs)
        return self

    def all(self):
        return [self.got[slot] for slot in range(len(self.parts))]


def tied(value, after):
    if not after:
        return value
    value, *ended = lax.optimization_barrier((value, *(where.got[slot] for where, slot in after)))
    for (where, slot), got in zip(after, ended):
        where.got[slot] = got
    return value


def local(
    saved_inputs, arrived_grad, loss_grad, norm_gain, w_gate, w_value, w_out, r_factor, l_factor
):
    count = lax.axis_size("seq")
    pipe = lax.axis_size("pipe")
    _, _, rows, width = saved_inputs.shape
    block = w_gate.shape[1]
    size = rows // count

    whole = pl.BlockSpec((rows, width), lambda j: (0, 0))
    whole3 = pl.BlockSpec((None, rows, width), lambda j: (0, 0, 0))
    cut = pl.BlockSpec((rows, block), lambda j: (0, j))
    cut3 = pl.BlockSpec((None, rows, block), lambda j: (0, 0, j))
    weight = pl.BlockSpec((None, block, block), lambda j: (0, 0, j))
    gain = pl.BlockSpec((1, block), lambda j: (0, j))
    square = pl.BlockSpec((None, rows, rows), lambda j: (0, 0, 0))
    small = pl.BlockSpec((None, size, count * count), lambda j: (0, 0, 0))
    slots = [pl.BlockSpec((size, block), lambda j: (0, j))] * count
    anywhere = pl.BlockSpec(memory_space=pl.ANY)
    x_at = [
        pl.BlockSpec((None, None, rows, width), lambda j: (0, 0, 0, 0)),
        pl.BlockSpec((None, None, rows, width), lambda j: (0, 1, 0, 0)),
    ]

    slot_shapes = [jax.ShapeDtypeStruct((size, width), BF16)] * count
    plain = jax.ShapeDtypeStruct((rows, width), BF16)
    exact = jax.ShapeDtypeStruct((rows, width), F32)
    output = jax.ShapeDtypeStruct(saved_inputs.shape, BF16)

    column = pltpu.VMEM((rows, 1), F32)
    wide = pltpu.VMEM((rows, block), F32)
    full = pltpu.VMEM((rows, width), F32)
    square_plain = pl.BlockSpec((rows, rows), lambda j: (0, 0))
    joining = pltpu.VMEM((rows, block), BF16 if size % 16 == 0 else F32)
    product = 2 * rows * width * block

    def call(name, kernel, cost, ins, outs, scratch, mebibytes=32, aliases=None, steps=None):
        return pl.pallas_call(
            kernel,
            grid=(steps or width // block,),
            in_specs=[spec for spec, _ in ins],
            out_specs=[spec for spec, _ in outs],
            out_shape=[shape for _, shape in outs],
            scratch_shapes=scratch,
            input_output_aliases=aliases or {},
            compiler_params=params(mebibytes),
            cost_estimate=pl.CostEstimate(
                flops=int(cost[0] * product),
                bytes_accessed=cost[1] * rows * width * 2,
                transcendentals=0,
            ),
            name=name,
        )(*(value for _, value in ins))

    gains = (gain, norm_gain)
    value_in, gate_in, out_in = (weight, w_value), (weight, w_gate), (weight, w_out)
    r_in = (square, r_factor)
    slots_out = [*zip(slots, slot_shapes)]
    every = range(1, count)

    def first(tick, mebibytes=32):
        return call(
            f"first_{tick}",
            functools.partial(first_kernel, count),
            (2, 4),
            [(x_at[tick], saved_inputs), gains, value_in, r_in],
            slots_out,
            [column, wide],
            mebibytes,
        )

    def grads(tick, incoming):
        *parts, factor = call(
            f"grads_{tick}",
            functools.partial(grad_kernel, count, len(incoming)),
            (2, 8),
            [(x_at[tick], saved_inputs), gains, gate_in, out_in, *incoming],
            [*slots_out, (cut, exact)],
            [column, wide],
        )
        return parts, factor

    def mix(name, parts, transposed):
        return call(
            name,
            functools.partial(mix_kernel, count, transposed),
            (1, 2),
            [(square_plain, matrix), *zip(slots, parts)],
            slots_out,
            [],
        )

    def back(tick, mixed, factor):
        return call(
            f"back_{tick}",
            functools.partial(back_kernel, count),
            (1, 6),
            [gate_in, (cut, factor), *zip(slots, mixed)],
            [(cut, exact)],
            [joining],
        )[0]

    def result(tick, gate_part, folded, incoming, stacked):
        ins = [(x_at[tick], saved_inputs), gains, value_in, r_in, (cut, gate_part)]
        ins += [*zip(slots, folded), *incoming]
        outs = [(x_at[tick], output)]
        aliases = {}
        if stacked is None:
            outs.append((whole, plain))
        else:
            ins.append((anywhere, stacked))
            aliases = {len(ins) - 1: 0}
        return call(
            f"result_{tick}",
            functools.partial(result_kernel, count, len(incoming)),
            (3, 8),
            ins,
            outs,
            [joining, full, column],
            aliases=aliases,
        )

    first_0 = Exchange(first(0, 60)).send(every)
    (matrix,) = call(
        "matrix",
        functools.partial(matrix_kernel, count),
        (0.3, 1),
        [(small, l_factor)],
        [(square_plain, jax.ShapeDtypeStruct((rows, rows), BF16))],
        [],
        steps=1,
    )
    parts, factor_0 = grads(0, [(cut3, arrived_grad)])
    grad_0 = Exchange(parts).send(every)
    mix_0 = Exchange(mix("mix_0", first_0.all(), False)).send(every)
    fold_0 = Exchange(mix("fold_0", grad_0.all(), True)).send(every)
    gate_0 = back(0, mix_0.all(), factor_0)
    first_1 = Exchange(first(1))
    gate_0, first_1.parts[0] = lax.optimization_barrier((gate_0, first_1.parts[0]))
    first_1.send(every)
    stacked, result_0 = result(0, gate_0, fold_0.all(), [(whole3, arrived_grad)], None)
    result_0 = tied(result_0, [(first_1, slot) for slot in every[: min(4, count // 2)]])
    passed = lax.ppermute(result_0, "pipe", [(s, s - 1) for s in range(1, pipe)])
    mix_1 = Exchange(mix("mix_1", first_1.all(), False)).send(every)
    parts, factor_1 = grads(1, [(cut, passed), (cut3, loss_grad)])
    grad_1 = Exchange(parts).send(every)
    fold_1 = Exchange(mix("fold_1", grad_1.all(), True)).send(every)
    gate_1 = back(1, mix_1.all(), factor_1)
    incoming = [(whole, passed), (whole3, loss_grad)]
    return result(1, gate_1, fold_1.all(), incoming, stacked)[0]


def solution(mesh):
    placed = (
        P("pipe", None, "seq", None),
        P("pipe", "seq", None),
        P(None, "seq", None),
        P("pipe", None),
        P("pipe", None, None),
        P("pipe", None, None),
        P("pipe", None, None),
        P("pipe", "seq", None),
        P("pipe", "seq", None),
    )
    return jax.shard_map(
        local, mesh=mesh, in_specs=placed, out_specs=P("pipe", None, "seq", None), check_vma=False
    )
```

profile of v0, /device:TPU:2, one launch (start us, length us, event | category | flops | bytes accessed | tf_op | source)
XLA Modules:
  0.0 164.8 jit_solution(14405189029807095964)
XLA Ops:
  0.0 5.1 %first_0.1 = (bf16[32,1536]{1,0:T(8,128)(2,1)}, bf16[32,1536]{1,0:T(8,128)(2,1)}, bf16[32,1536]{1,0:T(8,128)(2,1)}, bf16[32,1536]{1,0:T(8,128)(2,1)}, bf16[32,15...) custom-call(bf16[1,2,256,1536]{3,2,1,0:T(8,128)(2,1)} %x_ref.11, ...), custom_call_target="tpu_custom_call" | custom-call | flops 603979776 | bytes 3145728 | tf_op jit(solution)/shard_map/first_0/pallas_call | solution.py:232
  5.2 1.6 collective-permute-start
  6.7 1.6 collective-permute-start.1
  8.7 2.6 %collective-permute-start.3 = (bf16[32,1536]{1,0:T(8,128)(2,1)}, bf16[32,1536]{1,0:T(8,128)(2,1)S(1)}, u32[]{:S(2)}, u32[]{:S(2)}) collective-permute-start(bf16[32,1536]{1,0:T(8,128)(2,1)} %get-tuple-element.84), channel_id=1, source_target_pairs={{0,4},{1,5},{2,6},{3,7},{4,0},{5,1},{6,2},{7,3},{8,12},{9,13},{10,... | collective-permute-start | bytes 294920 | tf_op jit(solution)/shard_map/ppermute | solution.py:179
  11.3 1.3 collective-permute-start.4
  12.6 3.6 %collective-permute-start.5 = (bf16[32,1536]{1,0:T(8,128)(2,1)}, bf16[32,1536]{1,0:T(8,128)(2,1)S(1)}, u32[]{:S(2)}, u32[]{:S(2)}) collective-permute-start(bf16[32,1536]{1,0:T(8,128)(2,1)} %get-tuple-element.86), channel_id=1, source_target_pairs={{0,6},{1,7},{2,4},{3,5},{4,2},{5,3},{6,0},{7,1},{8,14},{9,15},{10,... | collective-permute-start | bytes 294920 | tf_op jit(solution)/shard_map/ppermute | solution.py:179
  16.4 1.3 copy-done.3
  17.6 1.1 copy-done.5
  18.8 3.2 %grads_0.1 = (bf16[32,1536]{1,0:T(8,128)(2,1)S(1)}, bf16[32,1536]{1,0:T(8,128)(2,1)S(1)}, bf16[32,1536]{1,0:T(8,128)(2,1)S(1)}, bf16[32,1536]{1,0:T(8,128)(2,1)S...) custom-call(bf16[1,2,256,1536]{3,2,1,0:T(8,128)(2,1)S(1)} %copy-done, ...), custom_call_target="tpu_custom_call" | custom-call | flops 603979776 | bytes 6291456 | tf_op jit(solution)/shard_map/grads_0/pallas_call | solution.py:232
  22.0 2.1 %collective-permute-start.14 = (bf16[32,1536]{1,0:T(8,128)(2,1)S(1)}, bf16[32,1536]{1,0:T(8,128)(2,1)S(1)}, u32[]{:S(2)}, u32[]{:S(2)}) collective-permute-start(bf16[32,1536]{1,0:T(8,128)(2,1)S(1)} %get-tuple-element.99), channel_id=1, source_target_pairs={{0,1},{1,0},{2,3},{3,2},{4,5},{5,4},{6,7},{7,6},{8,9},{9,8},{10,11... | collective-permute-start | bytes 294920 | tf_op jit(solution)/shard_map/ppermute | solution.py:179
  24.1 2.6 %collective-permute-done.4.refs_5_ = bf16[32,1536]{1,0:T(8,128)(2,1)S(1)} collective-permute-done((bf16[32,1536]{1,0:T(8,128)(2,1)}, bf16[32,1536]{1,0:T(8,128)(2,1)S(1)}, u32[]{:S(2)}, u32[]{:S(2)}) %collective-permute-start.4) | collective-permute-done | bytes 98336 | tf_op jit(solution)/shard_map/ppermute | solution.py:179
  26.8 3.5 %collective-permute-start.17 = (bf16[32,1536]{1,0:T(8,128)(2,1)S(1)}, bf16[32,1536]{1,0:T(8,128)(2,1)S(1)}, u32[]{:S(2)}, u32[]{:S(2)}) collective-permute-start(bf16[32,1536]{1,0:T(8,128)(2,1)S(1)} %get-tuple-element.102), channel_id=1, source_target_pairs={{0,4},{1,5},{2,6},{3,7},{4,0},{5,1},{6,2},{7,3},{8,12},{9,13},{10,... | collective-permute-start | bytes 294920 | tf_op jit(solution)/shard_map/ppermute | solution.py:179
  30.3 2.7 %collective-permute-start.18 = (bf16[32,1536]{1,0:T(8,128)(2,1)S(1)}, bf16[32,1536]{1,0:T(8,128)(2,1)S(1)}, u32[]{:S(2)}, u32[]{:S(2)}) collective-permute-start(bf16[32,1536]{1,0:T(8,128)(2,1)S(1)} %get-tuple-element.103), channel_id=1, source_target_pairs={{0,5},{1,4},{2,7},{3,6},{4,1},{5,0},{6,3},{7,2},{8,13},{9,12},{10,... | collective-permute-start | bytes 294920 | tf_op jit(solution)/shard_map/ppermute | solution.py:179
  33.0 0.8 collective-permute-start.19
  34.0 4.9 %collective-permute-start.20 = (bf16[32,1536]{1,0:T(8,128)(2,1)S(1)}, bf16[32,1536]{1,0:T(8,128)(2,1)S(1)}, u32[]{:S(2)}, u32[]{:S(2)}) collective-permute-start(bf16[32,1536]{1,0:T(8,128)(2,1)S(1)} %get-tuple-element.105), channel_id=1, source_target_pairs={{0,7},{1,6},{2,5},{3,4},{4,3},{5,2},{6,1},{7,0},{8,15},{9,14},{10,... | collective-permute-start | bytes 294920 | tf_op jit(solution)/shard_map/ppermute | solution.py:179
  38.9 1.2 mix_0.1
  40.2 4.4 %collective-permute-done.17.refs_4_ = bf16[32,1536]{1,0:T(8,128)(2,1)S(1)} collective-permute-done((bf16[32,1536]{1,0:T(8,128)(2,1)S(1)}, bf16[32,1536]{1,0:T(8,128)(2,1)S(1)}, u32[]{:S(2)}, u32[]{:S(2)}) %collective-permute-start.17) | collective-permute-done | bytes 98336 | tf_op jit(solution)/shard_map/ppermute | solution.py:179
  44.7 2.7 %collective-permute-done.18.refs_5_ = bf16[32,1536]{1,0:T(8,128)(2,1)S(1)} collective-permute-done((bf16[32,1536]{1,0:T(8,128)(2,1)S(1)}, bf16[32,1536]{1,0:T(8,128)(2,1)S(1)}, u32[]{:S(2)}, u32[]{:S(2)}) %collective-permute-start.18) | collective-permute-done | bytes 98336 | tf_op jit(solution)/shard_map/ppermute | solution.py:179
  47.4 2.2 %collective-permute-start.12 = (bf16[32,1536]{1,0:T(8,128)(2,1)S(1)}, bf16[32,1536]{1,0:T(8,128)(2,1)S(1)}, u32[]{:S(2)}, u32[]{:S(2)}) collective-permute-start(bf16[32,1536]{1,0:T(8,128)(2,1)S(1)} %get-tuple-element.94), channel_id=1, source_target_pairs={{0,6},{1,7},{2,4},{3,5},{4,2},{5,3},{6,0},{7,1},{8,14},{9,15},{10,... | collective-permute-start | bytes 294920 | tf_op jit(solution)/shard_map/ppermute | solution.py:179
  49.6 1.9 %collective-permute-start.13 = (bf16[32,1536]{1,0:T(8,128)(2,1)S(1)}, bf16[32,1536]{1,0:T(8,128)(2,1)S(1)}, u32[]{:S(2)}, u32[]{:S(2)}) collective-permute-start(bf16[32,1536]{1,0:T(8,128)(2,1)S(1)} %get-tuple-element.95), channel_id=1, source_target_pairs={{0,7},{1,6},{2,5},{3,4},{4,3},{5,2},{6,1},{7,0},{8,15},{9,14},{10,... | collective-permute-start | bytes 294920 | tf_op jit(solution)/shard_map/ppermute | solution.py:179
  51.4 1.2 collective-permute-start.7
  52.7 1.3 fold_0.1
  54.0 4.2 %collective-permute-done.10.refs_4_ = bf16[32,1536]{1,0:T(8,128)(2,1)S(1)} collective-permute-done((bf16[32,1536]{1,0:T(8,128)(2,1)S(1)}, bf16[32,1536]{1,0:T(8,128)(2,1)S(1)}, u32[]{:S(2)}, u32[]{:S(2)}) %collective-permute-start.10) | collective-permute-done | bytes 98336 | tf_op jit(solution)/shard_map/ppermute | solution.py:179
  58.6 2.5 %collective-permute-done.11.refs_5_ = bf16[32,1536]{1,0:T(8,128)(2,1)S(1)} collective-permute-done((bf16[32,1536]{1,0:T(8,128)(2,1)S(1)}, bf16[32,1536]{1,0:T(8,128)(2,1)S(1)}, u32[]{:S(2)}, u32[]{:S(2)}) %collective-permute-start.11) | collective-permute-done | bytes 98336 | tf_op jit(solution)/shard_map/ppermute | solution.py:179
  61.9 3.3 %collective-permute-start.22 = (bf16[32,1536]{1,0:T(8,128)(2,1)S(1)}, bf16[32,1536]{1,0:T(8,128)(2,1)S(1)}, u32[]{:S(2)}, u32[]{:S(2)}) collective-permute-start(bf16[32,1536]{1,0:T(8,128)(2,1)S(1)} %get-tuple-element.108), channel_id=1, source_target_pairs={{0,2},{1,3},{2,0},{3,1},{4,6},{5,7},{6,4},{7,5},{8,10},{9,11},{10,... | collective-permute-start | bytes 294920 | tf_op jit(solution)/shard_map/ppermute | solution.py:179
  65.5 2.9 %collective-permute-start.24 = (bf16[32,1536]{1,0:T(8,128)(2,1)S(1)}, bf16[32,1536]{1,0:T(8,128)(2,1)S(1)}, u32[]{:S(2)}, u32[]{:S(2)}) collective-permute-start(bf16[32,1536]{1,0:T(8,128)(2,1)S(1)} %get-tuple-element.110), channel_id=1, source_target_pairs={{0,4},{1,5},{2,6},{3,7},{4,0},{5,1},{6,2},{7,3},{8,12},{9,13},{10,... | collective-permute-start | bytes 294920 | tf_op jit(solution)/shard_map/ppermute | solution.py:179
  69.0 3.5 %collective-permute-start.26 = (bf16[32,1536]{1,0:T(8,128)(2,1)S(1)}, bf16[32,1536]{1,0:T(8,128)(2,1)S(1)}, u32[]{:S(2)}, u32[]{:S(2)}) collective-permute-start(bf16[32,1536]{1,0:T(8,128)(2,1)S(1)} %get-tuple-element.112), channel_id=1, source_target_pairs={{0,6},{1,7},{2,4},{3,5},{4,2},{5,3},{6,0},{7,1},{8,14},{9,15},{10,... | collective-permute-start | bytes 294920 | tf_op jit(solution)/shard_map/ppermute | solution.py:179
  73.2 2.9 %first_1.1 = (bf16[32,1536]{1,0:T(8,128)(2,1)S(1)}, bf16[32,1536]{1,0:T(8,128)(2,1)S(1)}, bf16[32,1536]{1,0:T(8,128)(2,1)S(1)}, bf16[32,1536]{1,0:T(8,128)(2,1)S...) custom-call(bf16[1,2,256,1536]{3,2,1,0:T(8,128)(2,1)S(1)} %copy-done, ...), custom_call_target="tpu_custom_call" | custom-call | flops 603979776 | bytes 3145728 | tf_op jit(solution)/shard_map/first_1/pallas_call | solution.py:232
  76.1 1.3 collective-permute-start.28
  77.4 1.0 collective-permute-done.24.refs_4_
  78.4 3.7 %collective-permute-done.25.refs_5_ = bf16[32,1536]{1,0:T(8,128)(2,1)S(1)} collective-permute-done((bf16[32,1536]{1,0:T(8,128)(2,1)S(1)}, bf16[32,1536]{1,0:T(8,128)(2,1)S(1)}, u32[]{:S(2)}, u32[]{:S(2)}) %collective-permute-start.25) | collective-permute-done | bytes 98336 | tf_op jit(solution)/shard_map/ppermute | solution.py:179
  82.7 3.0 %collective-permute-start.31 = (bf16[32,1536]{1,0:T(8,128)(2,1)S(1)}, bf16[32,1536]{1,0:T(8,128)(2,1)S(1)}, u32[]{:S(2)}, u32[]{:S(2)}) collective-permute-start(bf16[32,1536]{1,0:T(8,128)(2,1)S(1)} %get-tuple-element.118), channel_id=1, source_target_pairs={{0,4},{1,5},{2,6},{3,7},{4,0},{5,1},{6,2},{7,3},{8,12},{9,13},{10,... | collective-permute-start | bytes 294920 | tf_op jit(solution)/shard_map/ppermute | solution.py:179
  85.6 1.7 %back_0.1.back_ref = f32[256,1536]{1,0:T(8,128)S(1)} custom-call(bf16[1,384,1536]{2,1,0:T(8,128)(2,1)S(1)} %copy-done.2, f32[256,1536]{1,0:T(8,128)S(1)} %get-tuple-element.79.factor_ref, bf16[32,1536]{1,0:T(8,128)(2,1)S(1)} %get-tuple-element.88.refs_0_, bf16[32,1536]{1,0:T(8,128)(2,1)S(1)} %collective-permute-done.7.refs_1_, ...), custom_call_target="tpu_custom_call" | custom-call | flops 301989888 | bytes 4718592 | tf_op jit(solution)/shard_map/back_0/pallas_call | solution.py:232
  87.4 4.2 %result_0.1 = (bf16[1,2,256,1536]{3,2,1,0:T(8,128)(2,1)}, bf16[256,1536]{1,0:T(8,128)(2,1)S(1)}) custom-call(bf16[1,2,256,1536]{3,2,1,0:T(8,128)(2,1)S(1)} %copy-done, f32[1,1536]{1,0:T(1,128)S(1)} %copy-done.9, bf16[1,384,1536]{2,1,0:T(8,128)(2,1)S(1)} %copy-done.1, bf16[1,256,256]{2,1,0:T(8,128)(2,1)S(1)} %copy-done.8, f32[256,1536]{1,0:T(8,128)S(1)} %back_0.1.back_ref, ...), custom_call_target="tpu_custom_call" | custom-call | flops 905969664 | bytes 6291456 | tf_op jit(solution)/shard_map/result_0/pallas_call | solution.py:232
  91.6 1.9 %collective-permute-start.32 = (bf16[256,1536]{1,0:T(8,128)(2,1)S(1)}, bf16[256,1536]{1,0:T(8,128)(2,1)S(1)}, u32[]{:S(2)}, u32[]{:S(2)}) collective-permute-start(bf16[256,1536]{1,0:T(8,128)(2,1)S(1)} %get-tuple-element.119), channel_id=1, source_target_pairs={{8,0},{16,8},{24,16},{9,1},{17,9},{25,17},{10,2},{18,10},{26,18},{... | collective-permute-start | bytes 2359304 | tf_op jit(solution)/shard_map/ppermute | solution.py:337
  93.6 2.2 %collective-permute-start.33 = (bf16[32,1536]{1,0:T(8,128)(2,1)S(1)}, bf16[32,1536]{1,0:T(8,128)(2,1)S(1)}, u32[]{:S(2)}, u32[]{:S(2)}) collective-permute-start(bf16[32,1536]{1,0:T(8,128)(2,1)S(1)} %get-tuple-element.125), channel_id=1, source_target_pairs={{0,5},{1,4},{2,7},{3,6},{4,1},{5,0},{6,3},{7,2},{8,13},{9,12},{10,... | collective-permute-start | bytes 294920 | tf_op jit(solution)/shard_map/ppermute | solution.py:179
  95.8 1.6 collective-permute-start.34
  97.3 3.3 %collective-permute-start.35 = (bf16[32,1536]{1,0:T(8,128)(2,1)S(1)}, bf16[32,1536]{1,0:T(8,128)(2,1)S(1)}, u32[]{:S(2)}, u32[]{:S(2)}) collective-permute-start(bf16[32,1536]{1,0:T(8,128)(2,1)S(1)} %get-tuple-element.127), channel_id=1, source_target_pairs={{0,7},{1,6},{2,5},{3,4},{4,3},{5,2},{6,1},{7,0},{8,15},{9,14},{10,... | collective-permute-start | bytes 294920 | tf_op jit(solution)/shard_map/ppermute | solution.py:179
  100.6 2.4 %collective-permute-done.32.refs_0_.refs_8_ = bf16[256,1536]{1,0:T(8,128)(2,1)S(1)} collective-permute-done((bf16[256,1536]{1,0:T(8,128)(2,1)S(1)}, bf16[256,1536]{1,0:T(8,128)(2,1)S(1)}, u32[]{:S(2)}, u32[]{:S(2)}) %collective-permute-start.32) | collective-permute-done | bytes 786464 | tf_op jit(solution)/shard_map/ppermute | solution.py:337
  103.1 3.3 %grads_1.1 = (bf16[32,1536]{1,0:T(8,128)(2,1)S(1)}, bf16[32,1536]{1,0:T(8,128)(2,1)S(1)}, bf16[32,1536]{1,0:T(8,128)(2,1)S(1)}, bf16[32,1536]{1,0:T(8,128)(2,1)S...) custom-call(bf16[1,2,256,1536]{3,2,1,0:T(8,128)(2,1)S(1)} %copy-done, ...), custom_call_target="tpu_custom_call" | custom-call | flops 603979776 | bytes 6291456 | tf_op jit(solution)/shard_map/grads_1/pallas_call | solution.py:232
  106.4 2.7 %collective-permute-start.43 = (bf16[32,1536]{1,0:T(8,128)(2,1)S(1)}, bf16[32,1536]{1,0:T(8,128)(2,1)S(1)}, u32[]{:S(2)}, u32[]{:S(2)}) collective-permute-start(bf16[32,1536]{1,0:T(8,128)(2,1)S(1)} %get-tuple-element.137), channel_id=1, source_target_pairs={{0,1},{1,0},{2,3},{3,2},{4,5},{5,4},{6,7},{7,6},{8,9},{9,8},{10,11... | collective-permute-start | bytes 294920 | tf_op jit(solution)/shard_map/ppermute | solution.py:179
  109.1 1.5 collective-permute-start.45
  110.6 1.5 collective-permute-start.46
  112.2 2.8 %collective-permute-start.47 = (bf16[32,1536]{1,0:T(8,128)(2,1)S(1)}, bf16[32,1536]{1,0:T(8,128)(2,1)S(1)}, u32[]{:S(2)}, u32[]{:S(2)}) collective-permute-start(bf16[32,1536]{1,0:T(8,128)(2,1)S(1)} %get-tuple-element.141), channel_id=1, source_target_pairs={{0,5},{1,4},{2,7},{3,6},{4,1},{5,0},{6,3},{7,2},{8,13},{9,12},{10,... | collective-permute-start | bytes 294920 | tf_op jit(solution)/shard_map/ppermute | solution.py:179
  115.0 1.1 collective-permute-start.48
  116.1 2.2 %collective-permute-start.49 = (bf16[32,1536]{1,0:T(8,128)(2,1)S(1)}, bf16[32,1536]{1,0:T(8,128)(2,1)S(1)}, u32[]{:S(2)}, u32[]{:S(2)}) collective-permute-start(bf16[32,1536]{1,0:T(8,128)(2,1)S(1)} %get-tuple-element.143), channel_id=1, source_target_pairs={{0,7},{1,6},{2,5},{3,4},{4,3},{5,2},{6,1},{7,0},{8,15},{9,14},{10,... | collective-permute-start | bytes 294920 | tf_op jit(solution)/shard_map/ppermute | solution.py:179
  118.3 1.2 mix_1.1
  119.6 2.0 %collective-permute-start.36 = (bf16[32,1536]{1,0:T(8,128)(2,1)S(1)}, bf16[32,1536]{1,0:T(8,128)(2,1)S(1)}, u32[]{:S(2)}, u32[]{:S(2)}) collective-permute-start(bf16[32,1536]{1,0:T(8,128)(2,1)S(1)} %get-tuple-element.129), channel_id=1, source_target_pairs={{0,1},{1,0},{2,3},{3,2},{4,5},{5,4},{6,7},{7,6},{8,9},{9,8},{10,11... | collective-permute-start | bytes 294920 | tf_op jit(solution)/shard_map/ppermute | solution.py:179
  121.6 3.1 %collective-permute-done.46.refs_4_ = bf16[32,1536]{1,0:T(8,128)(2,1)S(1)} collective-permute-done((bf16[32,1536]{1,0:T(8,128)(2,1)S(1)}, bf16[32,1536]{1,0:T(8,128)(2,1)S(1)}, u32[]{:S(2)}, u32[]{:S(2)}) %collective-permute-start.46) | collective-permute-done | bytes 98336 | tf_op jit(solution)/shard_map/ppermute | solution.py:179
  124.7 2.5 %collective-permute-done.47.refs_5_ = bf16[32,1536]{1,0:T(8,128)(2,1)S(1)} collective-permute-done((bf16[32,1536]{1,0:T(8,128)(2,1)S(1)}, bf16[32,1536]{1,0:T(8,128)(2,1)S(1)}, u32[]{:S(2)}, u32[]{:S(2)}) %collective-permute-start.47) | collective-permute-done | bytes 98336 | tf_op jit(solution)/shard_map/ppermute | solution.py:179
  127.5 1.7 %collective-permute-start.39 = (bf16[32,1536]{1,0:T(8,128)(2,1)S(1)}, bf16[32,1536]{1,0:T(8,128)(2,1)S(1)}, u32[]{:S(2)}, u32[]{:S(2)}) collective-permute-start(bf16[32,1536]{1,0:T(8,128)(2,1)S(1)} %get-tuple-element.132), channel_id=1, source_target_pairs={{0,4},{1,5},{2,6},{3,7},{4,0},{5,1},{6,2},{7,3},{8,12},{9,13},{10,... | collective-permute-start | bytes 294920 | tf_op jit(solution)/shard_map/ppermute | solution.py:179
  129.2 3.8 %collective-permute-start.40 = (bf16[32,1536]{1,0:T(8,128)(2,1)S(1)}, bf16[32,1536]{1,0:T(8,128)(2,1)S(1)}, u32[]{:S(2)}, u32[]{:S(2)}) collective-permute-start(bf16[32,1536]{1,0:T(8,128)(2,1)S(1)} %get-tuple-element.133), channel_id=1, source_target_pairs={{0,5},{1,4},{2,7},{3,6},{4,1},{5,0},{6,3},{7,2},{8,13},{9,12},{10,... | collective-permute-start | bytes 294920 | tf_op jit(solution)/shard_map/ppermute | solution.py:179
  133.0 1.4 fold_1.1
  134.3 4.0 %collective-permute-start.41 = (bf16[32,1536]{1,0:T(8,128)(2,1)S(1)}, bf16[32,1536]{1,0:T(8,128)(2,1)S(1)}, u32[]{:S(2)}, u32[]{:S(2)}) collective-permute-start(bf16[32,1536]{1,0:T(8,128)(2,1)S(1)} %get-tuple-element.134), channel_id=1, source_target_pairs={{0,6},{1,7},{2,4},{3,5},{4,2},{5,3},{6,0},{7,1},{8,14},{9,15},{10,... | collective-permute-start | bytes 294920 | tf_op jit(solution)/shard_map/ppermute | solution.py:179
  138.9 0.9 collective-permute-start.50
  139.9 2.4 %collective-permute-done.40.refs_5_ = bf16[32,1536]{1,0:T(8,128)(2,1)S(1)} collective-permute-done((bf16[32,1536]{1,0:T(8,128)(2,1)S(1)}, bf16[32,1536]{1,0:T(8,128)(2,1)S(1)}, u32[]{:S(2)}, u32[]{:S(2)}) %collective-permute-start.40) | collective-permute-done | bytes 98336 | tf_op jit(solution)/shard_map/ppermute | solution.py:179
  142.4 4.6 %collective-permute-start.53 = (bf16[32,1536]{1,0:T(8,128)(2,1)S(1)}, bf16[32,1536]{1,0:T(8,128)(2,1)S(1)}, u32[]{:S(2)}, u32[]{:S(2)}) collective-permute-start(bf16[32,1536]{1,0:T(8,128)(2,1)S(1)} %get-tuple-element.148), channel_id=1, source_target_pairs={{0,4},{1,5},{2,6},{3,7},{4,0},{5,1},{6,2},{7,3},{8,12},{9,13},{10,... | collective-permute-start | bytes 294920 | tf_op jit(solution)/shard_map/ppermute | solution.py:179
  147.0 4.3 %collective-permute-start.54 = (bf16[32,1536]{1,0:T(8,128)(2,1)S(1)}, bf16[32,1536]{1,0:T(8,128)(2,1)S(1)}, u32[]{:S(2)}, u32[]{:S(2)}) collective-permute-start(bf16[32,1536]{1,0:T(8,128)(2,1)S(1)} %get-tuple-element.149), channel_id=1, source_target_pairs={{0,5},{1,4},{2,7},{3,6},{4,1},{5,0},{6,3},{7,2},{8,13},{9,12},{10,... | collective-permute-start | bytes 294920 | tf_op jit(solution)/shard_map/ppermute | solution.py:179
  151.4 1.8 %collective-permute-start.55 = (bf16[32,1536]{1,0:T(8,128)(2,1)S(1)}, bf16[32,1536]{1,0:T(8,128)(2,1)S(1)}, u32[]{:S(2)}, u32[]{:S(2)}) collective-permute-start(bf16[32,1536]{1,0:T(8,128)(2,1)S(1)} %get-tuple-element.150), channel_id=1, source_target_pairs={{0,6},{1,7},{2,4},{3,5},{4,2},{5,3},{6,0},{7,1},{8,14},{9,15},{10,... | collective-permute-start | bytes 294920 | tf_op jit(solution)/shard_map/ppermute | solution.py:179
  153.1 1.7 %collective-permute-start.56 = (bf16[32,1536]{1,0:T(8,128)(2,1)S(1)}, bf16[32,1536]{1,0:T(8,128)(2,1)S(1)}, u32[]{:S(2)}, u32[]{:S(2)}) collective-permute-start(bf16[32,1536]{1,0:T(8,128)(2,1)S(1)} %get-tuple-element.151), channel_id=1, source_target_pairs={{0,7},{1,6},{2,5},{3,4},{4,3},{5,2},{6,1},{7,0},{8,15},{9,14},{10,... | collective-permute-start | bytes 294920 | tf_op jit(solution)/shard_map/ppermute | solution.py:179
  154.8 1.7 %back_1.1.back_ref = f32[256,1536]{1,0:T(8,128)S(1)} custom-call(bf16[1,384,1536]{2,1,0:T(8,128)(2,1)S(1)} %copy-done.2, f32[256,1536]{1,0:T(8,128)S(1)} %get-tuple-element.120.factor_ref, bf16[32,1536]{1,0:T(8,128)(2,1)S(1)} %get-tuple-element.128.refs_0_, bf16[32,1536]{1,0:T(8,128)(2,1)S(1)} %collective-permute-done.36.refs_1_, ...), custom_call_target="tpu_custom_call" | custom-call | flops 301989888 | bytes 4718592 | tf_op jit(solution)/shard_map/back_1/pallas_call | solution.py:232
  156.6 2.9 %collective-permute-done.54.refs_5_ = bf16[32,1536]{1,0:T(8,128)(2,1)S(1)} collective-permute-done((bf16[32,1536]{1,0:T(8,128)(2,1)S(1)}, bf16[32,1536]{1,0:T(8,128)(2,1)S(1)}, u32[]{:S(2)}, u32[]{:S(2)}) %collective-permute-start.54) | collective-permute-done | bytes 98336 | tf_op jit(solution)/shard_map/ppermute | solution.py:179
  159.5 1.1 collective-permute-done.56.refs_7_
  160.5 4.2 %result_1.1 = bf16[1,2,256,1536]{3,2,1,0:T(8,128)(2,1)} custom-call(bf16[1,2,256,1536]{3,2,1,0:T(8,128)(2,1)S(1)} %copy-done, f32[1,1536]{1,0:T(1,128)S(1)} %copy-done.9, bf16[1,384,1536]{2,1,0:T(8,128)(2,1)S(1)} %copy-done.1, bf16[1,256,256]{2,1,0:T(8,128)(2,1)S(1)} %copy-done.8, f32[256,1536]{1,0:T(8,128)S(1)} %back_1.1.back_ref, ...), custom_call_target="tpu_custom_call", output_to_operand_aliasing={{}: (15, {})} | custom-call | flops 905969664 | bytes 6291456 | tf_op jit(solution)/shard_map/result_1/pallas_call | solution.py:232
  (87 shorter events, 5.6 us)
Async XLA Ops:
  0.0 16.4 %copy-start.9 = (f32[1,1536]{1,0:T(1,128)S(1)}, f32[1,1536]{1,0:T(1,128)}, u32[]{:S(2)}) copy-start(f32[1,1536]{1,0:T(1,128)} %gain_ref.11) | copy-start | bytes 18436
  0.0 16.4 %copy-start = (bf16[1,2,256,1536]{3,2,1,0:T(8,128)(2,1)S(1)}, bf16[1,2,256,1536]{3,2,1,0:T(8,128)(2,1)}, u32[]{:S(2)}) copy-start(bf16[1,2,256,1536]{3,2,1,0:T(8,128)(2,1)} %x_ref.11) | copy-start | bytes 4718596
  0.0 16.4 %copy-start.2 = (bf16[1,384,1536]{2,1,0:T(8,128)(2,1)S(1)}, bf16[1,384,1536]{2,1,0:T(8,128)(2,1)}, u32[]{:S(2)}) copy-start(bf16[1,384,1536]{2,1,0:T(8,128)(2,1)} %w_gate_ref.7) | copy-start | bytes 3538948
  5.2 7.4 %collective-permute-start = (bf16[32,1536]{1,0:T(8,128)(2,1)}, bf16[32,1536]{1,0:T(8,128)(2,1)S(1)}, u32[]{:S(2)}, u32[]{:S(2)}) collective-permute-start(bf16[32,1536]{1,0:T(8,128)(2,1)} %get-tuple-element.81), channel_id=1, source_target_pairs={{0,1},{1,0},{2,3},{3,2},{4,5},{5,4},{6,7},{7,6},{8,9},{9,8},{10,11... | collective-permute-start | bytes 294920 | tf_op jit(solution)/shard_map/ppermute | solution.py:179
  6.7 9.5 %collective-permute-start.1 = (bf16[32,1536]{1,0:T(8,128)(2,1)}, bf16[32,1536]{1,0:T(8,128)(2,1)S(1)}, u32[]{:S(2)}, u32[]{:S(2)}) collective-permute-start(bf16[32,1536]{1,0:T(8,128)(2,1)} %get-tuple-element.82), channel_id=1, source_target_pairs={{0,2},{1,3},{2,0},{3,1},{4,6},{5,7},{6,4},{7,5},{8,10},{9,11},{10,... | collective-permute-start | bytes 294920 | tf_op jit(solution)/shard_map/ppermute | solution.py:179
  8.3 13.7 %collective-permute-start.2 = (bf16[32,1536]{1,0:T(8,128)(2,1)}, bf16[32,1536]{1,0:T(8,128)(2,1)S(1)}, u32[]{:S(2)}, u32[]{:S(2)}) collective-permute-start(bf16[32,1536]{1,0:T(8,128)(2,1)} %get-tuple-element.83), channel_id=1, source_target_pairs={{0,3},{1,2},{2,1},{3,0},{4,7},{5,6},{6,5},{7,4},{8,11},{9,10},{10,... | collective-permute-start | bytes 294920 | tf_op jit(solution)/shard_map/ppermute | solution.py:179
  8.7 15.4 %collective-permute-start.3 = (bf16[32,1536]{1,0:T(8,128)(2,1)}, bf16[32,1536]{1,0:T(8,128)(2,1)S(1)}, u32[]{:S(2)}, u32[]{:S(2)}) collective-permute-start(bf16[32,1536]{1,0:T(8,128)(2,1)} %get-tuple-element.84), channel_id=1, source_target_pairs={{0,4},{1,5},{2,6},{3,7},{4,0},{5,1},{6,2},{7,3},{8,12},{9,13},{10,... | collective-permute-start | bytes 294920 | tf_op jit(solution)/shard_map/ppermute | solution.py:179
  11.3 15.4 %collective-permute-start.4 = (bf16[32,1536]{1,0:T(8,128)(2,1)}, bf16[32,1536]{1,0:T(8,128)(2,1)S(1)}, u32[]{:S(2)}, u32[]{:S(2)}) collective-permute-start(bf16[32,1536]{1,0:T(8,128)(2,1)} %get-tuple-element.85), channel_id=1, source_target_pairs={{0,5},{1,4},{2,7},{3,6},{4,1},{5,0},{6,3},{7,2},{8,13},{9,12},{10,... | collective-permute-start | bytes 294920 | tf_op jit(solution)/shard_map/ppermute | solution.py:179
  12.6 14.2 %collective-permute-start.5 = (bf16[32,1536]{1,0:T(8,128)(2,1)}, bf16[32,1536]{1,0:T(8,128)(2,1)S(1)}, u32[]{:S(2)}, u32[]{:S(2)}) collective-permute-start(bf16[32,1536]{1,0:T(8,128)(2,1)} %get-tuple-element.86), channel_id=1, source_target_pairs={{0,6},{1,7},{2,4},{3,5},{4,2},{5,3},{6,0},{7,1},{8,14},{9,15},{10,... | collective-permute-start | bytes 294920 | tf_op jit(solution)/shard_map/ppermute | solution.py:179
  16.2 14.1 %collective-permute-start.6 = (bf16[32,1536]{1,0:T(8,128)(2,1)}, bf16[32,1536]{1,0:T(8,128)(2,1)S(1)}, u32[]{:S(2)}, u32[]{:S(2)}) collective-permute-start(bf16[32,1536]{1,0:T(8,128)(2,1)} %get-tuple-element.87), channel_id=1, source_target_pairs={{0,7},{1,6},{2,5},{3,4},{4,3},{5,2},{6,1},{7,0},{8,15},{9,14},{10,... | collective-permute-start | bytes 294920 | tf_op jit(solution)/shard_map/ppermute | solution.py:179
  18.8 20.1 %copy-start.10 = (bf16[32,1536]{1,0:T(8,128)(2,1)S(1)}, bf16[32,1536]{1,0:T(8,128)(2,1)}, u32[]{:S(2)}) copy-start(bf16[32,1536]{1,0:T(8,128)(2,1)} %get-tuple-element.80.refs_0_) | copy-start | bytes 294916
  22.0 51.2 %copy-start.1 = (bf16[1,384,1536]{2,1,0:T(8,128)(2,1)S(1)}, bf16[1,384,1536]{2,1,0:T(8,128)(2,1)}, u32[]{:S(2)}) copy-start(bf16[1,384,1536]{2,1,0:T(8,128)(2,1)} %w_value_ref.3) | copy-start | bytes 3538948
  22.0 51.2 %copy-start.8 = (bf16[1,256,256]{2,1,0:T(8,128)(2,1)S(1)}, bf16[1,256,256]{2,1,0:T(8,128)(2,1)}, u32[]{:S(2)}) copy-start(bf16[1,256,256]{2,1,0:T(8,128)(2,1)} %r_ref.7) | copy-start | bytes 393220
  22.0 10.9 %collective-permute-start.14 = (bf16[32,1536]{1,0:T(8,128)(2,1)S(1)}, bf16[32,1536]{1,0:T(8,128)(2,1)S(1)}, u32[]{:S(2)}, u32[]{:S(2)}) collective-permute-start(bf16[32,1536]{1,0:T(8,128)(2,1)S(1)} %get-tuple-element.99), channel_id=1, source_target_pairs={{0,1},{1,0},{2,3},{3,2},{4,5},{5,4},{6,7},{7,6},{8,9},{9,8},{10,11... | collective-permute-start | bytes 294920 | tf_op jit(solution)/shard_map/ppermute | solution.py:179
  24.1 9.9 %collective-permute-start.15 = (bf16[32,1536]{1,0:T(8,128)(2,1)S(1)}, bf16[32,1536]{1,0:T(8,128)(2,1)S(1)}, u32[]{:S(2)}, u32[]{:S(2)}) collective-permute-start(bf16[32,1536]{1,0:T(8,128)(2,1)S(1)} %get-tuple-element.100), channel_id=1, source_target_pairs={{0,2},{1,3},{2,0},{3,1},{4,6},{5,7},{6,4},{7,5},{8,10},{9,11},{10,... | collective-permute-start | bytes 294920 | tf_op jit(solution)/shard_map/ppermute | solution.py:179
  26.7 13.4 %collective-permute-start.16 = (bf16[32,1536]{1,0:T(8,128)(2,1)S(1)}, bf16[32,1536]{1,0:T(8,128)(2,1)S(1)}, u32[]{:S(2)}, u32[]{:S(2)}) collective-permute-start(bf16[32,1536]{1,0:T(8,128)(2,1)S(1)} %get-tuple-element.101), channel_id=1, source_target_pairs={{0,3},{1,2},{2,1},{3,0},{4,7},{5,6},{6,5},{7,4},{8,11},{9,10},{10,... | collective-permute-start | bytes 294920 | tf_op jit(solution)/shard_map/ppermute | solution.py:179
  26.8 17.8 %collective-permute-start.17 = (bf16[32,1536]{1,0:T(8,128)(2,1)S(1)}, bf16[32,1536]{1,0:T(8,128)(2,1)S(1)}, u32[]{:S(2)}, u32[]{:S(2)}) collective-permute-start(bf16[32,1536]{1,0:T(8,128)(2,1)S(1)} %get-tuple-element.102), channel_id=1, source_target_pairs={{0,4},{1,5},{2,6},{3,7},{4,0},{5,1},{6,2},{7,3},{8,12},{9,13},{10,... | collective-permute-start | bytes 294920 | tf_op jit(solution)/shard_map/ppermute | solution.py:179
  30.3 17.1 %collective-permute-start.18 = (bf16[32,1536]{1,0:T(8,128)(2,1)S(1)}, bf16[32,1536]{1,0:T(8,128)(2,1)S(1)}, u32[]{:S(2)}, u32[]{:S(2)}) collective-permute-start(bf16[32,1536]{1,0:T(8,128)(2,1)S(1)} %get-tuple-element.103), channel_id=1, source_target_pairs={{0,5},{1,4},{2,7},{3,6},{4,1},{5,0},{6,3},{7,2},{8,13},{9,12},{10,... | collective-permute-start | bytes 294920 | tf_op jit(solution)/shard_map/ppermute | solution.py:179
  33.0 16.6 %collective-permute-start.19 = (bf16[32,1536]{1,0:T(8,128)(2,1)S(1)}, bf16[32,1536]{1,0:T(8,128)(2,1)S(1)}, u32[]{:S(2)}, u32[]{:S(2)}) collective-permute-start(bf16[32,1536]{1,0:T(8,128)(2,1)S(1)} %get-tuple-element.104), channel_id=1, source_target_pairs={{0,6},{1,7},{2,4},{3,5},{4,2},{5,3},{6,0},{7,1},{8,14},{9,15},{10,... | collective-permute-start | bytes 294920 | tf_op jit(solution)/shard_map/ppermute | solution.py:179
  34.0 17.4 %collective-permute-start.20 = (bf16[32,1536]{1,0:T(8,128)(2,1)S(1)}, bf16[32,1536]{1,0:T(8,128)(2,1)S(1)}, u32[]{:S(2)}, u32[]{:S(2)}) collective-permute-start(bf16[32,1536]{1,0:T(8,128)(2,1)S(1)} %get-tuple-element.105), channel_id=1, source_target_pairs={{0,7},{1,6},{2,5},{3,4},{4,3},{5,2},{6,1},{7,0},{8,15},{9,14},{10,... | collective-permute-start | bytes 294920 | tf_op jit(solution)/shard_map/ppermute | solution.py:179
  40.1 18.2 %collective-permute-start.10 = (bf16[32,1536]{1,0:T(8,128)(2,1)S(1)}, bf16[32,1536]{1,0:T(8,128)(2,1)S(1)}, u32[]{:S(2)}, u32[]{:S(2)}) collective-permute-start(bf16[32,1536]{1,0:T(8,128)(2,1)S(1)} %get-tuple-element.92), channel_id=1, source_target_pairs={{0,4},{1,5},{2,6},{3,7},{4,0},{5,1},{6,2},{7,3},{8,12},{9,13},{10,... | collective-permute-start | bytes 294920 | tf_op jit(solution)/shard_map/ppermute | solution.py:179
  44.6 16.5 %collective-permute-start.11 = (bf16[32,1536]{1,0:T(8,128)(2,1)S(1)}, bf16[32,1536]{1,0:T(8,128)(2,1)S(1)}, u32[]{:S(2)}, u32[]{:S(2)}) collective-permute-start(bf16[32,1536]{1,0:T(8,128)(2,1)S(1)} %get-tuple-element.93), channel_id=1, source_target_pairs={{0,5},{1,4},{2,7},{3,6},{4,1},{5,0},{6,3},{7,2},{8,13},{9,12},{10,... | collective-permute-start | bytes 294920 | tf_op jit(solution)/shard_map/ppermute | solution.py:179
  47.4 13.7 %collective-permute-start.12 = (bf16[32,1536]{1,0:T(8,128)(2,1)S(1)}, bf16[32,1536]{1,0:T(8,128)(2,1)S(1)}, u32[]{:S(2)}, u32[]{:S(2)}) collective-permute-start(bf16[32,1536]{1,0:T(8,128)(2,1)S(1)} %get-tuple-element.94), channel_id=1, source_target_pairs={{0,6},{1,7},{2,4},{3,5},{4,2},{5,3},{6,0},{7,1},{8,14},{9,15},{10,... | collective-permute-start | bytes 294920 | tf_op jit(solution)/shard_map/ppermute | solution.py:179
  49.6 12.3 %collective-permute-start.13 = (bf16[32,1536]{1,0:T(8,128)(2,1)S(1)}, bf16[32,1536]{1,0:T(8,128)(2,1)S(1)}, u32[]{:S(2)}, u32[]{:S(2)}) collective-permute-start(bf16[32,1536]{1,0:T(8,128)(2,1)S(1)} %get-tuple-element.95), channel_id=1, source_target_pairs={{0,7},{1,6},{2,5},{3,4},{4,3},{5,2},{6,1},{7,0},{8,15},{9,14},{10,... | collective-permute-start | bytes 294920 | tf_op jit(solution)/shard_map/ppermute | solution.py:179
  51.4 13.7 %collective-permute-start.7 = (bf16[32,1536]{1,0:T(8,128)(2,1)S(1)}, bf16[32,1536]{1,0:T(8,128)(2,1)S(1)}, u32[]{:S(2)}, u32[]{:S(2)}) collective-permute-start(bf16[32,1536]{1,0:T(8,128)(2,1)S(1)} %get-tuple-element.89), channel_id=1, source_target_pairs={{0,1},{1,0},{2,3},{3,2},{4,5},{5,4},{6,7},{7,6},{8,9},{9,8},{10,11... | collective-permute-start | bytes 294920 | tf_op jit(solution)/shard_map/ppermute | solution.py:179
  58.3 7.2 %collective-permute-start.8 = (bf16[32,1536]{1,0:T(8,128)(2,1)S(1)}, bf16[32,1536]{1,0:T(8,128)(2,1)S(1)}, u32[]{:S(2)}, u32[]{:S(2)}) collective-permute-start(bf16[32,1536]{1,0:T(8,128)(2,1)S(1)} %get-tuple-element.90), channel_id=1, source_target_pairs={{0,2},{1,3},{2,0},{3,1},{4,6},{5,7},{6,4},{7,5},{8,10},{9,11},{10,... | collective-permute-start | bytes 294920 | tf_op jit(solution)/shard_map/ppermute | solution.py:179
  61.1 7.3 %collective-permute-start.9 = (bf16[32,1536]{1,0:T(8,128)(2,1)S(1)}, bf16[32,1536]{1,0:T(8,128)(2,1)S(1)}, u32[]{:S(2)}, u32[]{:S(2)}) collective-permute-start(bf16[32,1536]{1,0:T(8,128)(2,1)S(1)} %get-tuple-element.91), channel_id=1, source_target_pairs={{0,3},{1,2},{2,1},{3,0},{4,7},{5,6},{6,5},{7,4},{8,11},{9,10},{10,... | collective-permute-start | bytes 294920 | tf_op jit(solution)/shard_map/ppermute | solution.py:179
  61.1 7.9 %collective-permute-start.21 = (bf16[32,1536]{1,0:T(8,128)(2,1)S(1)}, bf16[32,1536]{1,0:T(8,128)(2,1)S(1)}, u32[]{:S(2)}, u32[]{:S(2)}) collective-permute-start(bf16[32,1536]{1,0:T(8,128)(2,1)S(1)} %get-tuple-element.107), channel_id=1, source_target_pairs={{0,1},{1,0},{2,3},{3,2},{4,5},{5,4},{6,7},{7,6},{8,9},{9,8},{10,11... | collective-permute-start | bytes 294920 | tf_op jit(solution)/shard_map/ppermute | solution.py:179
  61.9 10.6 %collective-permute-start.22 = (bf16[32,1536]{1,0:T(8,128)(2,1)S(1)}, bf16[32,1536]{1,0:T(8,128)(2,1)S(1)}, u32[]{:S(2)}, u32[]{:S(2)}) collective-permute-start(bf16[32,1536]{1,0:T(8,128)(2,1)S(1)} %get-tuple-element.108), channel_id=1, source_target_pairs={{0,2},{1,3},{2,0},{3,1},{4,6},{5,7},{6,4},{7,5},{8,10},{9,11},{10,... | collective-permute-start | bytes 294920 | tf_op jit(solution)/shard_map/ppermute | solution.py:179
  65.2 11.0 %collective-permute-start.23 = (bf16[32,1536]{1,0:T(8,128)(2,1)S(1)}, bf16[32,1536]{1,0:T(8,128)(2,1)S(1)}, u32[]{:S(2)}, u32[]{:S(2)}) collective-permute-start(bf16[32,1536]{1,0:T(8,128)(2,1)S(1)} %get-tuple-element.109), channel_id=1, source_target_pairs={{0,3},{1,2},{2,1},{3,0},{4,7},{5,6},{6,5},{7,4},{8,11},{9,10},{10,... | collective-permute-start | bytes 294920 | tf_op jit(solution)/shard_map/ppermute | solution.py:179
  65.5 12.9 %collective-permute-start.24 = (bf16[32,1536]{1,0:T(8,128)(2,1)S(1)}, bf16[32,1536]{1,0:T(8,128)(2,1)S(1)}, u32[]{:S(2)}, u32[]{:S(2)}) collective-permute-start(bf16[32,1536]{1,0:T(8,128)(2,1)S(1)} %get-tuple-element.110), channel_id=1, source_target_pairs={{0,4},{1,5},{2,6},{3,7},{4,0},{5,1},{6,2},{7,3},{8,12},{9,13},{10,... | collective-permute-start | bytes 294920 | tf_op jit(solution)/shard_map/ppermute | solution.py:179
  68.4 13.7 %collective-permute-start.25 = (bf16[32,1536]{1,0:T(8,128)(2,1)S(1)}, bf16[32,1536]{1,0:T(8,128)(2,1)S(1)}, u32[]{:S(2)}, u32[]{:S(2)}) collective-permute-start(bf16[32,1536]{1,0:T(8,128)(2,1)S(1)} %get-tuple-element.111), channel_id=1, source_target_pairs={{0,5},{1,4},{2,7},{3,6},{4,1},{5,0},{6,3},{7,2},{8,13},{9,12},{10,... | collective-permute-start | bytes 294920 | tf_op jit(solution)/shard_map/ppermute | solution.py:179
  69.0 13.7 %collective-permute-start.26 = (bf16[32,1536]{1,0:T(8,128)(2,1)S(1)}, bf16[32,1536]{1,0:T(8,128)(2,1)S(1)}, u32[]{:S(2)}, u32[]{:S(2)}) collective-permute-start(bf16[32,1536]{1,0:T(8,128)(2,1)S(1)} %get-tuple-element.112), channel_id=1, source_target_pairs={{0,6},{1,7},{2,4},{3,5},{4,2},{5,3},{6,0},{7,1},{8,14},{9,15},{10,... | collective-permute-start | bytes 294920 | tf_op jit(solution)/shard_map/ppermute | solution.py:179
  72.5 14.9 %collective-permute-start.27 = (bf16[32,1536]{1,0:T(8,128)(2,1)S(1)}, bf16[32,1536]{1,0:T(8,128)(2,1)S(1)}, u32[]{:S(2)}, u32[]{:S(2)}) collective-permute-start(bf16[32,1536]{1,0:T(8,128)(2,1)S(1)} %get-tuple-element.113), channel_id=1, source_target_pairs={{0,7},{1,6},{2,5},{3,4},{4,3},{5,2},{6,1},{7,0},{8,15},{9,14},{10,... | collective-permute-start | bytes 294920 | tf_op jit(solution)/shard_map/ppermute | solution.py:179
  76.1 15.5 %collective-permute-start.28 = (bf16[32,1536]{1,0:T(8,128)(2,1)S(1)}, bf16[32,1536]{1,0:T(8,128)(2,1)S(1)}, u32[]{:S(2)}, u32[]{:S(2)}) collective-permute-start(bf16[32,1536]{1,0:T(8,128)(2,1)S(1)} %get-tuple-element.115), channel_id=1, source_target_pairs={{0,1},{1,0},{2,3},{3,2},{4,5},{5,4},{6,7},{7,6},{8,9},{9,8},{10,11... | collective-permute-start | bytes 294920 | tf_op jit(solution)/shard_map/ppermute | solution.py:179
  78.4 13.2 %collective-permute-start.29 = (bf16[32,1536]{1,0:T(8,128)(2,1)S(1)}, bf16[32,1536]{1,0:T(8,128)(2,1)S(1)}, u32[]{:S(2)}, u32[]{:S(2)}) collective-permute-start(bf16[32,1536]{1,0:T(8,128)(2,1)S(1)} %get-tuple-element.116), channel_id=1, source_target_pairs={{0,2},{1,3},{2,0},{3,1},{4,6},{5,7},{6,4},{7,5},{8,10},{9,11},{10,... | collective-permute-start | bytes 294920 | tf_op jit(solution)/shard_map/ppermute | solution.py:179
  82.1 9.5 %collective-permute-start.30 = (bf16[32,1536]{1,0:T(8,128)(2,1)S(1)}, bf16[32,1536]{1,0:T(8,128)(2,1)S(1)}, u32[]{:S(2)}, u32[]{:S(2)}) collective-permute-start(bf16[32,1536]{1,0:T(8,128)(2,1)S(1)} %get-tuple-element.117), channel_id=1, source_target_pairs={{0,3},{1,2},{2,1},{3,0},{4,7},{5,6},{6,5},{7,4},{8,11},{9,10},{10,... | collective-permute-start | bytes 294920 | tf_op jit(solution)/shard_map/ppermute | solution.py:179
  82.7 9.0 %collective-permute-start.31 = (bf16[32,1536]{1,0:T(8,128)(2,1)S(1)}, bf16[32,1536]{1,0:T(8,128)(2,1)S(1)}, u32[]{:S(2)}, u32[]{:S(2)}) collective-permute-start(bf16[32,1536]{1,0:T(8,128)(2,1)S(1)} %get-tuple-element.118), channel_id=1, source_target_pairs={{0,4},{1,5},{2,6},{3,7},{4,0},{5,1},{6,2},{7,3},{8,12},{9,13},{10,... | collective-permute-start | bytes 294920 | tf_op jit(solution)/shard_map/ppermute | solution.py:179
  87.4 15.7 %copy-start.4 = (bf16[1,384,1536]{2,1,0:T(8,128)(2,1)S(1)}, bf16[1,384,1536]{2,1,0:T(8,128)(2,1)}, u32[]{:S(2)}) copy-start(bf16[1,384,1536]{2,1,0:T(8,128)(2,1)} %w_out_ref.3) | copy-start | bytes 3538948
  91.6 11.4 %collective-permute-start.32 = (bf16[256,1536]{1,0:T(8,128)(2,1)S(1)}, bf16[256,1536]{1,0:T(8,128)(2,1)S(1)}, u32[]{:S(2)}, u32[]{:S(2)}) collective-permute-start(bf16[256,1536]{1,0:T(8,128)(2,1)S(1)} %get-tuple-element.119), channel_id=1, source_target_pairs={{8,0},{16,8},{24,16},{9,1},{17,9},{25,17},{10,2},{18,10},{26,18},{... | collective-permute-start | bytes 2359304 | tf_op jit(solution)/shard_map/ppermute | solution.py:337
  93.6 15.5 %collective-permute-start.33 = (bf16[32,1536]{1,0:T(8,128)(2,1)S(1)}, bf16[32,1536]{1,0:T(8,128)(2,1)S(1)}, u32[]{:S(2)}, u32[]{:S(2)}) collective-permute-start(bf16[32,1536]{1,0:T(8,128)(2,1)S(1)} %get-tuple-element.125), channel_id=1, source_target_pairs={{0,5},{1,4},{2,7},{3,6},{4,1},{5,0},{6,3},{7,2},{8,13},{9,12},{10,... | collective-permute-start | bytes 294920 | tf_op jit(solution)/shard_map/ppermute | solution.py:179
  95.8 14.9 %collective-permute-start.34 = (bf16[32,1536]{1,0:T(8,128)(2,1)S(1)}, bf16[32,1536]{1,0:T(8,128)(2,1)S(1)}, u32[]{:S(2)}, u32[]{:S(2)}) collective-permute-start(bf16[32,1536]{1,0:T(8,128)(2,1)S(1)} %get-tuple-element.126), channel_id=1, source_target_pairs={{0,6},{1,7},{2,4},{3,5},{4,2},{5,3},{6,0},{7,1},{8,14},{9,15},{10,... | collective-permute-start | bytes 294920 | tf_op jit(solution)/shard_map/ppermute | solution.py:179
  97.3 14.8 %collective-permute-start.35 = (bf16[32,1536]{1,0:T(8,128)(2,1)S(1)}, bf16[32,1536]{1,0:T(8,128)(2,1)S(1)}, u32[]{:S(2)}, u32[]{:S(2)}) collective-permute-start(bf16[32,1536]{1,0:T(8,128)(2,1)S(1)} %get-tuple-element.127), channel_id=1, source_target_pairs={{0,7},{1,6},{2,5},{3,4},{4,3},{5,2},{6,1},{7,0},{8,15},{9,14},{10,... | collective-permute-start | bytes 294920 | tf_op jit(solution)/shard_map/ppermute | solution.py:179
  106.4 8.6 %collective-permute-start.43 = (bf16[32,1536]{1,0:T(8,128)(2,1)S(1)}, bf16[32,1536]{1,0:T(8,128)(2,1)S(1)}, u32[]{:S(2)}, u32[]{:S(2)}) collective-permute-start(bf16[32,1536]{1,0:T(8,128)(2,1)S(1)} %get-tuple-element.137), channel_id=1, source_target_pairs={{0,1},{1,0},{2,3},{3,2},{4,5},{5,4},{6,7},{7,6},{8,9},{9,8},{10,11... | collective-permute-start | bytes 294920 | tf_op jit(solution)/shard_map/ppermute | solution.py:179
  109.1 7.0 %collective-permute-start.44 = (bf16[32,1536]{1,0:T(8,128)(2,1)S(1)}, bf16[32,1536]{1,0:T(8,128)(2,1)S(1)}, u32[]{:S(2)}, u32[]{:S(2)}) collective-permute-start(bf16[32,1536]{1,0:T(8,128)(2,1)S(1)} %get-tuple-element.138), channel_id=1, source_target_pairs={{0,2},{1,3},{2,0},{3,1},{4,6},{5,7},{6,4},{7,5},{8,10},{9,11},{10,... | collective-permute-start | bytes 294920 | tf_op jit(solution)/shard_map/ppermute | solution.py:179
  109.1 10.4 %collective-permute-start.45 = (bf16[32,1536]{1,0:T(8,128)(2,1)S(1)}, bf16[32,1536]{1,0:T(8,128)(2,1)S(1)}, u32[]{:S(2)}, u32[]{:S(2)}) collective-permute-start(bf16[32,1536]{1,0:T(8,128)(2,1)S(1)} %get-tuple-element.139), channel_id=1, source_target_pairs={{0,3},{1,2},{2,1},{3,0},{4,7},{5,6},{6,5},{7,4},{8,11},{9,10},{10,... | collective-permute-start | bytes 294920 | tf_op jit(solution)/shard_map/ppermute | solution.py:179
  110.6 14.0 %collective-permute-start.46 = (bf16[32,1536]{1,0:T(8,128)(2,1)S(1)}, bf16[32,1536]{1,0:T(8,128)(2,1)S(1)}, u32[]{:S(2)}, u32[]{:S(2)}) collective-permute-start(bf16[32,1536]{1,0:T(8,128)(2,1)S(1)} %get-tuple-element.140), channel_id=1, source_target_pairs={{0,4},{1,5},{2,6},{3,7},{4,0},{5,1},{6,2},{7,3},{8,12},{9,13},{10,... | collective-permute-start | bytes 294920 | tf_op jit(solution)/shard_map/ppermute | solution.py:179
  112.2 14.9 %collective-permute-start.47 = (bf16[32,1536]{1,0:T(8,128)(2,1)S(1)}, bf16[32,1536]{1,0:T(8,128)(2,1)S(1)}, u32[]{:S(2)}, u32[]{:S(2)}) collective-permute-start(bf16[32,1536]{1,0:T(8,128)(2,1)S(1)} %get-tuple-element.141), channel_id=1, source_target_pairs={{0,5},{1,4},{2,7},{3,6},{4,1},{5,0},{6,3},{7,2},{8,13},{9,12},{10,... | collective-permute-start | bytes 294920 | tf_op jit(solution)/shard_map/ppermute | solution.py:179
  115.0 12.6 %collective-permute-start.48 = (bf16[32,1536]{1,0:T(8,128)(2,1)S(1)}, bf16[32,1536]{1,0:T(8,128)(2,1)S(1)}, u32[]{:S(2)}, u32[]{:S(2)}) collective-permute-start(bf16[32,1536]{1,0:T(8,128)(2,1)S(1)} %get-tuple-element.142), channel_id=1, source_target_pairs={{0,6},{1,7},{2,4},{3,5},{4,2},{5,3},{6,0},{7,1},{8,14},{9,15},{10,... | collective-permute-start | bytes 294920 | tf_op jit(solution)/shard_map/ppermute | solution.py:179
  116.1 13.1 %collective-permute-start.49 = (bf16[32,1536]{1,0:T(8,128)(2,1)S(1)}, bf16[32,1536]{1,0:T(8,128)(2,1)S(1)}, u32[]{:S(2)}, u32[]{:S(2)}) collective-permute-start(bf16[32,1536]{1,0:T(8,128)(2,1)S(1)} %get-tuple-element.143), channel_id=1, source_target_pairs={{0,7},{1,6},{2,5},{3,4},{4,3},{5,2},{6,1},{7,0},{8,15},{9,14},{10,... | collective-permute-start | bytes 294920 | tf_op jit(solution)/shard_map/ppermute | solution.py:179
  119.6 14.8 %collective-permute-start.36 = (bf16[32,1536]{1,0:T(8,128)(2,1)S(1)}, bf16[32,1536]{1,0:T(8,128)(2,1)S(1)}, u32[]{:S(2)}, u32[]{:S(2)}) collective-permute-start(bf16[32,1536]{1,0:T(8,128)(2,1)S(1)} %get-tuple-element.129), channel_id=1, source_target_pairs={{0,1},{1,0},{2,3},{3,2},{4,5},{5,4},{6,7},{7,6},{8,9},{9,8},{10,11... | collective-permute-start | bytes 294920 | tf_op jit(solution)/shard_map/ppermute | solution.py:179
  124.7 13.6 %collective-permute-start.37 = (bf16[32,1536]{1,0:T(8,128)(2,1)S(1)}, bf16[32,1536]{1,0:T(8,128)(2,1)S(1)}, u32[]{:S(2)}, u32[]{:S(2)}) collective-permute-start(bf16[32,1536]{1,0:T(8,128)(2,1)S(1)} %get-tuple-element.130), channel_id=1, source_target_pairs={{0,2},{1,3},{2,0},{3,1},{4,6},{5,7},{6,4},{7,5},{8,10},{9,11},{10,... | collective-permute-start | bytes 294920 | tf_op jit(solution)/shard_map/ppermute | solution.py:179
  127.1 11.8 %collective-permute-start.38 = (bf16[32,1536]{1,0:T(8,128)(2,1)S(1)}, bf16[32,1536]{1,0:T(8,128)(2,1)S(1)}, u32[]{:S(2)}, u32[]{:S(2)}) collective-permute-start(bf16[32,1536]{1,0:T(8,128)(2,1)S(1)} %get-tuple-element.131), channel_id=1, source_target_pairs={{0,3},{1,2},{2,1},{3,0},{4,7},{5,6},{6,5},{7,4},{8,11},{9,10},{10,... | collective-permute-start | bytes 294920 | tf_op jit(solution)/shard_map/ppermute | solution.py:179
  127.5 12.3 %collective-permute-start.39 = (bf16[32,1536]{1,0:T(8,128)(2,1)S(1)}, bf16[32,1536]{1,0:T(8,128)(2,1)S(1)}, u32[]{:S(2)}, u32[]{:S(2)}) collective-permute-start(bf16[32,1536]{1,0:T(8,128)(2,1)S(1)} %get-tuple-element.132), channel_id=1, source_target_pairs={{0,4},{1,5},{2,6},{3,7},{4,0},{5,1},{6,2},{7,3},{8,12},{9,13},{10,... | collective-permute-start | bytes 294920 | tf_op jit(solution)/shard_map/ppermute | solution.py:179
  129.2 13.1 %collective-permute-start.40 = (bf16[32,1536]{1,0:T(8,128)(2,1)S(1)}, bf16[32,1536]{1,0:T(8,128)(2,1)S(1)}, u32[]{:S(2)}, u32[]{:S(2)}) collective-permute-start(bf16[32,1536]{1,0:T(8,128)(2,1)S(1)} %get-tuple-element.133), channel_id=1, source_target_pairs={{0,5},{1,4},{2,7},{3,6},{4,1},{5,0},{6,3},{7,2},{8,13},{9,12},{10,... | collective-permute-start | bytes 294920 | tf_op jit(solution)/shard_map/ppermute | solution.py:179
  134.3 8.1 %collective-permute-start.41 = (bf16[32,1536]{1,0:T(8,128)(2,1)S(1)}, bf16[32,1536]{1,0:T(8,128)(2,1)S(1)}, u32[]{:S(2)}, u32[]{:S(2)}) collective-permute-start(bf16[32,1536]{1,0:T(8,128)(2,1)S(1)} %get-tuple-element.134), channel_id=1, source_target_pairs={{0,6},{1,7},{2,4},{3,5},{4,2},{5,3},{6,0},{7,1},{8,14},{9,15},{10,... | collective-permute-start | bytes 294920 | tf_op jit(solution)/shard_map/ppermute | solution.py:179
  138.3 8.7 %collective-permute-start.42 = (bf16[32,1536]{1,0:T(8,128)(2,1)S(1)}, bf16[32,1536]{1,0:T(8,128)(2,1)S(1)}, u32[]{:S(2)}, u32[]{:S(2)}) collective-permute-start(bf16[32,1536]{1,0:T(8,128)(2,1)S(1)} %get-tuple-element.135), channel_id=1, source_target_pairs={{0,7},{1,6},{2,5},{3,4},{4,3},{5,2},{6,1},{7,0},{8,15},{9,14},{10,... | collective-permute-start | bytes 294920 | tf_op jit(solution)/shard_map/ppermute | solution.py:179
  138.9 12.4 %collective-permute-start.50 = (bf16[32,1536]{1,0:T(8,128)(2,1)S(1)}, bf16[32,1536]{1,0:T(8,128)(2,1)S(1)}, u32[]{:S(2)}, u32[]{:S(2)}) collective-permute-start(bf16[32,1536]{1,0:T(8,128)(2,1)S(1)} %get-tuple-element.145), channel_id=1, source_target_pairs={{0,1},{1,0},{2,3},{3,2},{4,5},{5,4},{6,7},{7,6},{8,9},{9,8},{10,11... | collective-permute-start | bytes 294920 | tf_op jit(solution)/shard_map/ppermute | solution.py:179
  139.9 13.3 %collective-permute-start.51 = (bf16[32,1536]{1,0:T(8,128)(2,1)S(1)}, bf16[32,1536]{1,0:T(8,128)(2,1)S(1)}, u32[]{:S(2)}, u32[]{:S(2)}) collective-permute-start(bf16[32,1536]{1,0:T(8,128)(2,1)S(1)} %get-tuple-element.146), channel_id=1, source_target_pairs={{0,2},{1,3},{2,0},{3,1},{4,6},{5,7},{6,4},{7,5},{8,10},{9,11},{10,... | collective-permute-start | bytes 294920 | tf_op jit(solution)/shard_map/ppermute | solution.py:179
  142.3 14.3 %collective-permute-start.52 = (bf16[32,1536]{1,0:T(8,128)(2,1)S(1)}, bf16[32,1536]{1,0:T(8,128)(2,1)S(1)}, u32[]{:S(2)}, u32[]{:S(2)}) collective-permute-start(bf16[32,1536]{1,0:T(8,128)(2,1)S(1)} %get-tuple-element.147), channel_id=1, source_target_pairs={{0,3},{1,2},{2,1},{3,0},{4,7},{5,6},{6,5},{7,4},{8,11},{9,10},{10,... | collective-permute-start | bytes 294920 | tf_op jit(solution)/shard_map/ppermute | solution.py:179
  142.4 14.1 %collective-permute-start.53 = (bf16[32,1536]{1,0:T(8,128)(2,1)S(1)}, bf16[32,1536]{1,0:T(8,128)(2,1)S(1)}, u32[]{:S(2)}, u32[]{:S(2)}) collective-permute-start(bf16[32,1536]{1,0:T(8,128)(2,1)S(1)} %get-tuple-element.148), channel_id=1, source_target_pairs={{0,4},{1,5},{2,6},{3,7},{4,0},{5,1},{6,2},{7,3},{8,12},{9,13},{10,... | collective-permute-start | bytes 294920 | tf_op jit(solution)/shard_map/ppermute | solution.py:179
  147.0 12.4 %collective-permute-start.54 = (bf16[32,1536]{1,0:T(8,128)(2,1)S(1)}, bf16[32,1536]{1,0:T(8,128)(2,1)S(1)}, u32[]{:S(2)}, u32[]{:S(2)}) collective-permute-start(bf16[32,1536]{1,0:T(8,128)(2,1)S(1)} %get-tuple-element.149), channel_id=1, source_target_pairs={{0,5},{1,4},{2,7},{3,6},{4,1},{5,0},{6,3},{7,2},{8,13},{9,12},{10,... | collective-permute-start | bytes 294920 | tf_op jit(solution)/shard_map/ppermute | solution.py:179
  151.4 8.1 %collective-permute-start.55 = (bf16[32,1536]{1,0:T(8,128)(2,1)S(1)}, bf16[32,1536]{1,0:T(8,128)(2,1)S(1)}, u32[]{:S(2)}, u32[]{:S(2)}) collective-permute-start(bf16[32,1536]{1,0:T(8,128)(2,1)S(1)} %get-tuple-element.150), channel_id=1, source_target_pairs={{0,6},{1,7},{2,4},{3,5},{4,2},{5,3},{6,0},{7,1},{8,14},{9,15},{10,... | collective-permute-start | bytes 294920 | tf_op jit(solution)/shard_map/ppermute | solution.py:179
  153.1 7.4 %collective-permute-start.56 = (bf16[32,1536]{1,0:T(8,128)(2,1)S(1)}, bf16[32,1536]{1,0:T(8,128)(2,1)S(1)}, u32[]{:S(2)}, u32[]{:S(2)}) collective-permute-start(bf16[32,1536]{1,0:T(8,128)(2,1)S(1)} %get-tuple-element.151), channel_id=1, source_target_pairs={{0,7},{1,6},{2,5},{3,4},{4,3},{5,2},{6,1},{7,0},{8,15},{9,14},{10,... | collective-permute-start | bytes 294920 | tf_op jit(solution)/shard_map/ppermute | solution.py:179
  (5 other events, 34.8 us)
where the time goes:
time: 168 us; the launch traced here: 165 us
  starting transfers between devices  94.6 us (56%)
  waiting for transfers between devices  35.7 us (21%)
  Pallas kernels  31.8 us (19%)
  local copies, waits for them, and re-layouts  2.45 us (1%)
    ppermute x56, starting transfers between devices, send(): self.got[slot] = lax.ppermute(tied(self.parts[slot], after), 'seq', pairs)  92.7 us
    ppermute x56, waiting for transfers between devices, send(): self.got[slot] = lax.ppermute(tied(self.parts[slot], after), 'seq', pairs)  33.2 us
    pallas_call x13, Pallas kernels, call(): pl.pallas_call(kernel, grid=(steps or width // block,), in_specs=[spec fo...  31.8 us
  transfers between devices with their start and end apart: 57, of which 13 were waited for; matrix products, arithmetic and copies ran while one was open for 0% of the time, Pallas kernels for 14%

commit v1 on v0

--- a/solution.py
+++ b/solution.py
@@ -168,15 +168,21 @@
     )
 
 
+WINDOW = 5
+
+
 class Exchange:
     def __init__(self, parts):
         self.parts = list(parts)
         self.got = {0: parts[0]}
 
-    def send(self, slots, after=()):
+    def send(self, slots, lane=None):
         for slot in slots:
             pairs = [(i, i ^ slot) for i in range(len(self.parts))]
+            after = lane[-WINDOW:][:1] if lane is not None and len(lane) >= WINDOW else []
             self.got[slot] = lax.ppermute(tied(self.parts[slot], after), "seq", pairs)
+            if lane is not None:
+                lane.append((self, slot))
         return self
 
     def all(self):
@@ -314,7 +320,11 @@
             aliases=aliases,
         )
 
-    first_0 = Exchange(first(0, 60)).send(every)
+    half = count // 2
+    turns = [slot for pair in zip(range(half, count), [*range(1, half), 0]) for slot in pair]
+    turns.remove(0)
+    lane = []
+    first_0 = Exchange(first(0, 60)).send(turns, lane)
     (matrix,) = call(
         "matrix",
         functools.partial(matrix_kernel, count),
@@ -325,18 +335,22 @@
         steps=1,
     )
     parts, factor_0 = grads(0, [(cut3, arrived_grad)])
-    grad_0 = Exchange(parts).send(every)
-    mix_0 = Exchange(mix("mix_0", first_0.all(), False)).send(every)
-    fold_0 = Exchange(mix("fold_0", grad_0.all(), True)).send(every)
+    grad_0 = Exchange(parts).send(turns, lane)
+    mix_0 = Exchange(mix("mix_0", first_0.all(), False)).send(turns, lane)
+    fold_0 = Exchange(mix("fold_0", grad_0.all(), True)).send(turns, lane)
     gate_0 = back(0, mix_0.all(), factor_0)
     first_1 = Exchange(first(1))
     gate_0, first_1.parts[0] = lax.optimization_barrier((gate_0, first_1.parts[0]))
-    first_1.send(every)
+    first_1.send(turns, lane)
+    gate_0 = tied(gate_0, [(first_1, slot) for slot in turns[:1]])
     stacked, result_0 = result(0, gate_0, fold_0.all(), [(whole3, arrived_grad)], None)
-    result_0 = tied(result_0, [(first_1, slot) for slot in every[: min(4, count // 2)]])
+    result_0 = tied(result_0, [(first_1, slot) for slot in turns[1:-1]])
     passed = lax.ppermute(result_0, "pipe", [(s, s - 1) for s in range(1, pipe)])
-    mix_1 = Exchange(mix("mix_1", first_1.all(), False)).send(every)
+    mix_1 = Exchange(mix("mix_1", first_1.all(), False)).send(range(half, count)).send(range(1, half))
+    passed, mix_1.parts[0] = lax.optimization_barrier((passed, mix_1.parts[0]))
     parts, factor_1 = grads(1, [(cut, passed), (cut3, loss_grad)])
+    for slot, other in zip([count - 1, half - 1, half - 2], range(half, count)):
+        parts[slot] = tied(parts[slot], [(mix_1, other)])
     grad_1 = Exchange(parts).send(every)
     fold_1 = Exchange(mix("fold_1", grad_1.all(), True)).send(every)
     gate_1 = back(1, mix_1.all(), factor_1)

time: 168 us -> 171 us (1.018)
  starting transfers between devices: 94.6 us -> 103 us
  waiting for transfers between devices: 35.7 us -> 31.6 us
    ppermute x56, starting transfers between devices: 92.7 us -> 101 us  [send(): self.got[slot] = lax.ppermute(tied(self.parts[slot], after), 'seq', pairs)]
    ppermute x1, waiting for transfers between devices: 2.45 us -> 0.01 us  [local(): lax.ppermute(result_0, 'pipe', [(s, s - 1) for s in range(1, pipe)])]
  transfers between devices with their start and end apart: 57 -> 57, of which waited for: 13 -> 16; matrix products, arithmetic and copies ran while one was open for 0% -> 0% of each run, Pallas kernels for 14% -> 13%
where the time goes in v1:
time: 171 us; the launch traced here: 169 us
  starting transfers between devices  103 us (60%)
  Pallas kernels  31.8 us (19%)
  waiting for transfers between devices  31.6 us (18%)
  local copies, waits for them, and re-layouts  2.45 us (1%)
    ppermute x56, starting transfers between devices, send(): self.got[slot] = lax.ppermute(tied(self.parts[slot], after), 'seq', pairs)  101 us
    pallas_call x13, Pallas kernels, call(): pl.pallas_call(kernel, grid=(steps or width // block,), in_specs=[spec fo...  31.8 us
    ppermute x56, waiting for transfers between devices, send(): self.got[slot] = lax.ppermute(tied(self.parts[slot], after), 'seq', pairs)  31.6 us
  transfers between devices with their start and end apart: 57, of which 16 were waited for; matrix products, arithmetic and copies ran while one was open for 0% of the time, Pallas kernels for 13%

profile of v1, /device:TPU:2, one launch (start us, length us, event | category | flops | bytes accessed | tf_op | source)
XLA Modules:
  0.0 168.9 jit_solution(11773845426494946660)
XLA Ops:
  0.0 5.1 %first_0.1 = (bf16[32,1536]{1,0:T(8,128)(2,1)}, bf16[32,1536]{1,0:T(8,128)(2,1)}, bf16[32,1536]{1,0:T(8,128)(2,1)}, bf16[32,1536]{1,0:T(8,128)(2,1)}, bf16[32,15...) custom-call(bf16[1,2,256,1536]{3,2,1,0:T(8,128)(2,1)} %x_ref.11, ...), custom_call_target="tpu_custom_call" | custom-call | flops 603979776 | bytes 3145728 | tf_op jit(solution)/shard_map/first_0/pallas_call | solution.py:238
  5.2 1.6 collective-permute-start
  6.7 2.6 %collective-permute-start.2 = (bf16[32,1536]{1,0:T(8,128)(2,1)}, bf16[32,1536]{1,0:T(8,128)(2,1)S(1)}, u32[]{:S(2)}, u32[]{:S(2)}) collective-permute-start(bf16[32,1536]{1,0:T(8,128)(2,1)} %get-tuple-element.159), channel_id=1, source_target_pairs={{0,4},{1,5},{2,6},{3,7},{4,0},{5,1},{6,2},{7,3},{8,12},{9,13},{10,... | collective-permute-start | bytes 294920 | tf_op jit(solution)/shard_map/ppermute | solution.py:183
  9.3 1.6 collective-permute-start.1
  11.2 2.5 %collective-permute-start.5 = (bf16[32,1536]{1,0:T(8,128)(2,1)}, bf16[32,1536]{1,0:T(8,128)(2,1)S(1)}, u32[]{:S(2)}, u32[]{:S(2)}) collective-permute-start(bf16[32,1536]{1,0:T(8,128)(2,1)} %get-tuple-element.167), channel_id=1, source_target_pairs={{0,6},{1,7},{2,4},{3,5},{4,2},{5,3},{6,0},{7,1},{8,14},{9,15},{10,... | collective-permute-start | bytes 294920 | tf_op jit(solution)/shard_map/ppermute | solution.py:183
  13.7 1.3 copy-done.3
  15.0 1.1 copy-done.5
  16.1 3.2 %grads_0.1 = (bf16[32,1536]{1,0:T(8,128)(2,1)S(1)}, bf16[32,1536]{1,0:T(8,128)(2,1)S(1)}, bf16[32,1536]{1,0:T(8,128)(2,1)S(1)}, bf16[32,1536]{1,0:T(8,128)(2,1)S...) custom-call(bf16[1,2,256,1536]{3,2,1,0:T(8,128)(2,1)S(1)} %copy-done, ...), custom_call_target="tpu_custom_call" | custom-call | flops 603979776 | bytes 6291456 | tf_op jit(solution)/shard_map/grads_0/pallas_call | solution.py:238
  19.4 2.4 %collective-permute-start.6 = (bf16[32,1536]{1,0:T(8,128)(2,1)S(1)}, bf16[32,1536]{1,0:T(8,128)(2,1)S(1)}, u32[]{:S(2)}, u32[]{:S(2)}) collective-permute-start(bf16[32,1536]{1,0:T(8,128)(2,1)S(1)} %copy-done.13), channel_id=1, source_target_pairs={{0,7},{1,6},{2,5},{3,4},{4,3},{5,2},{6,1},{7,0},{8,15},{9,14},{10,... | collective-permute-start | bytes 294920 | tf_op jit(solution)/shard_map/ppermute | solution.py:183
  21.8 0.8 collective-permute-start.9
  22.6 3.7 %collective-permute-start.10 = (bf16[32,1536]{1,0:T(8,128)(2,1)S(1)}, bf16[32,1536]{1,0:T(8,128)(2,1)S(1)}, u32[]{:S(2)}, u32[]{:S(2)}) collective-permute-start(bf16[32,1536]{1,0:T(8,128)(2,1)S(1)} %get-tuple-element.185), channel_id=1, source_target_pairs={{0,4},{1,5},{2,6},{3,7},{4,0},{5,1},{6,2},{7,3},{8,12},{9,13},{10,... | collective-permute-start | bytes 294920 | tf_op jit(solution)/shard_map/ppermute | solution.py:183
  26.3 1.9 %collective-permute-start.12 = (bf16[32,1536]{1,0:T(8,128)(2,1)S(1)}, bf16[32,1536]{1,0:T(8,128)(2,1)S(1)}, u32[]{:S(2)}, u32[]{:S(2)}) collective-permute-start(bf16[32,1536]{1,0:T(8,128)(2,1)S(1)} %get-tuple-element.190), channel_id=1, source_target_pairs={{0,5},{1,4},{2,7},{3,6},{4,1},{5,0},{6,3},{7,2},{8,13},{9,12},{10,... | collective-permute-start | bytes 294920 | tf_op jit(solution)/shard_map/ppermute | solution.py:183
  28.2 0.7 collective-permute-done.9.refs_1_
  28.9 2.8 %collective-permute-start.14 = (bf16[32,1536]{1,0:T(8,128)(2,1)S(1)}, bf16[32,1536]{1,0:T(8,128)(2,1)S(1)}, u32[]{:S(2)}, u32[]{:S(2)}) collective-permute-start(bf16[32,1536]{1,0:T(8,128)(2,1)S(1)} %get-tuple-element.196), channel_id=1, source_target_pairs={{0,7},{1,6},{2,5},{3,4},{4,3},{5,2},{6,1},{7,0},{8,15},{9,14},{10,... | collective-permute-start | bytes 294920 | tf_op jit(solution)/shard_map/ppermute | solution.py:183
  31.7 4.3 %collective-permute-done.10.refs_4_ = bf16[32,1536]{1,0:T(8,128)(2,1)S(1)} collective-permute-done((bf16[32,1536]{1,0:T(8,128)(2,1)S(1)}, bf16[32,1536]{1,0:T(8,128)(2,1)S(1)}, u32[]{:S(2)}, u32[]{:S(2)}) %collective-permute-start.10) | collective-permute-done | bytes 98336 | tf_op jit(solution)/shard_map/ppermute | solution.py:183
  36.4 3.0 %collective-permute-start.13 = (bf16[32,1536]{1,0:T(8,128)(2,1)S(1)}, bf16[32,1536]{1,0:T(8,128)(2,1)S(1)}, u32[]{:S(2)}, u32[]{:S(2)}) collective-permute-start(bf16[32,1536]{1,0:T(8,128)(2,1)S(1)} %get-tuple-element.193), channel_id=1, source_target_pairs={{0,6},{1,7},{2,4},{3,5},{4,2},{5,3},{6,0},{7,1},{8,14},{9,15},{10,... | collective-permute-start | bytes 294920 | tf_op jit(solution)/shard_map/ppermute | solution.py:183
  39.4 0.9 collective-permute-start.7
  40.5 1.3 mix_0.1
  43.3 1.6 collective-permute-done.13.refs_6_
  44.9 3.3 %collective-permute-start.18 = (bf16[32,1536]{1,0:T(8,128)(2,1)S(1)}, bf16[32,1536]{1,0:T(8,128)(2,1)S(1)}, u32[]{:S(2)}, u32[]{:S(2)}) collective-permute-start(bf16[32,1536]{1,0:T(8,128)(2,1)S(1)} %get-tuple-element.208), channel_id=1, source_target_pairs={{0,5},{1,4},{2,7},{3,6},{4,1},{5,0},{6,3},{7,2},{8,13},{9,12},{10,... | collective-permute-start | bytes 294920 | tf_op jit(solution)/shard_map/ppermute | solution.py:183
  48.4 1.8 %collective-permute-start.8 = (bf16[32,1536]{1,0:T(8,128)(2,1)S(1)}, bf16[32,1536]{1,0:T(8,128)(2,1)S(1)}, u32[]{:S(2)}, u32[]{:S(2)}) collective-permute-start(bf16[32,1536]{1,0:T(8,128)(2,1)S(1)} %get-tuple-element.176), channel_id=1, source_target_pairs={{0,1},{1,0},{2,3},{3,2},{4,5},{5,4},{6,7},{7,6},{8,9},{9,8},{10,11... | collective-permute-start | bytes 294920 | tf_op jit(solution)/shard_map/ppermute | solution.py:183
  50.6 1.4 fold_0.1
  51.9 3.8 %collective-permute-start.23 = (bf16[32,1536]{1,0:T(8,128)(2,1)S(1)}, bf16[32,1536]{1,0:T(8,128)(2,1)S(1)}, u32[]{:S(2)}, u32[]{:S(2)}) collective-permute-start(bf16[32,1536]{1,0:T(8,128)(2,1)S(1)} %get-tuple-element.226), channel_id=1, source_target_pairs={{0,1},{1,0},{2,3},{3,2},{4,5},{5,4},{6,7},{7,6},{8,9},{9,8},{10,11... | collective-permute-start | bytes 294920 | tf_op jit(solution)/shard_map/ppermute | solution.py:183
  56.3 2.6 %collective-permute-start.25 = (bf16[32,1536]{1,0:T(8,128)(2,1)S(1)}, bf16[32,1536]{1,0:T(8,128)(2,1)S(1)}, u32[]{:S(2)}, u32[]{:S(2)}) collective-permute-start(bf16[32,1536]{1,0:T(8,128)(2,1)S(1)} %get-tuple-element.233), channel_id=1, source_target_pairs={{0,4},{1,5},{2,6},{3,7},{4,0},{5,1},{6,2},{7,3},{8,12},{9,13},{10,... | collective-permute-start | bytes 294920 | tf_op jit(solution)/shard_map/ppermute | solution.py:183
  58.9 0.7 collective-permute-start.21
  59.6 3.0 %collective-permute-start.20 = (bf16[32,1536]{1,0:T(8,128)(2,1)S(1)}, bf16[32,1536]{1,0:T(8,128)(2,1)S(1)}, u32[]{:S(2)}, u32[]{:S(2)}) collective-permute-start(bf16[32,1536]{1,0:T(8,128)(2,1)S(1)} %get-tuple-element.214), channel_id=1, source_target_pairs={{0,7},{1,6},{2,5},{3,4},{4,3},{5,2},{6,1},{7,0},{8,15},{9,14},{10,... | collective-permute-start | bytes 294920 | tf_op jit(solution)/shard_map/ppermute | solution.py:183
  63.3 2.9 %first_1.1 = (bf16[32,1536]{1,0:T(8,128)(2,1)S(1)}, bf16[32,1536]{1,0:T(8,128)(2,1)S(1)}, bf16[32,1536]{1,0:T(8,128)(2,1)S(1)}, bf16[32,1536]{1,0:T(8,128)(2,1)S...) custom-call(bf16[1,2,256,1536]{3,2,1,0:T(8,128)(2,1)S(1)} %copy-done, ...), custom_call_target="tpu_custom_call" | custom-call | flops 603979776 | bytes 3145728 | tf_op jit(solution)/shard_map/first_1/pallas_call | solution.py:238
  66.2 2.2 %collective-permute-start.28 = (bf16[32,1536]{1,0:T(8,128)(2,1)S(1)}, bf16[32,1536]{1,0:T(8,128)(2,1)S(1)}, u32[]{:S(2)}, u32[]{:S(2)}) collective-permute-start(bf16[32,1536]{1,0:T(8,128)(2,1)S(1)} %get-tuple-element.242), channel_id=1, source_target_pairs={{0,7},{1,6},{2,5},{3,4},{4,3},{5,2},{6,1},{7,0},{8,15},{9,14},{10,... | collective-permute-start | bytes 294920 | tf_op jit(solution)/shard_map/ppermute | solution.py:183
  68.4 3.4 %collective-permute-start.26 = (bf16[32,1536]{1,0:T(8,128)(2,1)S(1)}, bf16[32,1536]{1,0:T(8,128)(2,1)S(1)}, u32[]{:S(2)}, u32[]{:S(2)}) collective-permute-start(bf16[32,1536]{1,0:T(8,128)(2,1)S(1)} %get-tuple-element.234), channel_id=1, source_target_pairs={{0,3},{1,2},{2,1},{3,0},{4,7},{5,6},{6,5},{7,4},{8,11},{9,10},{10,... | collective-permute-start | bytes 294920 | tf_op jit(solution)/shard_map/ppermute | solution.py:183
  71.9 3.7 %collective-permute-start.27 = (bf16[32,1536]{1,0:T(8,128)(2,1)S(1)}, bf16[32,1536]{1,0:T(8,128)(2,1)S(1)}, u32[]{:S(2)}, u32[]{:S(2)}) collective-permute-start(bf16[32,1536]{1,0:T(8,128)(2,1)S(1)} %get-tuple-element.239), channel_id=1, source_target_pairs={{0,6},{1,7},{2,4},{3,5},{4,2},{5,3},{6,0},{7,1},{8,14},{9,15},{10,... | collective-permute-start | bytes 294920 | tf_op jit(solution)/shard_map/ppermute | solution.py:183
  76.1 5.9 %collective-permute-done.22.refs_4_ = bf16[32,1536]{1,0:T(8,128)(2,1)S(1)} collective-permute-done((bf16[32,1536]{1,0:T(8,128)(2,1)S(1)}, bf16[32,1536]{1,0:T(8,128)(2,1)S(1)}, u32[]{:S(2)}, u32[]{:S(2)}) %collective-permute-start.22) | collective-permute-done | bytes 98336 | tf_op jit(solution)/shard_map/ppermute | solution.py:183
  82.1 2.6 %collective-permute-start.32 = (bf16[32,1536]{1,0:T(8,128)(2,1)S(1)}, bf16[32,1536]{1,0:T(8,128)(2,1)S(1)}, u32[]{:S(2)}, u32[]{:S(2)}) collective-permute-start(bf16[32,1536]{1,0:T(8,128)(2,1)S(1)} %get-tuple-element.250), channel_id=1, source_target_pairs={{0,6},{1,7},{2,4},{3,5},{4,2},{5,3},{6,0},{7,1},{8,14},{9,15},{10,... | collective-permute-start | bytes 294920 | tf_op jit(solution)/shard_map/ppermute | solution.py:183
  84.7 1.4 collective-permute-start.31
  86.2 1.4 collective-permute-start.33
  87.5 1.0 collective-permute-start.30
  88.5 1.7 %back_0.1.back_ref = f32[256,1536]{1,0:T(8,128)S(1)} custom-call(bf16[1,384,1536]{2,1,0:T(8,128)(2,1)S(1)} %copy-done.2, f32[256,1536]{1,0:T(8,128)S(1)} %get-tuple-element.149.factor_ref, bf16[32,1536]{1,0:T(8,128)(2,1)S(1)} %get-tuple-element.172.refs_0_, bf16[32,1536]{1,0:T(8,128)(2,1)S(1)} %collective-permute-done.8.refs_1_, ...), custom_call_target="tpu_custom_call" | custom-call | flops 301989888 | bytes 4718592 | tf_op jit(solution)/shard_map/back_0/pallas_call | solution.py:238
  90.3 4.2 %result_0.1 = (bf16[1,2,256,1536]{3,2,1,0:T(8,128)(2,1)}, bf16[256,1536]{1,0:T(8,128)(2,1)S(1)}) custom-call(bf16[1,2,256,1536]{3,2,1,0:T(8,128)(2,1)S(1)} %copy-done, f32[1,1536]{1,0:T(1,128)S(1)} %copy-done.9, bf16[1,384,1536]{2,1,0:T(8,128)(2,1)S(1)} %copy-done.1, bf16[1,256,256]{2,1,0:T(8,128)(2,1)S(1)} %copy-done.8, f32[256,1536]{1,0:T(8,128)S(1)} %back_0.1.back_ref, ...), custom_call_target="tpu_custom_call" | custom-call | flops 905969664 | bytes 6291456 | tf_op jit(solution)/shard_map/result_0/pallas_call | solution.py:238
  95.0 2.1 %collective-permute-start.34 = (bf16[256,1536]{1,0:T(8,128)(2,1)S(1)}, bf16[256,1536]{1,0:T(8,128)(2,1)S(1)}, u32[]{:S(2)}, u32[]{:S(2)}) collective-permute-start(bf16[256,1536]{1,0:T(8,128)(2,1)S(1)} %get-tuple-element.252), channel_id=1, source_target_pairs={{8,0},{16,8},{24,16},{9,1},{17,9},{25,17},{10,2},{18,10},{26,18},{... | collective-permute-start | bytes 2359304 | tf_op jit(solution)/shard_map/ppermute | solution.py:348
  97.1 2.7 %collective-permute-start.35 = (bf16[32,1536]{1,0:T(8,128)(2,1)S(1)}, bf16[32,1536]{1,0:T(8,128)(2,1)S(1)}, u32[]{:S(2)}, u32[]{:S(2)}) collective-permute-start(bf16[32,1536]{1,0:T(8,128)(2,1)S(1)} %get-tuple-element.259), channel_id=1, source_target_pairs={{0,7},{1,6},{2,5},{3,4},{4,3},{5,2},{6,1},{7,0},{8,15},{9,14},{10,... | collective-permute-start | bytes 294920 | tf_op jit(solution)/shard_map/ppermute | solution.py:183
  99.8 5.4 %collective-permute-done.35.refs_7_ = bf16[32,1536]{1,0:T(8,128)(2,1)S(1)} collective-permute-done((bf16[32,1536]{1,0:T(8,128)(2,1)S(1)}, bf16[32,1536]{1,0:T(8,128)(2,1)S(1)}, u32[]{:S(2)}, u32[]{:S(2)}) %collective-permute-start.35) | collective-permute-done | bytes 98336 | tf_op jit(solution)/shard_map/ppermute | solution.py:183
  105.2 1.2 mix_1.1
  106.4 2.7 %collective-permute-start.41 = (bf16[32,1536]{1,0:T(8,128)(2,1)S(1)}, bf16[32,1536]{1,0:T(8,128)(2,1)S(1)}, u32[]{:S(2)}, u32[]{:S(2)}) collective-permute-start(bf16[32,1536]{1,0:T(8,128)(2,1)S(1)} %get-tuple-element.273), channel_id=1, source_target_pairs={{0,6},{1,7},{2,4},{3,5},{4,2},{5,3},{6,0},{7,1},{8,14},{9,15},{10,... | collective-permute-start | bytes 294920 | tf_op jit(solution)/shard_map/ppermute | solution.py:183
  109.5 2.6 %collective-permute-start.39 = (bf16[32,1536]{1,0:T(8,128)(2,1)S(1)}, bf16[32,1536]{1,0:T(8,128)(2,1)S(1)}, u32[]{:S(2)}, u32[]{:S(2)}) collective-permute-start(bf16[32,1536]{1,0:T(8,128)(2,1)S(1)} %get-tuple-element.267), channel_id=1, source_target_pairs={{0,4},{1,5},{2,6},{3,7},{4,0},{5,1},{6,2},{7,3},{8,12},{9,13},{10,... | collective-permute-start | bytes 294920 | tf_op jit(solution)/shard_map/ppermute | solution.py:183
  112.1 3.3 %grads_1.1 = (bf16[32,1536]{1,0:T(8,128)(2,1)S(1)}, bf16[32,1536]{1,0:T(8,128)(2,1)S(1)}, bf16[32,1536]{1,0:T(8,128)(2,1)S(1)}, bf16[32,1536]{1,0:T(8,128)(2,1)S...) custom-call(bf16[1,2,256,1536]{3,2,1,0:T(8,128)(2,1)S(1)} %copy-done, ...), custom_call_target="tpu_custom_call" | custom-call | flops 603979776 | bytes 6291456 | tf_op jit(solution)/shard_map/grads_1/pallas_call | solution.py:238
  115.4 3.2 %collective-permute-start.44 = (bf16[32,1536]{1,0:T(8,128)(2,1)S(1)}, bf16[32,1536]{1,0:T(8,128)(2,1)S(1)}, u32[]{:S(2)}, u32[]{:S(2)}) collective-permute-start(bf16[32,1536]{1,0:T(8,128)(2,1)S(1)} %get-tuple-element.278), channel_id=1, source_target_pairs={{0,2},{1,3},{2,0},{3,1},{4,6},{5,7},{6,4},{7,5},{8,10},{9,11},{10,... | collective-permute-start | bytes 294920 | tf_op jit(solution)/shard_map/ppermute | solution.py:183
  118.7 2.8 %collective-permute-done.40.refs_5_ = bf16[32,1536]{1,0:T(8,128)(2,1)S(1)} collective-permute-done((bf16[32,1536]{1,0:T(8,128)(2,1)S(1)}, bf16[32,1536]{1,0:T(8,128)(2,1)S(1)}, u32[]{:S(2)}, u32[]{:S(2)}) %collective-permute-start.40) | collective-permute-done | bytes 98336 | tf_op jit(solution)/shard_map/ppermute | solution.py:183
  122.0 3.3 %collective-permute-start.49 = (bf16[32,1536]{1,0:T(8,128)(2,1)S(1)}, bf16[32,1536]{1,0:T(8,128)(2,1)S(1)}, u32[]{:S(2)}, u32[]{:S(2)}) collective-permute-start(bf16[32,1536]{1,0:T(8,128)(2,1)S(1)} %get-tuple-element.283), channel_id=1, source_target_pairs={{0,7},{1,6},{2,5},{3,4},{4,3},{5,2},{6,1},{7,0},{8,15},{9,14},{10,... | collective-permute-start | bytes 294920 | tf_op jit(solution)/shard_map/ppermute | solution.py:183
  125.2 0.8 collective-permute-start.43
  126.2 3.5 %collective-permute-start.47 = (bf16[32,1536]{1,0:T(8,128)(2,1)S(1)}, bf16[32,1536]{1,0:T(8,128)(2,1)S(1)}, u32[]{:S(2)}, u32[]{:S(2)}) collective-permute-start(bf16[32,1536]{1,0:T(8,128)(2,1)S(1)} %get-tuple-element.281), channel_id=1, source_target_pairs={{0,5},{1,4},{2,7},{3,6},{4,1},{5,0},{6,3},{7,2},{8,13},{9,12},{10,... | collective-permute-start | bytes 294920 | tf_op jit(solution)/shard_map/ppermute | solution.py:183
  129.6 1.2 collective-permute-start.48
  130.8 0.8 collective-permute-start.36
  131.7 7.4 %collective-permute-start.37 = (bf16[32,1536]{1,0:T(8,128)(2,1)S(1)}, bf16[32,1536]{1,0:T(8,128)(2,1)S(1)}, u32[]{:S(2)}, u32[]{:S(2)}) collective-permute-start(bf16[32,1536]{1,0:T(8,128)(2,1)S(1)} %get-tuple-element.264), channel_id=1, source_target_pairs={{0,2},{1,3},{2,0},{3,1},{4,6},{5,7},{6,4},{7,5},{8,10},{9,11},{10,... | collective-permute-start | bytes 294920 | tf_op jit(solution)/shard_map/ppermute | solution.py:183
  139.5 2.1 %collective-permute-done.47.refs_5_ = bf16[32,1536]{1,0:T(8,128)(2,1)S(1)} collective-permute-done((bf16[32,1536]{1,0:T(8,128)(2,1)S(1)}, bf16[32,1536]{1,0:T(8,128)(2,1)S(1)}, u32[]{:S(2)}, u32[]{:S(2)}) %collective-permute-start.47) | collective-permute-done | bytes 98336 | tf_op jit(solution)/shard_map/ppermute | solution.py:183
  141.6 2.8 %collective-permute-start.42 = (bf16[32,1536]{1,0:T(8,128)(2,1)S(1)}, bf16[32,1536]{1,0:T(8,128)(2,1)S(1)}, u32[]{:S(2)}, u32[]{:S(2)}) collective-permute-start(bf16[32,1536]{1,0:T(8,128)(2,1)S(1)} %get-tuple-element.275), channel_id=1, source_target_pairs={{0,7},{1,6},{2,5},{3,4},{4,3},{5,2},{6,1},{7,0},{8,15},{9,14},{10,... | collective-permute-start | bytes 294920 | tf_op jit(solution)/shard_map/ppermute | solution.py:183
  144.4 1.3 fold_1.1
  145.8 1.1 collective-permute-start.50
  146.9 2.5 %collective-permute-start.52 = (bf16[32,1536]{1,0:T(8,128)(2,1)S(1)}, bf16[32,1536]{1,0:T(8,128)(2,1)S(1)}, u32[]{:S(2)}, u32[]{:S(2)}) collective-permute-start(bf16[32,1536]{1,0:T(8,128)(2,1)S(1)} %get-tuple-element.287), channel_id=1, source_target_pairs={{0,3},{1,2},{2,1},{3,0},{4,7},{5,6},{6,5},{7,4},{8,11},{9,10},{10,... | collective-permute-start | bytes 294920 | tf_op jit(solution)/shard_map/ppermute | solution.py:183
  149.8 2.9 %collective-permute-start.54 = (bf16[32,1536]{1,0:T(8,128)(2,1)S(1)}, bf16[32,1536]{1,0:T(8,128)(2,1)S(1)}, u32[]{:S(2)}, u32[]{:S(2)}) collective-permute-start(bf16[32,1536]{1,0:T(8,128)(2,1)S(1)} %get-tuple-element.289), channel_id=1, source_target_pairs={{0,5},{1,4},{2,7},{3,6},{4,1},{5,0},{6,3},{7,2},{8,13},{9,12},{10,... | collective-permute-start | bytes 294920 | tf_op jit(solution)/shard_map/ppermute | solution.py:183
  152.7 1.4 collective-permute-start.55
  154.2 2.8 %collective-permute-start.56 = (bf16[32,1536]{1,0:T(8,128)(2,1)S(1)}, bf16[32,1536]{1,0:T(8,128)(2,1)S(1)}, u32[]{:S(2)}, u32[]{:S(2)}) collective-permute-start(bf16[32,1536]{1,0:T(8,128)(2,1)S(1)} %get-tuple-element.291), channel_id=1, source_target_pairs={{0,7},{1,6},{2,5},{3,4},{4,3},{5,2},{6,1},{7,0},{8,15},{9,14},{10,... | collective-permute-start | bytes 294920 | tf_op jit(solution)/shard_map/ppermute | solution.py:183
  157.0 1.7 %back_1.1.back_ref = f32[256,1536]{1,0:T(8,128)S(1)} custom-call(bf16[1,384,1536]{2,1,0:T(8,128)(2,1)S(1)} %copy-done.2, f32[256,1536]{1,0:T(8,128)S(1)} %get-tuple-element.262.factor_ref, bf16[32,1536]{1,0:T(8,128)(2,1)S(1)} %get-tuple-element.260.refs_0_, bf16[32,1536]{1,0:T(8,128)(2,1)S(1)} %collective-permute-done.36.refs_1_, ...), custom_call_target="tpu_custom_call" | custom-call | flops 301989888 | bytes 4718592 | tf_op jit(solution)/shard_map/back_1/pallas_call | solution.py:238
  158.7 3.6 %collective-permute-done.53.refs_4_ = bf16[32,1536]{1,0:T(8,128)(2,1)S(1)} collective-permute-done((bf16[32,1536]{1,0:T(8,128)(2,1)S(1)}, bf16[32,1536]{1,0:T(8,128)(2,1)S(1)}, u32[]{:S(2)}, u32[]{:S(2)}) %collective-permute-start.53) | collective-permute-done | bytes 98336 | tf_op jit(solution)/shard_map/ppermute | solution.py:183
  162.4 2.3 %collective-permute-done.54.refs_5_ = bf16[32,1536]{1,0:T(8,128)(2,1)S(1)} collective-permute-done((bf16[32,1536]{1,0:T(8,128)(2,1)S(1)}, bf16[32,1536]{1,0:T(8,128)(2,1)S(1)}, u32[]{:S(2)}, u32[]{:S(2)}) %collective-permute-start.54) | collective-permute-done | bytes 98336 | tf_op jit(solution)/shard_map/ppermute | solution.py:183
  164.6 4.2 %result_1.1 = bf16[1,2,256,1536]{3,2,1,0:T(8,128)(2,1)} custom-call(bf16[1,2,256,1536]{3,2,1,0:T(8,128)(2,1)S(1)} %copy-done, f32[1,1536]{1,0:T(1,128)S(1)} %copy-done.9, bf16[1,384,1536]{2,1,0:T(8,128)(2,1)S(1)} %copy-done.1, bf16[1,256,256]{2,1,0:T(8,128)(2,1)S(1)} %copy-done.8, f32[256,1536]{1,0:T(8,128)S(1)} %back_1.1.back_ref, ...), custom_call_target="tpu_custom_call", output_to_operand_aliasing={{}: (15, {})} | custom-call | flops 905969664 | bytes 6291456 | tf_op jit(solution)/shard_map/result_1/pallas_call | solution.py:238
  (91 shorter events, 7.1 us)
Async XLA Ops:
  0.0 13.7 %copy-start.2 = (bf16[1,384,1536]{2,1,0:T(8,128)(2,1)S(1)}, bf16[1,384,1536]{2,1,0:T(8,128)(2,1)}, u32[]{:S(2)}) copy-start(bf16[1,384,1536]{2,1,0:T(8,128)(2,1)} %w_gate_ref.7) | copy-start | bytes 3538948
  5.2 14.2 %collective-permute-start = (bf16[32,1536]{1,0:T(8,128)(2,1)}, bf16[32,1536]{1,0:T(8,128)(2,1)S(1)}, u32[]{:S(2)}, u32[]{:S(2)}) collective-permute-start(bf16[32,1536]{1,0:T(8,128)(2,1)} %get-tuple-element.152), channel_id=1, source_target_pairs={{0,1},{1,0},{2,3},{3,2},{4,5},{5,4},{6,7},{7,6},{8,9},{9,8},{10,11... | collective-permute-start | bytes 294920 | tf_op jit(solution)/shard_map/ppermute | solution.py:183
  6.7 15.0 %collective-permute-start.2 = (bf16[32,1536]{1,0:T(8,128)(2,1)}, bf16[32,1536]{1,0:T(8,128)(2,1)S(1)}, u32[]{:S(2)}, u32[]{:S(2)}) collective-permute-start(bf16[32,1536]{1,0:T(8,128)(2,1)} %get-tuple-element.159), channel_id=1, source_target_pairs={{0,4},{1,5},{2,6},{3,7},{4,0},{5,1},{6,2},{7,3},{8,12},{9,13},{10,... | collective-permute-start | bytes 294920 | tf_op jit(solution)/shard_map/ppermute | solution.py:183
  9.3 12.4 %collective-permute-start.1 = (bf16[32,1536]{1,0:T(8,128)(2,1)}, bf16[32,1536]{1,0:T(8,128)(2,1)S(1)}, u32[]{:S(2)}, u32[]{:S(2)}) collective-permute-start(bf16[32,1536]{1,0:T(8,128)(2,1)} %get-tuple-element.155), channel_id=1, source_target_pairs={{0,2},{1,3},{2,0},{3,1},{4,6},{5,7},{6,4},{7,5},{8,10},{9,11},{10,... | collective-permute-start | bytes 294920 | tf_op jit(solution)/shard_map/ppermute | solution.py:183
  10.9 11.6 %collective-permute-start.4 = (bf16[32,1536]{1,0:T(8,128)(2,1)}, bf16[32,1536]{1,0:T(8,128)(2,1)S(1)}, u32[]{:S(2)}, u32[]{:S(2)}) collective-permute-start(bf16[32,1536]{1,0:T(8,128)(2,1)} %get-tuple-element.164), channel_id=1, source_target_pairs={{0,5},{1,4},{2,7},{3,6},{4,1},{5,0},{6,3},{7,2},{8,13},{9,12},{10,... | collective-permute-start | bytes 294920 | tf_op jit(solution)/shard_map/ppermute | solution.py:183
  11.2 15.1 %collective-permute-start.5 = (bf16[32,1536]{1,0:T(8,128)(2,1)}, bf16[32,1536]{1,0:T(8,128)(2,1)S(1)}, u32[]{:S(2)}, u32[]{:S(2)}) collective-permute-start(bf16[32,1536]{1,0:T(8,128)(2,1)} %get-tuple-element.167), channel_id=1, source_target_pairs={{0,6},{1,7},{2,4},{3,5},{4,2},{5,3},{6,0},{7,1},{8,14},{9,15},{10,... | collective-permute-start | bytes 294920 | tf_op jit(solution)/shard_map/ppermute | solution.py:183
  16.1 24.2 %copy-start.11 = (bf16[1,32,64]{2,1,0:T(8,128)(2,1)S(1)}, bf16[1,32,64]{2,1,0:T(8,128)(2,1)}, u32[]{:S(2)}) copy-start(bf16[1,32,64]{2,1,0:T(8,128)(2,1)} %l_ref.1) | copy-start | bytes 12292
  16.1 24.4 %copy-start.10 = (bf16[32,1536]{1,0:T(8,128)(2,1)S(1)}, bf16[32,1536]{1,0:T(8,128)(2,1)}, u32[]{:S(2)}) copy-start(bf16[32,1536]{1,0:T(8,128)(2,1)} %get-tuple-element.150.refs_0_) | copy-start | bytes 294916
  19.3 44.0 %copy-start.1 = (bf16[1,384,1536]{2,1,0:T(8,128)(2,1)S(1)}, bf16[1,384,1536]{2,1,0:T(8,128)(2,1)}, u32[]{:S(2)}) copy-start(bf16[1,384,1536]{2,1,0:T(8,128)(2,1)} %w_value_ref.3) | copy-start | bytes 3538948
  19.3 44.0 %copy-start.8 = (bf16[1,256,256]{2,1,0:T(8,128)(2,1)S(1)}, bf16[1,256,256]{2,1,0:T(8,128)(2,1)}, u32[]{:S(2)}) copy-start(bf16[1,256,256]{2,1,0:T(8,128)(2,1)} %r_ref.7) | copy-start | bytes 393220
  19.4 8.8 %collective-permute-start.6 = (bf16[32,1536]{1,0:T(8,128)(2,1)S(1)}, bf16[32,1536]{1,0:T(8,128)(2,1)S(1)}, u32[]{:S(2)}, u32[]{:S(2)}) collective-permute-start(bf16[32,1536]{1,0:T(8,128)(2,1)S(1)} %copy-done.13), channel_id=1, source_target_pairs={{0,7},{1,6},{2,5},{3,4},{4,3},{5,2},{6,1},{7,0},{8,15},{9,14},{10,... | collective-permute-start | bytes 294920 | tf_op jit(solution)/shard_map/ppermute | solution.py:183
  21.8 6.5 %collective-permute-start.3 = (bf16[32,1536]{1,0:T(8,128)(2,1)S(1)}, bf16[32,1536]{1,0:T(8,128)(2,1)S(1)}, u32[]{:S(2)}, u32[]{:S(2)}) collective-permute-start(bf16[32,1536]{1,0:T(8,128)(2,1)S(1)} %copy-done.12), channel_id=1, source_target_pairs={{0,3},{1,2},{2,1},{3,0},{4,7},{5,6},{6,5},{7,4},{8,11},{9,10},{10,... | collective-permute-start | bytes 294920 | tf_op jit(solution)/shard_map/ppermute | solution.py:183
  21.8 7.1 %collective-permute-start.9 = (bf16[32,1536]{1,0:T(8,128)(2,1)S(1)}, bf16[32,1536]{1,0:T(8,128)(2,1)S(1)}, u32[]{:S(2)}, u32[]{:S(2)}) collective-permute-start(bf16[32,1536]{1,0:T(8,128)(2,1)S(1)} %get-tuple-element.180), channel_id=1, source_target_pairs={{0,1},{1,0},{2,3},{3,2},{4,5},{5,4},{6,7},{7,6},{8,9},{9,8},{10,11... | collective-permute-start | bytes 294920 | tf_op jit(solution)/shard_map/ppermute | solution.py:183
  22.6 13.5 %collective-permute-start.10 = (bf16[32,1536]{1,0:T(8,128)(2,1)S(1)}, bf16[32,1536]{1,0:T(8,128)(2,1)S(1)}, u32[]{:S(2)}, u32[]{:S(2)}) collective-permute-start(bf16[32,1536]{1,0:T(8,128)(2,1)S(1)} %get-tuple-element.185), channel_id=1, source_target_pairs={{0,4},{1,5},{2,6},{3,7},{4,0},{5,1},{6,2},{7,3},{8,12},{9,13},{10,... | collective-permute-start | bytes 294920 | tf_op jit(solution)/shard_map/ppermute | solution.py:183
  26.3 15.5 %collective-permute-start.12 = (bf16[32,1536]{1,0:T(8,128)(2,1)S(1)}, bf16[32,1536]{1,0:T(8,128)(2,1)S(1)}, u32[]{:S(2)}, u32[]{:S(2)}) collective-permute-start(bf16[32,1536]{1,0:T(8,128)(2,1)S(1)} %get-tuple-element.190), channel_id=1, source_target_pairs={{0,5},{1,4},{2,7},{3,6},{4,1},{5,0},{6,3},{7,2},{8,13},{9,12},{10,... | collective-permute-start | bytes 294920 | tf_op jit(solution)/shard_map/ppermute | solution.py:183
  28.9 19.3 %collective-permute-start.14 = (bf16[32,1536]{1,0:T(8,128)(2,1)S(1)}, bf16[32,1536]{1,0:T(8,128)(2,1)S(1)}, u32[]{:S(2)}, u32[]{:S(2)}) collective-permute-start(bf16[32,1536]{1,0:T(8,128)(2,1)S(1)} %get-tuple-element.196), channel_id=1, source_target_pairs={{0,7},{1,6},{2,5},{3,4},{4,3},{5,2},{6,1},{7,0},{8,15},{9,14},{10,... | collective-permute-start | bytes 294920 | tf_op jit(solution)/shard_map/ppermute | solution.py:183
  36.0 6.6 %collective-permute-start.11 = (bf16[32,1536]{1,0:T(8,128)(2,1)S(1)}, bf16[32,1536]{1,0:T(8,128)(2,1)S(1)}, u32[]{:S(2)}, u32[]{:S(2)}) collective-permute-start(bf16[32,1536]{1,0:T(8,128)(2,1)S(1)} %get-tuple-element.186), channel_id=1, source_target_pairs={{0,3},{1,2},{2,1},{3,0},{4,7},{5,6},{6,5},{7,4},{8,11},{9,10},{10,... | collective-permute-start | bytes 294920 | tf_op jit(solution)/shard_map/ppermute | solution.py:183
  36.4 8.6 %collective-permute-start.13 = (bf16[32,1536]{1,0:T(8,128)(2,1)S(1)}, bf16[32,1536]{1,0:T(8,128)(2,1)S(1)}, u32[]{:S(2)}, u32[]{:S(2)}) collective-permute-start(bf16[32,1536]{1,0:T(8,128)(2,1)S(1)} %get-tuple-element.193), channel_id=1, source_target_pairs={{0,6},{1,7},{2,4},{3,5},{4,2},{5,3},{6,0},{7,1},{8,14},{9,15},{10,... | collective-permute-start | bytes 294920 | tf_op jit(solution)/shard_map/ppermute | solution.py:183
  39.4 9.1 %collective-permute-start.7 = (bf16[32,1536]{1,0:T(8,128)(2,1)S(1)}, bf16[32,1536]{1,0:T(8,128)(2,1)S(1)}, u32[]{:S(2)}, u32[]{:S(2)}) collective-permute-start(bf16[32,1536]{1,0:T(8,128)(2,1)S(1)} %get-tuple-element.175), channel_id=1, source_target_pairs={{0,2},{1,3},{2,0},{3,1},{4,6},{5,7},{6,4},{7,5},{8,10},{9,11},{10,... | collective-permute-start | bytes 294920 | tf_op jit(solution)/shard_map/ppermute | solution.py:183
  41.8 8.5 %collective-permute-start.16 = (bf16[32,1536]{1,0:T(8,128)(2,1)S(1)}, bf16[32,1536]{1,0:T(8,128)(2,1)S(1)}, u32[]{:S(2)}, u32[]{:S(2)}) collective-permute-start(bf16[32,1536]{1,0:T(8,128)(2,1)S(1)} %get-tuple-element.203), channel_id=1, source_target_pairs={{0,4},{1,5},{2,6},{3,7},{4,0},{5,1},{6,2},{7,3},{8,12},{9,13},{10,... | collective-permute-start | bytes 294920 | tf_op jit(solution)/shard_map/ppermute | solution.py:183
  42.6 9.3 %collective-permute-start.15 = (bf16[32,1536]{1,0:T(8,128)(2,1)S(1)}, bf16[32,1536]{1,0:T(8,128)(2,1)S(1)}, u32[]{:S(2)}, u32[]{:S(2)}) collective-permute-start(bf16[32,1536]{1,0:T(8,128)(2,1)S(1)} %get-tuple-element.199), channel_id=1, source_target_pairs={{0,2},{1,3},{2,0},{3,1},{4,6},{5,7},{6,4},{7,5},{8,10},{9,11},{10,... | collective-permute-start | bytes 294920 | tf_op jit(solution)/shard_map/ppermute | solution.py:183
  44.9 11.4 %collective-permute-start.18 = (bf16[32,1536]{1,0:T(8,128)(2,1)S(1)}, bf16[32,1536]{1,0:T(8,128)(2,1)S(1)}, u32[]{:S(2)}, u32[]{:S(2)}) collective-permute-start(bf16[32,1536]{1,0:T(8,128)(2,1)S(1)} %get-tuple-element.208), channel_id=1, source_target_pairs={{0,5},{1,4},{2,7},{3,6},{4,1},{5,0},{6,3},{7,2},{8,13},{9,12},{10,... | collective-permute-start | bytes 294920 | tf_op jit(solution)/shard_map/ppermute | solution.py:183
  48.2 10.7 %collective-permute-start.19 = (bf16[32,1536]{1,0:T(8,128)(2,1)S(1)}, bf16[32,1536]{1,0:T(8,128)(2,1)S(1)}, u32[]{:S(2)}, u32[]{:S(2)}) collective-permute-start(bf16[32,1536]{1,0:T(8,128)(2,1)S(1)} %get-tuple-element.211), channel_id=1, source_target_pairs={{0,6},{1,7},{2,4},{3,5},{4,2},{5,3},{6,0},{7,1},{8,14},{9,15},{10,... | collective-permute-start | bytes 294920 | tf_op jit(solution)/shard_map/ppermute | solution.py:183
  48.4 11.2 %collective-permute-start.8 = (bf16[32,1536]{1,0:T(8,128)(2,1)S(1)}, bf16[32,1536]{1,0:T(8,128)(2,1)S(1)}, u32[]{:S(2)}, u32[]{:S(2)}) collective-permute-start(bf16[32,1536]{1,0:T(8,128)(2,1)S(1)} %get-tuple-element.176), channel_id=1, source_target_pairs={{0,1},{1,0},{2,3},{3,2},{4,5},{5,4},{6,7},{7,6},{8,9},{9,8},{10,11... | collective-permute-start | bytes 294920 | tf_op jit(solution)/shard_map/ppermute | solution.py:183
  50.3 12.4 %collective-permute-start.17 = (bf16[32,1536]{1,0:T(8,128)(2,1)S(1)}, bf16[32,1536]{1,0:T(8,128)(2,1)S(1)}, u32[]{:S(2)}, u32[]{:S(2)}) collective-permute-start(bf16[32,1536]{1,0:T(8,128)(2,1)S(1)} %get-tuple-element.204), channel_id=1, source_target_pairs={{0,3},{1,2},{2,1},{3,0},{4,7},{5,6},{6,5},{7,4},{8,11},{9,10},{10,... | collective-permute-start | bytes 294920 | tf_op jit(solution)/shard_map/ppermute | solution.py:183
  51.9 14.3 %collective-permute-start.23 = (bf16[32,1536]{1,0:T(8,128)(2,1)S(1)}, bf16[32,1536]{1,0:T(8,128)(2,1)S(1)}, u32[]{:S(2)}, u32[]{:S(2)}) collective-permute-start(bf16[32,1536]{1,0:T(8,128)(2,1)S(1)} %get-tuple-element.226), channel_id=1, source_target_pairs={{0,1},{1,0},{2,3},{3,2},{4,5},{5,4},{6,7},{7,6},{8,9},{9,8},{10,11... | collective-permute-start | bytes 294920 | tf_op jit(solution)/shard_map/ppermute | solution.py:183
  56.3 12.1 %collective-permute-start.25 = (bf16[32,1536]{1,0:T(8,128)(2,1)S(1)}, bf16[32,1536]{1,0:T(8,128)(2,1)S(1)}, u32[]{:S(2)}, u32[]{:S(2)}) collective-permute-start(bf16[32,1536]{1,0:T(8,128)(2,1)S(1)} %get-tuple-element.233), channel_id=1, source_target_pairs={{0,4},{1,5},{2,6},{3,7},{4,0},{5,1},{6,2},{7,3},{8,12},{9,13},{10,... | collective-permute-start | bytes 294920 | tf_op jit(solution)/shard_map/ppermute | solution.py:183
  58.9 12.9 %collective-permute-start.21 = (bf16[32,1536]{1,0:T(8,128)(2,1)S(1)}, bf16[32,1536]{1,0:T(8,128)(2,1)S(1)}, u32[]{:S(2)}, u32[]{:S(2)}) collective-permute-start(bf16[32,1536]{1,0:T(8,128)(2,1)S(1)} %get-tuple-element.220), channel_id=1, source_target_pairs={{0,5},{1,4},{2,7},{3,6},{4,1},{5,0},{6,3},{7,2},{8,13},{9,12},{10,... | collective-permute-start | bytes 294920 | tf_op jit(solution)/shard_map/ppermute | solution.py:183
  59.6 12.3 %collective-permute-start.20 = (bf16[32,1536]{1,0:T(8,128)(2,1)S(1)}, bf16[32,1536]{1,0:T(8,128)(2,1)S(1)}, u32[]{:S(2)}, u32[]{:S(2)}) collective-permute-start(bf16[32,1536]{1,0:T(8,128)(2,1)S(1)} %get-tuple-element.214), channel_id=1, source_target_pairs={{0,7},{1,6},{2,5},{3,4},{4,3},{5,2},{6,1},{7,0},{8,15},{9,14},{10,... | collective-permute-start | bytes 294920 | tf_op jit(solution)/shard_map/ppermute | solution.py:183
  62.7 12.9 %collective-permute-start.24 = (bf16[32,1536]{1,0:T(8,128)(2,1)S(1)}, bf16[32,1536]{1,0:T(8,128)(2,1)S(1)}, u32[]{:S(2)}, u32[]{:S(2)}) collective-permute-start(bf16[32,1536]{1,0:T(8,128)(2,1)S(1)} %get-tuple-element.229), channel_id=1, source_target_pairs={{0,2},{1,3},{2,0},{3,1},{4,6},{5,7},{6,4},{7,5},{8,10},{9,11},{10,... | collective-permute-start | bytes 294920 | tf_op jit(solution)/shard_map/ppermute | solution.py:183
  66.2 9.4 %collective-permute-start.28 = (bf16[32,1536]{1,0:T(8,128)(2,1)S(1)}, bf16[32,1536]{1,0:T(8,128)(2,1)S(1)}, u32[]{:S(2)}, u32[]{:S(2)}) collective-permute-start(bf16[32,1536]{1,0:T(8,128)(2,1)S(1)} %get-tuple-element.242), channel_id=1, source_target_pairs={{0,7},{1,6},{2,5},{3,4},{4,3},{5,2},{6,1},{7,0},{8,15},{9,14},{10,... | collective-permute-start | bytes 294920 | tf_op jit(solution)/shard_map/ppermute | solution.py:183
  68.4 7.7 %collective-permute-start.26 = (bf16[32,1536]{1,0:T(8,128)(2,1)S(1)}, bf16[32,1536]{1,0:T(8,128)(2,1)S(1)}, u32[]{:S(2)}, u32[]{:S(2)}) collective-permute-start(bf16[32,1536]{1,0:T(8,128)(2,1)S(1)} %get-tuple-element.234), channel_id=1, source_target_pairs={{0,3},{1,2},{2,1},{3,0},{4,7},{5,6},{6,5},{7,4},{8,11},{9,10},{10,... | collective-permute-start | bytes 294920 | tf_op jit(solution)/shard_map/ppermute | solution.py:183
  71.8 10.3 %collective-permute-start.22 = (bf16[32,1536]{1,0:T(8,128)(2,1)S(1)}, bf16[32,1536]{1,0:T(8,128)(2,1)S(1)}, u32[]{:S(2)}, u32[]{:S(2)}) collective-permute-start(bf16[32,1536]{1,0:T(8,128)(2,1)S(1)} %get-tuple-element.221), channel_id=1, source_target_pairs={{0,4},{1,5},{2,6},{3,7},{4,0},{5,1},{6,2},{7,3},{8,12},{9,13},{10,... | collective-permute-start | bytes 294920 | tf_op jit(solution)/shard_map/ppermute | solution.py:183
  71.9 10.2 %collective-permute-start.27 = (bf16[32,1536]{1,0:T(8,128)(2,1)S(1)}, bf16[32,1536]{1,0:T(8,128)(2,1)S(1)}, u32[]{:S(2)}, u32[]{:S(2)}) collective-permute-start(bf16[32,1536]{1,0:T(8,128)(2,1)S(1)} %get-tuple-element.239), channel_id=1, source_target_pairs={{0,6},{1,7},{2,4},{3,5},{4,2},{5,3},{6,0},{7,1},{8,14},{9,15},{10,... | collective-permute-start | bytes 294920 | tf_op jit(solution)/shard_map/ppermute | solution.py:183
  75.6 14.6 %collective-permute-start.29 = (bf16[32,1536]{1,0:T(8,128)(2,1)S(1)}, bf16[32,1536]{1,0:T(8,128)(2,1)S(1)}, u32[]{:S(2)}, u32[]{:S(2)}) collective-permute-start(bf16[32,1536]{1,0:T(8,128)(2,1)S(1)} %get-tuple-element.246), channel_id=1, source_target_pairs={{0,1},{1,0},{2,3},{3,2},{4,5},{5,4},{6,7},{7,6},{8,9},{9,8},{10,11... | collective-permute-start | bytes 294920 | tf_op jit(solution)/shard_map/ppermute | solution.py:183
  82.1 12.4 %collective-permute-start.32 = (bf16[32,1536]{1,0:T(8,128)(2,1)S(1)}, bf16[32,1536]{1,0:T(8,128)(2,1)S(1)}, u32[]{:S(2)}, u32[]{:S(2)}) collective-permute-start(bf16[32,1536]{1,0:T(8,128)(2,1)S(1)} %get-tuple-element.250), channel_id=1, source_target_pairs={{0,6},{1,7},{2,4},{3,5},{4,2},{5,3},{6,0},{7,1},{8,14},{9,15},{10,... | collective-permute-start | bytes 294920 | tf_op jit(solution)/shard_map/ppermute | solution.py:183
  84.7 9.8 %collective-permute-start.31 = (bf16[32,1536]{1,0:T(8,128)(2,1)S(1)}, bf16[32,1536]{1,0:T(8,128)(2,1)S(1)}, u32[]{:S(2)}, u32[]{:S(2)}) collective-permute-start(bf16[32,1536]{1,0:T(8,128)(2,1)S(1)} %get-tuple-element.249), channel_id=1, source_target_pairs={{0,2},{1,3},{2,0},{3,1},{4,6},{5,7},{6,4},{7,5},{8,10},{9,11},{10,... | collective-permute-start | bytes 294920 | tf_op jit(solution)/shard_map/ppermute | solution.py:183
  86.2 8.4 %collective-permute-start.33 = (bf16[32,1536]{1,0:T(8,128)(2,1)S(1)}, bf16[32,1536]{1,0:T(8,128)(2,1)S(1)}, u32[]{:S(2)}, u32[]{:S(2)}) collective-permute-start(bf16[32,1536]{1,0:T(8,128)(2,1)S(1)} %get-tuple-element.251), channel_id=1, source_target_pairs={{0,3},{1,2},{2,1},{3,0},{4,7},{5,6},{6,5},{7,4},{8,11},{9,10},{10,... | collective-permute-start | bytes 294920 | tf_op jit(solution)/shard_map/ppermute | solution.py:183
  87.5 7.5 %collective-permute-start.30 = (bf16[32,1536]{1,0:T(8,128)(2,1)S(1)}, bf16[32,1536]{1,0:T(8,128)(2,1)S(1)}, u32[]{:S(2)}, u32[]{:S(2)}) collective-permute-start(bf16[32,1536]{1,0:T(8,128)(2,1)S(1)} %get-tuple-element.248), channel_id=1, source_target_pairs={{0,5},{1,4},{2,7},{3,6},{4,1},{5,0},{6,3},{7,2},{8,13},{9,12},{10,... | collective-permute-start | bytes 294920 | tf_op jit(solution)/shard_map/ppermute | solution.py:183
  90.3 21.8 %copy-start.4 = (bf16[1,384,1536]{2,1,0:T(8,128)(2,1)S(1)}, bf16[1,384,1536]{2,1,0:T(8,128)(2,1)}, u32[]{:S(2)}) copy-start(bf16[1,384,1536]{2,1,0:T(8,128)(2,1)} %w_out_ref.3) | copy-start | bytes 3538948
  94.5 17.6 %copy-start.7 = (bf16[1,256,1536]{2,1,0:T(8,128)(2,1)S(1)}, bf16[1,256,1536]{2,1,0:T(8,128)(2,1)}, u32[]{:S(2)}) copy-start(bf16[1,256,1536]{2,1,0:T(8,128)(2,1)} %refs_9_.1) | copy-start | bytes 2359300
  95.0 17.1 %collective-permute-start.34 = (bf16[256,1536]{1,0:T(8,128)(2,1)S(1)}, bf16[256,1536]{1,0:T(8,128)(2,1)S(1)}, u32[]{:S(2)}, u32[]{:S(2)}) collective-permute-start(bf16[256,1536]{1,0:T(8,128)(2,1)S(1)} %get-tuple-element.252), channel_id=1, source_target_pairs={{8,0},{16,8},{24,16},{9,1},{17,9},{25,17},{10,2},{18,10},{26,18},{... | collective-permute-start | bytes 2359304 | tf_op jit(solution)/shard_map/ppermute | solution.py:348
  97.1 8.1 %collective-permute-start.35 = (bf16[32,1536]{1,0:T(8,128)(2,1)S(1)}, bf16[32,1536]{1,0:T(8,128)(2,1)S(1)}, u32[]{:S(2)}, u32[]{:S(2)}) collective-permute-start(bf16[32,1536]{1,0:T(8,128)(2,1)S(1)} %get-tuple-element.259), channel_id=1, source_target_pairs={{0,7},{1,6},{2,5},{3,4},{4,3},{5,2},{6,1},{7,0},{8,15},{9,14},{10,... | collective-permute-start | bytes 294920 | tf_op jit(solution)/shard_map/ppermute | solution.py:183
  106.4 9.0 %collective-permute-start.41 = (bf16[32,1536]{1,0:T(8,128)(2,1)S(1)}, bf16[32,1536]{1,0:T(8,128)(2,1)S(1)}, u32[]{:S(2)}, u32[]{:S(2)}) collective-permute-start(bf16[32,1536]{1,0:T(8,128)(2,1)S(1)} %get-tuple-element.273), channel_id=1, source_target_pairs={{0,6},{1,7},{2,4},{3,5},{4,2},{5,3},{6,0},{7,1},{8,14},{9,15},{10,... | collective-permute-start | bytes 294920 | tf_op jit(solution)/shard_map/ppermute | solution.py:183
  109.1 12.4 %collective-permute-start.40 = (bf16[32,1536]{1,0:T(8,128)(2,1)S(1)}, bf16[32,1536]{1,0:T(8,128)(2,1)S(1)}, u32[]{:S(2)}, u32[]{:S(2)}) collective-permute-start(bf16[32,1536]{1,0:T(8,128)(2,1)S(1)} %get-tuple-element.270), channel_id=1, source_target_pairs={{0,5},{1,4},{2,7},{3,6},{4,1},{5,0},{6,3},{7,2},{8,13},{9,12},{10,... | collective-permute-start | bytes 294920 | tf_op jit(solution)/shard_map/ppermute | solution.py:183
  109.5 12.5 %collective-permute-start.39 = (bf16[32,1536]{1,0:T(8,128)(2,1)S(1)}, bf16[32,1536]{1,0:T(8,128)(2,1)S(1)}, u32[]{:S(2)}, u32[]{:S(2)}) collective-permute-start(bf16[32,1536]{1,0:T(8,128)(2,1)S(1)} %get-tuple-element.267), channel_id=1, source_target_pairs={{0,4},{1,5},{2,6},{3,7},{4,0},{5,1},{6,2},{7,3},{8,12},{9,13},{10,... | collective-permute-start | bytes 294920 | tf_op jit(solution)/shard_map/ppermute | solution.py:183
  115.4 10.7 %collective-permute-start.44 = (bf16[32,1536]{1,0:T(8,128)(2,1)S(1)}, bf16[32,1536]{1,0:T(8,128)(2,1)S(1)}, u32[]{:S(2)}, u32[]{:S(2)}) collective-permute-start(bf16[32,1536]{1,0:T(8,128)(2,1)S(1)} %get-tuple-element.278), channel_id=1, source_target_pairs={{0,2},{1,3},{2,0},{3,1},{4,6},{5,7},{6,4},{7,5},{8,10},{9,11},{10,... | collective-permute-start | bytes 294920 | tf_op jit(solution)/shard_map/ppermute | solution.py:183
  121.5 8.1 %collective-permute-start.45 = (bf16[32,1536]{1,0:T(8,128)(2,1)S(1)}, bf16[32,1536]{1,0:T(8,128)(2,1)S(1)}, u32[]{:S(2)}, u32[]{:S(2)}) collective-permute-start(bf16[32,1536]{1,0:T(8,128)(2,1)S(1)} %get-tuple-element.279), channel_id=1, source_target_pairs={{0,3},{1,2},{2,1},{3,0},{4,7},{5,6},{6,5},{7,4},{8,11},{9,10},{10,... | collective-permute-start | bytes 294920 | tf_op jit(solution)/shard_map/ppermute | solution.py:183
  122.0 8.9 %collective-permute-start.49 = (bf16[32,1536]{1,0:T(8,128)(2,1)S(1)}, bf16[32,1536]{1,0:T(8,128)(2,1)S(1)}, u32[]{:S(2)}, u32[]{:S(2)}) collective-permute-start(bf16[32,1536]{1,0:T(8,128)(2,1)S(1)} %get-tuple-element.283), channel_id=1, source_target_pairs={{0,7},{1,6},{2,5},{3,4},{4,3},{5,2},{6,1},{7,0},{8,15},{9,14},{10,... | collective-permute-start | bytes 294920 | tf_op jit(solution)/shard_map/ppermute | solution.py:183
  125.2 6.4 %collective-permute-start.43 = (bf16[32,1536]{1,0:T(8,128)(2,1)S(1)}, bf16[32,1536]{1,0:T(8,128)(2,1)S(1)}, u32[]{:S(2)}, u32[]{:S(2)}) collective-permute-start(bf16[32,1536]{1,0:T(8,128)(2,1)S(1)} %get-tuple-element.277), channel_id=1, source_target_pairs={{0,1},{1,0},{2,3},{3,2},{4,5},{5,4},{6,7},{7,6},{8,9},{9,8},{10,11... | collective-permute-start | bytes 294920 | tf_op jit(solution)/shard_map/ppermute | solution.py:183
  126.1 13.1 %collective-permute-start.46 = (bf16[32,1536]{1,0:T(8,128)(2,1)S(1)}, bf16[32,1536]{1,0:T(8,128)(2,1)S(1)}, u32[]{:S(2)}, u32[]{:S(2)}) collective-permute-start(bf16[32,1536]{1,0:T(8,128)(2,1)S(1)} %get-tuple-element.280), channel_id=1, source_target_pairs={{0,4},{1,5},{2,6},{3,7},{4,0},{5,1},{6,2},{7,3},{8,12},{9,13},{10,... | collective-permute-start | bytes 294920 | tf_op jit(solution)/shard_map/ppermute | solution.py:183
  126.2 15.4 %collective-permute-start.47 = (bf16[32,1536]{1,0:T(8,128)(2,1)S(1)}, bf16[32,1536]{1,0:T(8,128)(2,1)S(1)}, u32[]{:S(2)}, u32[]{:S(2)}) collective-permute-start(bf16[32,1536]{1,0:T(8,128)(2,1)S(1)} %get-tuple-element.281), channel_id=1, source_target_pairs={{0,5},{1,4},{2,7},{3,6},{4,1},{5,0},{6,3},{7,2},{8,13},{9,12},{10,... | collective-permute-start | bytes 294920 | tf_op jit(solution)/shard_map/ppermute | solution.py:183
  129.6 14.8 %collective-permute-start.48 = (bf16[32,1536]{1,0:T(8,128)(2,1)S(1)}, bf16[32,1536]{1,0:T(8,128)(2,1)S(1)}, u32[]{:S(2)}, u32[]{:S(2)}) collective-permute-start(bf16[32,1536]{1,0:T(8,128)(2,1)S(1)} %get-tuple-element.282), channel_id=1, source_target_pairs={{0,6},{1,7},{2,4},{3,5},{4,2},{5,3},{6,0},{7,1},{8,14},{9,15},{10,... | collective-permute-start | bytes 294920 | tf_op jit(solution)/shard_map/ppermute | solution.py:183
  130.8 16.0 %collective-permute-start.36 = (bf16[32,1536]{1,0:T(8,128)(2,1)S(1)}, bf16[32,1536]{1,0:T(8,128)(2,1)S(1)}, u32[]{:S(2)}, u32[]{:S(2)}) collective-permute-start(bf16[32,1536]{1,0:T(8,128)(2,1)S(1)} %get-tuple-element.263), channel_id=1, source_target_pairs={{0,1},{1,0},{2,3},{3,2},{4,5},{5,4},{6,7},{7,6},{8,9},{9,8},{10,11... | collective-permute-start | bytes 294920 | tf_op jit(solution)/shard_map/ppermute | solution.py:183
  131.7 15.2 %collective-permute-start.37 = (bf16[32,1536]{1,0:T(8,128)(2,1)S(1)}, bf16[32,1536]{1,0:T(8,128)(2,1)S(1)}, u32[]{:S(2)}, u32[]{:S(2)}) collective-permute-start(bf16[32,1536]{1,0:T(8,128)(2,1)S(1)} %get-tuple-element.264), channel_id=1, source_target_pairs={{0,2},{1,3},{2,0},{3,1},{4,6},{5,7},{6,4},{7,5},{8,10},{9,11},{10,... | collective-permute-start | bytes 294920 | tf_op jit(solution)/shard_map/ppermute | solution.py:183
  139.2 10.1 %collective-permute-start.38 = (bf16[32,1536]{1,0:T(8,128)(2,1)S(1)}, bf16[32,1536]{1,0:T(8,128)(2,1)S(1)}, u32[]{:S(2)}, u32[]{:S(2)}) collective-permute-start(bf16[32,1536]{1,0:T(8,128)(2,1)S(1)} %get-tuple-element.265), channel_id=1, source_target_pairs={{0,3},{1,2},{2,1},{3,0},{4,7},{5,6},{6,5},{7,4},{8,11},{9,10},{10,... | collective-permute-start | bytes 294920 | tf_op jit(solution)/shard_map/ppermute | solution.py:183
  141.6 8.3 %collective-permute-start.42 = (bf16[32,1536]{1,0:T(8,128)(2,1)S(1)}, bf16[32,1536]{1,0:T(8,128)(2,1)S(1)}, u32[]{:S(2)}, u32[]{:S(2)}) collective-permute-start(bf16[32,1536]{1,0:T(8,128)(2,1)S(1)} %get-tuple-element.275), channel_id=1, source_target_pairs={{0,7},{1,6},{2,5},{3,4},{4,3},{5,2},{6,1},{7,0},{8,15},{9,14},{10,... | collective-permute-start | bytes 294920 | tf_op jit(solution)/shard_map/ppermute | solution.py:183
  145.8 7.0 %collective-permute-start.50 = (bf16[32,1536]{1,0:T(8,128)(2,1)S(1)}, bf16[32,1536]{1,0:T(8,128)(2,1)S(1)}, u32[]{:S(2)}, u32[]{:S(2)}) collective-permute-start(bf16[32,1536]{1,0:T(8,128)(2,1)S(1)} %get-tuple-element.285), channel_id=1, source_target_pairs={{0,1},{1,0},{2,3},{3,2},{4,5},{5,4},{6,7},{7,6},{8,9},{9,8},{10,11... | collective-permute-start | bytes 294920 | tf_op jit(solution)/shard_map/ppermute | solution.py:183
  146.9 7.3 %collective-permute-start.51 = (bf16[32,1536]{1,0:T(8,128)(2,1)S(1)}, bf16[32,1536]{1,0:T(8,128)(2,1)S(1)}, u32[]{:S(2)}, u32[]{:S(2)}) collective-permute-start(bf16[32,1536]{1,0:T(8,128)(2,1)S(1)} %get-tuple-element.286), channel_id=1, source_target_pairs={{0,2},{1,3},{2,0},{3,1},{4,6},{5,7},{6,4},{7,5},{8,10},{9,11},{10,... | collective-permute-start | bytes 294920 | tf_op jit(solution)/shard_map/ppermute | solution.py:183
  146.9 11.9 %collective-permute-start.52 = (bf16[32,1536]{1,0:T(8,128)(2,1)S(1)}, bf16[32,1536]{1,0:T(8,128)(2,1)S(1)}, u32[]{:S(2)}, u32[]{:S(2)}) collective-permute-start(bf16[32,1536]{1,0:T(8,128)(2,1)S(1)} %get-tuple-element.287), channel_id=1, source_target_pairs={{0,3},{1,2},{2,1},{3,0},{4,7},{5,6},{6,5},{7,4},{8,11},{9,10},{10,... | collective-permute-start | bytes 294920 | tf_op jit(solution)/shard_map/ppermute | solution.py:183
  149.3 13.0 %collective-permute-start.53 = (bf16[32,1536]{1,0:T(8,128)(2,1)S(1)}, bf16[32,1536]{1,0:T(8,128)(2,1)S(1)}, u32[]{:S(2)}, u32[]{:S(2)}) collective-permute-start(bf16[32,1536]{1,0:T(8,128)(2,1)S(1)} %get-tuple-element.288), channel_id=1, source_target_pairs={{0,4},{1,5},{2,6},{3,7},{4,0},{5,1},{6,2},{7,3},{8,12},{9,13},{10,... | collective-permute-start | bytes 294920 | tf_op jit(solution)/shard_map/ppermute | solution.py:183
  149.8 14.8 %collective-permute-start.54 = (bf16[32,1536]{1,0:T(8,128)(2,1)S(1)}, bf16[32,1536]{1,0:T(8,128)(2,1)S(1)}, u32[]{:S(2)}, u32[]{:S(2)}) collective-permute-start(bf16[32,1536]{1,0:T(8,128)(2,1)S(1)} %get-tuple-element.289), channel_id=1, source_target_pairs={{0,5},{1,4},{2,7},{3,6},{4,1},{5,0},{6,3},{7,2},{8,13},{9,12},{10,... | collective-permute-start | bytes 294920 | tf_op jit(solution)/shard_map/ppermute | solution.py:183
  152.7 11.9 %collective-permute-start.55 = (bf16[32,1536]{1,0:T(8,128)(2,1)S(1)}, bf16[32,1536]{1,0:T(8,128)(2,1)S(1)}, u32[]{:S(2)}, u32[]{:S(2)}) collective-permute-start(bf16[32,1536]{1,0:T(8,128)(2,1)S(1)} %get-tuple-element.290), channel_id=1, source_target_pairs={{0,6},{1,7},{2,4},{3,5},{4,2},{5,3},{6,0},{7,1},{8,14},{9,15},{10,... | collective-permute-start | bytes 294920 | tf_op jit(solution)/shard_map/ppermute | solution.py:183
  154.2 10.5 %collective-permute-start.56 = (bf16[32,1536]{1,0:T(8,128)(2,1)S(1)}, bf16[32,1536]{1,0:T(8,128)(2,1)S(1)}, u32[]{:S(2)}, u32[]{:S(2)}) collective-permute-start(bf16[32,1536]{1,0:T(8,128)(2,1)S(1)} %get-tuple-element.291), channel_id=1, source_target_pairs={{0,7},{1,6},{2,5},{3,4},{4,3},{5,2},{6,1},{7,0},{8,15},{9,14},{10,... | collective-permute-start | bytes 294920 | tf_op jit(solution)/shard_map/ppermute | solution.py:183
  (7 other events, 40.5 us)

commit v2 on v0

--- a/solution.py
+++ b/solution.py
@@ -21,8 +21,44 @@
     return lax.dot_general(a, b, (over, ((), ())), preferred_element_type=F32)
 
 
+PAIRINGS = (
+    ((0, 7), (1, 6), (2, 5), (3, 4)),
+    ((0, 1), (2, 4), (3, 7), (5, 6)),
+    ((0, 3), (1, 5), (2, 6), (4, 7)),
+    ((0, 4), (1, 2), (3, 5), (6, 7)),
+    ((0, 2), (1, 7), (3, 6), (4, 5)),
+    ((0, 6), (1, 4), (2, 3), (5, 7)),
+    ((0, 5), (1, 3), (2, 7), (4, 6)),
+)
+
+
+def partners(slot, count):
+    if slot == 0 or count != 8:
+        return [device ^ slot for device in range(count)]
+    both = dict(PAIRINGS[slot - 1])
+    both.update({b: a for a, b in both.items()})
+    return [both[device] for device in range(count)]
+
+
+def owner_of(slot, count):
+    me = lax.axis_index("seq")
+    if slot == 0 or count != 8:
+        return me ^ slot
+    packed = sum(partner << (3 * device) for device, partner in enumerate(partners(slot, count)))
+    return (packed >> (3 * me)) & 7
+
+
+def owners_of(slots, count):
+    if count != 8:
+        return slots ^ lax.axis_index("seq")
+    owners = jnp.zeros_like(slots)
+    for slot in range(count):
+        owners = jnp.where(slots == slot, owner_of(slot, count), owners)
+    return owners
+
+
 def rows_of(slot, size):
-    owner = lax.axis_index("seq") ^ slot
+    owner = owner_of(slot, lax.axis_size("seq"))
     return pl.ds(pl.multiple_of(owner * size, size), size)
 
 
@@ -87,16 +123,15 @@
     size = l_ref.shape[0]
     wide = count * size
     bits = count.bit_length() - 1
-    me = lax.axis_index("seq")
     iota = functools.partial(lax.broadcasted_iota, jnp.int32)
 
     shape = (count, size, count * count)
     tall = jnp.broadcast_to(l_ref[...].astype(F32)[None], shape)
-    tall = jnp.where(iota(shape, 2) >> bits == iota(shape, 0) ^ me, tall, 0.0)
+    tall = jnp.where(iota(shape, 2) >> bits == owners_of(iota(shape, 0), count), tall, 0.0)
     tall = tall.reshape(wide, count * count).astype(BF16)
 
     shape = (count * count, wide)
-    source = (iota(shape, 1) >> (size.bit_length() - 1)) ^ me
+    source = owners_of(iota(shape, 1) >> (size.bit_length() - 1), count)
     spread = dot(tall, jnp.where(iota(shape, 0) & (count - 1) == source, 1.0, 0.0).astype(BF16))
 
     row, column = iota((wide, wide), 0) & (size - 1), iota((wide, wide), 1) & (size - 1)
@@ -175,7 +210,7 @@
 
     def send(self, slots, after=()):
         for slot in slots:
-            pairs = [(i, i ^ slot) for i in range(len(self.parts))]
+            pairs = [*enumerate(partners(slot, len(self.parts)))]
             self.got[slot] = lax.ppermute(tied(self.parts[slot], after), "seq", pairs)
         return self
 
@@ -333,7 +368,7 @@
     gate_0, first_1.parts[0] = lax.optimization_barrier((gate_0, first_1.parts[0]))
     first_1.send(every)
     stacked, result_0 = result(0, gate_0, fold_0.all(), [(whole3, arrived_grad)], None)
-    result_0 = tied(result_0, [(first_1, slot) for slot in every[: min(4, count // 2)]])
+    result_0 = tied(result_0, [(first_1, slot) for slot in every[: min(3, count // 2)]])
     passed = lax.ppermute(result_0, "pipe", [(s, s - 1) for s in range(1, pipe)])
     mix_1 = Exchange(mix("mix_1", first_1.all(), False)).send(every)
     parts, factor_1 = grads(1, [(cut, passed), (cut3, loss_grad)])

time: 168 us -> 167 us (level); the launches traced: 165 us -> 167 us
  starting transfers between devices: 94.6 us -> 119 us
  waiting for transfers between devices: 35.7 us -> 13.3 us
    ppermute x56, starting transfers between devices: 92.7 us -> 117 us  [send(): self.got[slot] = lax.ppermute(tied(self.parts[slot], after), 'seq', pairs)]
    ppermute x56, waiting for transfers between devices: 33.2 us -> 10.4 us  [send(): self.got[slot] = lax.ppermute(tied(self.parts[slot], after), 'seq', pairs)]
  transfers between devices with their start and end apart: 57 -> 57, of which waited for: 13 -> 8; matrix products, arithmetic and copies ran while one was open for 0% -> 0% of each run, Pallas kernels for 14% -> 14%
where the time goes in v2:
time: 167 us
  starting transfers between devices  119 us (71%)
  Pallas kernels  32 us (19%)
  waiting for transfers between devices  13.3 us (8%)
  local copies, waits for them, and re-layouts  2.45 us (1%)
    ppermute x56, starting transfers between devices, send(): self.got[slot] = lax.ppermute(tied(self.parts[slot], after), 'seq', pairs)  117 us
    pallas_call x13, Pallas kernels, call(): pl.pallas_call(kernel, grid=(steps or width // block,), in_specs=[spec fo...  32 us
    ppermute x56, waiting for transfers between devices, send(): self.got[slot] = lax.ppermute(tied(self.parts[slot], after), 'seq', pairs)  10.4 us
  transfers between devices with their start and end apart: 57, of which 8 were waited for; matrix products, arithmetic and copies ran while one was open for 0% of the time, Pallas kernels for 14%

profile of v2, /device:TPU:2, one launch (start us, length us, event | category | flops | bytes accessed | tf_op | source)
XLA Modules:
  0.0 167.0 jit_solution(3894217360116128989)
XLA Ops:
  0.0 5.2 %first_0.1 = (bf16[32,1536]{1,0:T(8,128)(2,1)}, bf16[32,1536]{1,0:T(8,128)(2,1)}, bf16[32,1536]{1,0:T(8,128)(2,1)}, bf16[32,1536]{1,0:T(8,128)(2,1)}, bf16[32,15...) custom-call(bf16[1,2,256,1536]{3,2,1,0:T(8,128)(2,1)} %x_ref.11, ...), custom_call_target="tpu_custom_call" | custom-call | flops 603979776 | bytes 3145728 | tf_op jit(solution)/shard_map/first_0/pallas_call | solution.py:267
  5.2 4.6 %collective-permute-start = (bf16[32,1536]{1,0:T(8,128)(2,1)}, bf16[32,1536]{1,0:T(8,128)(2,1)S(1)}, u32[]{:S(2)}, u32[]{:S(2)}) collective-permute-start(bf16[32,1536]{1,0:T(8,128)(2,1)} %get-tuple-element.80), channel_id=1, source_target_pairs={{0,7},{1,6},{2,5},{3,4},{4,3},{5,2},{6,1},{7,0},{8,15},{9,14},{10,... | collective-permute-start | bytes 294920 | tf_op jit(solution)/shard_map/ppermute | solution.py:214
  10.6 1.7 %collective-permute-start.3 = (bf16[32,1536]{1,0:T(8,128)(2,1)}, bf16[32,1536]{1,0:T(8,128)(2,1)S(1)}, u32[]{:S(2)}, u32[]{:S(2)}) collective-permute-start(bf16[32,1536]{1,0:T(8,128)(2,1)} %get-tuple-element.83), channel_id=1, source_target_pairs={{0,4},{1,2},{2,1},{3,5},{4,0},{5,3},{6,7},{7,6},{8,12},{9,10},{10,... | collective-permute-start | bytes 294920 | tf_op jit(solution)/shard_map/ppermute | solution.py:214
  12.3 1.3 collective-permute-start.4
  13.9 3.5 %collective-permute-start.5 = (bf16[32,1536]{1,0:T(8,128)(2,1)}, bf16[32,1536]{1,0:T(8,128)(2,1)S(1)}, u32[]{:S(2)}, u32[]{:S(2)}) collective-permute-start(bf16[32,1536]{1,0:T(8,128)(2,1)} %get-tuple-element.85), channel_id=1, source_target_pairs={{0,6},{1,4},{2,3},{3,2},{4,1},{5,7},{6,0},{7,5},{8,14},{9,12},{10,... | collective-permute-start | bytes 294920 | tf_op jit(solution)/shard_map/ppermute | solution.py:214
  17.5 1.3 copy-done.3
  18.7 1.1 copy-done.5
  19.9 3.3 %grads_0.1 = (bf16[32,1536]{1,0:T(8,128)(2,1)S(1)}, bf16[32,1536]{1,0:T(8,128)(2,1)S(1)}, bf16[32,1536]{1,0:T(8,128)(2,1)S(1)}, bf16[32,1536]{1,0:T(8,128)(2,1)S...) custom-call(bf16[1,2,256,1536]{3,2,1,0:T(8,128)(2,1)S(1)} %copy-done, ...), custom_call_target="tpu_custom_call" | custom-call | flops 603979776 | bytes 6291456 | tf_op jit(solution)/shard_map/grads_0/pallas_call | solution.py:267
  23.2 1.7 %collective-permute-start.6 = (bf16[32,1536]{1,0:T(8,128)(2,1)S(1)}, bf16[32,1536]{1,0:T(8,128)(2,1)S(1)}, u32[]{:S(2)}, u32[]{:S(2)}) collective-permute-start(bf16[32,1536]{1,0:T(8,128)(2,1)S(1)} %copy-done.12), channel_id=1, source_target_pairs={{0,5},{1,3},{2,7},{3,1},{4,6},{5,0},{6,4},{7,2},{8,13},{9,11},{10,... | collective-permute-start | bytes 294920 | tf_op jit(solution)/shard_map/ppermute | solution.py:214
  24.9 7.5 %collective-permute-start.14 = (bf16[32,1536]{1,0:T(8,128)(2,1)S(1)}, bf16[32,1536]{1,0:T(8,128)(2,1)S(1)}, u32[]{:S(2)}, u32[]{:S(2)}) collective-permute-start(bf16[32,1536]{1,0:T(8,128)(2,1)S(1)} %get-tuple-element.98), channel_id=1, source_target_pairs={{0,7},{1,6},{2,5},{3,4},{4,3},{5,2},{6,1},{7,0},{8,15},{9,14},{10,... | collective-permute-start | bytes 294920 | tf_op jit(solution)/shard_map/ppermute | solution.py:214
  32.5 0.6 collective-permute-start.16
  33.2 2.9 %collective-permute-start.18 = (bf16[32,1536]{1,0:T(8,128)(2,1)S(1)}, bf16[32,1536]{1,0:T(8,128)(2,1)S(1)}, u32[]{:S(2)}, u32[]{:S(2)}) collective-permute-start(bf16[32,1536]{1,0:T(8,128)(2,1)S(1)} %get-tuple-element.102), channel_id=1, source_target_pairs={{0,2},{1,7},{2,0},{3,6},{4,5},{5,4},{6,3},{7,1},{8,10},{9,15},{10,... | collective-permute-start | bytes 294920 | tf_op jit(solution)/shard_map/ppermute | solution.py:214
  36.1 1.4 collective-permute-done.14.refs_1_
  37.6 2.2 %collective-permute-start.19 = (bf16[32,1536]{1,0:T(8,128)(2,1)S(1)}, bf16[32,1536]{1,0:T(8,128)(2,1)S(1)}, u32[]{:S(2)}, u32[]{:S(2)}) collective-permute-start(bf16[32,1536]{1,0:T(8,128)(2,1)S(1)} %get-tuple-element.103), channel_id=1, source_target_pairs={{0,6},{1,4},{2,3},{3,2},{4,1},{5,7},{6,0},{7,5},{8,14},{9,12},{10,... | collective-permute-start | bytes 294920 | tf_op jit(solution)/shard_map/ppermute | solution.py:214
  40.0 1.3 mix_0.1
  41.2 0.8 collective-permute-start.20
  42.0 1.6 collective-permute-start.10
  43.6 2.5 %collective-permute-done.17.refs_4_ = bf16[32,1536]{1,0:T(8,128)(2,1)S(1)} collective-permute-done((bf16[32,1536]{1,0:T(8,128)(2,1)S(1)}, bf16[32,1536]{1,0:T(8,128)(2,1)S(1)}, u32[]{:S(2)}, u32[]{:S(2)}) %collective-permute-start.17) | collective-permute-done | bytes 98336 | tf_op jit(solution)/shard_map/ppermute | solution.py:214
  46.0 3.5 %collective-permute-start.11 = (bf16[32,1536]{1,0:T(8,128)(2,1)S(1)}, bf16[32,1536]{1,0:T(8,128)(2,1)S(1)}, u32[]{:S(2)}, u32[]{:S(2)}) collective-permute-start(bf16[32,1536]{1,0:T(8,128)(2,1)S(1)} %get-tuple-element.92), channel_id=1, source_target_pairs={{0,2},{1,7},{2,0},{3,6},{4,5},{5,4},{6,3},{7,1},{8,10},{9,15},{10,... | collective-permute-start | bytes 294920 | tf_op jit(solution)/shard_map/ppermute | solution.py:214
  49.5 3.5 %collective-permute-start.12 = (bf16[32,1536]{1,0:T(8,128)(2,1)S(1)}, bf16[32,1536]{1,0:T(8,128)(2,1)S(1)}, u32[]{:S(2)}, u32[]{:S(2)}) collective-permute-start(bf16[32,1536]{1,0:T(8,128)(2,1)S(1)} %get-tuple-element.93), channel_id=1, source_target_pairs={{0,6},{1,4},{2,3},{3,2},{4,1},{5,7},{6,0},{7,5},{8,14},{9,12},{10,... | collective-permute-start | bytes 294920 | tf_op jit(solution)/shard_map/ppermute | solution.py:214
  53.0 1.8 %collective-permute-start.13 = (bf16[32,1536]{1,0:T(8,128)(2,1)S(1)}, bf16[32,1536]{1,0:T(8,128)(2,1)S(1)}, u32[]{:S(2)}, u32[]{:S(2)}) collective-permute-start(bf16[32,1536]{1,0:T(8,128)(2,1)S(1)} %get-tuple-element.94), channel_id=1, source_target_pairs={{0,5},{1,3},{2,7},{3,1},{4,6},{5,0},{6,4},{7,2},{8,13},{9,11},{10,... | collective-permute-start | bytes 294920 | tf_op jit(solution)/shard_map/ppermute | solution.py:214
  54.8 3.0 %collective-permute-start.7 = (bf16[32,1536]{1,0:T(8,128)(2,1)S(1)}, bf16[32,1536]{1,0:T(8,128)(2,1)S(1)}, u32[]{:S(2)}, u32[]{:S(2)}) collective-permute-start(bf16[32,1536]{1,0:T(8,128)(2,1)S(1)} %get-tuple-element.88), channel_id=1, source_target_pairs={{0,7},{1,6},{2,5},{3,4},{4,3},{5,2},{6,1},{7,0},{8,15},{9,14},{10,... | collective-permute-start | bytes 294920 | tf_op jit(solution)/shard_map/ppermute | solution.py:214
  57.8 2.0 %collective-permute-start.8 = (bf16[32,1536]{1,0:T(8,128)(2,1)S(1)}, bf16[32,1536]{1,0:T(8,128)(2,1)S(1)}, u32[]{:S(2)}, u32[]{:S(2)}) collective-permute-start(bf16[32,1536]{1,0:T(8,128)(2,1)S(1)} %get-tuple-element.89), channel_id=1, source_target_pairs={{0,1},{1,0},{2,4},{3,7},{4,2},{5,6},{6,5},{7,3},{8,9},{9,8},{10,12... | collective-permute-start | bytes 294920 | tf_op jit(solution)/shard_map/ppermute | solution.py:214
  60.4 1.4 fold_0.1
  61.8 1.1 collective-permute-start.21
  62.9 2.9 %collective-permute-done.13.refs_7_ = bf16[32,1536]{1,0:T(8,128)(2,1)S(1)} collective-permute-done((bf16[32,1536]{1,0:T(8,128)(2,1)S(1)}, bf16[32,1536]{1,0:T(8,128)(2,1)S(1)}, u32[]{:S(2)}, u32[]{:S(2)}) %collective-permute-start.13) | collective-permute-done | bytes 98336 | tf_op jit(solution)/shard_map/ppermute | solution.py:214
  65.8 0.9 collective-permute-start.22
  66.7 2.7 %collective-permute-start.23 = (bf16[32,1536]{1,0:T(8,128)(2,1)S(1)}, bf16[32,1536]{1,0:T(8,128)(2,1)S(1)}, u32[]{:S(2)}, u32[]{:S(2)}) collective-permute-start(bf16[32,1536]{1,0:T(8,128)(2,1)S(1)} %get-tuple-element.108), channel_id=1, source_target_pairs={{0,3},{1,5},{2,6},{3,0},{4,7},{5,1},{6,2},{7,4},{8,11},{9,13},{10,... | collective-permute-start | bytes 294920 | tf_op jit(solution)/shard_map/ppermute | solution.py:214
  69.4 1.9 %collective-permute-start.24 = (bf16[32,1536]{1,0:T(8,128)(2,1)S(1)}, bf16[32,1536]{1,0:T(8,128)(2,1)S(1)}, u32[]{:S(2)}, u32[]{:S(2)}) collective-permute-start(bf16[32,1536]{1,0:T(8,128)(2,1)S(1)} %get-tuple-element.109), channel_id=1, source_target_pairs={{0,4},{1,2},{2,1},{3,5},{4,0},{5,3},{6,7},{7,6},{8,12},{9,10},{10,... | collective-permute-start | bytes 294920 | tf_op jit(solution)/shard_map/ppermute | solution.py:214
  71.3 1.7 %collective-permute-start.25 = (bf16[32,1536]{1,0:T(8,128)(2,1)S(1)}, bf16[32,1536]{1,0:T(8,128)(2,1)S(1)}, u32[]{:S(2)}, u32[]{:S(2)}) collective-permute-start(bf16[32,1536]{1,0:T(8,128)(2,1)S(1)} %get-tuple-element.110), channel_id=1, source_target_pairs={{0,2},{1,7},{2,0},{3,6},{4,5},{5,4},{6,3},{7,1},{8,10},{9,15},{10,... | collective-permute-start | bytes 294920 | tf_op jit(solution)/shard_map/ppermute | solution.py:214
  73.0 1.3 collective-permute-start.26
  74.3 4.8 %collective-permute-start.27 = (bf16[32,1536]{1,0:T(8,128)(2,1)S(1)}, bf16[32,1536]{1,0:T(8,128)(2,1)S(1)}, u32[]{:S(2)}, u32[]{:S(2)}) collective-permute-start(bf16[32,1536]{1,0:T(8,128)(2,1)S(1)} %get-tuple-element.112), channel_id=1, source_target_pairs={{0,5},{1,3},{2,7},{3,1},{4,6},{5,0},{6,4},{7,2},{8,13},{9,11},{10,... | collective-permute-start | bytes 294920 | tf_op jit(solution)/shard_map/ppermute | solution.py:214
  79.2 3.0 %first_1.1 = (bf16[32,1536]{1,0:T(8,128)(2,1)S(1)}, bf16[32,1536]{1,0:T(8,128)(2,1)S(1)}, bf16[32,1536]{1,0:T(8,128)(2,1)S(1)}, bf16[32,1536]{1,0:T(8,128)(2,1)S...) custom-call(bf16[1,2,256,1536]{3,2,1,0:T(8,128)(2,1)S(1)} %copy-done, ...), custom_call_target="tpu_custom_call" | custom-call | flops 603979776 | bytes 3145728 | tf_op jit(solution)/shard_map/first_1/pallas_call | solution.py:267
  82.2 2.5 %collective-permute-start.28 = (bf16[32,1536]{1,0:T(8,128)(2,1)S(1)}, bf16[32,1536]{1,0:T(8,128)(2,1)S(1)}, u32[]{:S(2)}, u32[]{:S(2)}) collective-permute-start(bf16[32,1536]{1,0:T(8,128)(2,1)S(1)} %get-tuple-element.114), channel_id=1, source_target_pairs={{0,7},{1,6},{2,5},{3,4},{4,3},{5,2},{6,1},{7,0},{8,15},{9,14},{10,... | collective-permute-start | bytes 294920 | tf_op jit(solution)/shard_map/ppermute | solution.py:214
  84.7 2.8 %collective-permute-start.29 = (bf16[32,1536]{1,0:T(8,128)(2,1)S(1)}, bf16[32,1536]{1,0:T(8,128)(2,1)S(1)}, u32[]{:S(2)}, u32[]{:S(2)}) collective-permute-start(bf16[32,1536]{1,0:T(8,128)(2,1)S(1)} %get-tuple-element.115), channel_id=1, source_target_pairs={{0,1},{1,0},{2,4},{3,7},{4,2},{5,6},{6,5},{7,3},{8,9},{9,8},{10,12... | collective-permute-start | bytes 294920 | tf_op jit(solution)/shard_map/ppermute | solution.py:214
  87.5 1.7 %back_0.1.back_ref = f32[256,1536]{1,0:T(8,128)S(1)} custom-call(bf16[1,384,1536]{2,1,0:T(8,128)(2,1)S(1)} %copy-done.2, f32[256,1536]{1,0:T(8,128)S(1)} %get-tuple-element.78.factor_ref, bf16[32,1536]{1,0:T(8,128)(2,1)S(1)} %get-tuple-element.87.refs_0_, bf16[32,1536]{1,0:T(8,128)(2,1)S(1)} %collective-permute-done.7.refs_1_, ...), custom_call_target="tpu_custom_call" | custom-call | flops 301989888 | bytes 4718592 | tf_op jit(solution)/shard_map/back_0/pallas_call | solution.py:267
  89.3 4.1 %result_0.1 = (bf16[1,2,256,1536]{3,2,1,0:T(8,128)(2,1)}, bf16[256,1536]{1,0:T(8,128)(2,1)S(1)}) custom-call(bf16[1,2,256,1536]{3,2,1,0:T(8,128)(2,1)S(1)} %copy-done, f32[1,1536]{1,0:T(1,128)S(1)} %copy-done.9, bf16[1,384,1536]{2,1,0:T(8,128)(2,1)S(1)} %copy-done.1, bf16[1,256,256]{2,1,0:T(8,128)(2,1)S(1)} %copy-done.8, f32[256,1536]{1,0:T(8,128)S(1)} %back_0.1.back_ref, ...), custom_call_target="tpu_custom_call" | custom-call | flops 905969664 | bytes 6291456 | tf_op jit(solution)/shard_map/result_0/pallas_call | solution.py:267
  93.5 2.1 %collective-permute-start.31 = (bf16[256,1536]{1,0:T(8,128)(2,1)S(1)}, bf16[256,1536]{1,0:T(8,128)(2,1)S(1)}, u32[]{:S(2)}, u32[]{:S(2)}) collective-permute-start(bf16[256,1536]{1,0:T(8,128)(2,1)S(1)} %get-tuple-element.117), channel_id=1, source_target_pairs={{8,0},{16,8},{24,16},{9,1},{17,9},{25,17},{10,2},{18,10},{26,18},{... | collective-permute-start | bytes 2359304 | tf_op jit(solution)/shard_map/ppermute | solution.py:372
  95.6 1.4 collective-permute-start.32
  97.0 0.6 collective-permute-start.33
  97.7 3.3 %collective-permute-start.34 = (bf16[32,1536]{1,0:T(8,128)(2,1)S(1)}, bf16[32,1536]{1,0:T(8,128)(2,1)S(1)}, u32[]{:S(2)}, u32[]{:S(2)}) collective-permute-start(bf16[32,1536]{1,0:T(8,128)(2,1)S(1)} %get-tuple-element.124), channel_id=1, source_target_pairs={{0,6},{1,4},{2,3},{3,2},{4,1},{5,7},{6,0},{7,5},{8,14},{9,12},{10,... | collective-permute-start | bytes 294920 | tf_op jit(solution)/shard_map/ppermute | solution.py:214
  100.9 1.1 collective-permute-start.35
  102.1 2.9 %collective-permute-done.31.refs_0_.refs_8_ = bf16[256,1536]{1,0:T(8,128)(2,1)S(1)} collective-permute-done((bf16[256,1536]{1,0:T(8,128)(2,1)S(1)}, bf16[256,1536]{1,0:T(8,128)(2,1)S(1)}, u32[]{:S(2)}, u32[]{:S(2)}) %collective-permute-start.31) | collective-permute-done | bytes 786464 | tf_op jit(solution)/shard_map/ppermute | solution.py:372
  104.9 3.3 %grads_1.1 = (bf16[32,1536]{1,0:T(8,128)(2,1)S(1)}, bf16[32,1536]{1,0:T(8,128)(2,1)S(1)}, bf16[32,1536]{1,0:T(8,128)(2,1)S(1)}, bf16[32,1536]{1,0:T(8,128)(2,1)S...) custom-call(bf16[1,2,256,1536]{3,2,1,0:T(8,128)(2,1)S(1)} %copy-done, ...), custom_call_target="tpu_custom_call" | custom-call | flops 603979776 | bytes 6291456 | tf_op jit(solution)/shard_map/grads_1/pallas_call | solution.py:267
  108.3 1.5 collective-permute-start.43
  110.4 3.3 %collective-permute-start.45 = (bf16[32,1536]{1,0:T(8,128)(2,1)S(1)}, bf16[32,1536]{1,0:T(8,128)(2,1)S(1)}, u32[]{:S(2)}, u32[]{:S(2)}) collective-permute-start(bf16[32,1536]{1,0:T(8,128)(2,1)S(1)} %get-tuple-element.137), channel_id=1, source_target_pairs={{0,3},{1,5},{2,6},{3,0},{4,7},{5,1},{6,2},{7,4},{8,11},{9,13},{10,... | collective-permute-start | bytes 294920 | tf_op jit(solution)/shard_map/ppermute | solution.py:214
  114.2 1.4 collective-permute-start.47
  115.9 1.2 collective-permute-start.48
  117.1 3.2 %collective-permute-start.49 = (bf16[32,1536]{1,0:T(8,128)(2,1)S(1)}, bf16[32,1536]{1,0:T(8,128)(2,1)S(1)}, u32[]{:S(2)}, u32[]{:S(2)}) collective-permute-start(bf16[32,1536]{1,0:T(8,128)(2,1)S(1)} %get-tuple-element.141), channel_id=1, source_target_pairs={{0,5},{1,3},{2,7},{3,1},{4,6},{5,0},{6,4},{7,2},{8,13},{9,11},{10,... | collective-permute-start | bytes 294920 | tf_op jit(solution)/shard_map/ppermute | solution.py:214
  120.2 1.2 mix_1.1
  121.5 9.1 %collective-permute-start.36 = (bf16[32,1536]{1,0:T(8,128)(2,1)S(1)}, bf16[32,1536]{1,0:T(8,128)(2,1)S(1)}, u32[]{:S(2)}, u32[]{:S(2)}) collective-permute-start(bf16[32,1536]{1,0:T(8,128)(2,1)S(1)} %get-tuple-element.127), channel_id=1, source_target_pairs={{0,7},{1,6},{2,5},{3,4},{4,3},{5,2},{6,1},{7,0},{8,15},{9,14},{10,... | collective-permute-start | bytes 294920 | tf_op jit(solution)/shard_map/ppermute | solution.py:214
  130.6 1.5 collective-permute-start.37
  132.2 2.5 %collective-permute-start.40 = (bf16[32,1536]{1,0:T(8,128)(2,1)S(1)}, bf16[32,1536]{1,0:T(8,128)(2,1)S(1)}, u32[]{:S(2)}, u32[]{:S(2)}) collective-permute-start(bf16[32,1536]{1,0:T(8,128)(2,1)S(1)} %get-tuple-element.131), channel_id=1, source_target_pairs={{0,2},{1,7},{2,0},{3,6},{4,5},{5,4},{6,3},{7,1},{8,10},{9,15},{10,... | collective-permute-start | bytes 294920 | tf_op jit(solution)/shard_map/ppermute | solution.py:214
  134.7 1.4 fold_1.1
  136.0 3.3 %collective-permute-start.41 = (bf16[32,1536]{1,0:T(8,128)(2,1)S(1)}, bf16[32,1536]{1,0:T(8,128)(2,1)S(1)}, u32[]{:S(2)}, u32[]{:S(2)}) collective-permute-start(bf16[32,1536]{1,0:T(8,128)(2,1)S(1)} %get-tuple-element.132), channel_id=1, source_target_pairs={{0,6},{1,4},{2,3},{3,2},{4,1},{5,7},{6,0},{7,5},{8,14},{9,12},{10,... | collective-permute-start | bytes 294920 | tf_op jit(solution)/shard_map/ppermute | solution.py:214
  139.8 8.2 %collective-permute-start.50 = (bf16[32,1536]{1,0:T(8,128)(2,1)S(1)}, bf16[32,1536]{1,0:T(8,128)(2,1)S(1)}, u32[]{:S(2)}, u32[]{:S(2)}) collective-permute-start(bf16[32,1536]{1,0:T(8,128)(2,1)S(1)} %get-tuple-element.143), channel_id=1, source_target_pairs={{0,7},{1,6},{2,5},{3,4},{4,3},{5,2},{6,1},{7,0},{8,15},{9,14},{10,... | collective-permute-start | bytes 294920 | tf_op jit(solution)/shard_map/ppermute | solution.py:214
  148.0 1.3 collective-permute-start.52
  149.3 0.7 collective-permute-start.53
  150.0 3.4 %collective-permute-start.54 = (bf16[32,1536]{1,0:T(8,128)(2,1)S(1)}, bf16[32,1536]{1,0:T(8,128)(2,1)S(1)}, u32[]{:S(2)}, u32[]{:S(2)}) collective-permute-start(bf16[32,1536]{1,0:T(8,128)(2,1)S(1)} %get-tuple-element.147), channel_id=1, source_target_pairs={{0,2},{1,7},{2,0},{3,6},{4,5},{5,4},{6,3},{7,1},{8,10},{9,15},{10,... | collective-permute-start | bytes 294920 | tf_op jit(solution)/shard_map/ppermute | solution.py:214
  153.4 1.9 %collective-permute-start.55 = (bf16[32,1536]{1,0:T(8,128)(2,1)S(1)}, bf16[32,1536]{1,0:T(8,128)(2,1)S(1)}, u32[]{:S(2)}, u32[]{:S(2)}) collective-permute-start(bf16[32,1536]{1,0:T(8,128)(2,1)S(1)} %get-tuple-element.148), channel_id=1, source_target_pairs={{0,6},{1,4},{2,3},{3,2},{4,1},{5,7},{6,0},{7,5},{8,14},{9,12},{10,... | collective-permute-start | bytes 294920 | tf_op jit(solution)/shard_map/ppermute | solution.py:214
  155.3 2.8 %collective-permute-start.56 = (bf16[32,1536]{1,0:T(8,128)(2,1)S(1)}, bf16[32,1536]{1,0:T(8,128)(2,1)S(1)}, u32[]{:S(2)}, u32[]{:S(2)}) collective-permute-start(bf16[32,1536]{1,0:T(8,128)(2,1)S(1)} %get-tuple-element.149), channel_id=1, source_target_pairs={{0,5},{1,3},{2,7},{3,1},{4,6},{5,0},{6,4},{7,2},{8,13},{9,11},{10,... | collective-permute-start | bytes 294920 | tf_op jit(solution)/shard_map/ppermute | solution.py:214
  158.1 1.7 %back_1.1.back_ref = f32[256,1536]{1,0:T(8,128)S(1)} custom-call(bf16[1,384,1536]{2,1,0:T(8,128)(2,1)S(1)} %copy-done.2, f32[256,1536]{1,0:T(8,128)S(1)} %get-tuple-element.118.factor_ref, bf16[32,1536]{1,0:T(8,128)(2,1)S(1)} %get-tuple-element.126.refs_0_, bf16[32,1536]{1,0:T(8,128)(2,1)S(1)} %collective-permute-done.36.refs_1_, ...), custom_call_target="tpu_custom_call" | custom-call | flops 301989888 | bytes 4718592 | tf_op jit(solution)/shard_map/back_1/pallas_call | solution.py:267
  159.9 2.9 %collective-permute-done.56.refs_7_ = bf16[32,1536]{1,0:T(8,128)(2,1)S(1)} collective-permute-done((bf16[32,1536]{1,0:T(8,128)(2,1)S(1)}, bf16[32,1536]{1,0:T(8,128)(2,1)S(1)}, u32[]{:S(2)}, u32[]{:S(2)}) %collective-permute-start.56) | collective-permute-done | bytes 98336 | tf_op jit(solution)/shard_map/ppermute | solution.py:214
  162.8 4.1 %result_1.1 = bf16[1,2,256,1536]{3,2,1,0:T(8,128)(2,1)} custom-call(bf16[1,2,256,1536]{3,2,1,0:T(8,128)(2,1)S(1)} %copy-done, f32[1,1536]{1,0:T(1,128)S(1)} %copy-done.9, bf16[1,384,1536]{2,1,0:T(8,128)(2,1)S(1)} %copy-done.1, bf16[1,256,256]{2,1,0:T(8,128)(2,1)S(1)} %copy-done.8, f32[256,1536]{1,0:T(8,128)S(1)} %back_1.1.back_ref, ...), custom_call_target="tpu_custom_call", output_to_operand_aliasing={{}: (15, {})} | custom-call | flops 905969664 | bytes 6291456 | tf_op jit(solution)/shard_map/result_1/pallas_call | solution.py:267
  (89 shorter events, 4.3 us)
Async XLA Ops:
  0.0 17.5 %copy-start.9 = (f32[1,1536]{1,0:T(1,128)S(1)}, f32[1,1536]{1,0:T(1,128)}, u32[]{:S(2)}) copy-start(f32[1,1536]{1,0:T(1,128)} %gain_ref.11) | copy-start | bytes 18436
  0.0 17.5 %copy-start = (bf16[1,2,256,1536]{3,2,1,0:T(8,128)(2,1)S(1)}, bf16[1,2,256,1536]{3,2,1,0:T(8,128)(2,1)}, u32[]{:S(2)}) copy-start(bf16[1,2,256,1536]{3,2,1,0:T(8,128)(2,1)} %x_ref.11) | copy-start | bytes 4718596
  0.0 17.5 %copy-start.2 = (bf16[1,384,1536]{2,1,0:T(8,128)(2,1)S(1)}, bf16[1,384,1536]{2,1,0:T(8,128)(2,1)}, u32[]{:S(2)}) copy-start(bf16[1,384,1536]{2,1,0:T(8,128)(2,1)} %w_gate_ref.7) | copy-start | bytes 3538948
  5.2 8.7 %collective-permute-start = (bf16[32,1536]{1,0:T(8,128)(2,1)}, bf16[32,1536]{1,0:T(8,128)(2,1)S(1)}, u32[]{:S(2)}, u32[]{:S(2)}) collective-permute-start(bf16[32,1536]{1,0:T(8,128)(2,1)} %get-tuple-element.80), channel_id=1, source_target_pairs={{0,7},{1,6},{2,5},{3,4},{4,3},{5,2},{6,1},{7,0},{8,15},{9,14},{10,... | collective-permute-start | bytes 294920 | tf_op jit(solution)/shard_map/ppermute | solution.py:214
  9.9 13.3 %collective-permute-start.1 = (bf16[32,1536]{1,0:T(8,128)(2,1)}, bf16[32,1536]{1,0:T(8,128)(2,1)S(1)}, u32[]{:S(2)}, u32[]{:S(2)}) collective-permute-start(bf16[32,1536]{1,0:T(8,128)(2,1)} %get-tuple-element.81), channel_id=1, source_target_pairs={{0,1},{1,0},{2,4},{3,7},{4,2},{5,6},{6,5},{7,3},{8,9},{9,8},{10,12... | collective-permute-start | bytes 294920 | tf_op jit(solution)/shard_map/ppermute | solution.py:214
  10.4 14.5 %collective-permute-start.2 = (bf16[32,1536]{1,0:T(8,128)(2,1)}, bf16[32,1536]{1,0:T(8,128)(2,1)S(1)}, u32[]{:S(2)}, u32[]{:S(2)}) collective-permute-start(bf16[32,1536]{1,0:T(8,128)(2,1)} %get-tuple-element.82), channel_id=1, source_target_pairs={{0,3},{1,5},{2,6},{3,0},{4,7},{5,1},{6,2},{7,4},{8,11},{9,13},{10,... | collective-permute-start | bytes 294920 | tf_op jit(solution)/shard_map/ppermute | solution.py:214
  10.6 21.8 %collective-permute-start.3 = (bf16[32,1536]{1,0:T(8,128)(2,1)}, bf16[32,1536]{1,0:T(8,128)(2,1)S(1)}, u32[]{:S(2)}, u32[]{:S(2)}) collective-permute-start(bf16[32,1536]{1,0:T(8,128)(2,1)} %get-tuple-element.83), channel_id=1, source_target_pairs={{0,4},{1,2},{2,1},{3,5},{4,0},{5,3},{6,7},{7,6},{8,12},{9,10},{10,... | collective-permute-start | bytes 294920 | tf_op jit(solution)/shard_map/ppermute | solution.py:214
  12.3 20.2 %collective-permute-start.4 = (bf16[32,1536]{1,0:T(8,128)(2,1)}, bf16[32,1536]{1,0:T(8,128)(2,1)S(1)}, u32[]{:S(2)}, u32[]{:S(2)}) collective-permute-start(bf16[32,1536]{1,0:T(8,128)(2,1)} %get-tuple-element.84), channel_id=1, source_target_pairs={{0,2},{1,7},{2,0},{3,6},{4,5},{5,4},{6,3},{7,1},{8,10},{9,15},{10,... | collective-permute-start | bytes 294920 | tf_op jit(solution)/shard_map/ppermute | solution.py:214
  13.9 19.1 %collective-permute-start.5 = (bf16[32,1536]{1,0:T(8,128)(2,1)}, bf16[32,1536]{1,0:T(8,128)(2,1)S(1)}, u32[]{:S(2)}, u32[]{:S(2)}) collective-permute-start(bf16[32,1536]{1,0:T(8,128)(2,1)} %get-tuple-element.85), channel_id=1, source_target_pairs={{0,6},{1,4},{2,3},{3,2},{4,1},{5,7},{6,0},{7,5},{8,14},{9,12},{10,... | collective-permute-start | bytes 294920 | tf_op jit(solution)/shard_map/ppermute | solution.py:214
  19.9 19.9 %copy-start.11 = (bf16[1,32,64]{2,1,0:T(8,128)(2,1)S(1)}, bf16[1,32,64]{2,1,0:T(8,128)(2,1)}, u32[]{:S(2)}) copy-start(bf16[1,32,64]{2,1,0:T(8,128)(2,1)} %l_ref.1) | copy-start | bytes 12292
  19.9 20.1 %copy-start.10 = (bf16[32,1536]{1,0:T(8,128)(2,1)S(1)}, bf16[32,1536]{1,0:T(8,128)(2,1)}, u32[]{:S(2)}) copy-start(bf16[32,1536]{1,0:T(8,128)(2,1)} %get-tuple-element.79.refs_0_) | copy-start | bytes 294916
  23.1 56.0 %copy-start.1 = (bf16[1,384,1536]{2,1,0:T(8,128)(2,1)S(1)}, bf16[1,384,1536]{2,1,0:T(8,128)(2,1)}, u32[]{:S(2)}) copy-start(bf16[1,384,1536]{2,1,0:T(8,128)(2,1)} %w_value_ref.3) | copy-start | bytes 3538948
  23.2 56.0 %copy-start.8 = (bf16[1,256,256]{2,1,0:T(8,128)(2,1)S(1)}, bf16[1,256,256]{2,1,0:T(8,128)(2,1)}, u32[]{:S(2)}) copy-start(bf16[1,256,256]{2,1,0:T(8,128)(2,1)} %r_ref.7) | copy-start | bytes 393220
  23.2 10.0 %collective-permute-start.6 = (bf16[32,1536]{1,0:T(8,128)(2,1)S(1)}, bf16[32,1536]{1,0:T(8,128)(2,1)S(1)}, u32[]{:S(2)}, u32[]{:S(2)}) collective-permute-start(bf16[32,1536]{1,0:T(8,128)(2,1)S(1)} %copy-done.12), channel_id=1, source_target_pairs={{0,5},{1,3},{2,7},{3,1},{4,6},{5,0},{6,4},{7,2},{8,13},{9,11},{10,... | collective-permute-start | bytes 294920 | tf_op jit(solution)/shard_map/ppermute | solution.py:214
  24.9 12.7 %collective-permute-start.14 = (bf16[32,1536]{1,0:T(8,128)(2,1)S(1)}, bf16[32,1536]{1,0:T(8,128)(2,1)S(1)}, u32[]{:S(2)}, u32[]{:S(2)}) collective-permute-start(bf16[32,1536]{1,0:T(8,128)(2,1)S(1)} %get-tuple-element.98), channel_id=1, source_target_pairs={{0,7},{1,6},{2,5},{3,4},{4,3},{5,2},{6,1},{7,0},{8,15},{9,14},{10,... | collective-permute-start | bytes 294920 | tf_op jit(solution)/shard_map/ppermute | solution.py:214
  32.4 8.8 %collective-permute-start.15 = (bf16[32,1536]{1,0:T(8,128)(2,1)S(1)}, bf16[32,1536]{1,0:T(8,128)(2,1)S(1)}, u32[]{:S(2)}, u32[]{:S(2)}) collective-permute-start(bf16[32,1536]{1,0:T(8,128)(2,1)S(1)} %get-tuple-element.99), channel_id=1, source_target_pairs={{0,1},{1,0},{2,4},{3,7},{4,2},{5,6},{6,5},{7,3},{8,9},{9,8},{10,12... | collective-permute-start | bytes 294920 | tf_op jit(solution)/shard_map/ppermute | solution.py:214
  32.5 9.6 %collective-permute-start.16 = (bf16[32,1536]{1,0:T(8,128)(2,1)S(1)}, bf16[32,1536]{1,0:T(8,128)(2,1)S(1)}, u32[]{:S(2)}, u32[]{:S(2)}) collective-permute-start(bf16[32,1536]{1,0:T(8,128)(2,1)S(1)} %get-tuple-element.100), channel_id=1, source_target_pairs={{0,3},{1,5},{2,6},{3,0},{4,7},{5,1},{6,2},{7,4},{8,11},{9,13},{10,... | collective-permute-start | bytes 294920 | tf_op jit(solution)/shard_map/ppermute | solution.py:214
  33.1 13.0 %collective-permute-start.17 = (bf16[32,1536]{1,0:T(8,128)(2,1)S(1)}, bf16[32,1536]{1,0:T(8,128)(2,1)S(1)}, u32[]{:S(2)}, u32[]{:S(2)}) collective-permute-start(bf16[32,1536]{1,0:T(8,128)(2,1)S(1)} %get-tuple-element.101), channel_id=1, source_target_pairs={{0,4},{1,2},{2,1},{3,5},{4,0},{5,3},{6,7},{7,6},{8,12},{9,10},{10,... | collective-permute-start | bytes 294920 | tf_op jit(solution)/shard_map/ppermute | solution.py:214
  33.2 16.4 %collective-permute-start.18 = (bf16[32,1536]{1,0:T(8,128)(2,1)S(1)}, bf16[32,1536]{1,0:T(8,128)(2,1)S(1)}, u32[]{:S(2)}, u32[]{:S(2)}) collective-permute-start(bf16[32,1536]{1,0:T(8,128)(2,1)S(1)} %get-tuple-element.102), channel_id=1, source_target_pairs={{0,2},{1,7},{2,0},{3,6},{4,5},{5,4},{6,3},{7,1},{8,10},{9,15},{10,... | collective-permute-start | bytes 294920 | tf_op jit(solution)/shard_map/ppermute | solution.py:214
  37.6 15.5 %collective-permute-start.19 = (bf16[32,1536]{1,0:T(8,128)(2,1)S(1)}, bf16[32,1536]{1,0:T(8,128)(2,1)S(1)}, u32[]{:S(2)}, u32[]{:S(2)}) collective-permute-start(bf16[32,1536]{1,0:T(8,128)(2,1)S(1)} %get-tuple-element.103), channel_id=1, source_target_pairs={{0,6},{1,4},{2,3},{3,2},{4,1},{5,7},{6,0},{7,5},{8,14},{9,12},{10,... | collective-permute-start | bytes 294920 | tf_op jit(solution)/shard_map/ppermute | solution.py:214
  41.2 13.6 %collective-permute-start.20 = (bf16[32,1536]{1,0:T(8,128)(2,1)S(1)}, bf16[32,1536]{1,0:T(8,128)(2,1)S(1)}, u32[]{:S(2)}, u32[]{:S(2)}) collective-permute-start(bf16[32,1536]{1,0:T(8,128)(2,1)S(1)} %get-tuple-element.104), channel_id=1, source_target_pairs={{0,5},{1,3},{2,7},{3,1},{4,6},{5,0},{6,4},{7,2},{8,13},{9,11},{10,... | collective-permute-start | bytes 294920 | tf_op jit(solution)/shard_map/ppermute | solution.py:214
  42.0 15.8 %collective-permute-start.10 = (bf16[32,1536]{1,0:T(8,128)(2,1)S(1)}, bf16[32,1536]{1,0:T(8,128)(2,1)S(1)}, u32[]{:S(2)}, u32[]{:S(2)}) collective-permute-start(bf16[32,1536]{1,0:T(8,128)(2,1)S(1)} %get-tuple-element.91), channel_id=1, source_target_pairs={{0,4},{1,2},{2,1},{3,5},{4,0},{5,3},{6,7},{7,6},{8,12},{9,10},{10,... | collective-permute-start | bytes 294920 | tf_op jit(solution)/shard_map/ppermute | solution.py:214
  46.0 13.8 %collective-permute-start.11 = (bf16[32,1536]{1,0:T(8,128)(2,1)S(1)}, bf16[32,1536]{1,0:T(8,128)(2,1)S(1)}, u32[]{:S(2)}, u32[]{:S(2)}) collective-permute-start(bf16[32,1536]{1,0:T(8,128)(2,1)S(1)} %get-tuple-element.92), channel_id=1, source_target_pairs={{0,2},{1,7},{2,0},{3,6},{4,5},{5,4},{6,3},{7,1},{8,10},{9,15},{10,... | collective-permute-start | bytes 294920 | tf_op jit(solution)/shard_map/ppermute | solution.py:214
  49.5 12.3 %collective-permute-start.12 = (bf16[32,1536]{1,0:T(8,128)(2,1)S(1)}, bf16[32,1536]{1,0:T(8,128)(2,1)S(1)}, u32[]{:S(2)}, u32[]{:S(2)}) collective-permute-start(bf16[32,1536]{1,0:T(8,128)(2,1)S(1)} %get-tuple-element.93), channel_id=1, source_target_pairs={{0,6},{1,4},{2,3},{3,2},{4,1},{5,7},{6,0},{7,5},{8,14},{9,12},{10,... | collective-permute-start | bytes 294920 | tf_op jit(solution)/shard_map/ppermute | solution.py:214
  53.0 12.8 %collective-permute-start.13 = (bf16[32,1536]{1,0:T(8,128)(2,1)S(1)}, bf16[32,1536]{1,0:T(8,128)(2,1)S(1)}, u32[]{:S(2)}, u32[]{:S(2)}) collective-permute-start(bf16[32,1536]{1,0:T(8,128)(2,1)S(1)} %get-tuple-element.94), channel_id=1, source_target_pairs={{0,5},{1,3},{2,7},{3,1},{4,6},{5,0},{6,4},{7,2},{8,13},{9,11},{10,... | collective-permute-start | bytes 294920 | tf_op jit(solution)/shard_map/ppermute | solution.py:214
  54.8 11.9 %collective-permute-start.7 = (bf16[32,1536]{1,0:T(8,128)(2,1)S(1)}, bf16[32,1536]{1,0:T(8,128)(2,1)S(1)}, u32[]{:S(2)}, u32[]{:S(2)}) collective-permute-start(bf16[32,1536]{1,0:T(8,128)(2,1)S(1)} %get-tuple-element.88), channel_id=1, source_target_pairs={{0,7},{1,6},{2,5},{3,4},{4,3},{5,2},{6,1},{7,0},{8,15},{9,14},{10,... | collective-permute-start | bytes 294920 | tf_op jit(solution)/shard_map/ppermute | solution.py:214
  57.8 11.6 %collective-permute-start.8 = (bf16[32,1536]{1,0:T(8,128)(2,1)S(1)}, bf16[32,1536]{1,0:T(8,128)(2,1)S(1)}, u32[]{:S(2)}, u32[]{:S(2)}) collective-permute-start(bf16[32,1536]{1,0:T(8,128)(2,1)S(1)} %get-tuple-element.89), channel_id=1, source_target_pairs={{0,1},{1,0},{2,4},{3,7},{4,2},{5,6},{6,5},{7,3},{8,9},{9,8},{10,12... | collective-permute-start | bytes 294920 | tf_op jit(solution)/shard_map/ppermute | solution.py:214
  59.8 11.5 %collective-permute-start.9 = (bf16[32,1536]{1,0:T(8,128)(2,1)S(1)}, bf16[32,1536]{1,0:T(8,128)(2,1)S(1)}, u32[]{:S(2)}, u32[]{:S(2)}) collective-permute-start(bf16[32,1536]{1,0:T(8,128)(2,1)S(1)} %get-tuple-element.90), channel_id=1, source_target_pairs={{0,3},{1,5},{2,6},{3,0},{4,7},{5,1},{6,2},{7,4},{8,11},{9,13},{10,... | collective-permute-start | bytes 294920 | tf_op jit(solution)/shard_map/ppermute | solution.py:214
  61.8 11.2 %collective-permute-start.21 = (bf16[32,1536]{1,0:T(8,128)(2,1)S(1)}, bf16[32,1536]{1,0:T(8,128)(2,1)S(1)}, u32[]{:S(2)}, u32[]{:S(2)}) collective-permute-start(bf16[32,1536]{1,0:T(8,128)(2,1)S(1)} %get-tuple-element.106), channel_id=1, source_target_pairs={{0,7},{1,6},{2,5},{3,4},{4,3},{5,2},{6,1},{7,0},{8,15},{9,14},{10,... | collective-permute-start | bytes 294920 | tf_op jit(solution)/shard_map/ppermute | solution.py:214
  65.8 8.5 %collective-permute-start.22 = (bf16[32,1536]{1,0:T(8,128)(2,1)S(1)}, bf16[32,1536]{1,0:T(8,128)(2,1)S(1)}, u32[]{:S(2)}, u32[]{:S(2)}) collective-permute-start(bf16[32,1536]{1,0:T(8,128)(2,1)S(1)} %get-tuple-element.107), channel_id=1, source_target_pairs={{0,1},{1,0},{2,4},{3,7},{4,2},{5,6},{6,5},{7,3},{8,9},{9,8},{10,12... | collective-permute-start | bytes 294920 | tf_op jit(solution)/shard_map/ppermute | solution.py:214
  66.7 15.4 %collective-permute-start.23 = (bf16[32,1536]{1,0:T(8,128)(2,1)S(1)}, bf16[32,1536]{1,0:T(8,128)(2,1)S(1)}, u32[]{:S(2)}, u32[]{:S(2)}) collective-permute-start(bf16[32,1536]{1,0:T(8,128)(2,1)S(1)} %get-tuple-element.108), channel_id=1, source_target_pairs={{0,3},{1,5},{2,6},{3,0},{4,7},{5,1},{6,2},{7,4},{8,11},{9,13},{10,... | collective-permute-start | bytes 294920 | tf_op jit(solution)/shard_map/ppermute | solution.py:214
  69.4 15.2 %collective-permute-start.24 = (bf16[32,1536]{1,0:T(8,128)(2,1)S(1)}, bf16[32,1536]{1,0:T(8,128)(2,1)S(1)}, u32[]{:S(2)}, u32[]{:S(2)}) collective-permute-start(bf16[32,1536]{1,0:T(8,128)(2,1)S(1)} %get-tuple-element.109), channel_id=1, source_target_pairs={{0,4},{1,2},{2,1},{3,5},{4,0},{5,3},{6,7},{7,6},{8,12},{9,10},{10,... | collective-permute-start | bytes 294920 | tf_op jit(solution)/shard_map/ppermute | solution.py:214
  71.3 16.1 %collective-permute-start.25 = (bf16[32,1536]{1,0:T(8,128)(2,1)S(1)}, bf16[32,1536]{1,0:T(8,128)(2,1)S(1)}, u32[]{:S(2)}, u32[]{:S(2)}) collective-permute-start(bf16[32,1536]{1,0:T(8,128)(2,1)S(1)} %get-tuple-element.110), channel_id=1, source_target_pairs={{0,2},{1,7},{2,0},{3,6},{4,5},{5,4},{6,3},{7,1},{8,10},{9,15},{10,... | collective-permute-start | bytes 294920 | tf_op jit(solution)/shard_map/ppermute | solution.py:214
  73.0 16.3 %collective-permute-start.26 = (bf16[32,1536]{1,0:T(8,128)(2,1)S(1)}, bf16[32,1536]{1,0:T(8,128)(2,1)S(1)}, u32[]{:S(2)}, u32[]{:S(2)}) collective-permute-start(bf16[32,1536]{1,0:T(8,128)(2,1)S(1)} %get-tuple-element.111), channel_id=1, source_target_pairs={{0,6},{1,4},{2,3},{3,2},{4,1},{5,7},{6,0},{7,5},{8,14},{9,12},{10,... | collective-permute-start | bytes 294920 | tf_op jit(solution)/shard_map/ppermute | solution.py:214
  74.3 15.0 %collective-permute-start.27 = (bf16[32,1536]{1,0:T(8,128)(2,1)S(1)}, bf16[32,1536]{1,0:T(8,128)(2,1)S(1)}, u32[]{:S(2)}, u32[]{:S(2)}) collective-permute-start(bf16[32,1536]{1,0:T(8,128)(2,1)S(1)} %get-tuple-element.112), channel_id=1, source_target_pairs={{0,5},{1,3},{2,7},{3,1},{4,6},{5,0},{6,4},{7,2},{8,13},{9,11},{10,... | collective-permute-start | bytes 294920 | tf_op jit(solution)/shard_map/ppermute | solution.py:214
  82.2 11.3 %collective-permute-start.28 = (bf16[32,1536]{1,0:T(8,128)(2,1)S(1)}, bf16[32,1536]{1,0:T(8,128)(2,1)S(1)}, u32[]{:S(2)}, u32[]{:S(2)}) collective-permute-start(bf16[32,1536]{1,0:T(8,128)(2,1)S(1)} %get-tuple-element.114), channel_id=1, source_target_pairs={{0,7},{1,6},{2,5},{3,4},{4,3},{5,2},{6,1},{7,0},{8,15},{9,14},{10,... | collective-permute-start | bytes 294920 | tf_op jit(solution)/shard_map/ppermute | solution.py:214
  84.7 8.8 %collective-permute-start.29 = (bf16[32,1536]{1,0:T(8,128)(2,1)S(1)}, bf16[32,1536]{1,0:T(8,128)(2,1)S(1)}, u32[]{:S(2)}, u32[]{:S(2)}) collective-permute-start(bf16[32,1536]{1,0:T(8,128)(2,1)S(1)} %get-tuple-element.115), channel_id=1, source_target_pairs={{0,1},{1,0},{2,4},{3,7},{4,2},{5,6},{6,5},{7,3},{8,9},{9,8},{10,12... | collective-permute-start | bytes 294920 | tf_op jit(solution)/shard_map/ppermute | solution.py:214
  87.4 6.1 %collective-permute-start.30 = (bf16[32,1536]{1,0:T(8,128)(2,1)S(1)}, bf16[32,1536]{1,0:T(8,128)(2,1)S(1)}, u32[]{:S(2)}, u32[]{:S(2)}) collective-permute-start(bf16[32,1536]{1,0:T(8,128)(2,1)S(1)} %get-tuple-element.116), channel_id=1, source_target_pairs={{0,3},{1,5},{2,6},{3,0},{4,7},{5,1},{6,2},{7,4},{8,11},{9,13},{10,... | collective-permute-start | bytes 294920 | tf_op jit(solution)/shard_map/ppermute | solution.py:214
  93.5 11.4 %collective-permute-start.31 = (bf16[256,1536]{1,0:T(8,128)(2,1)S(1)}, bf16[256,1536]{1,0:T(8,128)(2,1)S(1)}, u32[]{:S(2)}, u32[]{:S(2)}) collective-permute-start(bf16[256,1536]{1,0:T(8,128)(2,1)S(1)} %get-tuple-element.117), channel_id=1, source_target_pairs={{8,0},{16,8},{24,16},{9,1},{17,9},{25,17},{10,2},{18,10},{26,18},{... | collective-permute-start | bytes 2359304 | tf_op jit(solution)/shard_map/ppermute | solution.py:372
  95.6 14.2 %collective-permute-start.32 = (bf16[32,1536]{1,0:T(8,128)(2,1)S(1)}, bf16[32,1536]{1,0:T(8,128)(2,1)S(1)}, u32[]{:S(2)}, u32[]{:S(2)}) collective-permute-start(bf16[32,1536]{1,0:T(8,128)(2,1)S(1)} %get-tuple-element.122), channel_id=1, source_target_pairs={{0,4},{1,2},{2,1},{3,5},{4,0},{5,3},{6,7},{7,6},{8,12},{9,10},{10,... | collective-permute-start | bytes 294920 | tf_op jit(solution)/shard_map/ppermute | solution.py:214
  97.0 13.3 %collective-permute-start.33 = (bf16[32,1536]{1,0:T(8,128)(2,1)S(1)}, bf16[32,1536]{1,0:T(8,128)(2,1)S(1)}, u32[]{:S(2)}, u32[]{:S(2)}) collective-permute-start(bf16[32,1536]{1,0:T(8,128)(2,1)S(1)} %get-tuple-element.123), channel_id=1, source_target_pairs={{0,2},{1,7},{2,0},{3,6},{4,5},{5,4},{6,3},{7,1},{8,10},{9,15},{10,... | collective-permute-start | bytes 294920 | tf_op jit(solution)/shard_map/ppermute | solution.py:214
  97.7 16.0 %collective-permute-start.34 = (bf16[32,1536]{1,0:T(8,128)(2,1)S(1)}, bf16[32,1536]{1,0:T(8,128)(2,1)S(1)}, u32[]{:S(2)}, u32[]{:S(2)}) collective-permute-start(bf16[32,1536]{1,0:T(8,128)(2,1)S(1)} %get-tuple-element.124), channel_id=1, source_target_pairs={{0,6},{1,4},{2,3},{3,2},{4,1},{5,7},{6,0},{7,5},{8,14},{9,12},{10,... | collective-permute-start | bytes 294920 | tf_op jit(solution)/shard_map/ppermute | solution.py:214
  100.9 13.3 %collective-permute-start.35 = (bf16[32,1536]{1,0:T(8,128)(2,1)S(1)}, bf16[32,1536]{1,0:T(8,128)(2,1)S(1)}, u32[]{:S(2)}, u32[]{:S(2)}) collective-permute-start(bf16[32,1536]{1,0:T(8,128)(2,1)S(1)} %get-tuple-element.125), channel_id=1, source_target_pairs={{0,5},{1,3},{2,7},{3,1},{4,6},{5,0},{6,4},{7,2},{8,13},{9,11},{10,... | collective-permute-start | bytes 294920 | tf_op jit(solution)/shard_map/ppermute | solution.py:214
  108.3 7.6 %collective-permute-start.43 = (bf16[32,1536]{1,0:T(8,128)(2,1)S(1)}, bf16[32,1536]{1,0:T(8,128)(2,1)S(1)}, u32[]{:S(2)}, u32[]{:S(2)}) collective-permute-start(bf16[32,1536]{1,0:T(8,128)(2,1)S(1)} %get-tuple-element.135), channel_id=1, source_target_pairs={{0,7},{1,6},{2,5},{3,4},{4,3},{5,2},{6,1},{7,0},{8,15},{9,14},{10,... | collective-permute-start | bytes 294920 | tf_op jit(solution)/shard_map/ppermute | solution.py:214
  109.8 7.3 %collective-permute-start.44 = (bf16[32,1536]{1,0:T(8,128)(2,1)S(1)}, bf16[32,1536]{1,0:T(8,128)(2,1)S(1)}, u32[]{:S(2)}, u32[]{:S(2)}) collective-permute-start(bf16[32,1536]{1,0:T(8,128)(2,1)S(1)} %get-tuple-element.136), channel_id=1, source_target_pairs={{0,1},{1,0},{2,4},{3,7},{4,2},{5,6},{6,5},{7,3},{8,9},{9,8},{10,12... | collective-permute-start | bytes 294920 | tf_op jit(solution)/shard_map/ppermute | solution.py:214
  110.4 11.1 %collective-permute-start.45 = (bf16[32,1536]{1,0:T(8,128)(2,1)S(1)}, bf16[32,1536]{1,0:T(8,128)(2,1)S(1)}, u32[]{:S(2)}, u32[]{:S(2)}) collective-permute-start(bf16[32,1536]{1,0:T(8,128)(2,1)S(1)} %get-tuple-element.137), channel_id=1, source_target_pairs={{0,3},{1,5},{2,6},{3,0},{4,7},{5,1},{6,2},{7,4},{8,11},{9,13},{10,... | collective-permute-start | bytes 294920 | tf_op jit(solution)/shard_map/ppermute | solution.py:214
  113.6 16.9 %collective-permute-start.46 = (bf16[32,1536]{1,0:T(8,128)(2,1)S(1)}, bf16[32,1536]{1,0:T(8,128)(2,1)S(1)}, u32[]{:S(2)}, u32[]{:S(2)}) collective-permute-start(bf16[32,1536]{1,0:T(8,128)(2,1)S(1)} %get-tuple-element.138), channel_id=1, source_target_pairs={{0,4},{1,2},{2,1},{3,5},{4,0},{5,3},{6,7},{7,6},{8,12},{9,10},{10,... | collective-permute-start | bytes 294920 | tf_op jit(solution)/shard_map/ppermute | solution.py:214
  114.2 17.9 %collective-permute-start.47 = (bf16[32,1536]{1,0:T(8,128)(2,1)S(1)}, bf16[32,1536]{1,0:T(8,128)(2,1)S(1)}, u32[]{:S(2)}, u32[]{:S(2)}) collective-permute-start(bf16[32,1536]{1,0:T(8,128)(2,1)S(1)} %get-tuple-element.139), channel_id=1, source_target_pairs={{0,2},{1,7},{2,0},{3,6},{4,5},{5,4},{6,3},{7,1},{8,10},{9,15},{10,... | collective-permute-start | bytes 294920 | tf_op jit(solution)/shard_map/ppermute | solution.py:214
  115.9 16.2 %collective-permute-start.48 = (bf16[32,1536]{1,0:T(8,128)(2,1)S(1)}, bf16[32,1536]{1,0:T(8,128)(2,1)S(1)}, u32[]{:S(2)}, u32[]{:S(2)}) collective-permute-start(bf16[32,1536]{1,0:T(8,128)(2,1)S(1)} %get-tuple-element.140), channel_id=1, source_target_pairs={{0,6},{1,4},{2,3},{3,2},{4,1},{5,7},{6,0},{7,5},{8,14},{9,12},{10,... | collective-permute-start | bytes 294920 | tf_op jit(solution)/shard_map/ppermute | solution.py:214
  117.1 15.1 %collective-permute-start.49 = (bf16[32,1536]{1,0:T(8,128)(2,1)S(1)}, bf16[32,1536]{1,0:T(8,128)(2,1)S(1)}, u32[]{:S(2)}, u32[]{:S(2)}) collective-permute-start(bf16[32,1536]{1,0:T(8,128)(2,1)S(1)} %get-tuple-element.141), channel_id=1, source_target_pairs={{0,5},{1,3},{2,7},{3,1},{4,6},{5,0},{6,4},{7,2},{8,13},{9,11},{10,... | collective-permute-start | bytes 294920 | tf_op jit(solution)/shard_map/ppermute | solution.py:214
  121.5 14.5 %collective-permute-start.36 = (bf16[32,1536]{1,0:T(8,128)(2,1)S(1)}, bf16[32,1536]{1,0:T(8,128)(2,1)S(1)}, u32[]{:S(2)}, u32[]{:S(2)}) collective-permute-start(bf16[32,1536]{1,0:T(8,128)(2,1)S(1)} %get-tuple-element.127), channel_id=1, source_target_pairs={{0,7},{1,6},{2,5},{3,4},{4,3},{5,2},{6,1},{7,0},{8,15},{9,14},{10,... | collective-permute-start | bytes 294920 | tf_op jit(solution)/shard_map/ppermute | solution.py:214
  130.6 8.8 %collective-permute-start.37 = (bf16[32,1536]{1,0:T(8,128)(2,1)S(1)}, bf16[32,1536]{1,0:T(8,128)(2,1)S(1)}, u32[]{:S(2)}, u32[]{:S(2)}) collective-permute-start(bf16[32,1536]{1,0:T(8,128)(2,1)S(1)} %get-tuple-element.128), channel_id=1, source_target_pairs={{0,1},{1,0},{2,4},{3,7},{4,2},{5,6},{6,5},{7,3},{8,9},{9,8},{10,12... | collective-permute-start | bytes 294920 | tf_op jit(solution)/shard_map/ppermute | solution.py:214
  132.0 7.8 %collective-permute-start.38 = (bf16[32,1536]{1,0:T(8,128)(2,1)S(1)}, bf16[32,1536]{1,0:T(8,128)(2,1)S(1)}, u32[]{:S(2)}, u32[]{:S(2)}) collective-permute-start(bf16[32,1536]{1,0:T(8,128)(2,1)S(1)} %get-tuple-element.129), channel_id=1, source_target_pairs={{0,3},{1,5},{2,6},{3,0},{4,7},{5,1},{6,2},{7,4},{8,11},{9,13},{10,... | collective-permute-start | bytes 294920 | tf_op jit(solution)/shard_map/ppermute | solution.py:214
  132.0 16.0 %collective-permute-start.39 = (bf16[32,1536]{1,0:T(8,128)(2,1)S(1)}, bf16[32,1536]{1,0:T(8,128)(2,1)S(1)}, u32[]{:S(2)}, u32[]{:S(2)}) collective-permute-start(bf16[32,1536]{1,0:T(8,128)(2,1)S(1)} %get-tuple-element.130), channel_id=1, source_target_pairs={{0,4},{1,2},{2,1},{3,5},{4,0},{5,3},{6,7},{7,6},{8,12},{9,10},{10,... | collective-permute-start | bytes 294920 | tf_op jit(solution)/shard_map/ppermute | solution.py:214
  132.2 15.8 %collective-permute-start.40 = (bf16[32,1536]{1,0:T(8,128)(2,1)S(1)}, bf16[32,1536]{1,0:T(8,128)(2,1)S(1)}, u32[]{:S(2)}, u32[]{:S(2)}) collective-permute-start(bf16[32,1536]{1,0:T(8,128)(2,1)S(1)} %get-tuple-element.131), channel_id=1, source_target_pairs={{0,2},{1,7},{2,0},{3,6},{4,5},{5,4},{6,3},{7,1},{8,10},{9,15},{10,... | collective-permute-start | bytes 294920 | tf_op jit(solution)/shard_map/ppermute | solution.py:214
  136.0 13.3 %collective-permute-start.41 = (bf16[32,1536]{1,0:T(8,128)(2,1)S(1)}, bf16[32,1536]{1,0:T(8,128)(2,1)S(1)}, u32[]{:S(2)}, u32[]{:S(2)}) collective-permute-start(bf16[32,1536]{1,0:T(8,128)(2,1)S(1)} %get-tuple-element.132), channel_id=1, source_target_pairs={{0,6},{1,4},{2,3},{3,2},{4,1},{5,7},{6,0},{7,5},{8,14},{9,12},{10,... | collective-permute-start | bytes 294920 | tf_op jit(solution)/shard_map/ppermute | solution.py:214
  139.3 10.7 %collective-permute-start.42 = (bf16[32,1536]{1,0:T(8,128)(2,1)S(1)}, bf16[32,1536]{1,0:T(8,128)(2,1)S(1)}, u32[]{:S(2)}, u32[]{:S(2)}) collective-permute-start(bf16[32,1536]{1,0:T(8,128)(2,1)S(1)} %get-tuple-element.133), channel_id=1, source_target_pairs={{0,5},{1,3},{2,7},{3,1},{4,6},{5,0},{6,4},{7,2},{8,13},{9,11},{10,... | collective-permute-start | bytes 294920 | tf_op jit(solution)/shard_map/ppermute | solution.py:214
  139.8 13.6 %collective-permute-start.50 = (bf16[32,1536]{1,0:T(8,128)(2,1)S(1)}, bf16[32,1536]{1,0:T(8,128)(2,1)S(1)}, u32[]{:S(2)}, u32[]{:S(2)}) collective-permute-start(bf16[32,1536]{1,0:T(8,128)(2,1)S(1)} %get-tuple-element.143), channel_id=1, source_target_pairs={{0,7},{1,6},{2,5},{3,4},{4,3},{5,2},{6,1},{7,0},{8,15},{9,14},{10,... | collective-permute-start | bytes 294920 | tf_op jit(solution)/shard_map/ppermute | solution.py:214
  148.0 7.3 %collective-permute-start.51 = (bf16[32,1536]{1,0:T(8,128)(2,1)S(1)}, bf16[32,1536]{1,0:T(8,128)(2,1)S(1)}, u32[]{:S(2)}, u32[]{:S(2)}) collective-permute-start(bf16[32,1536]{1,0:T(8,128)(2,1)S(1)} %get-tuple-element.144), channel_id=1, source_target_pairs={{0,1},{1,0},{2,4},{3,7},{4,2},{5,6},{6,5},{7,3},{8,9},{9,8},{10,12... | collective-permute-start | bytes 294920 | tf_op jit(solution)/shard_map/ppermute | solution.py:214
  148.0 11.8 %collective-permute-start.52 = (bf16[32,1536]{1,0:T(8,128)(2,1)S(1)}, bf16[32,1536]{1,0:T(8,128)(2,1)S(1)}, u32[]{:S(2)}, u32[]{:S(2)}) collective-permute-start(bf16[32,1536]{1,0:T(8,128)(2,1)S(1)} %get-tuple-element.145), channel_id=1, source_target_pairs={{0,3},{1,5},{2,6},{3,0},{4,7},{5,1},{6,2},{7,4},{8,11},{9,13},{10,... | collective-permute-start | bytes 294920 | tf_op jit(solution)/shard_map/ppermute | solution.py:214
  149.3 10.6 %collective-permute-start.53 = (bf16[32,1536]{1,0:T(8,128)(2,1)S(1)}, bf16[32,1536]{1,0:T(8,128)(2,1)S(1)}, u32[]{:S(2)}, u32[]{:S(2)}) collective-permute-start(bf16[32,1536]{1,0:T(8,128)(2,1)S(1)} %get-tuple-element.146), channel_id=1, source_target_pairs={{0,4},{1,2},{2,1},{3,5},{4,0},{5,3},{6,7},{7,6},{8,12},{9,10},{10,... | collective-permute-start | bytes 294920 | tf_op jit(solution)/shard_map/ppermute | solution.py:214
  150.0 9.9 %collective-permute-start.54 = (bf16[32,1536]{1,0:T(8,128)(2,1)S(1)}, bf16[32,1536]{1,0:T(8,128)(2,1)S(1)}, u32[]{:S(2)}, u32[]{:S(2)}) collective-permute-start(bf16[32,1536]{1,0:T(8,128)(2,1)S(1)} %get-tuple-element.147), channel_id=1, source_target_pairs={{0,2},{1,7},{2,0},{3,6},{4,5},{5,4},{6,3},{7,1},{8,10},{9,15},{10,... | collective-permute-start | bytes 294920 | tf_op jit(solution)/shard_map/ppermute | solution.py:214
  153.4 6.5 %collective-permute-start.55 = (bf16[32,1536]{1,0:T(8,128)(2,1)S(1)}, bf16[32,1536]{1,0:T(8,128)(2,1)S(1)}, u32[]{:S(2)}, u32[]{:S(2)}) collective-permute-start(bf16[32,1536]{1,0:T(8,128)(2,1)S(1)} %get-tuple-element.148), channel_id=1, source_target_pairs={{0,6},{1,4},{2,3},{3,2},{4,1},{5,7},{6,0},{7,5},{8,14},{9,12},{10,... | collective-permute-start | bytes 294920 | tf_op jit(solution)/shard_map/ppermute | solution.py:214
  155.3 7.5 %collective-permute-start.56 = (bf16[32,1536]{1,0:T(8,128)(2,1)S(1)}, bf16[32,1536]{1,0:T(8,128)(2,1)S(1)}, u32[]{:S(2)}, u32[]{:S(2)}) collective-permute-start(bf16[32,1536]{1,0:T(8,128)(2,1)S(1)} %get-tuple-element.149), channel_id=1, source_target_pairs={{0,5},{1,3},{2,7},{3,1},{4,6},{5,0},{6,4},{7,2},{8,13},{9,11},{10,... | collective-permute-start | bytes 294920 | tf_op jit(solution)/shard_map/ppermute | solution.py:214
  (6 other events, 38.7 us)

commit v3 on v2

--- a/solution.py
+++ b/solution.py
@@ -368,10 +368,14 @@
     gate_0, first_1.parts[0] = lax.optimization_barrier((gate_0, first_1.parts[0]))
     first_1.send(every)
     stacked, result_0 = result(0, gate_0, fold_0.all(), [(whole3, arrived_grad)], None)
-    result_0 = tied(result_0, [(first_1, slot) for slot in every[: min(3, count // 2)]])
+    result_0 = tied(result_0, [(first_1, slot) for slot in every[: min(4, count // 2)]])
     passed = lax.ppermute(result_0, "pipe", [(s, s - 1) for s in range(1, pipe)])
     mix_1 = Exchange(mix("mix_1", first_1.all(), False)).send(every)
+    passed, mix_1.parts[0] = lax.optimization_barrier((passed, mix_1.parts[0]))
+    mix_1.got[0] = mix_1.parts[0]
     parts, factor_1 = grads(1, [(cut, passed), (cut3, loss_grad)])
+    for slot in every[:3]:
+        parts[count - slot] = tied(parts[count - slot], [(mix_1, slot)])
     grad_1 = Exchange(parts).send(every)
     fold_1 = Exchange(mix("fold_1", grad_1.all(), True)).send(every)
     gate_1 = back(1, mix_1.all(), factor_1)

time: 167 us -> 174 us (1.042)
  the two profiles are of different devices: /device:TPU:2 before, /device:TPU:8 now
where the time goes in v3:
time: 174 us
  starting transfers between devices  87.1 us (50%)
  waiting for transfers between devices  51.9 us (30%)
  Pallas kernels  31.9 us (18%)
  local copies, waits for them, and re-layouts  2.44 us (1%)
    ppermute x56, starting transfers between devices, send(): self.got[slot] = lax.ppermute(tied(self.parts[slot], after), 'seq', pairs)  85.5 us
    ppermute x56, waiting for transfers between devices, send(): self.got[slot] = lax.ppermute(tied(self.parts[slot], after), 'seq', pairs)  51.9 us
    pallas_call x13, Pallas kernels, call(): pl.pallas_call(kernel, grid=(steps or width // block,), in_specs=[spec fo...  31.9 us
  transfers between devices with their start and end apart: 57, of which 16 were waited for; matrix products, arithmetic and copies ran while one was open for 0% of the time, Pallas kernels for 13%

profile of v3, /device:TPU:8, one launch (start us, length us, event | category | flops | bytes accessed | tf_op | source)
XLA Modules:
  0.0 173.7 jit_solution(14785398026830533850)
XLA Ops:
  0.0 5.2 %first_0.1 = (bf16[32,1536]{1,0:T(8,128)(2,1)}, bf16[32,1536]{1,0:T(8,128)(2,1)}, bf16[32,1536]{1,0:T(8,128)(2,1)}, bf16[32,1536]{1,0:T(8,128)(2,1)}, bf16[32,15...) custom-call(bf16[1,2,256,1536]{3,2,1,0:T(8,128)(2,1)} %x_ref.11, ...), custom_call_target="tpu_custom_call" | custom-call | flops 603979776 | bytes 3145728 | tf_op jit(solution)/shard_map/first_0/pallas_call | solution.py:267
  5.2 2.6 %collective-permute-start = (bf16[32,1536]{1,0:T(8,128)(2,1)}, bf16[32,1536]{1,0:T(8,128)(2,1)S(1)}, u32[]{:S(2)}, u32[]{:S(2)}) collective-permute-start(bf16[32,1536]{1,0:T(8,128)(2,1)} %get-tuple-element.89), channel_id=1, source_target_pairs={{0,7},{1,6},{2,5},{3,4},{4,3},{5,2},{6,1},{7,0},{8,15},{9,14},{10,... | collective-permute-start | bytes 294920 | tf_op jit(solution)/shard_map/ppermute | solution.py:214
  8.3 1.4 collective-permute-start.2
  9.7 2.3 %collective-permute-start.3 = (bf16[32,1536]{1,0:T(8,128)(2,1)}, bf16[32,1536]{1,0:T(8,128)(2,1)S(1)}, u32[]{:S(2)}, u32[]{:S(2)}) collective-permute-start(bf16[32,1536]{1,0:T(8,128)(2,1)} %get-tuple-element.92), channel_id=1, source_target_pairs={{0,4},{1,2},{2,1},{3,5},{4,0},{5,3},{6,7},{7,6},{8,12},{9,10},{10,... | collective-permute-start | bytes 294920 | tf_op jit(solution)/shard_map/ppermute | solution.py:214
  12.0 0.7 collective-permute-start.4
  12.7 4.3 %collective-permute-done.refs_1_ = bf16[32,1536]{1,0:T(8,128)(2,1)S(1)} collective-permute-done((bf16[32,1536]{1,0:T(8,128)(2,1)}, bf16[32,1536]{1,0:T(8,128)(2,1)S(1)}, u32[]{:S(2)}, u32[]{:S(2)}) %collective-permute-start) | collective-permute-done | bytes 98336 | tf_op jit(solution)/shard_map/ppermute | solution.py:214
  17.0 4.8 %collective-permute-start.5 = (bf16[32,1536]{1,0:T(8,128)(2,1)}, bf16[32,1536]{1,0:T(8,128)(2,1)S(1)}, u32[]{:S(2)}, u32[]{:S(2)}) collective-permute-start(bf16[32,1536]{1,0:T(8,128)(2,1)} %get-tuple-element.94), channel_id=1, source_target_pairs={{0,6},{1,4},{2,3},{3,2},{4,1},{5,7},{6,0},{7,5},{8,14},{9,12},{10,... | collective-permute-start | bytes 294920 | tf_op jit(solution)/shard_map/ppermute | solution.py:214
  21.8 0.6 collective-permute-done.1.refs_2_
  22.4 1.6 collective-permute-start.6
  24.0 1.3 copy-done.3
  25.3 1.1 copy-done.5
  26.4 3.3 %grads_0.1 = (bf16[32,1536]{1,0:T(8,128)(2,1)S(1)}, bf16[32,1536]{1,0:T(8,128)(2,1)S(1)}, bf16[32,1536]{1,0:T(8,128)(2,1)S(1)}, bf16[32,1536]{1,0:T(8,128)(2,1)S...) custom-call(bf16[1,2,256,1536]{3,2,1,0:T(8,128)(2,1)S(1)} %copy-done, ...), custom_call_target="tpu_custom_call" | custom-call | flops 603979776 | bytes 6291456 | tf_op jit(solution)/shard_map/grads_0/pallas_call | solution.py:267
  29.9 4.3 %collective-permute-start.16 = (bf16[32,1536]{1,0:T(8,128)(2,1)S(1)}, bf16[32,1536]{1,0:T(8,128)(2,1)S(1)}, u32[]{:S(2)}, u32[]{:S(2)}) collective-permute-start(bf16[32,1536]{1,0:T(8,128)(2,1)S(1)} %get-tuple-element.109), channel_id=1, source_target_pairs={{0,3},{1,5},{2,6},{3,0},{4,7},{5,1},{6,2},{7,4},{8,11},{9,13},{10,... | collective-permute-start | bytes 294920 | tf_op jit(solution)/shard_map/ppermute | solution.py:214
  34.2 0.8 collective-permute-start.17
  35.1 4.1 %collective-permute-done.14.refs_1_ = bf16[32,1536]{1,0:T(8,128)(2,1)S(1)} collective-permute-done((bf16[32,1536]{1,0:T(8,128)(2,1)S(1)}, bf16[32,1536]{1,0:T(8,128)(2,1)S(1)}, u32[]{:S(2)}, u32[]{:S(2)}) %collective-permute-start.14) | collective-permute-done | bytes 98336 | tf_op jit(solution)/shard_map/ppermute | solution.py:214
  39.3 3.8 %collective-permute-start.20 = (bf16[32,1536]{1,0:T(8,128)(2,1)S(1)}, bf16[32,1536]{1,0:T(8,128)(2,1)S(1)}, u32[]{:S(2)}, u32[]{:S(2)}) collective-permute-start(bf16[32,1536]{1,0:T(8,128)(2,1)S(1)} %get-tuple-element.113), channel_id=1, source_target_pairs={{0,5},{1,3},{2,7},{3,1},{4,6},{5,0},{6,4},{7,2},{8,13},{9,11},{10,... | collective-permute-start | bytes 294920 | tf_op jit(solution)/shard_map/ppermute | solution.py:214
  43.1 1.2 mix_0.1
  44.8 1.2 collective-permute-start.11
  46.0 2.8 %collective-permute-start.12 = (bf16[32,1536]{1,0:T(8,128)(2,1)S(1)}, bf16[32,1536]{1,0:T(8,128)(2,1)S(1)}, u32[]{:S(2)}, u32[]{:S(2)}) collective-permute-start(bf16[32,1536]{1,0:T(8,128)(2,1)S(1)} %get-tuple-element.102), channel_id=1, source_target_pairs={{0,6},{1,4},{2,3},{3,2},{4,1},{5,7},{6,0},{7,5},{8,14},{9,12},{10,... | collective-permute-start | bytes 294920 | tf_op jit(solution)/shard_map/ppermute | solution.py:214
  48.7 1.1 collective-permute-start.13
  49.8 5.6 %collective-permute-start.7 = (bf16[32,1536]{1,0:T(8,128)(2,1)S(1)}, bf16[32,1536]{1,0:T(8,128)(2,1)S(1)}, u32[]{:S(2)}, u32[]{:S(2)}) collective-permute-start(bf16[32,1536]{1,0:T(8,128)(2,1)S(1)} %get-tuple-element.97), channel_id=1, source_target_pairs={{0,7},{1,6},{2,5},{3,4},{4,3},{5,2},{6,1},{7,0},{8,15},{9,14},{10,... | collective-permute-start | bytes 294920 | tf_op jit(solution)/shard_map/ppermute | solution.py:214
  55.4 1.4 fold_0.1
  56.9 4.2 %collective-permute-start.9 = (bf16[32,1536]{1,0:T(8,128)(2,1)S(1)}, bf16[32,1536]{1,0:T(8,128)(2,1)S(1)}, u32[]{:S(2)}, u32[]{:S(2)}) collective-permute-start(bf16[32,1536]{1,0:T(8,128)(2,1)S(1)} %get-tuple-element.99), channel_id=1, source_target_pairs={{0,3},{1,5},{2,6},{3,0},{4,7},{5,1},{6,2},{7,4},{8,11},{9,13},{10,... | collective-permute-start | bytes 294920 | tf_op jit(solution)/shard_map/ppermute | solution.py:214
  61.1 0.9 collective-permute-start.22
  62.0 4.0 %collective-permute-done.7.refs_1_ = bf16[32,1536]{1,0:T(8,128)(2,1)S(1)} collective-permute-done((bf16[32,1536]{1,0:T(8,128)(2,1)S(1)}, bf16[32,1536]{1,0:T(8,128)(2,1)S(1)}, u32[]{:S(2)}, u32[]{:S(2)}) %collective-permute-start.7) | collective-permute-done | bytes 98336 | tf_op jit(solution)/shard_map/ppermute | solution.py:214
  66.0 0.5 collective-permute-start.24
  66.5 2.2 %collective-permute-start.25 = (bf16[32,1536]{1,0:T(8,128)(2,1)S(1)}, bf16[32,1536]{1,0:T(8,128)(2,1)S(1)}, u32[]{:S(2)}, u32[]{:S(2)}) collective-permute-start(bf16[32,1536]{1,0:T(8,128)(2,1)S(1)} %get-tuple-element.119), channel_id=1, source_target_pairs={{0,2},{1,7},{2,0},{3,6},{4,5},{5,4},{6,3},{7,1},{8,10},{9,15},{10,... | collective-permute-start | bytes 294920 | tf_op jit(solution)/shard_map/ppermute | solution.py:214
  68.6 4.2 %collective-permute-done.21.refs_1_ = bf16[32,1536]{1,0:T(8,128)(2,1)S(1)} collective-permute-done((bf16[32,1536]{1,0:T(8,128)(2,1)S(1)}, bf16[32,1536]{1,0:T(8,128)(2,1)S(1)}, u32[]{:S(2)}, u32[]{:S(2)}) %collective-permute-start.21) | collective-permute-done | bytes 98336 | tf_op jit(solution)/shard_map/ppermute | solution.py:214
  72.8 2.6 %collective-permute-done.22.refs_2_ = bf16[32,1536]{1,0:T(8,128)(2,1)S(1)} collective-permute-done((bf16[32,1536]{1,0:T(8,128)(2,1)S(1)}, bf16[32,1536]{1,0:T(8,128)(2,1)S(1)}, u32[]{:S(2)}, u32[]{:S(2)}) %collective-permute-start.22) | collective-permute-done | bytes 98336 | tf_op jit(solution)/shard_map/ppermute | solution.py:214
  75.4 2.5 %collective-permute-start.27 = (bf16[32,1536]{1,0:T(8,128)(2,1)S(1)}, bf16[32,1536]{1,0:T(8,128)(2,1)S(1)}, u32[]{:S(2)}, u32[]{:S(2)}) collective-permute-start(bf16[32,1536]{1,0:T(8,128)(2,1)S(1)} %get-tuple-element.121), channel_id=1, source_target_pairs={{0,5},{1,3},{2,7},{3,1},{4,6},{5,0},{6,4},{7,2},{8,13},{9,11},{10,... | collective-permute-start | bytes 294920 | tf_op jit(solution)/shard_map/ppermute | solution.py:214
  77.9 3.0 %first_1.1 = (bf16[32,1536]{1,0:T(8,128)(2,1)S(1)}, bf16[32,1536]{1,0:T(8,128)(2,1)S(1)}, bf16[32,1536]{1,0:T(8,128)(2,1)S(1)}, bf16[32,1536]{1,0:T(8,128)(2,1)S...) custom-call(bf16[1,2,256,1536]{3,2,1,0:T(8,128)(2,1)S(1)} %copy-done, ...), custom_call_target="tpu_custom_call" | custom-call | flops 603979776 | bytes 3145728 | tf_op jit(solution)/shard_map/first_1/pallas_call | solution.py:267
  81.1 4.3 %collective-permute-start.30 = (bf16[32,1536]{1,0:T(8,128)(2,1)S(1)}, bf16[32,1536]{1,0:T(8,128)(2,1)S(1)}, u32[]{:S(2)}, u32[]{:S(2)}) collective-permute-start(bf16[32,1536]{1,0:T(8,128)(2,1)S(1)} %get-tuple-element.125), channel_id=1, source_target_pairs={{0,3},{1,5},{2,6},{3,0},{4,7},{5,1},{6,2},{7,4},{8,11},{9,13},{10,... | collective-permute-start | bytes 294920 | tf_op jit(solution)/shard_map/ppermute | solution.py:214
  85.5 1.7 back_0.1.back_ref
  87.2 4.1 %result_0.1 = (bf16[1,2,256,1536]{3,2,1,0:T(8,128)(2,1)}, bf16[256,1536]{1,0:T(8,128)(2,1)S(1)}) custom-call(bf16[1,2,256,1536]{3,2,1,0:T(8,128)(2,1)S(1)} %copy-done, f32[1,1536]{1,0:T(1,128)S(1)} %copy-done.9, bf16[1,384,1536]{2,1,0:T(8,128)(2,1)S(1)} %copy-done.1, bf16[1,256,256]{2,1,0:T(8,128)(2,1)S(1)} %copy-done.8, f32[256,1536]{1,0:T(8,128)S(1)} %back_0.1.back_ref, ...), custom_call_target="tpu_custom_call" | custom-call | flops 905969664 | bytes 6291456 | tf_op jit(solution)/shard_map/result_0/pallas_call | solution.py:267
  91.4 1.6 collective-permute-start.32
  93.0 0.9 collective-permute-start.33
  93.9 2.1 %collective-permute-start.34 = (bf16[32,1536]{1,0:T(8,128)(2,1)S(1)}, bf16[32,1536]{1,0:T(8,128)(2,1)S(1)}, u32[]{:S(2)}, u32[]{:S(2)}) collective-permute-start(bf16[32,1536]{1,0:T(8,128)(2,1)S(1)} %get-tuple-element.133), channel_id=1, source_target_pairs={{0,6},{1,4},{2,3},{3,2},{4,1},{5,7},{6,0},{7,5},{8,14},{9,12},{10,... | collective-permute-start | bytes 294920 | tf_op jit(solution)/shard_map/ppermute | solution.py:214
  96.0 2.3 %collective-permute-start.35 = (bf16[32,1536]{1,0:T(8,128)(2,1)S(1)}, bf16[32,1536]{1,0:T(8,128)(2,1)S(1)}, u32[]{:S(2)}, u32[]{:S(2)}) collective-permute-start(bf16[32,1536]{1,0:T(8,128)(2,1)S(1)} %get-tuple-element.134), channel_id=1, source_target_pairs={{0,5},{1,3},{2,7},{3,1},{4,6},{5,0},{6,4},{7,2},{8,13},{9,11},{10,... | collective-permute-start | bytes 294920 | tf_op jit(solution)/shard_map/ppermute | solution.py:214
  98.6 2.6 %collective-permute-done.34.refs_6_ = bf16[32,1536]{1,0:T(8,128)(2,1)S(1)} collective-permute-done((bf16[32,1536]{1,0:T(8,128)(2,1)S(1)}, bf16[32,1536]{1,0:T(8,128)(2,1)S(1)}, u32[]{:S(2)}, u32[]{:S(2)}) %collective-permute-start.34) | collective-permute-done | bytes 98336 | tf_op jit(solution)/shard_map/ppermute | solution.py:214
  101.2 4.9 %collective-permute-done.35.refs_7_ = bf16[32,1536]{1,0:T(8,128)(2,1)S(1)} collective-permute-done((bf16[32,1536]{1,0:T(8,128)(2,1)S(1)}, bf16[32,1536]{1,0:T(8,128)(2,1)S(1)}, u32[]{:S(2)}, u32[]{:S(2)}) %collective-permute-start.35) | collective-permute-done | bytes 98336 | tf_op jit(solution)/shard_map/ppermute | solution.py:214
  106.1 1.2 mix_1.1
  107.5 4.1 %collective-permute-start.37 = (bf16[32,1536]{1,0:T(8,128)(2,1)S(1)}, bf16[32,1536]{1,0:T(8,128)(2,1)S(1)}, u32[]{:S(2)}, u32[]{:S(2)}) collective-permute-start(bf16[32,1536]{1,0:T(8,128)(2,1)S(1)} %get-tuple-element.143), channel_id=1, source_target_pairs={{0,1},{1,0},{2,4},{3,7},{4,2},{5,6},{6,5},{7,3},{8,9},{9,8},{10,12... | collective-permute-start | bytes 294920 | tf_op jit(solution)/shard_map/ppermute | solution.py:214
  111.8 3.4 %grads_1.1 = (bf16[32,1536]{1,0:T(8,128)(2,1)S(1)}, bf16[32,1536]{1,0:T(8,128)(2,1)S(1)}, bf16[32,1536]{1,0:T(8,128)(2,1)S(1)}, bf16[32,1536]{1,0:T(8,128)(2,1)S...) custom-call(bf16[1,2,256,1536]{3,2,1,0:T(8,128)(2,1)S(1)} %copy-done, ...), custom_call_target="tpu_custom_call" | custom-call | flops 603979776 | bytes 6291456 | tf_op jit(solution)/shard_map/grads_1/pallas_call | solution.py:267
  115.2 2.8 %collective-permute-start.47 = (bf16[32,1536]{1,0:T(8,128)(2,1)S(1)}, bf16[32,1536]{1,0:T(8,128)(2,1)S(1)}, u32[]{:S(2)}, u32[]{:S(2)}) collective-permute-start(bf16[32,1536]{1,0:T(8,128)(2,1)S(1)} %get-tuple-element.157), channel_id=1, source_target_pairs={{0,2},{1,7},{2,0},{3,6},{4,5},{5,4},{6,3},{7,1},{8,10},{9,15},{10,... | collective-permute-start | bytes 294920 | tf_op jit(solution)/shard_map/ppermute | solution.py:214
  118.0 3.6 %collective-permute-done.36.refs_1_ = bf16[32,1536]{1,0:T(8,128)(2,1)S(1)} collective-permute-done((bf16[32,1536]{1,0:T(8,128)(2,1)S(1)}, bf16[32,1536]{1,0:T(8,128)(2,1)S(1)}, u32[]{:S(2)}, u32[]{:S(2)}) %collective-permute-start.36) | collective-permute-done | bytes 98336 | tf_op jit(solution)/shard_map/ppermute | solution.py:214
  121.6 2.2 %collective-permute-start.43 = (bf16[32,1536]{1,0:T(8,128)(2,1)S(1)}, bf16[32,1536]{1,0:T(8,128)(2,1)S(1)}, u32[]{:S(2)}, u32[]{:S(2)}) collective-permute-start(bf16[32,1536]{1,0:T(8,128)(2,1)S(1)} %get-tuple-element.153), channel_id=1, source_target_pairs={{0,7},{1,6},{2,5},{3,4},{4,3},{5,2},{6,1},{7,0},{8,15},{9,14},{10,... | collective-permute-start | bytes 294920 | tf_op jit(solution)/shard_map/ppermute | solution.py:214
  123.8 2.3 %collective-permute-start.44 = (bf16[32,1536]{1,0:T(8,128)(2,1)S(1)}, bf16[32,1536]{1,0:T(8,128)(2,1)S(1)}, u32[]{:S(2)}, u32[]{:S(2)}) collective-permute-start(bf16[32,1536]{1,0:T(8,128)(2,1)S(1)} %get-tuple-element.154), channel_id=1, source_target_pairs={{0,1},{1,0},{2,4},{3,7},{4,2},{5,6},{6,5},{7,3},{8,9},{9,8},{10,12... | collective-permute-start | bytes 294920 | tf_op jit(solution)/shard_map/ppermute | solution.py:214
  126.2 3.2 %collective-permute-start.45 = (bf16[32,1536]{1,0:T(8,128)(2,1)S(1)}, bf16[32,1536]{1,0:T(8,128)(2,1)S(1)}, u32[]{:S(2)}, u32[]{:S(2)}) collective-permute-start(bf16[32,1536]{1,0:T(8,128)(2,1)S(1)} %get-tuple-element.155), channel_id=1, source_target_pairs={{0,3},{1,5},{2,6},{3,0},{4,7},{5,1},{6,2},{7,4},{8,11},{9,13},{10,... | collective-permute-start | bytes 294920 | tf_op jit(solution)/shard_map/ppermute | solution.py:214
  129.4 2.0 %collective-permute-start.46 = (bf16[32,1536]{1,0:T(8,128)(2,1)S(1)}, bf16[32,1536]{1,0:T(8,128)(2,1)S(1)}, u32[]{:S(2)}, u32[]{:S(2)}) collective-permute-start(bf16[32,1536]{1,0:T(8,128)(2,1)S(1)} %get-tuple-element.156), channel_id=1, source_target_pairs={{0,4},{1,2},{2,1},{3,5},{4,0},{5,3},{6,7},{7,6},{8,12},{9,10},{10,... | collective-permute-start | bytes 294920 | tf_op jit(solution)/shard_map/ppermute | solution.py:214
  131.4 0.9 collective-permute-start.39
  132.3 4.7 %collective-permute-done.43.refs_1_ = bf16[32,1536]{1,0:T(8,128)(2,1)S(1)} collective-permute-done((bf16[32,1536]{1,0:T(8,128)(2,1)S(1)}, bf16[32,1536]{1,0:T(8,128)(2,1)S(1)}, u32[]{:S(2)}, u32[]{:S(2)}) %collective-permute-start.43) | collective-permute-done | bytes 98336 | tf_op jit(solution)/shard_map/ppermute | solution.py:214
  137.0 0.9 collective-permute-done.44.refs_2_
  137.9 6.3 %collective-permute-done.45.refs_3_ = bf16[32,1536]{1,0:T(8,128)(2,1)S(1)} collective-permute-done((bf16[32,1536]{1,0:T(8,128)(2,1)S(1)}, bf16[32,1536]{1,0:T(8,128)(2,1)S(1)}, u32[]{:S(2)}, u32[]{:S(2)}) %collective-permute-start.45) | collective-permute-done | bytes 98336 | tf_op jit(solution)/shard_map/ppermute | solution.py:214
  144.2 1.4 fold_1.1
  145.6 4.0 %collective-permute-start.51 = (bf16[32,1536]{1,0:T(8,128)(2,1)S(1)}, bf16[32,1536]{1,0:T(8,128)(2,1)S(1)}, u32[]{:S(2)}, u32[]{:S(2)}) collective-permute-start(bf16[32,1536]{1,0:T(8,128)(2,1)S(1)} %get-tuple-element.162), channel_id=1, source_target_pairs={{0,1},{1,0},{2,4},{3,7},{4,2},{5,6},{6,5},{7,3},{8,9},{9,8},{10,12... | collective-permute-start | bytes 294920 | tf_op jit(solution)/shard_map/ppermute | solution.py:214
  150.0 2.4 %collective-permute-start.53 = (bf16[32,1536]{1,0:T(8,128)(2,1)S(1)}, bf16[32,1536]{1,0:T(8,128)(2,1)S(1)}, u32[]{:S(2)}, u32[]{:S(2)}) collective-permute-start(bf16[32,1536]{1,0:T(8,128)(2,1)S(1)} %get-tuple-element.164), channel_id=1, source_target_pairs={{0,4},{1,2},{2,1},{3,5},{4,0},{5,3},{6,7},{7,6},{8,12},{9,10},{10,... | collective-permute-start | bytes 294920 | tf_op jit(solution)/shard_map/ppermute | solution.py:214
  152.4 3.0 %collective-permute-start.54 = (bf16[32,1536]{1,0:T(8,128)(2,1)S(1)}, bf16[32,1536]{1,0:T(8,128)(2,1)S(1)}, u32[]{:S(2)}, u32[]{:S(2)}) collective-permute-start(bf16[32,1536]{1,0:T(8,128)(2,1)S(1)} %get-tuple-element.165), channel_id=1, source_target_pairs={{0,2},{1,7},{2,0},{3,6},{4,5},{5,4},{6,3},{7,1},{8,10},{9,15},{10,... | collective-permute-start | bytes 294920 | tf_op jit(solution)/shard_map/ppermute | solution.py:214
  155.4 2.4 %collective-permute-done.50.refs_1_ = bf16[32,1536]{1,0:T(8,128)(2,1)S(1)} collective-permute-done((bf16[32,1536]{1,0:T(8,128)(2,1)S(1)}, bf16[32,1536]{1,0:T(8,128)(2,1)S(1)}, u32[]{:S(2)}, u32[]{:S(2)}) %collective-permute-start.50) | collective-permute-done | bytes 98336 | tf_op jit(solution)/shard_map/ppermute | solution.py:214
  157.8 0.7 collective-permute-start.55
  158.5 4.7 %collective-permute-done.51.refs_2_ = bf16[32,1536]{1,0:T(8,128)(2,1)S(1)} collective-permute-done((bf16[32,1536]{1,0:T(8,128)(2,1)S(1)}, bf16[32,1536]{1,0:T(8,128)(2,1)S(1)}, u32[]{:S(2)}, u32[]{:S(2)}) %collective-permute-start.51) | collective-permute-done | bytes 98336 | tf_op jit(solution)/shard_map/ppermute | solution.py:214
  163.1 2.9 %collective-permute-start.56 = (bf16[32,1536]{1,0:T(8,128)(2,1)S(1)}, bf16[32,1536]{1,0:T(8,128)(2,1)S(1)}, u32[]{:S(2)}, u32[]{:S(2)}) collective-permute-start(bf16[32,1536]{1,0:T(8,128)(2,1)S(1)} %get-tuple-element.167), channel_id=1, source_target_pairs={{0,5},{1,3},{2,7},{3,1},{4,6},{5,0},{6,4},{7,2},{8,13},{9,11},{10,... | collective-permute-start | bytes 294920 | tf_op jit(solution)/shard_map/ppermute | solution.py:214
  166.0 1.7 back_1.1.back_ref
  167.8 1.7 %collective-permute-done.56.refs_7_ = bf16[32,1536]{1,0:T(8,128)(2,1)S(1)} collective-permute-done((bf16[32,1536]{1,0:T(8,128)(2,1)S(1)}, bf16[32,1536]{1,0:T(8,128)(2,1)S(1)}, u32[]{:S(2)}, u32[]{:S(2)}) %collective-permute-start.56) | collective-permute-done | bytes 98336 | tf_op jit(solution)/shard_map/ppermute | solution.py:214
  169.5 4.1 %result_1.1 = bf16[1,2,256,1536]{3,2,1,0:T(8,128)(2,1)} custom-call(bf16[1,2,256,1536]{3,2,1,0:T(8,128)(2,1)S(1)} %copy-done, f32[1,1536]{1,0:T(1,128)S(1)} %copy-done.9, bf16[1,384,1536]{2,1,0:T(8,128)(2,1)S(1)} %copy-done.1, bf16[1,256,256]{2,1,0:T(8,128)(2,1)S(1)} %copy-done.8, f32[256,1536]{1,0:T(8,128)S(1)} %back_1.1.back_ref, ...), custom_call_target="tpu_custom_call", output_to_operand_aliasing={{}: (15, {})} | custom-call | flops 905969664 | bytes 6291456 | tf_op jit(solution)/shard_map/result_1/pallas_call | solution.py:267
  (87 shorter events, 2.7 us)
Async XLA Ops:
  0.0 24.0 %copy-start.9 = (f32[1,1536]{1,0:T(1,128)S(1)}, f32[1,1536]{1,0:T(1,128)}, u32[]{:S(2)}) copy-start(f32[1,1536]{1,0:T(1,128)} %gain_ref.11) | copy-start | bytes 18436
  0.0 24.0 %copy-start = (bf16[1,2,256,1536]{3,2,1,0:T(8,128)(2,1)S(1)}, bf16[1,2,256,1536]{3,2,1,0:T(8,128)(2,1)}, u32[]{:S(2)}) copy-start(bf16[1,2,256,1536]{3,2,1,0:T(8,128)(2,1)} %x_ref.11) | copy-start | bytes 4718596
  0.0 24.0 %copy-start.2 = (bf16[1,384,1536]{2,1,0:T(8,128)(2,1)S(1)}, bf16[1,384,1536]{2,1,0:T(8,128)(2,1)}, u32[]{:S(2)}) copy-start(bf16[1,384,1536]{2,1,0:T(8,128)(2,1)} %w_gate_ref.7) | copy-start | bytes 3538948
  5.2 11.8 %collective-permute-start = (bf16[32,1536]{1,0:T(8,128)(2,1)}, bf16[32,1536]{1,0:T(8,128)(2,1)S(1)}, u32[]{:S(2)}, u32[]{:S(2)}) collective-permute-start(bf16[32,1536]{1,0:T(8,128)(2,1)} %get-tuple-element.89), channel_id=1, source_target_pairs={{0,7},{1,6},{2,5},{3,4},{4,3},{5,2},{6,1},{7,0},{8,15},{9,14},{10,... | collective-permute-start | bytes 294920 | tf_op jit(solution)/shard_map/ppermute | solution.py:214
  7.8 14.6 %collective-permute-start.1 = (bf16[32,1536]{1,0:T(8,128)(2,1)}, bf16[32,1536]{1,0:T(8,128)(2,1)S(1)}, u32[]{:S(2)}, u32[]{:S(2)}) collective-permute-start(bf16[32,1536]{1,0:T(8,128)(2,1)} %get-tuple-element.90), channel_id=1, source_target_pairs={{0,1},{1,0},{2,4},{3,7},{4,2},{5,6},{6,5},{7,3},{8,9},{9,8},{10,12... | collective-permute-start | bytes 294920 | tf_op jit(solution)/shard_map/ppermute | solution.py:214
  8.3 21.4 %collective-permute-start.2 = (bf16[32,1536]{1,0:T(8,128)(2,1)}, bf16[32,1536]{1,0:T(8,128)(2,1)S(1)}, u32[]{:S(2)}, u32[]{:S(2)}) collective-permute-start(bf16[32,1536]{1,0:T(8,128)(2,1)} %get-tuple-element.91), channel_id=1, source_target_pairs={{0,3},{1,5},{2,6},{3,0},{4,7},{5,1},{6,2},{7,4},{8,11},{9,13},{10,... | collective-permute-start | bytes 294920 | tf_op jit(solution)/shard_map/ppermute | solution.py:214
  9.7 20.1 %collective-permute-start.3 = (bf16[32,1536]{1,0:T(8,128)(2,1)}, bf16[32,1536]{1,0:T(8,128)(2,1)S(1)}, u32[]{:S(2)}, u32[]{:S(2)}) collective-permute-start(bf16[32,1536]{1,0:T(8,128)(2,1)} %get-tuple-element.92), channel_id=1, source_target_pairs={{0,4},{1,2},{2,1},{3,5},{4,0},{5,3},{6,7},{7,6},{8,12},{9,10},{10,... | collective-permute-start | bytes 294920 | tf_op jit(solution)/shard_map/ppermute | solution.py:214
  12.0 17.9 %collective-permute-start.4 = (bf16[32,1536]{1,0:T(8,128)(2,1)}, bf16[32,1536]{1,0:T(8,128)(2,1)S(1)}, u32[]{:S(2)}, u32[]{:S(2)}) collective-permute-start(bf16[32,1536]{1,0:T(8,128)(2,1)} %get-tuple-element.93), channel_id=1, source_target_pairs={{0,2},{1,7},{2,0},{3,6},{4,5},{5,4},{6,3},{7,1},{8,10},{9,15},{10,... | collective-permute-start | bytes 294920 | tf_op jit(solution)/shard_map/ppermute | solution.py:214
  17.0 17.2 %collective-permute-start.5 = (bf16[32,1536]{1,0:T(8,128)(2,1)}, bf16[32,1536]{1,0:T(8,128)(2,1)S(1)}, u32[]{:S(2)}, u32[]{:S(2)}) collective-permute-start(bf16[32,1536]{1,0:T(8,128)(2,1)} %get-tuple-element.94), channel_id=1, source_target_pairs={{0,6},{1,4},{2,3},{3,2},{4,1},{5,7},{6,0},{7,5},{8,14},{9,12},{10,... | collective-permute-start | bytes 294920 | tf_op jit(solution)/shard_map/ppermute | solution.py:214
  22.4 12.6 %collective-permute-start.6 = (bf16[32,1536]{1,0:T(8,128)(2,1)}, bf16[32,1536]{1,0:T(8,128)(2,1)S(1)}, u32[]{:S(2)}, u32[]{:S(2)}) collective-permute-start(bf16[32,1536]{1,0:T(8,128)(2,1)} %get-tuple-element.95), channel_id=1, source_target_pairs={{0,5},{1,3},{2,7},{3,1},{4,6},{5,0},{6,4},{7,2},{8,13},{9,11},{10,... | collective-permute-start | bytes 294920 | tf_op jit(solution)/shard_map/ppermute | solution.py:214
  29.7 48.2 %copy-start.1 = (bf16[1,384,1536]{2,1,0:T(8,128)(2,1)S(1)}, bf16[1,384,1536]{2,1,0:T(8,128)(2,1)}, u32[]{:S(2)}) copy-start(bf16[1,384,1536]{2,1,0:T(8,128)(2,1)} %w_value_ref.3) | copy-start | bytes 3538948
  29.7 48.2 %copy-start.8 = (bf16[1,256,256]{2,1,0:T(8,128)(2,1)S(1)}, bf16[1,256,256]{2,1,0:T(8,128)(2,1)}, u32[]{:S(2)}) copy-start(bf16[1,256,256]{2,1,0:T(8,128)(2,1)} %r_ref.7) | copy-start | bytes 393220
  29.7 9.4 %collective-permute-start.14 = (bf16[32,1536]{1,0:T(8,128)(2,1)S(1)}, bf16[32,1536]{1,0:T(8,128)(2,1)S(1)}, u32[]{:S(2)}, u32[]{:S(2)}) collective-permute-start(bf16[32,1536]{1,0:T(8,128)(2,1)S(1)} %get-tuple-element.107), channel_id=1, source_target_pairs={{0,7},{1,6},{2,5},{3,4},{4,3},{5,2},{6,1},{7,0},{8,15},{9,14},{10,... | collective-permute-start | bytes 294920 | tf_op jit(solution)/shard_map/ppermute | solution.py:214
  29.8 9.5 %collective-permute-start.15 = (bf16[32,1536]{1,0:T(8,128)(2,1)S(1)}, bf16[32,1536]{1,0:T(8,128)(2,1)S(1)}, u32[]{:S(2)}, u32[]{:S(2)}) collective-permute-start(bf16[32,1536]{1,0:T(8,128)(2,1)S(1)} %get-tuple-element.108), channel_id=1, source_target_pairs={{0,1},{1,0},{2,4},{3,7},{4,2},{5,6},{6,5},{7,3},{8,9},{9,8},{10,12... | collective-permute-start | bytes 294920 | tf_op jit(solution)/shard_map/ppermute | solution.py:214
  29.9 14.5 %collective-permute-start.16 = (bf16[32,1536]{1,0:T(8,128)(2,1)S(1)}, bf16[32,1536]{1,0:T(8,128)(2,1)S(1)}, u32[]{:S(2)}, u32[]{:S(2)}) collective-permute-start(bf16[32,1536]{1,0:T(8,128)(2,1)S(1)} %get-tuple-element.109), channel_id=1, source_target_pairs={{0,3},{1,5},{2,6},{3,0},{4,7},{5,1},{6,2},{7,4},{8,11},{9,13},{10,... | collective-permute-start | bytes 294920 | tf_op jit(solution)/shard_map/ppermute | solution.py:214
  34.2 10.6 %collective-permute-start.17 = (bf16[32,1536]{1,0:T(8,128)(2,1)S(1)}, bf16[32,1536]{1,0:T(8,128)(2,1)S(1)}, u32[]{:S(2)}, u32[]{:S(2)}) collective-permute-start(bf16[32,1536]{1,0:T(8,128)(2,1)S(1)} %get-tuple-element.110), channel_id=1, source_target_pairs={{0,4},{1,2},{2,1},{3,5},{4,0},{5,3},{6,7},{7,6},{8,12},{9,10},{10,... | collective-permute-start | bytes 294920 | tf_op jit(solution)/shard_map/ppermute | solution.py:214
  35.1 10.9 %collective-permute-start.18 = (bf16[32,1536]{1,0:T(8,128)(2,1)S(1)}, bf16[32,1536]{1,0:T(8,128)(2,1)S(1)}, u32[]{:S(2)}, u32[]{:S(2)}) collective-permute-start(bf16[32,1536]{1,0:T(8,128)(2,1)S(1)} %get-tuple-element.111), channel_id=1, source_target_pairs={{0,2},{1,7},{2,0},{3,6},{4,5},{5,4},{6,3},{7,1},{8,10},{9,15},{10,... | collective-permute-start | bytes 294920 | tf_op jit(solution)/shard_map/ppermute | solution.py:214
  39.1 9.6 %collective-permute-start.19 = (bf16[32,1536]{1,0:T(8,128)(2,1)S(1)}, bf16[32,1536]{1,0:T(8,128)(2,1)S(1)}, u32[]{:S(2)}, u32[]{:S(2)}) collective-permute-start(bf16[32,1536]{1,0:T(8,128)(2,1)S(1)} %get-tuple-element.112), channel_id=1, source_target_pairs={{0,6},{1,4},{2,3},{3,2},{4,1},{5,7},{6,0},{7,5},{8,14},{9,12},{10,... | collective-permute-start | bytes 294920 | tf_op jit(solution)/shard_map/ppermute | solution.py:214
  39.3 10.5 %collective-permute-start.20 = (bf16[32,1536]{1,0:T(8,128)(2,1)S(1)}, bf16[32,1536]{1,0:T(8,128)(2,1)S(1)}, u32[]{:S(2)}, u32[]{:S(2)}) collective-permute-start(bf16[32,1536]{1,0:T(8,128)(2,1)S(1)} %get-tuple-element.113), channel_id=1, source_target_pairs={{0,5},{1,3},{2,7},{3,1},{4,6},{5,0},{6,4},{7,2},{8,13},{9,11},{10,... | collective-permute-start | bytes 294920 | tf_op jit(solution)/shard_map/ppermute | solution.py:214
  44.4 12.4 %collective-permute-start.10 = (bf16[32,1536]{1,0:T(8,128)(2,1)S(1)}, bf16[32,1536]{1,0:T(8,128)(2,1)S(1)}, u32[]{:S(2)}, u32[]{:S(2)}) collective-permute-start(bf16[32,1536]{1,0:T(8,128)(2,1)S(1)} %get-tuple-element.100), channel_id=1, source_target_pairs={{0,4},{1,2},{2,1},{3,5},{4,0},{5,3},{6,7},{7,6},{8,12},{9,10},{10,... | collective-permute-start | bytes 294920 | tf_op jit(solution)/shard_map/ppermute | solution.py:214
  44.8 12.1 %collective-permute-start.11 = (bf16[32,1536]{1,0:T(8,128)(2,1)S(1)}, bf16[32,1536]{1,0:T(8,128)(2,1)S(1)}, u32[]{:S(2)}, u32[]{:S(2)}) collective-permute-start(bf16[32,1536]{1,0:T(8,128)(2,1)S(1)} %get-tuple-element.101), channel_id=1, source_target_pairs={{0,2},{1,7},{2,0},{3,6},{4,5},{5,4},{6,3},{7,1},{8,10},{9,15},{10,... | collective-permute-start | bytes 294920 | tf_op jit(solution)/shard_map/ppermute | solution.py:214
  46.0 15.1 %collective-permute-start.12 = (bf16[32,1536]{1,0:T(8,128)(2,1)S(1)}, bf16[32,1536]{1,0:T(8,128)(2,1)S(1)}, u32[]{:S(2)}, u32[]{:S(2)}) collective-permute-start(bf16[32,1536]{1,0:T(8,128)(2,1)S(1)} %get-tuple-element.102), channel_id=1, source_target_pairs={{0,6},{1,4},{2,3},{3,2},{4,1},{5,7},{6,0},{7,5},{8,14},{9,12},{10,... | collective-permute-start | bytes 294920 | tf_op jit(solution)/shard_map/ppermute | solution.py:214
  48.7 12.3 %collective-permute-start.13 = (bf16[32,1536]{1,0:T(8,128)(2,1)S(1)}, bf16[32,1536]{1,0:T(8,128)(2,1)S(1)}, u32[]{:S(2)}, u32[]{:S(2)}) collective-permute-start(bf16[32,1536]{1,0:T(8,128)(2,1)S(1)} %get-tuple-element.103), channel_id=1, source_target_pairs={{0,5},{1,3},{2,7},{3,1},{4,6},{5,0},{6,4},{7,2},{8,13},{9,11},{10,... | collective-permute-start | bytes 294920 | tf_op jit(solution)/shard_map/ppermute | solution.py:214
  49.8 16.1 %collective-permute-start.7 = (bf16[32,1536]{1,0:T(8,128)(2,1)S(1)}, bf16[32,1536]{1,0:T(8,128)(2,1)S(1)}, u32[]{:S(2)}, u32[]{:S(2)}) collective-permute-start(bf16[32,1536]{1,0:T(8,128)(2,1)S(1)} %get-tuple-element.97), channel_id=1, source_target_pairs={{0,7},{1,6},{2,5},{3,4},{4,3},{5,2},{6,1},{7,0},{8,15},{9,14},{10,... | collective-permute-start | bytes 294920 | tf_op jit(solution)/shard_map/ppermute | solution.py:214
  56.8 9.2 %collective-permute-start.8 = (bf16[32,1536]{1,0:T(8,128)(2,1)S(1)}, bf16[32,1536]{1,0:T(8,128)(2,1)S(1)}, u32[]{:S(2)}, u32[]{:S(2)}) collective-permute-start(bf16[32,1536]{1,0:T(8,128)(2,1)S(1)} %get-tuple-element.98), channel_id=1, source_target_pairs={{0,1},{1,0},{2,4},{3,7},{4,2},{5,6},{6,5},{7,3},{8,9},{9,8},{10,12... | collective-permute-start | bytes 294920 | tf_op jit(solution)/shard_map/ppermute | solution.py:214
  56.9 9.6 %collective-permute-start.9 = (bf16[32,1536]{1,0:T(8,128)(2,1)S(1)}, bf16[32,1536]{1,0:T(8,128)(2,1)S(1)}, u32[]{:S(2)}, u32[]{:S(2)}) collective-permute-start(bf16[32,1536]{1,0:T(8,128)(2,1)S(1)} %get-tuple-element.99), channel_id=1, source_target_pairs={{0,3},{1,5},{2,6},{3,0},{4,7},{5,1},{6,2},{7,4},{8,11},{9,13},{10,... | collective-permute-start | bytes 294920 | tf_op jit(solution)/shard_map/ppermute | solution.py:214
  61.0 11.8 %collective-permute-start.21 = (bf16[32,1536]{1,0:T(8,128)(2,1)S(1)}, bf16[32,1536]{1,0:T(8,128)(2,1)S(1)}, u32[]{:S(2)}, u32[]{:S(2)}) collective-permute-start(bf16[32,1536]{1,0:T(8,128)(2,1)S(1)} %get-tuple-element.115), channel_id=1, source_target_pairs={{0,7},{1,6},{2,5},{3,4},{4,3},{5,2},{6,1},{7,0},{8,15},{9,14},{10,... | collective-permute-start | bytes 294920 | tf_op jit(solution)/shard_map/ppermute | solution.py:214
  61.1 14.4 %collective-permute-start.22 = (bf16[32,1536]{1,0:T(8,128)(2,1)S(1)}, bf16[32,1536]{1,0:T(8,128)(2,1)S(1)}, u32[]{:S(2)}, u32[]{:S(2)}) collective-permute-start(bf16[32,1536]{1,0:T(8,128)(2,1)S(1)} %get-tuple-element.116), channel_id=1, source_target_pairs={{0,1},{1,0},{2,4},{3,7},{4,2},{5,6},{6,5},{7,3},{8,9},{9,8},{10,12... | collective-permute-start | bytes 294920 | tf_op jit(solution)/shard_map/ppermute | solution.py:214
  66.0 15.0 %collective-permute-start.23 = (bf16[32,1536]{1,0:T(8,128)(2,1)S(1)}, bf16[32,1536]{1,0:T(8,128)(2,1)S(1)}, u32[]{:S(2)}, u32[]{:S(2)}) collective-permute-start(bf16[32,1536]{1,0:T(8,128)(2,1)S(1)} %get-tuple-element.117), channel_id=1, source_target_pairs={{0,3},{1,5},{2,6},{3,0},{4,7},{5,1},{6,2},{7,4},{8,11},{9,13},{10,... | collective-permute-start | bytes 294920 | tf_op jit(solution)/shard_map/ppermute | solution.py:214
  66.0 15.0 %collective-permute-start.24 = (bf16[32,1536]{1,0:T(8,128)(2,1)S(1)}, bf16[32,1536]{1,0:T(8,128)(2,1)S(1)}, u32[]{:S(2)}, u32[]{:S(2)}) collective-permute-start(bf16[32,1536]{1,0:T(8,128)(2,1)S(1)} %get-tuple-element.118), channel_id=1, source_target_pairs={{0,4},{1,2},{2,1},{3,5},{4,0},{5,3},{6,7},{7,6},{8,12},{9,10},{10,... | collective-permute-start | bytes 294920 | tf_op jit(solution)/shard_map/ppermute | solution.py:214
  66.5 14.6 %collective-permute-start.25 = (bf16[32,1536]{1,0:T(8,128)(2,1)S(1)}, bf16[32,1536]{1,0:T(8,128)(2,1)S(1)}, u32[]{:S(2)}, u32[]{:S(2)}) collective-permute-start(bf16[32,1536]{1,0:T(8,128)(2,1)S(1)} %get-tuple-element.119), channel_id=1, source_target_pairs={{0,2},{1,7},{2,0},{3,6},{4,5},{5,4},{6,3},{7,1},{8,10},{9,15},{10,... | collective-permute-start | bytes 294920 | tf_op jit(solution)/shard_map/ppermute | solution.py:214
  72.8 12.6 %collective-permute-start.26 = (bf16[32,1536]{1,0:T(8,128)(2,1)S(1)}, bf16[32,1536]{1,0:T(8,128)(2,1)S(1)}, u32[]{:S(2)}, u32[]{:S(2)}) collective-permute-start(bf16[32,1536]{1,0:T(8,128)(2,1)S(1)} %get-tuple-element.120), channel_id=1, source_target_pairs={{0,6},{1,4},{2,3},{3,2},{4,1},{5,7},{6,0},{7,5},{8,14},{9,12},{10,... | collective-permute-start | bytes 294920 | tf_op jit(solution)/shard_map/ppermute | solution.py:214
  75.4 11.8 %collective-permute-start.27 = (bf16[32,1536]{1,0:T(8,128)(2,1)S(1)}, bf16[32,1536]{1,0:T(8,128)(2,1)S(1)}, u32[]{:S(2)}, u32[]{:S(2)}) collective-permute-start(bf16[32,1536]{1,0:T(8,128)(2,1)S(1)} %get-tuple-element.121), channel_id=1, source_target_pairs={{0,5},{1,3},{2,7},{3,1},{4,6},{5,0},{6,4},{7,2},{8,13},{9,11},{10,... | collective-permute-start | bytes 294920 | tf_op jit(solution)/shard_map/ppermute | solution.py:214
  80.9 10.4 %collective-permute-start.28 = (bf16[32,1536]{1,0:T(8,128)(2,1)S(1)}, bf16[32,1536]{1,0:T(8,128)(2,1)S(1)}, u32[]{:S(2)}, u32[]{:S(2)}) collective-permute-start(bf16[32,1536]{1,0:T(8,128)(2,1)S(1)} %get-tuple-element.123), channel_id=1, source_target_pairs={{0,7},{1,6},{2,5},{3,4},{4,3},{5,2},{6,1},{7,0},{8,15},{9,14},{10,... | collective-permute-start | bytes 294920 | tf_op jit(solution)/shard_map/ppermute | solution.py:214
  81.0 10.4 %collective-permute-start.29 = (bf16[32,1536]{1,0:T(8,128)(2,1)S(1)}, bf16[32,1536]{1,0:T(8,128)(2,1)S(1)}, u32[]{:S(2)}, u32[]{:S(2)}) collective-permute-start(bf16[32,1536]{1,0:T(8,128)(2,1)S(1)} %get-tuple-element.124), channel_id=1, source_target_pairs={{0,1},{1,0},{2,4},{3,7},{4,2},{5,6},{6,5},{7,3},{8,9},{9,8},{10,12... | collective-permute-start | bytes 294920 | tf_op jit(solution)/shard_map/ppermute | solution.py:214
  81.1 10.3 %collective-permute-start.30 = (bf16[32,1536]{1,0:T(8,128)(2,1)S(1)}, bf16[32,1536]{1,0:T(8,128)(2,1)S(1)}, u32[]{:S(2)}, u32[]{:S(2)}) collective-permute-start(bf16[32,1536]{1,0:T(8,128)(2,1)S(1)} %get-tuple-element.125), channel_id=1, source_target_pairs={{0,3},{1,5},{2,6},{3,0},{4,7},{5,1},{6,2},{7,4},{8,11},{9,13},{10,... | collective-permute-start | bytes 294920 | tf_op jit(solution)/shard_map/ppermute | solution.py:214
  85.4 6.0 %collective-permute-start.31 = (bf16[32,1536]{1,0:T(8,128)(2,1)S(1)}, bf16[32,1536]{1,0:T(8,128)(2,1)S(1)}, u32[]{:S(2)}, u32[]{:S(2)}) collective-permute-start(bf16[32,1536]{1,0:T(8,128)(2,1)S(1)} %get-tuple-element.126), channel_id=1, source_target_pairs={{0,4},{1,2},{2,1},{3,5},{4,0},{5,3},{6,7},{7,6},{8,12},{9,10},{10,... | collective-permute-start | bytes 294920 | tf_op jit(solution)/shard_map/ppermute | solution.py:214
  87.2 24.6 %copy-start.4 = (bf16[1,384,1536]{2,1,0:T(8,128)(2,1)S(1)}, bf16[1,384,1536]{2,1,0:T(8,128)(2,1)}, u32[]{:S(2)}) copy-start(bf16[1,384,1536]{2,1,0:T(8,128)(2,1)} %w_out_ref.3) | copy-start | bytes 3538948
  91.4 20.4 %copy-start.7 = (bf16[1,256,1536]{2,1,0:T(8,128)(2,1)S(1)}, bf16[1,256,1536]{2,1,0:T(8,128)(2,1)}, u32[]{:S(2)}) copy-start(bf16[1,256,1536]{2,1,0:T(8,128)(2,1)} %refs_9_.1) | copy-start | bytes 2359300
  91.4 20.4 %collective-permute-start.32 = (bf16[256,1536]{1,0:T(8,128)(2,1)S(1)}, bf16[256,1536]{1,0:T(8,128)(2,1)S(1)}, u32[]{:S(2)}, u32[]{:S(2)}) collective-permute-start(bf16[256,1536]{1,0:T(8,128)(2,1)S(1)} %get-tuple-element.127), channel_id=1, source_target_pairs={{8,0},{16,8},{24,16},{9,1},{17,9},{25,17},{10,2},{18,10},{26,18},{... | collective-permute-start | bytes 2359304 | tf_op jit(solution)/shard_map/ppermute | solution.py:372
  93.0 5.6 %collective-permute-start.33 = (bf16[32,1536]{1,0:T(8,128)(2,1)S(1)}, bf16[32,1536]{1,0:T(8,128)(2,1)S(1)}, u32[]{:S(2)}, u32[]{:S(2)}) collective-permute-start(bf16[32,1536]{1,0:T(8,128)(2,1)S(1)} %get-tuple-element.132), channel_id=1, source_target_pairs={{0,2},{1,7},{2,0},{3,6},{4,5},{5,4},{6,3},{7,1},{8,10},{9,15},{10,... | collective-permute-start | bytes 294920 | tf_op jit(solution)/shard_map/ppermute | solution.py:214
  93.9 7.3 %collective-permute-start.34 = (bf16[32,1536]{1,0:T(8,128)(2,1)S(1)}, bf16[32,1536]{1,0:T(8,128)(2,1)S(1)}, u32[]{:S(2)}, u32[]{:S(2)}) collective-permute-start(bf16[32,1536]{1,0:T(8,128)(2,1)S(1)} %get-tuple-element.133), channel_id=1, source_target_pairs={{0,6},{1,4},{2,3},{3,2},{4,1},{5,7},{6,0},{7,5},{8,14},{9,12},{10,... | collective-permute-start | bytes 294920 | tf_op jit(solution)/shard_map/ppermute | solution.py:214
  96.0 10.1 %collective-permute-start.35 = (bf16[32,1536]{1,0:T(8,128)(2,1)S(1)}, bf16[32,1536]{1,0:T(8,128)(2,1)S(1)}, u32[]{:S(2)}, u32[]{:S(2)}) collective-permute-start(bf16[32,1536]{1,0:T(8,128)(2,1)S(1)} %get-tuple-element.134), channel_id=1, source_target_pairs={{0,5},{1,3},{2,7},{3,1},{4,6},{5,0},{6,4},{7,2},{8,13},{9,11},{10,... | collective-permute-start | bytes 294920 | tf_op jit(solution)/shard_map/ppermute | solution.py:214
  107.3 7.8 %collective-permute-start.38 = (bf16[32,1536]{1,0:T(8,128)(2,1)S(1)}, bf16[32,1536]{1,0:T(8,128)(2,1)S(1)}, u32[]{:S(2)}, u32[]{:S(2)}) collective-permute-start(bf16[32,1536]{1,0:T(8,128)(2,1)S(1)} %get-tuple-element.146), channel_id=1, source_target_pairs={{0,3},{1,5},{2,6},{3,0},{4,7},{5,1},{6,2},{7,4},{8,11},{9,13},{10,... | collective-permute-start | bytes 294920 | tf_op jit(solution)/shard_map/ppermute | solution.py:214
  107.5 10.5 %collective-permute-start.37 = (bf16[32,1536]{1,0:T(8,128)(2,1)S(1)}, bf16[32,1536]{1,0:T(8,128)(2,1)S(1)}, u32[]{:S(2)}, u32[]{:S(2)}) collective-permute-start(bf16[32,1536]{1,0:T(8,128)(2,1)S(1)} %get-tuple-element.143), channel_id=1, source_target_pairs={{0,1},{1,0},{2,4},{3,7},{4,2},{5,6},{6,5},{7,3},{8,9},{9,8},{10,12... | collective-permute-start | bytes 294920 | tf_op jit(solution)/shard_map/ppermute | solution.py:214
  111.6 10.0 %collective-permute-start.36 = (bf16[32,1536]{1,0:T(8,128)(2,1)S(1)}, bf16[32,1536]{1,0:T(8,128)(2,1)S(1)}, u32[]{:S(2)}, u32[]{:S(2)}) collective-permute-start(bf16[32,1536]{1,0:T(8,128)(2,1)S(1)} %get-tuple-element.140), channel_id=1, source_target_pairs={{0,7},{1,6},{2,5},{3,4},{4,3},{5,2},{6,1},{7,0},{8,15},{9,14},{10,... | collective-permute-start | bytes 294920 | tf_op jit(solution)/shard_map/ppermute | solution.py:214
  115.2 11.0 %collective-permute-start.47 = (bf16[32,1536]{1,0:T(8,128)(2,1)S(1)}, bf16[32,1536]{1,0:T(8,128)(2,1)S(1)}, u32[]{:S(2)}, u32[]{:S(2)}) collective-permute-start(bf16[32,1536]{1,0:T(8,128)(2,1)S(1)} %get-tuple-element.157), channel_id=1, source_target_pairs={{0,2},{1,7},{2,0},{3,6},{4,5},{5,4},{6,3},{7,1},{8,10},{9,15},{10,... | collective-permute-start | bytes 294920 | tf_op jit(solution)/shard_map/ppermute | solution.py:214
  118.0 11.4 %collective-permute-start.48 = (bf16[32,1536]{1,0:T(8,128)(2,1)S(1)}, bf16[32,1536]{1,0:T(8,128)(2,1)S(1)}, u32[]{:S(2)}, u32[]{:S(2)}) collective-permute-start(bf16[32,1536]{1,0:T(8,128)(2,1)S(1)} %get-tuple-element.158), channel_id=1, source_target_pairs={{0,6},{1,4},{2,3},{3,2},{4,1},{5,7},{6,0},{7,5},{8,14},{9,12},{10,... | collective-permute-start | bytes 294920 | tf_op jit(solution)/shard_map/ppermute | solution.py:214
  121.6 9.8 %collective-permute-start.49 = (bf16[32,1536]{1,0:T(8,128)(2,1)S(1)}, bf16[32,1536]{1,0:T(8,128)(2,1)S(1)}, u32[]{:S(2)}, u32[]{:S(2)}) collective-permute-start(bf16[32,1536]{1,0:T(8,128)(2,1)S(1)} %get-tuple-element.159), channel_id=1, source_target_pairs={{0,5},{1,3},{2,7},{3,1},{4,6},{5,0},{6,4},{7,2},{8,13},{9,11},{10,... | collective-permute-start | bytes 294920 | tf_op jit(solution)/shard_map/ppermute | solution.py:214
  121.6 15.4 %collective-permute-start.43 = (bf16[32,1536]{1,0:T(8,128)(2,1)S(1)}, bf16[32,1536]{1,0:T(8,128)(2,1)S(1)}, u32[]{:S(2)}, u32[]{:S(2)}) collective-permute-start(bf16[32,1536]{1,0:T(8,128)(2,1)S(1)} %get-tuple-element.153), channel_id=1, source_target_pairs={{0,7},{1,6},{2,5},{3,4},{4,3},{5,2},{6,1},{7,0},{8,15},{9,14},{10,... | collective-permute-start | bytes 294920 | tf_op jit(solution)/shard_map/ppermute | solution.py:214
  123.8 14.0 %collective-permute-start.44 = (bf16[32,1536]{1,0:T(8,128)(2,1)S(1)}, bf16[32,1536]{1,0:T(8,128)(2,1)S(1)}, u32[]{:S(2)}, u32[]{:S(2)}) collective-permute-start(bf16[32,1536]{1,0:T(8,128)(2,1)S(1)} %get-tuple-element.154), channel_id=1, source_target_pairs={{0,1},{1,0},{2,4},{3,7},{4,2},{5,6},{6,5},{7,3},{8,9},{9,8},{10,12... | collective-permute-start | bytes 294920 | tf_op jit(solution)/shard_map/ppermute | solution.py:214
  126.2 18.0 %collective-permute-start.45 = (bf16[32,1536]{1,0:T(8,128)(2,1)S(1)}, bf16[32,1536]{1,0:T(8,128)(2,1)S(1)}, u32[]{:S(2)}, u32[]{:S(2)}) collective-permute-start(bf16[32,1536]{1,0:T(8,128)(2,1)S(1)} %get-tuple-element.155), channel_id=1, source_target_pairs={{0,3},{1,5},{2,6},{3,0},{4,7},{5,1},{6,2},{7,4},{8,11},{9,13},{10,... | collective-permute-start | bytes 294920 | tf_op jit(solution)/shard_map/ppermute | solution.py:214
  129.4 14.8 %collective-permute-start.46 = (bf16[32,1536]{1,0:T(8,128)(2,1)S(1)}, bf16[32,1536]{1,0:T(8,128)(2,1)S(1)}, u32[]{:S(2)}, u32[]{:S(2)}) collective-permute-start(bf16[32,1536]{1,0:T(8,128)(2,1)S(1)} %get-tuple-element.156), channel_id=1, source_target_pairs={{0,4},{1,2},{2,1},{3,5},{4,0},{5,3},{6,7},{7,6},{8,12},{9,10},{10,... | collective-permute-start | bytes 294920 | tf_op jit(solution)/shard_map/ppermute | solution.py:214
  131.4 14.2 %collective-permute-start.39 = (bf16[32,1536]{1,0:T(8,128)(2,1)S(1)}, bf16[32,1536]{1,0:T(8,128)(2,1)S(1)}, u32[]{:S(2)}, u32[]{:S(2)}) collective-permute-start(bf16[32,1536]{1,0:T(8,128)(2,1)S(1)} %get-tuple-element.148), channel_id=1, source_target_pairs={{0,4},{1,2},{2,1},{3,5},{4,0},{5,3},{6,7},{7,6},{8,12},{9,10},{10,... | collective-permute-start | bytes 294920 | tf_op jit(solution)/shard_map/ppermute | solution.py:214
  137.0 12.6 %collective-permute-start.40 = (bf16[32,1536]{1,0:T(8,128)(2,1)S(1)}, bf16[32,1536]{1,0:T(8,128)(2,1)S(1)}, u32[]{:S(2)}, u32[]{:S(2)}) collective-permute-start(bf16[32,1536]{1,0:T(8,128)(2,1)S(1)} %get-tuple-element.149), channel_id=1, source_target_pairs={{0,2},{1,7},{2,0},{3,6},{4,5},{5,4},{6,3},{7,1},{8,10},{9,15},{10,... | collective-permute-start | bytes 294920 | tf_op jit(solution)/shard_map/ppermute | solution.py:214
  137.9 12.1 %collective-permute-start.41 = (bf16[32,1536]{1,0:T(8,128)(2,1)S(1)}, bf16[32,1536]{1,0:T(8,128)(2,1)S(1)}, u32[]{:S(2)}, u32[]{:S(2)}) collective-permute-start(bf16[32,1536]{1,0:T(8,128)(2,1)S(1)} %get-tuple-element.150), channel_id=1, source_target_pairs={{0,6},{1,4},{2,3},{3,2},{4,1},{5,7},{6,0},{7,5},{8,14},{9,12},{10,... | collective-permute-start | bytes 294920 | tf_op jit(solution)/shard_map/ppermute | solution.py:214
  144.2 8.3 %collective-permute-start.42 = (bf16[32,1536]{1,0:T(8,128)(2,1)S(1)}, bf16[32,1536]{1,0:T(8,128)(2,1)S(1)}, u32[]{:S(2)}, u32[]{:S(2)}) collective-permute-start(bf16[32,1536]{1,0:T(8,128)(2,1)S(1)} %get-tuple-element.151), channel_id=1, source_target_pairs={{0,5},{1,3},{2,7},{3,1},{4,6},{5,0},{6,4},{7,2},{8,13},{9,11},{10,... | collective-permute-start | bytes 294920 | tf_op jit(solution)/shard_map/ppermute | solution.py:214
  145.6 12.2 %collective-permute-start.50 = (bf16[32,1536]{1,0:T(8,128)(2,1)S(1)}, bf16[32,1536]{1,0:T(8,128)(2,1)S(1)}, u32[]{:S(2)}, u32[]{:S(2)}) collective-permute-start(bf16[32,1536]{1,0:T(8,128)(2,1)S(1)} %get-tuple-element.161), channel_id=1, source_target_pairs={{0,7},{1,6},{2,5},{3,4},{4,3},{5,2},{6,1},{7,0},{8,15},{9,14},{10,... | collective-permute-start | bytes 294920 | tf_op jit(solution)/shard_map/ppermute | solution.py:214
  145.6 17.5 %collective-permute-start.51 = (bf16[32,1536]{1,0:T(8,128)(2,1)S(1)}, bf16[32,1536]{1,0:T(8,128)(2,1)S(1)}, u32[]{:S(2)}, u32[]{:S(2)}) collective-permute-start(bf16[32,1536]{1,0:T(8,128)(2,1)S(1)} %get-tuple-element.162), channel_id=1, source_target_pairs={{0,1},{1,0},{2,4},{3,7},{4,2},{5,6},{6,5},{7,3},{8,9},{9,8},{10,12... | collective-permute-start | bytes 294920 | tf_op jit(solution)/shard_map/ppermute | solution.py:214
  149.6 18.1 %collective-permute-start.52 = (bf16[32,1536]{1,0:T(8,128)(2,1)S(1)}, bf16[32,1536]{1,0:T(8,128)(2,1)S(1)}, u32[]{:S(2)}, u32[]{:S(2)}) collective-permute-start(bf16[32,1536]{1,0:T(8,128)(2,1)S(1)} %get-tuple-element.163), channel_id=1, source_target_pairs={{0,3},{1,5},{2,6},{3,0},{4,7},{5,1},{6,2},{7,4},{8,11},{9,13},{10,... | collective-permute-start | bytes 294920 | tf_op jit(solution)/shard_map/ppermute | solution.py:214
  150.0 17.7 %collective-permute-start.53 = (bf16[32,1536]{1,0:T(8,128)(2,1)S(1)}, bf16[32,1536]{1,0:T(8,128)(2,1)S(1)}, u32[]{:S(2)}, u32[]{:S(2)}) collective-permute-start(bf16[32,1536]{1,0:T(8,128)(2,1)S(1)} %get-tuple-element.164), channel_id=1, source_target_pairs={{0,4},{1,2},{2,1},{3,5},{4,0},{5,3},{6,7},{7,6},{8,12},{9,10},{10,... | collective-permute-start | bytes 294920 | tf_op jit(solution)/shard_map/ppermute | solution.py:214
  152.4 15.3 %collective-permute-start.54 = (bf16[32,1536]{1,0:T(8,128)(2,1)S(1)}, bf16[32,1536]{1,0:T(8,128)(2,1)S(1)}, u32[]{:S(2)}, u32[]{:S(2)}) collective-permute-start(bf16[32,1536]{1,0:T(8,128)(2,1)S(1)} %get-tuple-element.165), channel_id=1, source_target_pairs={{0,2},{1,7},{2,0},{3,6},{4,5},{5,4},{6,3},{7,1},{8,10},{9,15},{10,... | collective-permute-start | bytes 294920 | tf_op jit(solution)/shard_map/ppermute | solution.py:214
  157.8 10.0 %collective-permute-start.55 = (bf16[32,1536]{1,0:T(8,128)(2,1)S(1)}, bf16[32,1536]{1,0:T(8,128)(2,1)S(1)}, u32[]{:S(2)}, u32[]{:S(2)}) collective-permute-start(bf16[32,1536]{1,0:T(8,128)(2,1)S(1)} %get-tuple-element.166), channel_id=1, source_target_pairs={{0,6},{1,4},{2,3},{3,2},{4,1},{5,7},{6,0},{7,5},{8,14},{9,12},{10,... | collective-permute-start | bytes 294920 | tf_op jit(solution)/shard_map/ppermute | solution.py:214
  163.1 6.4 %collective-permute-start.56 = (bf16[32,1536]{1,0:T(8,128)(2,1)S(1)}, bf16[32,1536]{1,0:T(8,128)(2,1)S(1)}, u32[]{:S(2)}, u32[]{:S(2)}) collective-permute-start(bf16[32,1536]{1,0:T(8,128)(2,1)S(1)} %get-tuple-element.167), channel_id=1, source_target_pairs={{0,5},{1,3},{2,7},{3,1},{4,6},{5,0},{6,4},{7,2},{8,13},{9,11},{10,... | collective-permute-start | bytes 294920 | tf_op jit(solution)/shard_map/ppermute | solution.py:214
  (5 other events, 33.5 us)

commit v4 on v3

--- a/solution.py
+++ b/solution.py
@@ -313,7 +313,7 @@
         return call(
             name,
             functools.partial(mix_kernel, count, transposed),
-            (1, 2),
+            (40 if name == "mix_1" else 1, 2),
             [(square_plain, matrix), *zip(slots, parts)],
             slots_out,
             [],
@@ -368,13 +368,12 @@
     gate_0, first_1.parts[0] = lax.optimization_barrier((gate_0, first_1.parts[0]))
     first_1.send(every)
     stacked, result_0 = result(0, gate_0, fold_0.all(), [(whole3, arrived_grad)], None)
-    result_0 = tied(result_0, [(first_1, slot) for slot in every[: min(4, count // 2)]])
     passed = lax.ppermute(result_0, "pipe", [(s, s - 1) for s in range(1, pipe)])
     mix_1 = Exchange(mix("mix_1", first_1.all(), False)).send(every)
     passed, mix_1.parts[0] = lax.optimization_barrier((passed, mix_1.parts[0]))
     mix_1.got[0] = mix_1.parts[0]
     parts, factor_1 = grads(1, [(cut, passed), (cut3, loss_grad)])
-    for slot in every[:3]:
+    for slot in every[:2]:
         parts[count - slot] = tied(parts[count - slot], [(mix_1, slot)])
     grad_1 = Exchange(parts).send(every)
     fold_1 = Exchange(mix("fold_1", grad_1.all(), True)).send(every)

time: 174 us -> 168 us (0.966)
  the two profiles are of different devices: /device:TPU:8 before, /device:TPU:2 now
where the time goes in v4:
time: 168 us
  starting transfers between devices  112 us (67%)
  Pallas kernels  32 us (19%)
  waiting for transfers between devices  21 us (12%)
  local copies, waits for them, and re-layouts  2.44 us (1%)
    ppermute x56, starting transfers between devices, send(): self.got[slot] = lax.ppermute(tied(self.parts[slot], after), 'seq', pairs)  110 us
    pallas_call x13, Pallas kernels, call(): pl.pallas_call(kernel, grid=(steps or width // block,), in_specs=[spec fo...  32 us
    ppermute x56, waiting for transfers between devices, send(): self.got[slot] = lax.ppermute(tied(self.parts[slot], after), 'seq', pairs)  16.2 us
    ppermute x1, waiting for transfers between devices, local(): lax.ppermute(result_0, 'pipe', [(s, s - 1) for s in range(1, pipe)])  4.86 us
  transfers between devices with their start and end apart: 57, of which 7 were waited for; matrix products, arithmetic and copies ran while one was open for 0% of the time, Pallas kernels for 13%

profile of v4, /device:TPU:2, one launch (start us, length us, event | category | flops | bytes accessed | tf_op | source)
XLA Modules:
  0.0 167.5 jit_solution(10208760578992089287)
XLA Ops:
  0.0 5.2 %first_0.1 = (bf16[32,1536]{1,0:T(8,128)(2,1)}, bf16[32,1536]{1,0:T(8,128)(2,1)}, bf16[32,1536]{1,0:T(8,128)(2,1)}, bf16[32,1536]{1,0:T(8,128)(2,1)}, bf16[32,15...) custom-call(bf16[1,2,256,1536]{3,2,1,0:T(8,128)(2,1)} %x_ref.11, ...), custom_call_target="tpu_custom_call" | custom-call | flops 603979776 | bytes 3145728 | tf_op jit(solution)/shard_map/first_0/pallas_call | solution.py:267
  5.2 4.6 %collective-permute-start = (bf16[32,1536]{1,0:T(8,128)(2,1)}, bf16[32,1536]{1,0:T(8,128)(2,1)S(1)}, u32[]{:S(2)}, u32[]{:S(2)}) collective-permute-start(bf16[32,1536]{1,0:T(8,128)(2,1)} %get-tuple-element.82), channel_id=1, source_target_pairs={{0,7},{1,6},{2,5},{3,4},{4,3},{5,2},{6,1},{7,0},{8,15},{9,14},{10,... | collective-permute-start | bytes 294920 | tf_op jit(solution)/shard_map/ppermute | solution.py:214
  9.9 0.5 collective-permute-start.1
  10.4 0.2 collective-permute-start.2
  10.6 1.7 %collective-permute-start.3 = (bf16[32,1536]{1,0:T(8,128)(2,1)}, bf16[32,1536]{1,0:T(8,128)(2,1)S(1)}, u32[]{:S(2)}, u32[]{:S(2)}) collective-permute-start(bf16[32,1536]{1,0:T(8,128)(2,1)} %get-tuple-element.85), channel_id=1, source_target_pairs={{0,4},{1,2},{2,1},{3,5},{4,0},{5,3},{6,7},{7,6},{8,12},{9,10},{10,... | collective-permute-start | bytes 294920 | tf_op jit(solution)/shard_map/ppermute | solution.py:214
  12.3 1.3 collective-permute-start.4
  13.6 1.3 copy-done.3
  14.9 1.1 copy-done.5
  16.0 3.3 %grads_0.1 = (bf16[32,1536]{1,0:T(8,128)(2,1)S(1)}, bf16[32,1536]{1,0:T(8,128)(2,1)S(1)}, bf16[32,1536]{1,0:T(8,128)(2,1)S(1)}, bf16[32,1536]{1,0:T(8,128)(2,1)S...) custom-call(bf16[1,2,256,1536]{3,2,1,0:T(8,128)(2,1)S(1)} %copy-done, ...), custom_call_target="tpu_custom_call" | custom-call | flops 603979776 | bytes 6291456 | tf_op jit(solution)/shard_map/grads_0/pallas_call | solution.py:267
  19.3 3.7 %collective-permute-start.5 = (bf16[32,1536]{1,0:T(8,128)(2,1)S(1)}, bf16[32,1536]{1,0:T(8,128)(2,1)S(1)}, u32[]{:S(2)}, u32[]{:S(2)}) collective-permute-start(bf16[32,1536]{1,0:T(8,128)(2,1)S(1)} %copy-done.12), channel_id=1, source_target_pairs={{0,6},{1,4},{2,3},{3,2},{4,1},{5,7},{6,0},{7,5},{8,14},{9,12},{10,... | collective-permute-start | bytes 294920 | tf_op jit(solution)/shard_map/ppermute | solution.py:214
  23.0 2.2 %collective-permute-start.14 = (bf16[32,1536]{1,0:T(8,128)(2,1)S(1)}, bf16[32,1536]{1,0:T(8,128)(2,1)S(1)}, u32[]{:S(2)}, u32[]{:S(2)}) collective-permute-start(bf16[32,1536]{1,0:T(8,128)(2,1)S(1)} %get-tuple-element.100), channel_id=1, source_target_pairs={{0,7},{1,6},{2,5},{3,4},{4,3},{5,2},{6,1},{7,0},{8,15},{9,14},{10,... | collective-permute-start | bytes 294920 | tf_op jit(solution)/shard_map/ppermute | solution.py:214
  25.4 6.3 %collective-permute-start.16 = (bf16[32,1536]{1,0:T(8,128)(2,1)S(1)}, bf16[32,1536]{1,0:T(8,128)(2,1)S(1)}, u32[]{:S(2)}, u32[]{:S(2)}) collective-permute-start(bf16[32,1536]{1,0:T(8,128)(2,1)S(1)} %get-tuple-element.102), channel_id=1, source_target_pairs={{0,3},{1,5},{2,6},{3,0},{4,7},{5,1},{6,2},{7,4},{8,11},{9,13},{10,... | collective-permute-start | bytes 294920 | tf_op jit(solution)/shard_map/ppermute | solution.py:214
  31.7 3.0 %first_1.1 = (bf16[32,1536]{1,0:T(8,128)(2,1)S(1)}, bf16[32,1536]{1,0:T(8,128)(2,1)S(1)}, bf16[32,1536]{1,0:T(8,128)(2,1)S(1)}, bf16[32,1536]{1,0:T(8,128)(2,1)S...) custom-call(bf16[1,2,256,1536]{3,2,1,0:T(8,128)(2,1)S(1)} %copy-done, ...), custom_call_target="tpu_custom_call" | custom-call | flops 603979776 | bytes 3145728 | tf_op jit(solution)/shard_map/first_1/pallas_call | solution.py:267
  34.8 3.5 %collective-permute-start.18 = (bf16[32,1536]{1,0:T(8,128)(2,1)S(1)}, bf16[32,1536]{1,0:T(8,128)(2,1)S(1)}, u32[]{:S(2)}, u32[]{:S(2)}) collective-permute-start(bf16[32,1536]{1,0:T(8,128)(2,1)S(1)} %get-tuple-element.104), channel_id=1, source_target_pairs={{0,2},{1,7},{2,0},{3,6},{4,5},{5,4},{6,3},{7,1},{8,10},{9,15},{10,... | collective-permute-start | bytes 294920 | tf_op jit(solution)/shard_map/ppermute | solution.py:214
  38.3 5.2 %collective-permute-start.20 = (bf16[32,1536]{1,0:T(8,128)(2,1)S(1)}, bf16[32,1536]{1,0:T(8,128)(2,1)S(1)}, u32[]{:S(2)}, u32[]{:S(2)}) collective-permute-start(bf16[32,1536]{1,0:T(8,128)(2,1)S(1)} %get-tuple-element.106), channel_id=1, source_target_pairs={{0,5},{1,3},{2,7},{3,1},{4,6},{5,0},{6,4},{7,2},{8,13},{9,11},{10,... | collective-permute-start | bytes 294920 | tf_op jit(solution)/shard_map/ppermute | solution.py:214
  43.5 0.2 matrix.1.m_ref
  43.7 1.3 mix_0.1
  45.0 5.1 %collective-permute-start.30 = (bf16[32,1536]{1,0:T(8,128)(2,1)S(1)}, bf16[32,1536]{1,0:T(8,128)(2,1)S(1)}, u32[]{:S(2)}, u32[]{:S(2)}) collective-permute-start(bf16[32,1536]{1,0:T(8,128)(2,1)S(1)} %get-tuple-element.117), channel_id=1, source_target_pairs={{0,1},{1,0},{2,4},{3,7},{4,2},{5,6},{6,5},{7,3},{8,9},{9,8},{10,12... | collective-permute-start | bytes 294920 | tf_op jit(solution)/shard_map/ppermute | solution.py:214
  50.0 1.5 collective-permute-start.11
  51.6 1.4 collective-permute-start.12
  53.0 5.1 %collective-permute-start.13 = (bf16[32,1536]{1,0:T(8,128)(2,1)S(1)}, bf16[32,1536]{1,0:T(8,128)(2,1)S(1)}, u32[]{:S(2)}, u32[]{:S(2)}) collective-permute-start(bf16[32,1536]{1,0:T(8,128)(2,1)S(1)} %get-tuple-element.96), channel_id=1, source_target_pairs={{0,5},{1,3},{2,7},{3,1},{4,6},{5,0},{6,4},{7,2},{8,13},{9,11},{10,... | collective-permute-start | bytes 294920 | tf_op jit(solution)/shard_map/ppermute | solution.py:214
  58.1 1.3 fold_0.1
  59.4 3.7 %collective-permute-start.7 = (bf16[32,1536]{1,0:T(8,128)(2,1)S(1)}, bf16[32,1536]{1,0:T(8,128)(2,1)S(1)}, u32[]{:S(2)}, u32[]{:S(2)}) collective-permute-start(bf16[32,1536]{1,0:T(8,128)(2,1)S(1)} %get-tuple-element.90), channel_id=1, source_target_pairs={{0,7},{1,6},{2,5},{3,4},{4,3},{5,2},{6,1},{7,0},{8,15},{9,14},{10,... | collective-permute-start | bytes 294920 | tf_op jit(solution)/shard_map/ppermute | solution.py:214
  63.1 1.7 collective-permute-start.9
  64.8 0.5 collective-permute-start.21
  65.3 1.7 %collective-permute-done.13.refs_7_ = bf16[32,1536]{1,0:T(8,128)(2,1)S(1)} collective-permute-done((bf16[32,1536]{1,0:T(8,128)(2,1)S(1)}, bf16[32,1536]{1,0:T(8,128)(2,1)S(1)}, u32[]{:S(2)}, u32[]{:S(2)}) %collective-permute-start.13) | collective-permute-done | bytes 98336 | tf_op jit(solution)/shard_map/ppermute | solution.py:214
  67.0 3.1 %collective-permute-start.22 = (bf16[32,1536]{1,0:T(8,128)(2,1)S(1)}, bf16[32,1536]{1,0:T(8,128)(2,1)S(1)}, u32[]{:S(2)}, u32[]{:S(2)}) collective-permute-start(bf16[32,1536]{1,0:T(8,128)(2,1)S(1)} %get-tuple-element.109), channel_id=1, source_target_pairs={{0,1},{1,0},{2,4},{3,7},{4,2},{5,6},{6,5},{7,3},{8,9},{9,8},{10,12... | collective-permute-start | bytes 294920 | tf_op jit(solution)/shard_map/ppermute | solution.py:214
  70.1 3.0 %collective-permute-start.24 = (bf16[32,1536]{1,0:T(8,128)(2,1)S(1)}, bf16[32,1536]{1,0:T(8,128)(2,1)S(1)}, u32[]{:S(2)}, u32[]{:S(2)}) collective-permute-start(bf16[32,1536]{1,0:T(8,128)(2,1)S(1)} %get-tuple-element.111), channel_id=1, source_target_pairs={{0,4},{1,2},{2,1},{3,5},{4,0},{5,3},{6,7},{7,6},{8,12},{9,10},{10,... | collective-permute-start | bytes 294920 | tf_op jit(solution)/shard_map/ppermute | solution.py:214
  73.1 1.2 collective-permute-start.25
  74.3 2.8 %collective-permute-start.26 = (bf16[32,1536]{1,0:T(8,128)(2,1)S(1)}, bf16[32,1536]{1,0:T(8,128)(2,1)S(1)}, u32[]{:S(2)}, u32[]{:S(2)}) collective-permute-start(bf16[32,1536]{1,0:T(8,128)(2,1)S(1)} %get-tuple-element.113), channel_id=1, source_target_pairs={{0,6},{1,4},{2,3},{3,2},{4,1},{5,7},{6,0},{7,5},{8,14},{9,12},{10,... | collective-permute-start | bytes 294920 | tf_op jit(solution)/shard_map/ppermute | solution.py:214
  77.2 4.2 %collective-permute-start.27 = (bf16[32,1536]{1,0:T(8,128)(2,1)S(1)}, bf16[32,1536]{1,0:T(8,128)(2,1)S(1)}, u32[]{:S(2)}, u32[]{:S(2)}) collective-permute-start(bf16[32,1536]{1,0:T(8,128)(2,1)S(1)} %get-tuple-element.114), channel_id=1, source_target_pairs={{0,5},{1,3},{2,7},{3,1},{4,6},{5,0},{6,4},{7,2},{8,13},{9,11},{10,... | collective-permute-start | bytes 294920 | tf_op jit(solution)/shard_map/ppermute | solution.py:214
  81.4 0.8 collective-permute-start.31
  82.1 2.9 %collective-permute-done.24.refs_4_ = bf16[32,1536]{1,0:T(8,128)(2,1)S(1)} collective-permute-done((bf16[32,1536]{1,0:T(8,128)(2,1)S(1)}, bf16[32,1536]{1,0:T(8,128)(2,1)S(1)}, u32[]{:S(2)}, u32[]{:S(2)}) %collective-permute-start.24) | collective-permute-done | bytes 98336 | tf_op jit(solution)/shard_map/ppermute | solution.py:214
  85.0 1.4 collective-permute-start.32
  86.5 2.8 %collective-permute-start.33 = (bf16[32,1536]{1,0:T(8,128)(2,1)S(1)}, bf16[32,1536]{1,0:T(8,128)(2,1)S(1)}, u32[]{:S(2)}, u32[]{:S(2)}) collective-permute-start(bf16[32,1536]{1,0:T(8,128)(2,1)S(1)} %get-tuple-element.120), channel_id=1, source_target_pairs={{0,2},{1,7},{2,0},{3,6},{4,5},{5,4},{6,3},{7,1},{8,10},{9,15},{10,... | collective-permute-start | bytes 294920 | tf_op jit(solution)/shard_map/ppermute | solution.py:214
  89.3 2.9 %collective-permute-start.34 = (bf16[32,1536]{1,0:T(8,128)(2,1)S(1)}, bf16[32,1536]{1,0:T(8,128)(2,1)S(1)}, u32[]{:S(2)}, u32[]{:S(2)}) collective-permute-start(bf16[32,1536]{1,0:T(8,128)(2,1)S(1)} %get-tuple-element.121), channel_id=1, source_target_pairs={{0,6},{1,4},{2,3},{3,2},{4,1},{5,7},{6,0},{7,5},{8,14},{9,12},{10,... | collective-permute-start | bytes 294920 | tf_op jit(solution)/shard_map/ppermute | solution.py:214
  92.2 2.3 %collective-permute-start.35 = (bf16[32,1536]{1,0:T(8,128)(2,1)S(1)}, bf16[32,1536]{1,0:T(8,128)(2,1)S(1)}, u32[]{:S(2)}, u32[]{:S(2)}) collective-permute-start(bf16[32,1536]{1,0:T(8,128)(2,1)S(1)} %get-tuple-element.122), channel_id=1, source_target_pairs={{0,5},{1,3},{2,7},{3,1},{4,6},{5,0},{6,4},{7,2},{8,13},{9,11},{10,... | collective-permute-start | bytes 294920 | tf_op jit(solution)/shard_map/ppermute | solution.py:214
  94.5 1.7 %back_0.1.back_ref = f32[256,1536]{1,0:T(8,128)S(1)} custom-call(bf16[1,384,1536]{2,1,0:T(8,128)(2,1)S(1)} %copy-done.2, f32[256,1536]{1,0:T(8,128)S(1)} %get-tuple-element.80.factor_ref, bf16[32,1536]{1,0:T(8,128)(2,1)S(1)} %get-tuple-element.89.refs_0_, bf16[32,1536]{1,0:T(8,128)(2,1)S(1)} %collective-permute-done.7.refs_1_, ...), custom_call_target="tpu_custom_call" | custom-call | flops 301989888 | bytes 4718592 | tf_op jit(solution)/shard_map/back_0/pallas_call | solution.py:267
  96.2 4.1 %result_0.1 = (bf16[1,2,256,1536]{3,2,1,0:T(8,128)(2,1)}, bf16[256,1536]{1,0:T(8,128)(2,1)S(1)}) custom-call(bf16[1,2,256,1536]{3,2,1,0:T(8,128)(2,1)S(1)} %copy-done, f32[1,1536]{1,0:T(1,128)S(1)} %copy-done.8, bf16[1,384,1536]{2,1,0:T(8,128)(2,1)S(1)} %copy-done.1, bf16[1,256,256]{2,1,0:T(8,128)(2,1)S(1)} %copy-done.7, f32[256,1536]{1,0:T(8,128)S(1)} %back_0.1.back_ref, ...), custom_call_target="tpu_custom_call" | custom-call | flops 905969664 | bytes 6291456 | tf_op jit(solution)/shard_map/result_0/pallas_call | solution.py:267
  100.4 2.2 %collective-permute-start.28 = (bf16[256,1536]{1,0:T(8,128)(2,1)S(1)}, bf16[256,1536]{1,0:T(8,128)(2,1)S(1)}, u32[]{:S(2)}, u32[]{:S(2)}) collective-permute-start(bf16[256,1536]{1,0:T(8,128)(2,1)S(1)} %get-tuple-element.115), channel_id=1, source_target_pairs={{8,0},{16,8},{24,16},{9,1},{17,9},{25,17},{10,2},{18,10},{26,18},{... | collective-permute-start | bytes 2359304 | tf_op jit(solution)/shard_map/ppermute | solution.py:371
  102.6 1.3 mix_1.1
  104.0 3.1 %collective-permute-start.36 = (bf16[32,1536]{1,0:T(8,128)(2,1)S(1)}, bf16[32,1536]{1,0:T(8,128)(2,1)S(1)}, u32[]{:S(2)}, u32[]{:S(2)}) collective-permute-start(bf16[32,1536]{1,0:T(8,128)(2,1)S(1)} %get-tuple-element.128), channel_id=1, source_target_pairs={{0,7},{1,6},{2,5},{3,4},{4,3},{5,2},{6,1},{7,0},{8,15},{9,14},{10,... | collective-permute-start | bytes 294920 | tf_op jit(solution)/shard_map/ppermute | solution.py:214
  107.0 4.9 %collective-permute-done.28.refs_0_.refs_8_ = bf16[256,1536]{1,0:T(8,128)(2,1)S(1)} collective-permute-done((bf16[256,1536]{1,0:T(8,128)(2,1)S(1)}, bf16[256,1536]{1,0:T(8,128)(2,1)S(1)}, u32[]{:S(2)}, u32[]{:S(2)}) %collective-permute-start.28) | collective-permute-done | bytes 786464 | tf_op jit(solution)/shard_map/ppermute | solution.py:371
  111.9 3.3 %grads_1.1 = (bf16[32,1536]{1,0:T(8,128)(2,1)S(1)}, bf16[32,1536]{1,0:T(8,128)(2,1)S(1)}, bf16[32,1536]{1,0:T(8,128)(2,1)S(1)}, bf16[32,1536]{1,0:T(8,128)(2,1)S...) custom-call(bf16[1,2,256,1536]{3,2,1,0:T(8,128)(2,1)S(1)} %copy-done, ...), custom_call_target="tpu_custom_call" | custom-call | flops 603979776 | bytes 6291456 | tf_op jit(solution)/shard_map/grads_1/pallas_call | solution.py:267
  115.4 3.5 %collective-permute-start.49 = (bf16[32,1536]{1,0:T(8,128)(2,1)S(1)}, bf16[32,1536]{1,0:T(8,128)(2,1)S(1)}, u32[]{:S(2)}, u32[]{:S(2)}) collective-permute-start(bf16[32,1536]{1,0:T(8,128)(2,1)S(1)} %get-tuple-element.145), channel_id=1, source_target_pairs={{0,5},{1,3},{2,7},{3,1},{4,6},{5,0},{6,4},{7,2},{8,13},{9,11},{10,... | collective-permute-start | bytes 294920 | tf_op jit(solution)/shard_map/ppermute | solution.py:214
  118.9 0.4 collective-permute-start.43
  119.3 1.3 collective-permute-start.44
  120.6 3.5 %collective-permute-start.45 = (bf16[32,1536]{1,0:T(8,128)(2,1)S(1)}, bf16[32,1536]{1,0:T(8,128)(2,1)S(1)}, u32[]{:S(2)}, u32[]{:S(2)}) collective-permute-start(bf16[32,1536]{1,0:T(8,128)(2,1)S(1)} %get-tuple-element.141), channel_id=1, source_target_pairs={{0,3},{1,5},{2,6},{3,0},{4,7},{5,1},{6,2},{7,4},{8,11},{9,13},{10,... | collective-permute-start | bytes 294920 | tf_op jit(solution)/shard_map/ppermute | solution.py:214
  124.2 3.3 %collective-permute-done.49.refs_7_ = bf16[32,1536]{1,0:T(8,128)(2,1)S(1)} collective-permute-done((bf16[32,1536]{1,0:T(8,128)(2,1)S(1)}, bf16[32,1536]{1,0:T(8,128)(2,1)S(1)}, u32[]{:S(2)}, u32[]{:S(2)}) %collective-permute-start.49) | collective-permute-done | bytes 98336 | tf_op jit(solution)/shard_map/ppermute | solution.py:214
  127.5 5.2 %collective-permute-start.38 = (bf16[32,1536]{1,0:T(8,128)(2,1)S(1)}, bf16[32,1536]{1,0:T(8,128)(2,1)S(1)}, u32[]{:S(2)}, u32[]{:S(2)}) collective-permute-start(bf16[32,1536]{1,0:T(8,128)(2,1)S(1)} %get-tuple-element.133), channel_id=1, source_target_pairs={{0,3},{1,5},{2,6},{3,0},{4,7},{5,1},{6,2},{7,4},{8,11},{9,13},{10,... | collective-permute-start | bytes 294920 | tf_op jit(solution)/shard_map/ppermute | solution.py:214
  132.6 1.2 collective-permute-start.39
  133.9 1.1 collective-permute-start.40
  135.0 3.6 %collective-permute-done.46.refs_4_ = bf16[32,1536]{1,0:T(8,128)(2,1)S(1)} collective-permute-done((bf16[32,1536]{1,0:T(8,128)(2,1)S(1)}, bf16[32,1536]{1,0:T(8,128)(2,1)S(1)}, u32[]{:S(2)}, u32[]{:S(2)}) %collective-permute-start.46) | collective-permute-done | bytes 98336 | tf_op jit(solution)/shard_map/ppermute | solution.py:214
  138.6 1.6 collective-permute-start.42
  140.2 1.4 fold_1.1
  141.6 3.4 %collective-permute-start.50 = (bf16[32,1536]{1,0:T(8,128)(2,1)S(1)}, bf16[32,1536]{1,0:T(8,128)(2,1)S(1)}, u32[]{:S(2)}, u32[]{:S(2)}) collective-permute-start(bf16[32,1536]{1,0:T(8,128)(2,1)S(1)} %get-tuple-element.147), channel_id=1, source_target_pairs={{0,7},{1,6},{2,5},{3,4},{4,3},{5,2},{6,1},{7,0},{8,15},{9,14},{10,... | collective-permute-start | bytes 294920 | tf_op jit(solution)/shard_map/ppermute | solution.py:214
  145.0 4.9 %collective-permute-start.51 = (bf16[32,1536]{1,0:T(8,128)(2,1)S(1)}, bf16[32,1536]{1,0:T(8,128)(2,1)S(1)}, u32[]{:S(2)}, u32[]{:S(2)}) collective-permute-start(bf16[32,1536]{1,0:T(8,128)(2,1)S(1)} %get-tuple-element.148), channel_id=1, source_target_pairs={{0,1},{1,0},{2,4},{3,7},{4,2},{5,6},{6,5},{7,3},{8,9},{9,8},{10,12... | collective-permute-start | bytes 294920 | tf_op jit(solution)/shard_map/ppermute | solution.py:214
  149.9 0.6 collective-permute-start.52
  150.5 2.9 %collective-permute-start.53 = (bf16[32,1536]{1,0:T(8,128)(2,1)S(1)}, bf16[32,1536]{1,0:T(8,128)(2,1)S(1)}, u32[]{:S(2)}, u32[]{:S(2)}) collective-permute-start(bf16[32,1536]{1,0:T(8,128)(2,1)S(1)} %get-tuple-element.150), channel_id=1, source_target_pairs={{0,4},{1,2},{2,1},{3,5},{4,0},{5,3},{6,7},{7,6},{8,12},{9,10},{10,... | collective-permute-start | bytes 294920 | tf_op jit(solution)/shard_map/ppermute | solution.py:214
  153.4 3.6 %collective-permute-start.55 = (bf16[32,1536]{1,0:T(8,128)(2,1)S(1)}, bf16[32,1536]{1,0:T(8,128)(2,1)S(1)}, u32[]{:S(2)}, u32[]{:S(2)}) collective-permute-start(bf16[32,1536]{1,0:T(8,128)(2,1)S(1)} %get-tuple-element.152), channel_id=1, source_target_pairs={{0,6},{1,4},{2,3},{3,2},{4,1},{5,7},{6,0},{7,5},{8,14},{9,12},{10,... | collective-permute-start | bytes 294920 | tf_op jit(solution)/shard_map/ppermute | solution.py:214
  157.1 1.7 %back_1.1.back_ref = f32[256,1536]{1,0:T(8,128)S(1)} custom-call(bf16[1,384,1536]{2,1,0:T(8,128)(2,1)S(1)} %copy-done.2, f32[256,1536]{1,0:T(8,128)S(1)} %get-tuple-element.125.factor_ref, bf16[32,1536]{1,0:T(8,128)(2,1)S(1)} %get-tuple-element.126.refs_0_, bf16[32,1536]{1,0:T(8,128)(2,1)S(1)} %collective-permute-done.36.refs_1_, ...), custom_call_target="tpu_custom_call" | custom-call | flops 301989888 | bytes 4718592 | tf_op jit(solution)/shard_map/back_1/pallas_call | solution.py:267
  158.8 1.7 %collective-permute-done.53.refs_4_ = bf16[32,1536]{1,0:T(8,128)(2,1)S(1)} collective-permute-done((bf16[32,1536]{1,0:T(8,128)(2,1)S(1)}, bf16[32,1536]{1,0:T(8,128)(2,1)S(1)}, u32[]{:S(2)}, u32[]{:S(2)}) %collective-permute-start.53) | collective-permute-done | bytes 98336 | tf_op jit(solution)/shard_map/ppermute | solution.py:214
  160.6 2.8 %collective-permute-done.56.refs_7_ = bf16[32,1536]{1,0:T(8,128)(2,1)S(1)} collective-permute-done((bf16[32,1536]{1,0:T(8,128)(2,1)S(1)}, bf16[32,1536]{1,0:T(8,128)(2,1)S(1)}, u32[]{:S(2)}, u32[]{:S(2)}) %collective-permute-start.56) | collective-permute-done | bytes 98336 | tf_op jit(solution)/shard_map/ppermute | solution.py:214
  163.4 4.1 %result_1.1 = bf16[1,2,256,1536]{3,2,1,0:T(8,128)(2,1)} custom-call(bf16[1,2,256,1536]{3,2,1,0:T(8,128)(2,1)S(1)} %copy-done, f32[1,1536]{1,0:T(1,128)S(1)} %copy-done.8, bf16[1,384,1536]{2,1,0:T(8,128)(2,1)S(1)} %copy-done.1, bf16[1,256,256]{2,1,0:T(8,128)(2,1)S(1)} %copy-done.7, f32[256,1536]{1,0:T(8,128)S(1)} %back_1.1.back_ref, ...), custom_call_target="tpu_custom_call", output_to_operand_aliasing={{}: (15, {})} | custom-call | flops 905969664 | bytes 6291456 | tf_op jit(solution)/shard_map/result_1/pallas_call | solution.py:267
  (89 shorter events, 0.8 us)
Async XLA Ops:
  0.0 13.6 %copy-start.8 = (f32[1,1536]{1,0:T(1,128)S(1)}, f32[1,1536]{1,0:T(1,128)}, u32[]{:S(2)}) copy-start(f32[1,1536]{1,0:T(1,128)} %gain_ref.11) | copy-start | bytes 18436
  0.0 13.6 %copy-start = (bf16[1,2,256,1536]{3,2,1,0:T(8,128)(2,1)S(1)}, bf16[1,2,256,1536]{3,2,1,0:T(8,128)(2,1)}, u32[]{:S(2)}) copy-start(bf16[1,2,256,1536]{3,2,1,0:T(8,128)(2,1)} %x_ref.11) | copy-start | bytes 4718596
  0.0 13.6 %copy-start.2 = (bf16[1,384,1536]{2,1,0:T(8,128)(2,1)S(1)}, bf16[1,384,1536]{2,1,0:T(8,128)(2,1)}, u32[]{:S(2)}) copy-start(bf16[1,384,1536]{2,1,0:T(8,128)(2,1)} %w_gate_ref.7) | copy-start | bytes 3538948
  5.2 14.0 %collective-permute-start = (bf16[32,1536]{1,0:T(8,128)(2,1)}, bf16[32,1536]{1,0:T(8,128)(2,1)S(1)}, u32[]{:S(2)}, u32[]{:S(2)}) collective-permute-start(bf16[32,1536]{1,0:T(8,128)(2,1)} %get-tuple-element.82), channel_id=1, source_target_pairs={{0,7},{1,6},{2,5},{3,4},{4,3},{5,2},{6,1},{7,0},{8,15},{9,14},{10,... | collective-permute-start | bytes 294920 | tf_op jit(solution)/shard_map/ppermute | solution.py:214
  9.9 13.1 %collective-permute-start.1 = (bf16[32,1536]{1,0:T(8,128)(2,1)}, bf16[32,1536]{1,0:T(8,128)(2,1)S(1)}, u32[]{:S(2)}, u32[]{:S(2)}) collective-permute-start(bf16[32,1536]{1,0:T(8,128)(2,1)} %get-tuple-element.83), channel_id=1, source_target_pairs={{0,1},{1,0},{2,4},{3,7},{4,2},{5,6},{6,5},{7,3},{8,9},{9,8},{10,12... | collective-permute-start | bytes 294920 | tf_op jit(solution)/shard_map/ppermute | solution.py:214
  10.4 12.6 %collective-permute-start.2 = (bf16[32,1536]{1,0:T(8,128)(2,1)}, bf16[32,1536]{1,0:T(8,128)(2,1)S(1)}, u32[]{:S(2)}, u32[]{:S(2)}) collective-permute-start(bf16[32,1536]{1,0:T(8,128)(2,1)} %get-tuple-element.84), channel_id=1, source_target_pairs={{0,3},{1,5},{2,6},{3,0},{4,7},{5,1},{6,2},{7,4},{8,11},{9,13},{10,... | collective-permute-start | bytes 294920 | tf_op jit(solution)/shard_map/ppermute | solution.py:214
  10.6 14.6 %collective-permute-start.3 = (bf16[32,1536]{1,0:T(8,128)(2,1)}, bf16[32,1536]{1,0:T(8,128)(2,1)S(1)}, u32[]{:S(2)}, u32[]{:S(2)}) collective-permute-start(bf16[32,1536]{1,0:T(8,128)(2,1)} %get-tuple-element.85), channel_id=1, source_target_pairs={{0,4},{1,2},{2,1},{3,5},{4,0},{5,3},{6,7},{7,6},{8,12},{9,10},{10,... | collective-permute-start | bytes 294920 | tf_op jit(solution)/shard_map/ppermute | solution.py:214
  12.3 19.4 %copy-start.1 = (bf16[1,384,1536]{2,1,0:T(8,128)(2,1)S(1)}, bf16[1,384,1536]{2,1,0:T(8,128)(2,1)}, u32[]{:S(2)}) copy-start(bf16[1,384,1536]{2,1,0:T(8,128)(2,1)} %w_value_ref.3) | copy-start | bytes 3538948
  12.3 13.1 %collective-permute-start.4 = (bf16[32,1536]{1,0:T(8,128)(2,1)}, bf16[32,1536]{1,0:T(8,128)(2,1)S(1)}, u32[]{:S(2)}, u32[]{:S(2)}) collective-permute-start(bf16[32,1536]{1,0:T(8,128)(2,1)} %get-tuple-element.86), channel_id=1, source_target_pairs={{0,2},{1,7},{2,0},{3,6},{4,5},{5,4},{6,3},{7,1},{8,10},{9,15},{10,... | collective-permute-start | bytes 294920 | tf_op jit(solution)/shard_map/ppermute | solution.py:214
  16.0 15.7 %copy-start.7 = (bf16[1,256,256]{2,1,0:T(8,128)(2,1)S(1)}, bf16[1,256,256]{2,1,0:T(8,128)(2,1)}, u32[]{:S(2)}) copy-start(bf16[1,256,256]{2,1,0:T(8,128)(2,1)} %r_ref.7) | copy-start | bytes 393220
  19.3 24.2 %copy-start.10 = (bf16[1,32,64]{2,1,0:T(8,128)(2,1)S(1)}, bf16[1,32,64]{2,1,0:T(8,128)(2,1)}, u32[]{:S(2)}) copy-start(bf16[1,32,64]{2,1,0:T(8,128)(2,1)} %l_ref.1) | copy-start | bytes 12292
  19.3 15.4 %collective-permute-start.5 = (bf16[32,1536]{1,0:T(8,128)(2,1)S(1)}, bf16[32,1536]{1,0:T(8,128)(2,1)S(1)}, u32[]{:S(2)}, u32[]{:S(2)}) collective-permute-start(bf16[32,1536]{1,0:T(8,128)(2,1)S(1)} %copy-done.12), channel_id=1, source_target_pairs={{0,6},{1,4},{2,3},{3,2},{4,1},{5,7},{6,0},{7,5},{8,14},{9,12},{10,... | collective-permute-start | bytes 294920 | tf_op jit(solution)/shard_map/ppermute | solution.py:214
  23.0 11.8 %collective-permute-start.6 = (bf16[32,1536]{1,0:T(8,128)(2,1)S(1)}, bf16[32,1536]{1,0:T(8,128)(2,1)S(1)}, u32[]{:S(2)}, u32[]{:S(2)}) collective-permute-start(bf16[32,1536]{1,0:T(8,128)(2,1)S(1)} %copy-done.11), channel_id=1, source_target_pairs={{0,5},{1,3},{2,7},{3,1},{4,6},{5,0},{6,4},{7,2},{8,13},{9,11},{10,... | collective-permute-start | bytes 294920 | tf_op jit(solution)/shard_map/ppermute | solution.py:214
  23.0 15.3 %collective-permute-start.14 = (bf16[32,1536]{1,0:T(8,128)(2,1)S(1)}, bf16[32,1536]{1,0:T(8,128)(2,1)S(1)}, u32[]{:S(2)}, u32[]{:S(2)}) collective-permute-start(bf16[32,1536]{1,0:T(8,128)(2,1)S(1)} %get-tuple-element.100), channel_id=1, source_target_pairs={{0,7},{1,6},{2,5},{3,4},{4,3},{5,2},{6,1},{7,0},{8,15},{9,14},{10,... | collective-permute-start | bytes 294920 | tf_op jit(solution)/shard_map/ppermute | solution.py:214
  25.2 13.1 %collective-permute-start.15 = (bf16[32,1536]{1,0:T(8,128)(2,1)S(1)}, bf16[32,1536]{1,0:T(8,128)(2,1)S(1)}, u32[]{:S(2)}, u32[]{:S(2)}) collective-permute-start(bf16[32,1536]{1,0:T(8,128)(2,1)S(1)} %get-tuple-element.101), channel_id=1, source_target_pairs={{0,1},{1,0},{2,4},{3,7},{4,2},{5,6},{6,5},{7,3},{8,9},{9,8},{10,12... | collective-permute-start | bytes 294920 | tf_op jit(solution)/shard_map/ppermute | solution.py:214
  25.4 18.3 %copy-start.9 = (bf16[32,1536]{1,0:T(8,128)(2,1)S(1)}, bf16[32,1536]{1,0:T(8,128)(2,1)}, u32[]{:S(2)}) copy-start(bf16[32,1536]{1,0:T(8,128)(2,1)} %get-tuple-element.81.refs_0_) | copy-start | bytes 294916
  25.4 18.1 %collective-permute-start.16 = (bf16[32,1536]{1,0:T(8,128)(2,1)S(1)}, bf16[32,1536]{1,0:T(8,128)(2,1)S(1)}, u32[]{:S(2)}, u32[]{:S(2)}) collective-permute-start(bf16[32,1536]{1,0:T(8,128)(2,1)S(1)} %get-tuple-element.102), channel_id=1, source_target_pairs={{0,3},{1,5},{2,6},{3,0},{4,7},{5,1},{6,2},{7,4},{8,11},{9,13},{10,... | collective-permute-start | bytes 294920 | tf_op jit(solution)/shard_map/ppermute | solution.py:214
  34.7 10.3 %collective-permute-start.17 = (bf16[32,1536]{1,0:T(8,128)(2,1)S(1)}, bf16[32,1536]{1,0:T(8,128)(2,1)S(1)}, u32[]{:S(2)}, u32[]{:S(2)}) collective-permute-start(bf16[32,1536]{1,0:T(8,128)(2,1)S(1)} %get-tuple-element.103), channel_id=1, source_target_pairs={{0,4},{1,2},{2,1},{3,5},{4,0},{5,3},{6,7},{7,6},{8,12},{9,10},{10,... | collective-permute-start | bytes 294920 | tf_op jit(solution)/shard_map/ppermute | solution.py:214
  34.8 15.2 %collective-permute-start.18 = (bf16[32,1536]{1,0:T(8,128)(2,1)S(1)}, bf16[32,1536]{1,0:T(8,128)(2,1)S(1)}, u32[]{:S(2)}, u32[]{:S(2)}) collective-permute-start(bf16[32,1536]{1,0:T(8,128)(2,1)S(1)} %get-tuple-element.104), channel_id=1, source_target_pairs={{0,2},{1,7},{2,0},{3,6},{4,5},{5,4},{6,3},{7,1},{8,10},{9,15},{10,... | collective-permute-start | bytes 294920 | tf_op jit(solution)/shard_map/ppermute | solution.py:214
  38.3 11.8 %collective-permute-start.19 = (bf16[32,1536]{1,0:T(8,128)(2,1)S(1)}, bf16[32,1536]{1,0:T(8,128)(2,1)S(1)}, u32[]{:S(2)}, u32[]{:S(2)}) collective-permute-start(bf16[32,1536]{1,0:T(8,128)(2,1)S(1)} %get-tuple-element.105), channel_id=1, source_target_pairs={{0,6},{1,4},{2,3},{3,2},{4,1},{5,7},{6,0},{7,5},{8,14},{9,12},{10,... | collective-permute-start | bytes 294920 | tf_op jit(solution)/shard_map/ppermute | solution.py:214
  38.3 13.3 %collective-permute-start.20 = (bf16[32,1536]{1,0:T(8,128)(2,1)S(1)}, bf16[32,1536]{1,0:T(8,128)(2,1)S(1)}, u32[]{:S(2)}, u32[]{:S(2)}) collective-permute-start(bf16[32,1536]{1,0:T(8,128)(2,1)S(1)} %get-tuple-element.106), channel_id=1, source_target_pairs={{0,5},{1,3},{2,7},{3,1},{4,6},{5,0},{6,4},{7,2},{8,13},{9,11},{10,... | collective-permute-start | bytes 294920 | tf_op jit(solution)/shard_map/ppermute | solution.py:214
  43.5 9.5 %collective-permute-start.29 = (bf16[32,1536]{1,0:T(8,128)(2,1)S(1)}, bf16[32,1536]{1,0:T(8,128)(2,1)S(1)}, u32[]{:S(2)}, u32[]{:S(2)}) collective-permute-start(bf16[32,1536]{1,0:T(8,128)(2,1)S(1)} %get-tuple-element.116), channel_id=1, source_target_pairs={{0,7},{1,6},{2,5},{3,4},{4,3},{5,2},{6,1},{7,0},{8,15},{9,14},{10,... | collective-permute-start | bytes 294920 | tf_op jit(solution)/shard_map/ppermute | solution.py:214
  45.0 14.5 %collective-permute-start.30 = (bf16[32,1536]{1,0:T(8,128)(2,1)S(1)}, bf16[32,1536]{1,0:T(8,128)(2,1)S(1)}, u32[]{:S(2)}, u32[]{:S(2)}) collective-permute-start(bf16[32,1536]{1,0:T(8,128)(2,1)S(1)} %get-tuple-element.117), channel_id=1, source_target_pairs={{0,1},{1,0},{2,4},{3,7},{4,2},{5,6},{6,5},{7,3},{8,9},{9,8},{10,12... | collective-permute-start | bytes 294920 | tf_op jit(solution)/shard_map/ppermute | solution.py:214
  50.0 13.1 %collective-permute-start.10 = (bf16[32,1536]{1,0:T(8,128)(2,1)S(1)}, bf16[32,1536]{1,0:T(8,128)(2,1)S(1)}, u32[]{:S(2)}, u32[]{:S(2)}) collective-permute-start(bf16[32,1536]{1,0:T(8,128)(2,1)S(1)} %get-tuple-element.93), channel_id=1, source_target_pairs={{0,4},{1,2},{2,1},{3,5},{4,0},{5,3},{6,7},{7,6},{8,12},{9,10},{10,... | collective-permute-start | bytes 294920 | tf_op jit(solution)/shard_map/ppermute | solution.py:214
  50.0 13.1 %collective-permute-start.11 = (bf16[32,1536]{1,0:T(8,128)(2,1)S(1)}, bf16[32,1536]{1,0:T(8,128)(2,1)S(1)}, u32[]{:S(2)}, u32[]{:S(2)}) collective-permute-start(bf16[32,1536]{1,0:T(8,128)(2,1)S(1)} %get-tuple-element.94), channel_id=1, source_target_pairs={{0,2},{1,7},{2,0},{3,6},{4,5},{5,4},{6,3},{7,1},{8,10},{9,15},{10,... | collective-permute-start | bytes 294920 | tf_op jit(solution)/shard_map/ppermute | solution.py:214
  51.6 13.2 %collective-permute-start.12 = (bf16[32,1536]{1,0:T(8,128)(2,1)S(1)}, bf16[32,1536]{1,0:T(8,128)(2,1)S(1)}, u32[]{:S(2)}, u32[]{:S(2)}) collective-permute-start(bf16[32,1536]{1,0:T(8,128)(2,1)S(1)} %get-tuple-element.95), channel_id=1, source_target_pairs={{0,6},{1,4},{2,3},{3,2},{4,1},{5,7},{6,0},{7,5},{8,14},{9,12},{10,... | collective-permute-start | bytes 294920 | tf_op jit(solution)/shard_map/ppermute | solution.py:214
  53.0 14.1 %collective-permute-start.13 = (bf16[32,1536]{1,0:T(8,128)(2,1)S(1)}, bf16[32,1536]{1,0:T(8,128)(2,1)S(1)}, u32[]{:S(2)}, u32[]{:S(2)}) collective-permute-start(bf16[32,1536]{1,0:T(8,128)(2,1)S(1)} %get-tuple-element.96), channel_id=1, source_target_pairs={{0,5},{1,3},{2,7},{3,1},{4,6},{5,0},{6,4},{7,2},{8,13},{9,11},{10,... | collective-permute-start | bytes 294920 | tf_op jit(solution)/shard_map/ppermute | solution.py:214
  59.4 10.6 %collective-permute-start.7 = (bf16[32,1536]{1,0:T(8,128)(2,1)S(1)}, bf16[32,1536]{1,0:T(8,128)(2,1)S(1)}, u32[]{:S(2)}, u32[]{:S(2)}) collective-permute-start(bf16[32,1536]{1,0:T(8,128)(2,1)S(1)} %get-tuple-element.90), channel_id=1, source_target_pairs={{0,7},{1,6},{2,5},{3,4},{4,3},{5,2},{6,1},{7,0},{8,15},{9,14},{10,... | collective-permute-start | bytes 294920 | tf_op jit(solution)/shard_map/ppermute | solution.py:214
  63.1 7.0 %collective-permute-start.8 = (bf16[32,1536]{1,0:T(8,128)(2,1)S(1)}, bf16[32,1536]{1,0:T(8,128)(2,1)S(1)}, u32[]{:S(2)}, u32[]{:S(2)}) collective-permute-start(bf16[32,1536]{1,0:T(8,128)(2,1)S(1)} %get-tuple-element.91), channel_id=1, source_target_pairs={{0,1},{1,0},{2,4},{3,7},{4,2},{5,6},{6,5},{7,3},{8,9},{9,8},{10,12... | collective-permute-start | bytes 294920 | tf_op jit(solution)/shard_map/ppermute | solution.py:214
  63.1 10.0 %collective-permute-start.9 = (bf16[32,1536]{1,0:T(8,128)(2,1)S(1)}, bf16[32,1536]{1,0:T(8,128)(2,1)S(1)}, u32[]{:S(2)}, u32[]{:S(2)}) collective-permute-start(bf16[32,1536]{1,0:T(8,128)(2,1)S(1)} %get-tuple-element.92), channel_id=1, source_target_pairs={{0,3},{1,5},{2,6},{3,0},{4,7},{5,1},{6,2},{7,4},{8,11},{9,13},{10,... | collective-permute-start | bytes 294920 | tf_op jit(solution)/shard_map/ppermute | solution.py:214
  64.8 9.5 %collective-permute-start.21 = (bf16[32,1536]{1,0:T(8,128)(2,1)S(1)}, bf16[32,1536]{1,0:T(8,128)(2,1)S(1)}, u32[]{:S(2)}, u32[]{:S(2)}) collective-permute-start(bf16[32,1536]{1,0:T(8,128)(2,1)S(1)} %get-tuple-element.108), channel_id=1, source_target_pairs={{0,7},{1,6},{2,5},{3,4},{4,3},{5,2},{6,1},{7,0},{8,15},{9,14},{10,... | collective-permute-start | bytes 294920 | tf_op jit(solution)/shard_map/ppermute | solution.py:214
  67.0 10.1 %collective-permute-start.22 = (bf16[32,1536]{1,0:T(8,128)(2,1)S(1)}, bf16[32,1536]{1,0:T(8,128)(2,1)S(1)}, u32[]{:S(2)}, u32[]{:S(2)}) collective-permute-start(bf16[32,1536]{1,0:T(8,128)(2,1)S(1)} %get-tuple-element.109), channel_id=1, source_target_pairs={{0,1},{1,0},{2,4},{3,7},{4,2},{5,6},{6,5},{7,3},{8,9},{9,8},{10,12... | collective-permute-start | bytes 294920 | tf_op jit(solution)/shard_map/ppermute | solution.py:214
  70.1 11.3 %collective-permute-start.23 = (bf16[32,1536]{1,0:T(8,128)(2,1)S(1)}, bf16[32,1536]{1,0:T(8,128)(2,1)S(1)}, u32[]{:S(2)}, u32[]{:S(2)}) collective-permute-start(bf16[32,1536]{1,0:T(8,128)(2,1)S(1)} %get-tuple-element.110), channel_id=1, source_target_pairs={{0,3},{1,5},{2,6},{3,0},{4,7},{5,1},{6,2},{7,4},{8,11},{9,13},{10,... | collective-permute-start | bytes 294920 | tf_op jit(solution)/shard_map/ppermute | solution.py:214
  70.1 14.9 %collective-permute-start.24 = (bf16[32,1536]{1,0:T(8,128)(2,1)S(1)}, bf16[32,1536]{1,0:T(8,128)(2,1)S(1)}, u32[]{:S(2)}, u32[]{:S(2)}) collective-permute-start(bf16[32,1536]{1,0:T(8,128)(2,1)S(1)} %get-tuple-element.111), channel_id=1, source_target_pairs={{0,4},{1,2},{2,1},{3,5},{4,0},{5,3},{6,7},{7,6},{8,12},{9,10},{10,... | collective-permute-start | bytes 294920 | tf_op jit(solution)/shard_map/ppermute | solution.py:214
  73.1 13.4 %collective-permute-start.25 = (bf16[32,1536]{1,0:T(8,128)(2,1)S(1)}, bf16[32,1536]{1,0:T(8,128)(2,1)S(1)}, u32[]{:S(2)}, u32[]{:S(2)}) collective-permute-start(bf16[32,1536]{1,0:T(8,128)(2,1)S(1)} %get-tuple-element.112), channel_id=1, source_target_pairs={{0,2},{1,7},{2,0},{3,6},{4,5},{5,4},{6,3},{7,1},{8,10},{9,15},{10,... | collective-permute-start | bytes 294920 | tf_op jit(solution)/shard_map/ppermute | solution.py:214
  74.3 14.9 %collective-permute-start.26 = (bf16[32,1536]{1,0:T(8,128)(2,1)S(1)}, bf16[32,1536]{1,0:T(8,128)(2,1)S(1)}, u32[]{:S(2)}, u32[]{:S(2)}) collective-permute-start(bf16[32,1536]{1,0:T(8,128)(2,1)S(1)} %get-tuple-element.113), channel_id=1, source_target_pairs={{0,6},{1,4},{2,3},{3,2},{4,1},{5,7},{6,0},{7,5},{8,14},{9,12},{10,... | collective-permute-start | bytes 294920 | tf_op jit(solution)/shard_map/ppermute | solution.py:214
  77.2 15.0 %collective-permute-start.27 = (bf16[32,1536]{1,0:T(8,128)(2,1)S(1)}, bf16[32,1536]{1,0:T(8,128)(2,1)S(1)}, u32[]{:S(2)}, u32[]{:S(2)}) collective-permute-start(bf16[32,1536]{1,0:T(8,128)(2,1)S(1)} %get-tuple-element.114), channel_id=1, source_target_pairs={{0,5},{1,3},{2,7},{3,1},{4,6},{5,0},{6,4},{7,2},{8,13},{9,11},{10,... | collective-permute-start | bytes 294920 | tf_op jit(solution)/shard_map/ppermute | solution.py:214
  81.4 19.0 %collective-permute-start.31 = (bf16[32,1536]{1,0:T(8,128)(2,1)S(1)}, bf16[32,1536]{1,0:T(8,128)(2,1)S(1)}, u32[]{:S(2)}, u32[]{:S(2)}) collective-permute-start(bf16[32,1536]{1,0:T(8,128)(2,1)S(1)} %get-tuple-element.118), channel_id=1, source_target_pairs={{0,3},{1,5},{2,6},{3,0},{4,7},{5,1},{6,2},{7,4},{8,11},{9,13},{10,... | collective-permute-start | bytes 294920 | tf_op jit(solution)/shard_map/ppermute | solution.py:214
  85.0 17.6 %collective-permute-start.32 = (bf16[32,1536]{1,0:T(8,128)(2,1)S(1)}, bf16[32,1536]{1,0:T(8,128)(2,1)S(1)}, u32[]{:S(2)}, u32[]{:S(2)}) collective-permute-start(bf16[32,1536]{1,0:T(8,128)(2,1)S(1)} %get-tuple-element.119), channel_id=1, source_target_pairs={{0,4},{1,2},{2,1},{3,5},{4,0},{5,3},{6,7},{7,6},{8,12},{9,10},{10,... | collective-permute-start | bytes 294920 | tf_op jit(solution)/shard_map/ppermute | solution.py:214
  86.5 16.2 %collective-permute-start.33 = (bf16[32,1536]{1,0:T(8,128)(2,1)S(1)}, bf16[32,1536]{1,0:T(8,128)(2,1)S(1)}, u32[]{:S(2)}, u32[]{:S(2)}) collective-permute-start(bf16[32,1536]{1,0:T(8,128)(2,1)S(1)} %get-tuple-element.120), channel_id=1, source_target_pairs={{0,2},{1,7},{2,0},{3,6},{4,5},{5,4},{6,3},{7,1},{8,10},{9,15},{10,... | collective-permute-start | bytes 294920 | tf_op jit(solution)/shard_map/ppermute | solution.py:214
  89.3 13.4 %collective-permute-start.34 = (bf16[32,1536]{1,0:T(8,128)(2,1)S(1)}, bf16[32,1536]{1,0:T(8,128)(2,1)S(1)}, u32[]{:S(2)}, u32[]{:S(2)}) collective-permute-start(bf16[32,1536]{1,0:T(8,128)(2,1)S(1)} %get-tuple-element.121), channel_id=1, source_target_pairs={{0,6},{1,4},{2,3},{3,2},{4,1},{5,7},{6,0},{7,5},{8,14},{9,12},{10,... | collective-permute-start | bytes 294920 | tf_op jit(solution)/shard_map/ppermute | solution.py:214
  92.2 10.4 %collective-permute-start.35 = (bf16[32,1536]{1,0:T(8,128)(2,1)S(1)}, bf16[32,1536]{1,0:T(8,128)(2,1)S(1)}, u32[]{:S(2)}, u32[]{:S(2)}) collective-permute-start(bf16[32,1536]{1,0:T(8,128)(2,1)S(1)} %get-tuple-element.122), channel_id=1, source_target_pairs={{0,5},{1,3},{2,7},{3,1},{4,6},{5,0},{6,4},{7,2},{8,13},{9,11},{10,... | collective-permute-start | bytes 294920 | tf_op jit(solution)/shard_map/ppermute | solution.py:214
  100.4 11.5 %collective-permute-start.28 = (bf16[256,1536]{1,0:T(8,128)(2,1)S(1)}, bf16[256,1536]{1,0:T(8,128)(2,1)S(1)}, u32[]{:S(2)}, u32[]{:S(2)}) collective-permute-start(bf16[256,1536]{1,0:T(8,128)(2,1)S(1)} %get-tuple-element.115), channel_id=1, source_target_pairs={{8,0},{16,8},{24,16},{9,1},{17,9},{25,17},{10,2},{18,10},{26,18},{... | collective-permute-start | bytes 2359304 | tf_op jit(solution)/shard_map/ppermute | solution.py:371
  103.9 11.4 %collective-permute-start.37 = (bf16[32,1536]{1,0:T(8,128)(2,1)S(1)}, bf16[32,1536]{1,0:T(8,128)(2,1)S(1)}, u32[]{:S(2)}, u32[]{:S(2)}) collective-permute-start(bf16[32,1536]{1,0:T(8,128)(2,1)S(1)} %get-tuple-element.131), channel_id=1, source_target_pairs={{0,1},{1,0},{2,4},{3,7},{4,2},{5,6},{6,5},{7,3},{8,9},{9,8},{10,12... | collective-permute-start | bytes 294920 | tf_op jit(solution)/shard_map/ppermute | solution.py:214
  104.0 11.4 %collective-permute-start.36 = (bf16[32,1536]{1,0:T(8,128)(2,1)S(1)}, bf16[32,1536]{1,0:T(8,128)(2,1)S(1)}, u32[]{:S(2)}, u32[]{:S(2)}) collective-permute-start(bf16[32,1536]{1,0:T(8,128)(2,1)S(1)} %get-tuple-element.128), channel_id=1, source_target_pairs={{0,7},{1,6},{2,5},{3,4},{4,3},{5,2},{6,1},{7,0},{8,15},{9,14},{10,... | collective-permute-start | bytes 294920 | tf_op jit(solution)/shard_map/ppermute | solution.py:214
  115.3 8.9 %collective-permute-start.48 = (bf16[32,1536]{1,0:T(8,128)(2,1)S(1)}, bf16[32,1536]{1,0:T(8,128)(2,1)S(1)}, u32[]{:S(2)}, u32[]{:S(2)}) collective-permute-start(bf16[32,1536]{1,0:T(8,128)(2,1)S(1)} %get-tuple-element.144), channel_id=1, source_target_pairs={{0,6},{1,4},{2,3},{3,2},{4,1},{5,7},{6,0},{7,5},{8,14},{9,12},{10,... | collective-permute-start | bytes 294920 | tf_op jit(solution)/shard_map/ppermute | solution.py:214
  115.4 12.1 %collective-permute-start.49 = (bf16[32,1536]{1,0:T(8,128)(2,1)S(1)}, bf16[32,1536]{1,0:T(8,128)(2,1)S(1)}, u32[]{:S(2)}, u32[]{:S(2)}) collective-permute-start(bf16[32,1536]{1,0:T(8,128)(2,1)S(1)} %get-tuple-element.145), channel_id=1, source_target_pairs={{0,5},{1,3},{2,7},{3,1},{4,6},{5,0},{6,4},{7,2},{8,13},{9,11},{10,... | collective-permute-start | bytes 294920 | tf_op jit(solution)/shard_map/ppermute | solution.py:214
  118.9 8.6 %collective-permute-start.43 = (bf16[32,1536]{1,0:T(8,128)(2,1)S(1)}, bf16[32,1536]{1,0:T(8,128)(2,1)S(1)}, u32[]{:S(2)}, u32[]{:S(2)}) collective-permute-start(bf16[32,1536]{1,0:T(8,128)(2,1)S(1)} %get-tuple-element.139), channel_id=1, source_target_pairs={{0,7},{1,6},{2,5},{3,4},{4,3},{5,2},{6,1},{7,0},{8,15},{9,14},{10,... | collective-permute-start | bytes 294920 | tf_op jit(solution)/shard_map/ppermute | solution.py:214
  119.3 13.3 %collective-permute-start.44 = (bf16[32,1536]{1,0:T(8,128)(2,1)S(1)}, bf16[32,1536]{1,0:T(8,128)(2,1)S(1)}, u32[]{:S(2)}, u32[]{:S(2)}) collective-permute-start(bf16[32,1536]{1,0:T(8,128)(2,1)S(1)} %get-tuple-element.140), channel_id=1, source_target_pairs={{0,1},{1,0},{2,4},{3,7},{4,2},{5,6},{6,5},{7,3},{8,9},{9,8},{10,12... | collective-permute-start | bytes 294920 | tf_op jit(solution)/shard_map/ppermute | solution.py:214
  120.6 13.2 %collective-permute-start.45 = (bf16[32,1536]{1,0:T(8,128)(2,1)S(1)}, bf16[32,1536]{1,0:T(8,128)(2,1)S(1)}, u32[]{:S(2)}, u32[]{:S(2)}) collective-permute-start(bf16[32,1536]{1,0:T(8,128)(2,1)S(1)} %get-tuple-element.141), channel_id=1, source_target_pairs={{0,3},{1,5},{2,6},{3,0},{4,7},{5,1},{6,2},{7,4},{8,11},{9,13},{10,... | collective-permute-start | bytes 294920 | tf_op jit(solution)/shard_map/ppermute | solution.py:214
  124.2 14.4 %collective-permute-start.46 = (bf16[32,1536]{1,0:T(8,128)(2,1)S(1)}, bf16[32,1536]{1,0:T(8,128)(2,1)S(1)}, u32[]{:S(2)}, u32[]{:S(2)}) collective-permute-start(bf16[32,1536]{1,0:T(8,128)(2,1)S(1)} %get-tuple-element.142), channel_id=1, source_target_pairs={{0,4},{1,2},{2,1},{3,5},{4,0},{5,3},{6,7},{7,6},{8,12},{9,10},{10,... | collective-permute-start | bytes 294920 | tf_op jit(solution)/shard_map/ppermute | solution.py:214
  127.5 11.1 %collective-permute-start.47 = (bf16[32,1536]{1,0:T(8,128)(2,1)S(1)}, bf16[32,1536]{1,0:T(8,128)(2,1)S(1)}, u32[]{:S(2)}, u32[]{:S(2)}) collective-permute-start(bf16[32,1536]{1,0:T(8,128)(2,1)S(1)} %get-tuple-element.143), channel_id=1, source_target_pairs={{0,2},{1,7},{2,0},{3,6},{4,5},{5,4},{6,3},{7,1},{8,10},{9,15},{10,... | collective-permute-start | bytes 294920 | tf_op jit(solution)/shard_map/ppermute | solution.py:214
  127.5 14.1 %collective-permute-start.38 = (bf16[32,1536]{1,0:T(8,128)(2,1)S(1)}, bf16[32,1536]{1,0:T(8,128)(2,1)S(1)}, u32[]{:S(2)}, u32[]{:S(2)}) collective-permute-start(bf16[32,1536]{1,0:T(8,128)(2,1)S(1)} %get-tuple-element.133), channel_id=1, source_target_pairs={{0,3},{1,5},{2,6},{3,0},{4,7},{5,1},{6,2},{7,4},{8,11},{9,13},{10,... | collective-permute-start | bytes 294920 | tf_op jit(solution)/shard_map/ppermute | solution.py:214
  132.6 12.4 %collective-permute-start.39 = (bf16[32,1536]{1,0:T(8,128)(2,1)S(1)}, bf16[32,1536]{1,0:T(8,128)(2,1)S(1)}, u32[]{:S(2)}, u32[]{:S(2)}) collective-permute-start(bf16[32,1536]{1,0:T(8,128)(2,1)S(1)} %get-tuple-element.134), channel_id=1, source_target_pairs={{0,4},{1,2},{2,1},{3,5},{4,0},{5,3},{6,7},{7,6},{8,12},{9,10},{10,... | collective-permute-start | bytes 294920 | tf_op jit(solution)/shard_map/ppermute | solution.py:214
  133.9 16.0 %collective-permute-start.40 = (bf16[32,1536]{1,0:T(8,128)(2,1)S(1)}, bf16[32,1536]{1,0:T(8,128)(2,1)S(1)}, u32[]{:S(2)}, u32[]{:S(2)}) collective-permute-start(bf16[32,1536]{1,0:T(8,128)(2,1)S(1)} %get-tuple-element.135), channel_id=1, source_target_pairs={{0,2},{1,7},{2,0},{3,6},{4,5},{5,4},{6,3},{7,1},{8,10},{9,15},{10,... | collective-permute-start | bytes 294920 | tf_op jit(solution)/shard_map/ppermute | solution.py:214
  138.6 12.0 %collective-permute-start.41 = (bf16[32,1536]{1,0:T(8,128)(2,1)S(1)}, bf16[32,1536]{1,0:T(8,128)(2,1)S(1)}, u32[]{:S(2)}, u32[]{:S(2)}) collective-permute-start(bf16[32,1536]{1,0:T(8,128)(2,1)S(1)} %get-tuple-element.136), channel_id=1, source_target_pairs={{0,6},{1,4},{2,3},{3,2},{4,1},{5,7},{6,0},{7,5},{8,14},{9,12},{10,... | collective-permute-start | bytes 294920 | tf_op jit(solution)/shard_map/ppermute | solution.py:214
  138.6 14.8 %collective-permute-start.42 = (bf16[32,1536]{1,0:T(8,128)(2,1)S(1)}, bf16[32,1536]{1,0:T(8,128)(2,1)S(1)}, u32[]{:S(2)}, u32[]{:S(2)}) collective-permute-start(bf16[32,1536]{1,0:T(8,128)(2,1)S(1)} %get-tuple-element.137), channel_id=1, source_target_pairs={{0,5},{1,3},{2,7},{3,1},{4,6},{5,0},{6,4},{7,2},{8,13},{9,11},{10,... | collective-permute-start | bytes 294920 | tf_op jit(solution)/shard_map/ppermute | solution.py:214
  141.6 11.8 %collective-permute-start.50 = (bf16[32,1536]{1,0:T(8,128)(2,1)S(1)}, bf16[32,1536]{1,0:T(8,128)(2,1)S(1)}, u32[]{:S(2)}, u32[]{:S(2)}) collective-permute-start(bf16[32,1536]{1,0:T(8,128)(2,1)S(1)} %get-tuple-element.147), channel_id=1, source_target_pairs={{0,7},{1,6},{2,5},{3,4},{4,3},{5,2},{6,1},{7,0},{8,15},{9,14},{10,... | collective-permute-start | bytes 294920 | tf_op jit(solution)/shard_map/ppermute | solution.py:214
  145.0 12.0 %collective-permute-start.51 = (bf16[32,1536]{1,0:T(8,128)(2,1)S(1)}, bf16[32,1536]{1,0:T(8,128)(2,1)S(1)}, u32[]{:S(2)}, u32[]{:S(2)}) collective-permute-start(bf16[32,1536]{1,0:T(8,128)(2,1)S(1)} %get-tuple-element.148), channel_id=1, source_target_pairs={{0,1},{1,0},{2,4},{3,7},{4,2},{5,6},{6,5},{7,3},{8,9},{9,8},{10,12... | collective-permute-start | bytes 294920 | tf_op jit(solution)/shard_map/ppermute | solution.py:214
  149.9 8.9 %collective-permute-start.52 = (bf16[32,1536]{1,0:T(8,128)(2,1)S(1)}, bf16[32,1536]{1,0:T(8,128)(2,1)S(1)}, u32[]{:S(2)}, u32[]{:S(2)}) collective-permute-start(bf16[32,1536]{1,0:T(8,128)(2,1)S(1)} %get-tuple-element.149), channel_id=1, source_target_pairs={{0,3},{1,5},{2,6},{3,0},{4,7},{5,1},{6,2},{7,4},{8,11},{9,13},{10,... | collective-permute-start | bytes 294920 | tf_op jit(solution)/shard_map/ppermute | solution.py:214
  150.5 10.0 %collective-permute-start.53 = (bf16[32,1536]{1,0:T(8,128)(2,1)S(1)}, bf16[32,1536]{1,0:T(8,128)(2,1)S(1)}, u32[]{:S(2)}, u32[]{:S(2)}) collective-permute-start(bf16[32,1536]{1,0:T(8,128)(2,1)S(1)} %get-tuple-element.150), channel_id=1, source_target_pairs={{0,4},{1,2},{2,1},{3,5},{4,0},{5,3},{6,7},{7,6},{8,12},{9,10},{10,... | collective-permute-start | bytes 294920 | tf_op jit(solution)/shard_map/ppermute | solution.py:214
  153.4 7.2 %collective-permute-start.54 = (bf16[32,1536]{1,0:T(8,128)(2,1)S(1)}, bf16[32,1536]{1,0:T(8,128)(2,1)S(1)}, u32[]{:S(2)}, u32[]{:S(2)}) collective-permute-start(bf16[32,1536]{1,0:T(8,128)(2,1)S(1)} %get-tuple-element.151), channel_id=1, source_target_pairs={{0,2},{1,7},{2,0},{3,6},{4,5},{5,4},{6,3},{7,1},{8,10},{9,15},{10,... | collective-permute-start | bytes 294920 | tf_op jit(solution)/shard_map/ppermute | solution.py:214
  153.4 7.2 %collective-permute-start.55 = (bf16[32,1536]{1,0:T(8,128)(2,1)S(1)}, bf16[32,1536]{1,0:T(8,128)(2,1)S(1)}, u32[]{:S(2)}, u32[]{:S(2)}) collective-permute-start(bf16[32,1536]{1,0:T(8,128)(2,1)S(1)} %get-tuple-element.152), channel_id=1, source_target_pairs={{0,6},{1,4},{2,3},{3,2},{4,1},{5,7},{6,0},{7,5},{8,14},{9,12},{10,... | collective-permute-start | bytes 294920 | tf_op jit(solution)/shard_map/ppermute | solution.py:214
  157.0 6.4 %collective-permute-start.56 = (bf16[32,1536]{1,0:T(8,128)(2,1)S(1)}, bf16[32,1536]{1,0:T(8,128)(2,1)S(1)}, u32[]{:S(2)}, u32[]{:S(2)}) collective-permute-start(bf16[32,1536]{1,0:T(8,128)(2,1)S(1)} %get-tuple-element.153), channel_id=1, source_target_pairs={{0,5},{1,3},{2,7},{3,1},{4,6},{5,0},{6,4},{7,2},{8,13},{9,11},{10,... | collective-permute-start | bytes 294920 | tf_op jit(solution)/shard_map/ppermute | solution.py:214
  (6 other events, 35.8 us)

commit v5 on v4

--- a/solution.py
+++ b/solution.py
@@ -32,33 +32,33 @@
 )
 
 
-def partners(slot, count):
-    if slot == 0 or count != 8:
+def partners(slot, count, plain):
+    if slot == 0 or count != 8 or plain:
         return [device ^ slot for device in range(count)]
     both = dict(PAIRINGS[slot - 1])
     both.update({b: a for a, b in both.items()})
     return [both[device] for device in range(count)]
 
 
-def owner_of(slot, count):
+def owner_of(slot, count, plain):
     me = lax.axis_index("seq")
-    if slot == 0 or count != 8:
+    if slot == 0 or count != 8 or plain:
         return me ^ slot
-    packed = sum(partner << (3 * device) for device, partner in enumerate(partners(slot, count)))
+    packed = sum(partner << (3 * device) for device, partner in enumerate(partners(slot, count, plain)))
     return (packed >> (3 * me)) & 7
 
 
-def owners_of(slots, count):
-    if count != 8:
+def owners_of(slots, count, plain):
+    if count != 8 or plain:
         return slots ^ lax.axis_index("seq")
     owners = jnp.zeros_like(slots)
     for slot in range(count):
-        owners = jnp.where(slots == slot, owner_of(slot, count), owners)
+        owners = jnp.where(slots == slot, owner_of(slot, count, plain), owners)
     return owners
 
 
-def rows_of(slot, size):
-    owner = owner_of(slot, lax.axis_size("seq"))
+def rows_of(slot, size, plain):
+    owner = owner_of(slot, lax.axis_size("seq"), plain)
     return pl.ds(pl.multiple_of(owner * size, size), size)
 
 
@@ -71,9 +71,9 @@
     return pl.ds(pl.multiple_of(j * width, 128), width)
 
 
-def split(outs, wide_ref):
+def split(outs, wide_ref, plain):
     for slot, out in enumerate(outs):
-        out[...] = wide_ref[rows_of(slot, out.shape[0]), :].astype(BF16)
+        out[...] = wide_ref[rows_of(slot, out.shape[0], plain), :].astype(BF16)
 
 
 def normed_block(j, x_ref, gain_ref, q_ref, width):
@@ -97,11 +97,11 @@
     return inner * gate * sigmoid
 
 
-def first_kernel(count, x_ref, gain_ref, w_ref, r_ref, *refs):
+def first_kernel(count, plain, x_ref, gain_ref, w_ref, r_ref, *refs):
     outs, (q_ref, wide_ref) = refs[:count], refs[count:]
     normed = normed_block(pl.program_id(0), x_ref, gain_ref, q_ref, w_ref.shape[1])
     wide_ref[...] = first_of(normed, w_ref, r_ref)
-    split(outs, wide_ref)
+    split(outs, wide_ref, plain)
 
 
 def pick_gradient(refs):
@@ -116,10 +116,10 @@
     outs, (factor_ref, q_ref, wide_ref) = refs[:count], refs[count:]
     normed = normed_block(pl.program_id(0), x_ref, gain_ref, q_ref, w_gate_ref.shape[1])
     wide_ref[...] = grads_of(normed, pick_gradient(grads), w_gate_ref, w_out_ref, factor_ref)
-    split(outs, wide_ref)
-
-
-def matrix_kernel(count, l_ref, out_ref):
+    split(outs, wide_ref, False)
+
+
+def matrix_kernel(count, plain, l_ref, out_ref):
     size = l_ref.shape[0]
     wide = count * size
     bits = count.bit_length() - 1
@@ -127,11 +127,11 @@
 
     shape = (count, size, count * count)
     tall = jnp.broadcast_to(l_ref[...].astype(F32)[None], shape)
-    tall = jnp.where(iota(shape, 2) >> bits == owners_of(iota(shape, 0), count), tall, 0.0)
+    tall = jnp.where(iota(shape, 2) >> bits == owners_of(iota(shape, 0), count, plain), tall, 0.0)
     tall = tall.reshape(wide, count * count).astype(BF16)
 
     shape = (count * count, wide)
-    source = owners_of(iota(shape, 1) >> (size.bit_length() - 1), count)
+    source = owners_of(iota(shape, 1) >> (size.bit_length() - 1), count, plain)
     spread = dot(tall, jnp.where(iota(shape, 0) & (count - 1) == source, 1.0, 0.0).astype(BF16))
 
     row, column = iota((wide, wide), 0) & (size - 1), iota((wide, wide), 1) & (size - 1)
@@ -150,9 +150,9 @@
         out[...] = value[slot * size : (slot + 1) * size].astype(BF16)
 
 
-def joined(ins, wide_ref):
+def joined(ins, wide_ref, plain):
     for slot, part in enumerate(ins):
-        wide_ref[rows_of(slot, part.shape[0]), :] = part[...].astype(wide_ref.dtype)
+        wide_ref[rows_of(slot, part.shape[0], plain), :] = part[...].astype(wide_ref.dtype)
     return wide_ref[...]
 
 
@@ -162,9 +162,9 @@
     spread_slots(outs, dot(m_ref[...], stacked_slots(ins), over))
 
 
-def back_kernel(count, w_gate_ref, factor_ref, *refs):
+def back_kernel(count, plain, w_gate_ref, factor_ref, *refs):
     mixed, (out_ref, wide_ref) = refs[:count], refs[count:]
-    gate_grad = (factor_ref[...] * joined(mixed, wide_ref).astype(F32)).astype(BF16)
+    gate_grad = (factor_ref[...] * joined(mixed, wide_ref, plain).astype(F32)).astype(BF16)
     out_ref[...] = dot(gate_grad, w_gate_ref[...], ((1,), (1,)))
 
 
@@ -198,19 +198,19 @@
     grads, refs = refs[:sources], refs[sources:]
     outs, (wide_ref, e_ref, sum_ref) = refs[sources - 1 : -3], refs[-3:]
     finish(
-        pl.program_id(0), back_ref[...], joined(folded, wide_ref), grads, outs,
+        pl.program_id(0), back_ref[...], joined(folded, wide_ref, False), grads, outs,
         x_ref, gain_ref, w_value_ref, r_ref, e_ref, sum_ref,
     )
 
 
 class Exchange:
-    def __init__(self, parts):
-        self.parts = list(parts)
+    def __init__(self, parts, plain=False):
+        self.parts, self.plain = list(parts), plain
         self.got = {0: parts[0]}
 
     def send(self, slots, after=()):
         for slot in slots:
-            pairs = [*enumerate(partners(slot, len(self.parts)))]
+            pairs = [*enumerate(partners(slot, len(self.parts), self.plain))]
             self.got[slot] = lax.ppermute(tied(self.parts[slot], after), "seq", pairs)
         return self
 
@@ -290,7 +290,7 @@
     def first(tick, mebibytes=32):
         return call(
             f"first_{tick}",
-            functools.partial(first_kernel, count),
+            functools.partial(first_kernel, count, tick > 0),
             (2, 4),
             [(x_at[tick], saved_inputs), gains, value_in, r_in],
             slots_out,
@@ -309,7 +309,7 @@
         )
         return parts, factor
 
-    def mix(name, parts, transposed):
+    def mix(name, parts, transposed, matrix):
         return call(
             name,
             functools.partial(mix_kernel, count, transposed),
@@ -322,7 +322,7 @@
     def back(tick, mixed, factor):
         return call(
             f"back_{tick}",
-            functools.partial(back_kernel, count),
+            functools.partial(back_kernel, count, tick > 0),
             (1, 6),
             [gate_in, (cut, factor), *zip(slots, mixed)],
             [(cut, exact)],
@@ -350,33 +350,36 @@
         )
 
     first_0 = Exchange(first(0, 60)).send(every)
-    (matrix,) = call(
-        "matrix",
-        functools.partial(matrix_kernel, count),
-        (0.3, 1),
-        [(small, l_factor)],
-        [(square_plain, jax.ShapeDtypeStruct((rows, rows), BF16))],
-        [],
-        steps=1,
+    matrix, plain_matrix = (
+        call(
+            f"matrix_{plain}",
+            functools.partial(matrix_kernel, count, plain),
+            (0.3, 1),
+            [(small, l_factor)],
+            [(square_plain, jax.ShapeDtypeStruct((rows, rows), BF16))],
+            [],
+            steps=1,
+        )[0]
+        for plain in (False, True)
     )
     parts, factor_0 = grads(0, [(cut3, arrived_grad)])
     grad_0 = Exchange(parts).send(every)
-    mix_0 = Exchange(mix("mix_0", first_0.all(), False)).send(every)
-    fold_0 = Exchange(mix("fold_0", grad_0.all(), True)).send(every)
+    mix_0 = Exchange(mix("mix_0", first_0.all(), False, matrix)).send(every)
+    fold_0 = Exchange(mix("fold_0", grad_0.all(), True, matrix)).send(every)
     gate_0 = back(0, mix_0.all(), factor_0)
-    first_1 = Exchange(first(1))
+    first_1 = Exchange(first(1), True)
     gate_0, first_1.parts[0] = lax.optimization_barrier((gate_0, first_1.parts[0]))
     first_1.send(every)
     stacked, result_0 = result(0, gate_0, fold_0.all(), [(whole3, arrived_grad)], None)
     passed = lax.ppermute(result_0, "pipe", [(s, s - 1) for s in range(1, pipe)])
-    mix_1 = Exchange(mix("mix_1", first_1.all(), False)).send(every)
+    mix_1 = Exchange(mix("mix_1", first_1.all(), False, plain_matrix), True).send(every)
     passed, mix_1.parts[0] = lax.optimization_barrier((passed, mix_1.parts[0]))
     mix_1.got[0] = mix_1.parts[0]
     parts, factor_1 = grads(1, [(cut, passed), (cut3, loss_grad)])
     for slot in every[:2]:
-        parts[count - slot] = tied(parts[count - slot], [(mix_1, slot)])
+        parts[count - slot] = tied(parts[count - slot], [(mix_1, count // 2 - 1 + slot)])
     grad_1 = Exchange(parts).send(every)
-    fold_1 = Exchange(mix("fold_1", grad_1.all(), True)).send(every)
+    fold_1 = Exchange(mix("fold_1", grad_1.all(), True, matrix)).send(every)
     gate_1 = back(1, mix_1.all(), factor_1)
     incoming = [(whole, passed), (whole3, loss_grad)]
     return result(1, gate_1, fold_1.all(), incoming, stacked)[0]

time: 168 us -> 169 us (level)
  starting transfers between devices: 112 us -> 104 us
  waiting for transfers between devices: 21 us -> 29 us
    ppermute x56, waiting for transfers between devices: 16.2 us -> 24.8 us  [send(): self.got[slot] = lax.ppermute(tied(self.parts[slot], after), 'seq', pairs)]
    ppermute x56, starting transfers between devices: 110 us -> 102 us  [send(): self.got[slot] = lax.ppermute(tied(self.parts[slot], after), 'seq', pairs)]
    pallas_call x13 -> x14, Pallas kernels: 32 us -> 32.1 us  [call(): pl.pallas_call(kernel, grid=(steps or width // block,), in_specs=[spec fo...]
  transfers between devices with their start and end apart: 57 -> 57, of which waited for: 7 -> 10; matrix products, arithmetic and copies ran while one was open for 0% -> 0% of each run, Pallas kernels for 13% -> 14%
where the time goes in v5:
time: 169 us; the launch traced here: 168 us
  starting transfers between devices  104 us (62%)
  Pallas kernels  32.1 us (19%)
  waiting for transfers between devices  29 us (17%)
  local copies, waits for them, and re-layouts  2.44 us (1%)
    ppermute x56, starting transfers between devices, send(): self.got[slot] = lax.ppermute(tied(self.parts[slot], after), 'seq', pairs)  102 us
    pallas_call x14, Pallas kernels, call(): pl.pallas_call(kernel, grid=(steps or width // block,), in_specs=[spec fo...  32.1 us
    ppermute x56, waiting for transfers between devices, send(): self.got[slot] = lax.ppermute(tied(self.parts[slot], after), 'seq', pairs)  24.8 us
    ppermute x1, waiting for transfers between devices, local(): lax.ppermute(result_0, 'pipe', [(s, s - 1) for s in range(1, pipe)])  4.13 us
  transfers between devices with their start and end apart: 57, of which 10 were waited for; matrix products, arithmetic and copies ran while one was open for 0% of the time, Pallas kernels for 14%

profile of v5, /device:TPU:2, one launch (start us, length us, event | category | flops | bytes accessed | tf_op | source)
XLA Modules:
  0.0 167.6 jit_solution(1155721847693755563)
XLA Ops:
  0.0 5.2 %first_0.1 = (bf16[32,1536]{1,0:T(8,128)(2,1)}, bf16[32,1536]{1,0:T(8,128)(2,1)}, bf16[32,1536]{1,0:T(8,128)(2,1)}, bf16[32,1536]{1,0:T(8,128)(2,1)}, bf16[32,15...) custom-call(bf16[1,2,256,1536]{3,2,1,0:T(8,128)(2,1)} %x_ref.11, ...), custom_call_target="tpu_custom_call" | custom-call | flops 603979776 | bytes 3145728 | tf_op jit(solution)/shard_map/first_0/pallas_call | solution.py:267
  5.2 4.6 %collective-permute-start = (bf16[32,1536]{1,0:T(8,128)(2,1)}, bf16[32,1536]{1,0:T(8,128)(2,1)S(1)}, u32[]{:S(2)}, u32[]{:S(2)}) collective-permute-start(bf16[32,1536]{1,0:T(8,128)(2,1)} %get-tuple-element.82), channel_id=1, source_target_pairs={{0,7},{1,6},{2,5},{3,4},{4,3},{5,2},{6,1},{7,0},{8,15},{9,14},{10,... | collective-permute-start | bytes 294920 | tf_op jit(solution)/shard_map/ppermute | solution.py:214
  9.9 0.5 collective-permute-start.1
  10.6 1.7 %collective-permute-start.3 = (bf16[32,1536]{1,0:T(8,128)(2,1)}, bf16[32,1536]{1,0:T(8,128)(2,1)S(1)}, u32[]{:S(2)}, u32[]{:S(2)}) collective-permute-start(bf16[32,1536]{1,0:T(8,128)(2,1)} %get-tuple-element.85), channel_id=1, source_target_pairs={{0,4},{1,2},{2,1},{3,5},{4,0},{5,3},{6,7},{7,6},{8,12},{9,10},{10,... | collective-permute-start | bytes 294920 | tf_op jit(solution)/shard_map/ppermute | solution.py:214
  12.3 1.3 collective-permute-start.4
  13.6 1.3 copy-done.3
  14.9 1.1 copy-done.5
  16.0 3.3 %grads_0.1 = (bf16[32,1536]{1,0:T(8,128)(2,1)S(1)}, bf16[32,1536]{1,0:T(8,128)(2,1)S(1)}, bf16[32,1536]{1,0:T(8,128)(2,1)S(1)}, bf16[32,1536]{1,0:T(8,128)(2,1)S...) custom-call(bf16[1,2,256,1536]{3,2,1,0:T(8,128)(2,1)S(1)} %copy-done, ...), custom_call_target="tpu_custom_call" | custom-call | flops 603979776 | bytes 6291456 | tf_op jit(solution)/shard_map/grads_0/pallas_call | solution.py:267
  19.3 3.7 %collective-permute-start.5 = (bf16[32,1536]{1,0:T(8,128)(2,1)S(1)}, bf16[32,1536]{1,0:T(8,128)(2,1)S(1)}, u32[]{:S(2)}, u32[]{:S(2)}) collective-permute-start(bf16[32,1536]{1,0:T(8,128)(2,1)S(1)} %copy-done.12), channel_id=1, source_target_pairs={{0,6},{1,4},{2,3},{3,2},{4,1},{5,7},{6,0},{7,5},{8,14},{9,12},{10,... | collective-permute-start | bytes 294920 | tf_op jit(solution)/shard_map/ppermute | solution.py:214
  23.0 2.2 %collective-permute-start.14 = (bf16[32,1536]{1,0:T(8,128)(2,1)S(1)}, bf16[32,1536]{1,0:T(8,128)(2,1)S(1)}, u32[]{:S(2)}, u32[]{:S(2)}) collective-permute-start(bf16[32,1536]{1,0:T(8,128)(2,1)S(1)} %get-tuple-element.100), channel_id=1, source_target_pairs={{0,7},{1,6},{2,5},{3,4},{4,3},{5,2},{6,1},{7,0},{8,15},{9,14},{10,... | collective-permute-start | bytes 294920 | tf_op jit(solution)/shard_map/ppermute | solution.py:214
  25.4 6.3 %collective-permute-start.16 = (bf16[32,1536]{1,0:T(8,128)(2,1)S(1)}, bf16[32,1536]{1,0:T(8,128)(2,1)S(1)}, u32[]{:S(2)}, u32[]{:S(2)}) collective-permute-start(bf16[32,1536]{1,0:T(8,128)(2,1)S(1)} %get-tuple-element.102), channel_id=1, source_target_pairs={{0,3},{1,5},{2,6},{3,0},{4,7},{5,1},{6,2},{7,4},{8,11},{9,13},{10,... | collective-permute-start | bytes 294920 | tf_op jit(solution)/shard_map/ppermute | solution.py:214
  31.7 2.9 %first_1.1 = (bf16[32,1536]{1,0:T(8,128)(2,1)S(1)}, bf16[32,1536]{1,0:T(8,128)(2,1)S(1)}, bf16[32,1536]{1,0:T(8,128)(2,1)S(1)}, bf16[32,1536]{1,0:T(8,128)(2,1)S...) custom-call(bf16[1,2,256,1536]{3,2,1,0:T(8,128)(2,1)S(1)} %copy-done, ...), custom_call_target="tpu_custom_call" | custom-call | flops 603979776 | bytes 3145728 | tf_op jit(solution)/shard_map/first_1/pallas_call | solution.py:267
  34.7 3.5 %collective-permute-start.18 = (bf16[32,1536]{1,0:T(8,128)(2,1)S(1)}, bf16[32,1536]{1,0:T(8,128)(2,1)S(1)}, u32[]{:S(2)}, u32[]{:S(2)}) collective-permute-start(bf16[32,1536]{1,0:T(8,128)(2,1)S(1)} %get-tuple-element.104), channel_id=1, source_target_pairs={{0,2},{1,7},{2,0},{3,6},{4,5},{5,4},{6,3},{7,1},{8,10},{9,15},{10,... | collective-permute-start | bytes 294920 | tf_op jit(solution)/shard_map/ppermute | solution.py:214
  38.2 5.2 %collective-permute-start.20 = (bf16[32,1536]{1,0:T(8,128)(2,1)S(1)}, bf16[32,1536]{1,0:T(8,128)(2,1)S(1)}, u32[]{:S(2)}, u32[]{:S(2)}) collective-permute-start(bf16[32,1536]{1,0:T(8,128)(2,1)S(1)} %get-tuple-element.106), channel_id=1, source_target_pairs={{0,5},{1,3},{2,7},{3,1},{4,6},{5,0},{6,4},{7,2},{8,13},{9,11},{10,... | collective-permute-start | bytes 294920 | tf_op jit(solution)/shard_map/ppermute | solution.py:214
  43.6 1.3 mix_0.1
  45.0 2.1 %collective-permute-done.18.refs_5_ = bf16[32,1536]{1,0:T(8,128)(2,1)S(1)} collective-permute-done((bf16[32,1536]{1,0:T(8,128)(2,1)S(1)}, bf16[32,1536]{1,0:T(8,128)(2,1)S(1)}, u32[]{:S(2)}, u32[]{:S(2)}) %collective-permute-start.18) | collective-permute-done | bytes 98336 | tf_op jit(solution)/shard_map/ppermute | solution.py:214
  47.1 1.4 collective-permute-start.11
  48.5 2.8 %collective-permute-start.12 = (bf16[32,1536]{1,0:T(8,128)(2,1)S(1)}, bf16[32,1536]{1,0:T(8,128)(2,1)S(1)}, u32[]{:S(2)}, u32[]{:S(2)}) collective-permute-start(bf16[32,1536]{1,0:T(8,128)(2,1)S(1)} %get-tuple-element.95), channel_id=1, source_target_pairs={{0,6},{1,4},{2,3},{3,2},{4,1},{5,7},{6,0},{7,5},{8,14},{9,12},{10,... | collective-permute-start | bytes 294920 | tf_op jit(solution)/shard_map/ppermute | solution.py:214
  51.3 1.0 collective-permute-start.13
  52.3 1.4 fold_0.1
  53.6 2.3 %collective-permute-start.7 = (bf16[32,1536]{1,0:T(8,128)(2,1)S(1)}, bf16[32,1536]{1,0:T(8,128)(2,1)S(1)}, u32[]{:S(2)}, u32[]{:S(2)}) collective-permute-start(bf16[32,1536]{1,0:T(8,128)(2,1)S(1)} %get-tuple-element.90), channel_id=1, source_target_pairs={{0,7},{1,6},{2,5},{3,4},{4,3},{5,2},{6,1},{7,0},{8,15},{9,14},{10,... | collective-permute-start | bytes 294920 | tf_op jit(solution)/shard_map/ppermute | solution.py:214
  55.9 0.9 collective-permute-done.10.refs_4_
  56.9 0.8 collective-permute-done.11.refs_5_
  57.7 3.2 %collective-permute-start.9 = (bf16[32,1536]{1,0:T(8,128)(2,1)S(1)}, bf16[32,1536]{1,0:T(8,128)(2,1)S(1)}, u32[]{:S(2)}, u32[]{:S(2)}) collective-permute-start(bf16[32,1536]{1,0:T(8,128)(2,1)S(1)} %get-tuple-element.92), channel_id=1, source_target_pairs={{0,3},{1,5},{2,6},{3,0},{4,7},{5,1},{6,2},{7,4},{8,11},{9,13},{10,... | collective-permute-start | bytes 294920 | tf_op jit(solution)/shard_map/ppermute | solution.py:214
  61.0 4.0 %collective-permute-done.13.refs_7_ = bf16[32,1536]{1,0:T(8,128)(2,1)S(1)} collective-permute-done((bf16[32,1536]{1,0:T(8,128)(2,1)S(1)}, bf16[32,1536]{1,0:T(8,128)(2,1)S(1)}, u32[]{:S(2)}, u32[]{:S(2)}) %collective-permute-start.13) | collective-permute-done | bytes 98336 | tf_op jit(solution)/shard_map/ppermute | solution.py:214
  65.0 1.5 collective-permute-start.22
  66.7 3.4 %collective-permute-start.24 = (bf16[32,1536]{1,0:T(8,128)(2,1)S(1)}, bf16[32,1536]{1,0:T(8,128)(2,1)S(1)}, u32[]{:S(2)}, u32[]{:S(2)}) collective-permute-start(bf16[32,1536]{1,0:T(8,128)(2,1)S(1)} %get-tuple-element.111), channel_id=1, source_target_pairs={{0,4},{1,2},{2,1},{3,5},{4,0},{5,3},{6,7},{7,6},{8,12},{9,10},{10,... | collective-permute-start | bytes 294920 | tf_op jit(solution)/shard_map/ppermute | solution.py:214
  70.1 0.4 collective-permute-start.25
  70.5 3.6 %collective-permute-start.26 = (bf16[32,1536]{1,0:T(8,128)(2,1)S(1)}, bf16[32,1536]{1,0:T(8,128)(2,1)S(1)}, u32[]{:S(2)}, u32[]{:S(2)}) collective-permute-start(bf16[32,1536]{1,0:T(8,128)(2,1)S(1)} %get-tuple-element.113), channel_id=1, source_target_pairs={{0,6},{1,4},{2,3},{3,2},{4,1},{5,7},{6,0},{7,5},{8,14},{9,12},{10,... | collective-permute-start | bytes 294920 | tf_op jit(solution)/shard_map/ppermute | solution.py:214
  74.2 3.2 %collective-permute-start.27 = (bf16[32,1536]{1,0:T(8,128)(2,1)S(1)}, bf16[32,1536]{1,0:T(8,128)(2,1)S(1)}, u32[]{:S(2)}, u32[]{:S(2)}) collective-permute-start(bf16[32,1536]{1,0:T(8,128)(2,1)S(1)} %get-tuple-element.114), channel_id=1, source_target_pairs={{0,5},{1,3},{2,7},{3,1},{4,6},{5,0},{6,4},{7,2},{8,13},{9,11},{10,... | collective-permute-start | bytes 294920 | tf_op jit(solution)/shard_map/ppermute | solution.py:214
  77.6 4.8 %collective-permute-done.24.refs_4_ = bf16[32,1536]{1,0:T(8,128)(2,1)S(1)} collective-permute-done((bf16[32,1536]{1,0:T(8,128)(2,1)S(1)}, bf16[32,1536]{1,0:T(8,128)(2,1)S(1)}, u32[]{:S(2)}, u32[]{:S(2)}) %collective-permute-start.24) | collective-permute-done | bytes 98336 | tf_op jit(solution)/shard_map/ppermute | solution.py:214
  82.4 1.5 collective-permute-start.32
  83.9 5.6 %collective-permute-start.33 = (bf16[32,1536]{1,0:T(8,128)(2,1)S(1)}, bf16[32,1536]{1,0:T(8,128)(2,1)S(1)}, u32[]{:S(2)}, u32[]{:S(2)}) collective-permute-start(bf16[32,1536]{1,0:T(8,128)(2,1)S(1)} %get-tuple-element.120), channel_id=1, source_target_pairs={{0,5},{1,4},{2,7},{3,6},{4,1},{5,0},{6,3},{7,2},{8,13},{9,12},{10,... | collective-permute-start | bytes 294920 | tf_op jit(solution)/shard_map/ppermute | solution.py:214
  89.5 3.8 %collective-permute-start.35 = (bf16[32,1536]{1,0:T(8,128)(2,1)S(1)}, bf16[32,1536]{1,0:T(8,128)(2,1)S(1)}, u32[]{:S(2)}, u32[]{:S(2)}) collective-permute-start(bf16[32,1536]{1,0:T(8,128)(2,1)S(1)} %get-tuple-element.122), channel_id=1, source_target_pairs={{0,7},{1,6},{2,5},{3,4},{4,3},{5,2},{6,1},{7,0},{8,15},{9,14},{10,... | collective-permute-start | bytes 294920 | tf_op jit(solution)/shard_map/ppermute | solution.py:214
  93.3 1.7 %back_0.1.back_ref = f32[256,1536]{1,0:T(8,128)S(1)} custom-call(bf16[1,384,1536]{2,1,0:T(8,128)(2,1)S(1)} %copy-done.2, f32[256,1536]{1,0:T(8,128)S(1)} %get-tuple-element.80.factor_ref, bf16[32,1536]{1,0:T(8,128)(2,1)S(1)} %get-tuple-element.89.refs_0_, bf16[32,1536]{1,0:T(8,128)(2,1)S(1)} %collective-permute-done.7.refs_1_, ...), custom_call_target="tpu_custom_call" | custom-call | flops 301989888 | bytes 4718592 | tf_op jit(solution)/shard_map/back_0/pallas_call | solution.py:267
  95.1 4.1 %result_0.1 = (bf16[1,2,256,1536]{3,2,1,0:T(8,128)(2,1)}, bf16[256,1536]{1,0:T(8,128)(2,1)S(1)}) custom-call(bf16[1,2,256,1536]{3,2,1,0:T(8,128)(2,1)S(1)} %copy-done, f32[1,1536]{1,0:T(1,128)S(1)} %copy-done.8, bf16[1,384,1536]{2,1,0:T(8,128)(2,1)S(1)} %copy-done.1, bf16[1,256,256]{2,1,0:T(8,128)(2,1)S(1)} %copy-done.7, f32[256,1536]{1,0:T(8,128)S(1)} %back_0.1.back_ref, ...), custom_call_target="tpu_custom_call" | custom-call | flops 905969664 | bytes 6291456 | tf_op jit(solution)/shard_map/result_0/pallas_call | solution.py:267
  99.2 2.2 %collective-permute-start.28 = (bf16[256,1536]{1,0:T(8,128)(2,1)S(1)}, bf16[256,1536]{1,0:T(8,128)(2,1)S(1)}, u32[]{:S(2)}, u32[]{:S(2)}) collective-permute-start(bf16[256,1536]{1,0:T(8,128)(2,1)S(1)} %get-tuple-element.115), channel_id=1, source_target_pairs={{8,0},{16,8},{24,16},{9,1},{17,9},{25,17},{10,2},{18,10},{26,18},{... | collective-permute-start | bytes 2359304 | tf_op jit(solution)/shard_map/ppermute | solution.py:374
  101.5 1.3 mix_1.1
  102.7 2.0 %collective-permute-start.40 = (bf16[32,1536]{1,0:T(8,128)(2,1)S(1)}, bf16[32,1536]{1,0:T(8,128)(2,1)S(1)}, u32[]{:S(2)}, u32[]{:S(2)}) collective-permute-start(bf16[32,1536]{1,0:T(8,128)(2,1)S(1)} %get-tuple-element.134), channel_id=1, source_target_pairs={{0,5},{1,4},{2,7},{3,6},{4,1},{5,0},{6,3},{7,2},{8,13},{9,12},{10,... | collective-permute-start | bytes 294920 | tf_op jit(solution)/shard_map/ppermute | solution.py:214
  104.7 1.9 %collective-permute-start.39 = (bf16[32,1536]{1,0:T(8,128)(2,1)S(1)}, bf16[32,1536]{1,0:T(8,128)(2,1)S(1)}, u32[]{:S(2)}, u32[]{:S(2)}) collective-permute-start(bf16[32,1536]{1,0:T(8,128)(2,1)S(1)} %get-tuple-element.131), channel_id=1, source_target_pairs={{0,4},{1,5},{2,6},{3,7},{4,0},{5,1},{6,2},{7,3},{8,12},{9,13},{10,... | collective-permute-start | bytes 294920 | tf_op jit(solution)/shard_map/ppermute | solution.py:214
  106.6 4.1 %collective-permute-done.28.refs_0_.refs_8_ = bf16[256,1536]{1,0:T(8,128)(2,1)S(1)} collective-permute-done((bf16[256,1536]{1,0:T(8,128)(2,1)S(1)}, bf16[256,1536]{1,0:T(8,128)(2,1)S(1)}, u32[]{:S(2)}, u32[]{:S(2)}) %collective-permute-start.28) | collective-permute-done | bytes 786464 | tf_op jit(solution)/shard_map/ppermute | solution.py:374
  110.7 3.3 %grads_1.1 = (bf16[32,1536]{1,0:T(8,128)(2,1)S(1)}, bf16[32,1536]{1,0:T(8,128)(2,1)S(1)}, bf16[32,1536]{1,0:T(8,128)(2,1)S(1)}, bf16[32,1536]{1,0:T(8,128)(2,1)S...) custom-call(bf16[1,2,256,1536]{3,2,1,0:T(8,128)(2,1)S(1)} %copy-done, ...), custom_call_target="tpu_custom_call" | custom-call | flops 603979776 | bytes 6291456 | tf_op jit(solution)/shard_map/grads_1/pallas_call | solution.py:267
  114.1 2.4 %collective-permute-start.48 = (bf16[32,1536]{1,0:T(8,128)(2,1)S(1)}, bf16[32,1536]{1,0:T(8,128)(2,1)S(1)}, u32[]{:S(2)}, u32[]{:S(2)}) collective-permute-start(bf16[32,1536]{1,0:T(8,128)(2,1)S(1)} %get-tuple-element.144), channel_id=1, source_target_pairs={{0,6},{1,4},{2,3},{3,2},{4,1},{5,7},{6,0},{7,5},{8,14},{9,12},{10,... | collective-permute-start | bytes 294920 | tf_op jit(solution)/shard_map/ppermute | solution.py:214
  116.5 2.1 %collective-permute-start.43 = (bf16[32,1536]{1,0:T(8,128)(2,1)S(1)}, bf16[32,1536]{1,0:T(8,128)(2,1)S(1)}, u32[]{:S(2)}, u32[]{:S(2)}) collective-permute-start(bf16[32,1536]{1,0:T(8,128)(2,1)S(1)} %get-tuple-element.139), channel_id=1, source_target_pairs={{0,7},{1,6},{2,5},{3,4},{4,3},{5,2},{6,1},{7,0},{8,15},{9,14},{10,... | collective-permute-start | bytes 294920 | tf_op jit(solution)/shard_map/ppermute | solution.py:214
  118.5 2.4 %collective-permute-start.44 = (bf16[32,1536]{1,0:T(8,128)(2,1)S(1)}, bf16[32,1536]{1,0:T(8,128)(2,1)S(1)}, u32[]{:S(2)}, u32[]{:S(2)}) collective-permute-start(bf16[32,1536]{1,0:T(8,128)(2,1)S(1)} %get-tuple-element.140), channel_id=1, source_target_pairs={{0,1},{1,0},{2,4},{3,7},{4,2},{5,6},{6,5},{7,3},{8,9},{9,8},{10,12... | collective-permute-start | bytes 294920 | tf_op jit(solution)/shard_map/ppermute | solution.py:214
  120.9 0.9 collective-permute-start.45
  121.8 1.6 collective-permute-start.46
  123.3 4.6 %collective-permute-done.49.refs_7_ = bf16[32,1536]{1,0:T(8,128)(2,1)S(1)} collective-permute-done((bf16[32,1536]{1,0:T(8,128)(2,1)S(1)}, bf16[32,1536]{1,0:T(8,128)(2,1)S(1)}, u32[]{:S(2)}, u32[]{:S(2)}) %collective-permute-start.49) | collective-permute-done | bytes 98336 | tf_op jit(solution)/shard_map/ppermute | solution.py:214
  128.0 2.9 %collective-permute-start.36 = (bf16[32,1536]{1,0:T(8,128)(2,1)S(1)}, bf16[32,1536]{1,0:T(8,128)(2,1)S(1)}, u32[]{:S(2)}, u32[]{:S(2)}) collective-permute-start(bf16[32,1536]{1,0:T(8,128)(2,1)S(1)} %get-tuple-element.127), channel_id=1, source_target_pairs={{0,1},{1,0},{2,3},{3,2},{4,5},{5,4},{6,7},{7,6},{8,9},{9,8},{10,11... | collective-permute-start | bytes 294920 | tf_op jit(solution)/shard_map/ppermute | solution.py:214
  130.9 2.9 %collective-permute-start.37 = (bf16[32,1536]{1,0:T(8,128)(2,1)S(1)}, bf16[32,1536]{1,0:T(8,128)(2,1)S(1)}, u32[]{:S(2)}, u32[]{:S(2)}) collective-permute-start(bf16[32,1536]{1,0:T(8,128)(2,1)S(1)} %get-tuple-element.128), channel_id=1, source_target_pairs={{0,2},{1,3},{2,0},{3,1},{4,6},{5,7},{6,4},{7,5},{8,10},{9,11},{10,... | collective-permute-start | bytes 294920 | tf_op jit(solution)/shard_map/ppermute | solution.py:214
  133.8 0.7 collective-permute-done.46.refs_4_
  134.5 2.2 %collective-permute-start.41 = (bf16[32,1536]{1,0:T(8,128)(2,1)S(1)}, bf16[32,1536]{1,0:T(8,128)(2,1)S(1)}, u32[]{:S(2)}, u32[]{:S(2)}) collective-permute-start(bf16[32,1536]{1,0:T(8,128)(2,1)S(1)} %get-tuple-element.136), channel_id=1, source_target_pairs={{0,6},{1,7},{2,4},{3,5},{4,2},{5,3},{6,0},{7,1},{8,14},{9,15},{10,... | collective-permute-start | bytes 294920 | tf_op jit(solution)/shard_map/ppermute | solution.py:214
  136.7 1.8 %collective-permute-start.42 = (bf16[32,1536]{1,0:T(8,128)(2,1)S(1)}, bf16[32,1536]{1,0:T(8,128)(2,1)S(1)}, u32[]{:S(2)}, u32[]{:S(2)}) collective-permute-start(bf16[32,1536]{1,0:T(8,128)(2,1)S(1)} %get-tuple-element.137), channel_id=1, source_target_pairs={{0,7},{1,6},{2,5},{3,4},{4,3},{5,2},{6,1},{7,0},{8,15},{9,14},{10,... | collective-permute-start | bytes 294920 | tf_op jit(solution)/shard_map/ppermute | solution.py:214
  138.6 1.4 fold_1.1
  139.9 2.9 %collective-permute-start.50 = (bf16[32,1536]{1,0:T(8,128)(2,1)S(1)}, bf16[32,1536]{1,0:T(8,128)(2,1)S(1)}, u32[]{:S(2)}, u32[]{:S(2)}) collective-permute-start(bf16[32,1536]{1,0:T(8,128)(2,1)S(1)} %get-tuple-element.147), channel_id=1, source_target_pairs={{0,7},{1,6},{2,5},{3,4},{4,3},{5,2},{6,1},{7,0},{8,15},{9,14},{10,... | collective-permute-start | bytes 294920 | tf_op jit(solution)/shard_map/ppermute | solution.py:214
  142.9 2.4 %collective-permute-start.52 = (bf16[32,1536]{1,0:T(8,128)(2,1)S(1)}, bf16[32,1536]{1,0:T(8,128)(2,1)S(1)}, u32[]{:S(2)}, u32[]{:S(2)}) collective-permute-start(bf16[32,1536]{1,0:T(8,128)(2,1)S(1)} %get-tuple-element.149), channel_id=1, source_target_pairs={{0,3},{1,5},{2,6},{3,0},{4,7},{5,1},{6,2},{7,4},{8,11},{9,13},{10,... | collective-permute-start | bytes 294920 | tf_op jit(solution)/shard_map/ppermute | solution.py:214
  145.3 0.7 collective-permute-start.53
  146.0 7.1 %collective-permute-start.54 = (bf16[32,1536]{1,0:T(8,128)(2,1)S(1)}, bf16[32,1536]{1,0:T(8,128)(2,1)S(1)}, u32[]{:S(2)}, u32[]{:S(2)}) collective-permute-start(bf16[32,1536]{1,0:T(8,128)(2,1)S(1)} %get-tuple-element.151), channel_id=1, source_target_pairs={{0,2},{1,7},{2,0},{3,6},{4,5},{5,4},{6,3},{7,1},{8,10},{9,15},{10,... | collective-permute-start | bytes 294920 | tf_op jit(solution)/shard_map/ppermute | solution.py:214
  153.1 1.5 collective-permute-start.55
  154.7 0.2 collective-permute-start.56
  154.9 1.7 %back_1.1.back_ref = f32[256,1536]{1,0:T(8,128)S(1)} custom-call(bf16[1,384,1536]{2,1,0:T(8,128)(2,1)S(1)} %copy-done.2, f32[256,1536]{1,0:T(8,128)S(1)} %get-tuple-element.125.factor_ref, bf16[32,1536]{1,0:T(8,128)(2,1)S(1)} %get-tuple-element.126.refs_0_, bf16[32,1536]{1,0:T(8,128)(2,1)S(1)} %collective-permute-done.36.refs_1_, ...), custom_call_target="tpu_custom_call" | custom-call | flops 301989888 | bytes 4718592 | tf_op jit(solution)/shard_map/back_1/pallas_call | solution.py:267
  156.7 5.3 %collective-permute-done.53.refs_4_ = bf16[32,1536]{1,0:T(8,128)(2,1)S(1)} collective-permute-done((bf16[32,1536]{1,0:T(8,128)(2,1)S(1)}, bf16[32,1536]{1,0:T(8,128)(2,1)S(1)}, u32[]{:S(2)}, u32[]{:S(2)}) %collective-permute-start.53) | collective-permute-done | bytes 98336 | tf_op jit(solution)/shard_map/ppermute | solution.py:214
  162.0 1.4 collective-permute-done.56.refs_7_
  163.4 4.1 %result_1.1 = bf16[1,2,256,1536]{3,2,1,0:T(8,128)(2,1)} custom-call(bf16[1,2,256,1536]{3,2,1,0:T(8,128)(2,1)S(1)} %copy-done, f32[1,1536]{1,0:T(1,128)S(1)} %copy-done.8, bf16[1,384,1536]{2,1,0:T(8,128)(2,1)S(1)} %copy-done.1, bf16[1,256,256]{2,1,0:T(8,128)(2,1)S(1)} %copy-done.7, f32[256,1536]{1,0:T(8,128)S(1)} %back_1.1.back_ref, ...), custom_call_target="tpu_custom_call", output_to_operand_aliasing={{}: (15, {})} | custom-call | flops 905969664 | bytes 6291456 | tf_op jit(solution)/shard_map/result_1/pallas_call | solution.py:267
  (90 shorter events, 1.5 us)
Async XLA Ops:
  0.0 13.6 %copy-start.8 = (f32[1,1536]{1,0:T(1,128)S(1)}, f32[1,1536]{1,0:T(1,128)}, u32[]{:S(2)}) copy-start(f32[1,1536]{1,0:T(1,128)} %gain_ref.11) | copy-start | bytes 18436
  0.0 13.6 %copy-start = (bf16[1,2,256,1536]{3,2,1,0:T(8,128)(2,1)S(1)}, bf16[1,2,256,1536]{3,2,1,0:T(8,128)(2,1)}, u32[]{:S(2)}) copy-start(bf16[1,2,256,1536]{3,2,1,0:T(8,128)(2,1)} %x_ref.11) | copy-start | bytes 4718596
  0.0 13.6 %copy-start.2 = (bf16[1,384,1536]{2,1,0:T(8,128)(2,1)S(1)}, bf16[1,384,1536]{2,1,0:T(8,128)(2,1)}, u32[]{:S(2)}) copy-start(bf16[1,384,1536]{2,1,0:T(8,128)(2,1)} %w_gate_ref.7) | copy-start | bytes 3538948
  5.2 14.0 %collective-permute-start = (bf16[32,1536]{1,0:T(8,128)(2,1)}, bf16[32,1536]{1,0:T(8,128)(2,1)S(1)}, u32[]{:S(2)}, u32[]{:S(2)}) collective-permute-start(bf16[32,1536]{1,0:T(8,128)(2,1)} %get-tuple-element.82), channel_id=1, source_target_pairs={{0,7},{1,6},{2,5},{3,4},{4,3},{5,2},{6,1},{7,0},{8,15},{9,14},{10,... | collective-permute-start | bytes 294920 | tf_op jit(solution)/shard_map/ppermute | solution.py:214
  9.9 13.1 %collective-permute-start.1 = (bf16[32,1536]{1,0:T(8,128)(2,1)}, bf16[32,1536]{1,0:T(8,128)(2,1)S(1)}, u32[]{:S(2)}, u32[]{:S(2)}) collective-permute-start(bf16[32,1536]{1,0:T(8,128)(2,1)} %get-tuple-element.83), channel_id=1, source_target_pairs={{0,1},{1,0},{2,4},{3,7},{4,2},{5,6},{6,5},{7,3},{8,9},{9,8},{10,12... | collective-permute-start | bytes 294920 | tf_op jit(solution)/shard_map/ppermute | solution.py:214
  10.4 12.6 %collective-permute-start.2 = (bf16[32,1536]{1,0:T(8,128)(2,1)}, bf16[32,1536]{1,0:T(8,128)(2,1)S(1)}, u32[]{:S(2)}, u32[]{:S(2)}) collective-permute-start(bf16[32,1536]{1,0:T(8,128)(2,1)} %get-tuple-element.84), channel_id=1, source_target_pairs={{0,3},{1,5},{2,6},{3,0},{4,7},{5,1},{6,2},{7,4},{8,11},{9,13},{10,... | collective-permute-start | bytes 294920 | tf_op jit(solution)/shard_map/ppermute | solution.py:214
  10.6 14.6 %collective-permute-start.3 = (bf16[32,1536]{1,0:T(8,128)(2,1)}, bf16[32,1536]{1,0:T(8,128)(2,1)S(1)}, u32[]{:S(2)}, u32[]{:S(2)}) collective-permute-start(bf16[32,1536]{1,0:T(8,128)(2,1)} %get-tuple-element.85), channel_id=1, source_target_pairs={{0,4},{1,2},{2,1},{3,5},{4,0},{5,3},{6,7},{7,6},{8,12},{9,10},{10,... | collective-permute-start | bytes 294920 | tf_op jit(solution)/shard_map/ppermute | solution.py:214
  12.3 19.4 %copy-start.1 = (bf16[1,384,1536]{2,1,0:T(8,128)(2,1)S(1)}, bf16[1,384,1536]{2,1,0:T(8,128)(2,1)}, u32[]{:S(2)}) copy-start(bf16[1,384,1536]{2,1,0:T(8,128)(2,1)} %w_value_ref.3) | copy-start | bytes 3538948
  12.3 13.1 %collective-permute-start.4 = (bf16[32,1536]{1,0:T(8,128)(2,1)}, bf16[32,1536]{1,0:T(8,128)(2,1)S(1)}, u32[]{:S(2)}, u32[]{:S(2)}) collective-permute-start(bf16[32,1536]{1,0:T(8,128)(2,1)} %get-tuple-element.86), channel_id=1, source_target_pairs={{0,2},{1,7},{2,0},{3,6},{4,5},{5,4},{6,3},{7,1},{8,10},{9,15},{10,... | collective-permute-start | bytes 294920 | tf_op jit(solution)/shard_map/ppermute | solution.py:214
  16.0 15.7 %copy-start.7 = (bf16[1,256,256]{2,1,0:T(8,128)(2,1)S(1)}, bf16[1,256,256]{2,1,0:T(8,128)(2,1)}, u32[]{:S(2)}) copy-start(bf16[1,256,256]{2,1,0:T(8,128)(2,1)} %r_ref.7) | copy-start | bytes 393220
  19.3 24.1 %copy-start.10 = (bf16[1,32,64]{2,1,0:T(8,128)(2,1)S(1)}, bf16[1,32,64]{2,1,0:T(8,128)(2,1)}, u32[]{:S(2)}) copy-start(bf16[1,32,64]{2,1,0:T(8,128)(2,1)} %l_ref.3) | copy-start | bytes 12292
  19.3 15.3 %collective-permute-start.5 = (bf16[32,1536]{1,0:T(8,128)(2,1)S(1)}, bf16[32,1536]{1,0:T(8,128)(2,1)S(1)}, u32[]{:S(2)}, u32[]{:S(2)}) collective-permute-start(bf16[32,1536]{1,0:T(8,128)(2,1)S(1)} %copy-done.12), channel_id=1, source_target_pairs={{0,6},{1,4},{2,3},{3,2},{4,1},{5,7},{6,0},{7,5},{8,14},{9,12},{10,... | collective-permute-start | bytes 294920 | tf_op jit(solution)/shard_map/ppermute | solution.py:214
  23.0 11.7 %collective-permute-start.6 = (bf16[32,1536]{1,0:T(8,128)(2,1)S(1)}, bf16[32,1536]{1,0:T(8,128)(2,1)S(1)}, u32[]{:S(2)}, u32[]{:S(2)}) collective-permute-start(bf16[32,1536]{1,0:T(8,128)(2,1)S(1)} %copy-done.11), channel_id=1, source_target_pairs={{0,5},{1,3},{2,7},{3,1},{4,6},{5,0},{6,4},{7,2},{8,13},{9,11},{10,... | collective-permute-start | bytes 294920 | tf_op jit(solution)/shard_map/ppermute | solution.py:214
  23.0 15.2 %collective-permute-start.14 = (bf16[32,1536]{1,0:T(8,128)(2,1)S(1)}, bf16[32,1536]{1,0:T(8,128)(2,1)S(1)}, u32[]{:S(2)}, u32[]{:S(2)}) collective-permute-start(bf16[32,1536]{1,0:T(8,128)(2,1)S(1)} %get-tuple-element.100), channel_id=1, source_target_pairs={{0,7},{1,6},{2,5},{3,4},{4,3},{5,2},{6,1},{7,0},{8,15},{9,14},{10,... | collective-permute-start | bytes 294920 | tf_op jit(solution)/shard_map/ppermute | solution.py:214
  25.2 13.0 %collective-permute-start.15 = (bf16[32,1536]{1,0:T(8,128)(2,1)S(1)}, bf16[32,1536]{1,0:T(8,128)(2,1)S(1)}, u32[]{:S(2)}, u32[]{:S(2)}) collective-permute-start(bf16[32,1536]{1,0:T(8,128)(2,1)S(1)} %get-tuple-element.101), channel_id=1, source_target_pairs={{0,1},{1,0},{2,4},{3,7},{4,2},{5,6},{6,5},{7,3},{8,9},{9,8},{10,12... | collective-permute-start | bytes 294920 | tf_op jit(solution)/shard_map/ppermute | solution.py:214
  25.4 18.2 %copy-start.9 = (bf16[32,1536]{1,0:T(8,128)(2,1)S(1)}, bf16[32,1536]{1,0:T(8,128)(2,1)}, u32[]{:S(2)}) copy-start(bf16[32,1536]{1,0:T(8,128)(2,1)} %get-tuple-element.81.refs_0_) | copy-start | bytes 294916
  25.4 18.0 %collective-permute-start.16 = (bf16[32,1536]{1,0:T(8,128)(2,1)S(1)}, bf16[32,1536]{1,0:T(8,128)(2,1)S(1)}, u32[]{:S(2)}, u32[]{:S(2)}) collective-permute-start(bf16[32,1536]{1,0:T(8,128)(2,1)S(1)} %get-tuple-element.102), channel_id=1, source_target_pairs={{0,3},{1,5},{2,6},{3,0},{4,7},{5,1},{6,2},{7,4},{8,11},{9,13},{10,... | collective-permute-start | bytes 294920 | tf_op jit(solution)/shard_map/ppermute | solution.py:214
  34.6 10.3 %collective-permute-start.17 = (bf16[32,1536]{1,0:T(8,128)(2,1)S(1)}, bf16[32,1536]{1,0:T(8,128)(2,1)S(1)}, u32[]{:S(2)}, u32[]{:S(2)}) collective-permute-start(bf16[32,1536]{1,0:T(8,128)(2,1)S(1)} %get-tuple-element.103), channel_id=1, source_target_pairs={{0,4},{1,2},{2,1},{3,5},{4,0},{5,3},{6,7},{7,6},{8,12},{9,10},{10,... | collective-permute-start | bytes 294920 | tf_op jit(solution)/shard_map/ppermute | solution.py:214
  34.7 12.4 %collective-permute-start.18 = (bf16[32,1536]{1,0:T(8,128)(2,1)S(1)}, bf16[32,1536]{1,0:T(8,128)(2,1)S(1)}, u32[]{:S(2)}, u32[]{:S(2)}) collective-permute-start(bf16[32,1536]{1,0:T(8,128)(2,1)S(1)} %get-tuple-element.104), channel_id=1, source_target_pairs={{0,2},{1,7},{2,0},{3,6},{4,5},{5,4},{6,3},{7,1},{8,10},{9,15},{10,... | collective-permute-start | bytes 294920 | tf_op jit(solution)/shard_map/ppermute | solution.py:214
  38.2 8.9 %collective-permute-start.19 = (bf16[32,1536]{1,0:T(8,128)(2,1)S(1)}, bf16[32,1536]{1,0:T(8,128)(2,1)S(1)}, u32[]{:S(2)}, u32[]{:S(2)}) collective-permute-start(bf16[32,1536]{1,0:T(8,128)(2,1)S(1)} %get-tuple-element.105), channel_id=1, source_target_pairs={{0,6},{1,4},{2,3},{3,2},{4,1},{5,7},{6,0},{7,5},{8,14},{9,12},{10,... | collective-permute-start | bytes 294920 | tf_op jit(solution)/shard_map/ppermute | solution.py:214
  38.2 10.3 %collective-permute-start.20 = (bf16[32,1536]{1,0:T(8,128)(2,1)S(1)}, bf16[32,1536]{1,0:T(8,128)(2,1)S(1)}, u32[]{:S(2)}, u32[]{:S(2)}) collective-permute-start(bf16[32,1536]{1,0:T(8,128)(2,1)S(1)} %get-tuple-element.106), channel_id=1, source_target_pairs={{0,5},{1,3},{2,7},{3,1},{4,6},{5,0},{6,4},{7,2},{8,13},{9,11},{10,... | collective-permute-start | bytes 294920 | tf_op jit(solution)/shard_map/ppermute | solution.py:214
  43.4 7.9 %collective-permute-start.29 = (bf16[32,1536]{1,0:T(8,128)(2,1)S(1)}, bf16[32,1536]{1,0:T(8,128)(2,1)S(1)}, u32[]{:S(2)}, u32[]{:S(2)}) collective-permute-start(bf16[32,1536]{1,0:T(8,128)(2,1)S(1)} %get-tuple-element.116), channel_id=1, source_target_pairs={{0,1},{1,0},{2,3},{3,2},{4,5},{5,4},{6,7},{7,6},{8,9},{9,8},{10,11... | collective-permute-start | bytes 294920 | tf_op jit(solution)/shard_map/ppermute | solution.py:214
  44.9 8.8 %collective-permute-start.30 = (bf16[32,1536]{1,0:T(8,128)(2,1)S(1)}, bf16[32,1536]{1,0:T(8,128)(2,1)S(1)}, u32[]{:S(2)}, u32[]{:S(2)}) collective-permute-start(bf16[32,1536]{1,0:T(8,128)(2,1)S(1)} %get-tuple-element.117), channel_id=1, source_target_pairs={{0,2},{1,3},{2,0},{3,1},{4,6},{5,7},{6,4},{7,5},{8,10},{9,11},{10,... | collective-permute-start | bytes 294920 | tf_op jit(solution)/shard_map/ppermute | solution.py:214
  47.1 9.8 %collective-permute-start.10 = (bf16[32,1536]{1,0:T(8,128)(2,1)S(1)}, bf16[32,1536]{1,0:T(8,128)(2,1)S(1)}, u32[]{:S(2)}, u32[]{:S(2)}) collective-permute-start(bf16[32,1536]{1,0:T(8,128)(2,1)S(1)} %get-tuple-element.93), channel_id=1, source_target_pairs={{0,4},{1,2},{2,1},{3,5},{4,0},{5,3},{6,7},{7,6},{8,12},{9,10},{10,... | collective-permute-start | bytes 294920 | tf_op jit(solution)/shard_map/ppermute | solution.py:214
  47.1 10.6 %collective-permute-start.11 = (bf16[32,1536]{1,0:T(8,128)(2,1)S(1)}, bf16[32,1536]{1,0:T(8,128)(2,1)S(1)}, u32[]{:S(2)}, u32[]{:S(2)}) collective-permute-start(bf16[32,1536]{1,0:T(8,128)(2,1)S(1)} %get-tuple-element.94), channel_id=1, source_target_pairs={{0,2},{1,7},{2,0},{3,6},{4,5},{5,4},{6,3},{7,1},{8,10},{9,15},{10,... | collective-permute-start | bytes 294920 | tf_op jit(solution)/shard_map/ppermute | solution.py:214
  48.5 12.4 %collective-permute-start.12 = (bf16[32,1536]{1,0:T(8,128)(2,1)S(1)}, bf16[32,1536]{1,0:T(8,128)(2,1)S(1)}, u32[]{:S(2)}, u32[]{:S(2)}) collective-permute-start(bf16[32,1536]{1,0:T(8,128)(2,1)S(1)} %get-tuple-element.95), channel_id=1, source_target_pairs={{0,6},{1,4},{2,3},{3,2},{4,1},{5,7},{6,0},{7,5},{8,14},{9,12},{10,... | collective-permute-start | bytes 294920 | tf_op jit(solution)/shard_map/ppermute | solution.py:214
  51.3 13.7 %collective-permute-start.13 = (bf16[32,1536]{1,0:T(8,128)(2,1)S(1)}, bf16[32,1536]{1,0:T(8,128)(2,1)S(1)}, u32[]{:S(2)}, u32[]{:S(2)}) collective-permute-start(bf16[32,1536]{1,0:T(8,128)(2,1)S(1)} %get-tuple-element.96), channel_id=1, source_target_pairs={{0,5},{1,3},{2,7},{3,1},{4,6},{5,0},{6,4},{7,2},{8,13},{9,11},{10,... | collective-permute-start | bytes 294920 | tf_op jit(solution)/shard_map/ppermute | solution.py:214
  53.6 12.8 %collective-permute-start.7 = (bf16[32,1536]{1,0:T(8,128)(2,1)S(1)}, bf16[32,1536]{1,0:T(8,128)(2,1)S(1)}, u32[]{:S(2)}, u32[]{:S(2)}) collective-permute-start(bf16[32,1536]{1,0:T(8,128)(2,1)S(1)} %get-tuple-element.90), channel_id=1, source_target_pairs={{0,7},{1,6},{2,5},{3,4},{4,3},{5,2},{6,1},{7,0},{8,15},{9,14},{10,... | collective-permute-start | bytes 294920 | tf_op jit(solution)/shard_map/ppermute | solution.py:214
  56.9 9.8 %collective-permute-start.8 = (bf16[32,1536]{1,0:T(8,128)(2,1)S(1)}, bf16[32,1536]{1,0:T(8,128)(2,1)S(1)}, u32[]{:S(2)}, u32[]{:S(2)}) collective-permute-start(bf16[32,1536]{1,0:T(8,128)(2,1)S(1)} %get-tuple-element.91), channel_id=1, source_target_pairs={{0,1},{1,0},{2,4},{3,7},{4,2},{5,6},{6,5},{7,3},{8,9},{9,8},{10,12... | collective-permute-start | bytes 294920 | tf_op jit(solution)/shard_map/ppermute | solution.py:214
  57.7 12.4 %collective-permute-start.9 = (bf16[32,1536]{1,0:T(8,128)(2,1)S(1)}, bf16[32,1536]{1,0:T(8,128)(2,1)S(1)}, u32[]{:S(2)}, u32[]{:S(2)}) collective-permute-start(bf16[32,1536]{1,0:T(8,128)(2,1)S(1)} %get-tuple-element.92), channel_id=1, source_target_pairs={{0,3},{1,5},{2,6},{3,0},{4,7},{5,1},{6,2},{7,4},{8,11},{9,13},{10,... | collective-permute-start | bytes 294920 | tf_op jit(solution)/shard_map/ppermute | solution.py:214
  60.9 9.7 %collective-permute-start.21 = (bf16[32,1536]{1,0:T(8,128)(2,1)S(1)}, bf16[32,1536]{1,0:T(8,128)(2,1)S(1)}, u32[]{:S(2)}, u32[]{:S(2)}) collective-permute-start(bf16[32,1536]{1,0:T(8,128)(2,1)S(1)} %get-tuple-element.108), channel_id=1, source_target_pairs={{0,7},{1,6},{2,5},{3,4},{4,3},{5,2},{6,1},{7,0},{8,15},{9,14},{10,... | collective-permute-start | bytes 294920 | tf_op jit(solution)/shard_map/ppermute | solution.py:214
  65.0 9.2 %collective-permute-start.22 = (bf16[32,1536]{1,0:T(8,128)(2,1)S(1)}, bf16[32,1536]{1,0:T(8,128)(2,1)S(1)}, u32[]{:S(2)}, u32[]{:S(2)}) collective-permute-start(bf16[32,1536]{1,0:T(8,128)(2,1)S(1)} %get-tuple-element.109), channel_id=1, source_target_pairs={{0,1},{1,0},{2,4},{3,7},{4,2},{5,6},{6,5},{7,3},{8,9},{9,8},{10,12... | collective-permute-start | bytes 294920 | tf_op jit(solution)/shard_map/ppermute | solution.py:214
  66.5 11.0 %collective-permute-start.23 = (bf16[32,1536]{1,0:T(8,128)(2,1)S(1)}, bf16[32,1536]{1,0:T(8,128)(2,1)S(1)}, u32[]{:S(2)}, u32[]{:S(2)}) collective-permute-start(bf16[32,1536]{1,0:T(8,128)(2,1)S(1)} %get-tuple-element.110), channel_id=1, source_target_pairs={{0,3},{1,5},{2,6},{3,0},{4,7},{5,1},{6,2},{7,4},{8,11},{9,13},{10,... | collective-permute-start | bytes 294920 | tf_op jit(solution)/shard_map/ppermute | solution.py:214
  66.7 15.7 %collective-permute-start.24 = (bf16[32,1536]{1,0:T(8,128)(2,1)S(1)}, bf16[32,1536]{1,0:T(8,128)(2,1)S(1)}, u32[]{:S(2)}, u32[]{:S(2)}) collective-permute-start(bf16[32,1536]{1,0:T(8,128)(2,1)S(1)} %get-tuple-element.111), channel_id=1, source_target_pairs={{0,4},{1,2},{2,1},{3,5},{4,0},{5,3},{6,7},{7,6},{8,12},{9,10},{10,... | collective-permute-start | bytes 294920 | tf_op jit(solution)/shard_map/ppermute | solution.py:214
  70.1 13.8 %collective-permute-start.25 = (bf16[32,1536]{1,0:T(8,128)(2,1)S(1)}, bf16[32,1536]{1,0:T(8,128)(2,1)S(1)}, u32[]{:S(2)}, u32[]{:S(2)}) collective-permute-start(bf16[32,1536]{1,0:T(8,128)(2,1)S(1)} %get-tuple-element.112), channel_id=1, source_target_pairs={{0,2},{1,7},{2,0},{3,6},{4,5},{5,4},{6,3},{7,1},{8,10},{9,15},{10,... | collective-permute-start | bytes 294920 | tf_op jit(solution)/shard_map/ppermute | solution.py:214
  70.5 19.0 %collective-permute-start.26 = (bf16[32,1536]{1,0:T(8,128)(2,1)S(1)}, bf16[32,1536]{1,0:T(8,128)(2,1)S(1)}, u32[]{:S(2)}, u32[]{:S(2)}) collective-permute-start(bf16[32,1536]{1,0:T(8,128)(2,1)S(1)} %get-tuple-element.113), channel_id=1, source_target_pairs={{0,6},{1,4},{2,3},{3,2},{4,1},{5,7},{6,0},{7,5},{8,14},{9,12},{10,... | collective-permute-start | bytes 294920 | tf_op jit(solution)/shard_map/ppermute | solution.py:214
  74.2 15.3 %collective-permute-start.27 = (bf16[32,1536]{1,0:T(8,128)(2,1)S(1)}, bf16[32,1536]{1,0:T(8,128)(2,1)S(1)}, u32[]{:S(2)}, u32[]{:S(2)}) collective-permute-start(bf16[32,1536]{1,0:T(8,128)(2,1)S(1)} %get-tuple-element.114), channel_id=1, source_target_pairs={{0,5},{1,3},{2,7},{3,1},{4,6},{5,0},{6,4},{7,2},{8,13},{9,11},{10,... | collective-permute-start | bytes 294920 | tf_op jit(solution)/shard_map/ppermute | solution.py:214
  77.5 21.7 %collective-permute-start.31 = (bf16[32,1536]{1,0:T(8,128)(2,1)S(1)}, bf16[32,1536]{1,0:T(8,128)(2,1)S(1)}, u32[]{:S(2)}, u32[]{:S(2)}) collective-permute-start(bf16[32,1536]{1,0:T(8,128)(2,1)S(1)} %get-tuple-element.118), channel_id=1, source_target_pairs={{0,3},{1,2},{2,1},{3,0},{4,7},{5,6},{6,5},{7,4},{8,11},{9,10},{10,... | collective-permute-start | bytes 294920 | tf_op jit(solution)/shard_map/ppermute | solution.py:214
  82.4 19.0 %collective-permute-start.32 = (bf16[32,1536]{1,0:T(8,128)(2,1)S(1)}, bf16[32,1536]{1,0:T(8,128)(2,1)S(1)}, u32[]{:S(2)}, u32[]{:S(2)}) collective-permute-start(bf16[32,1536]{1,0:T(8,128)(2,1)S(1)} %get-tuple-element.119), channel_id=1, source_target_pairs={{0,4},{1,5},{2,6},{3,7},{4,0},{5,1},{6,2},{7,3},{8,12},{9,13},{10,... | collective-permute-start | bytes 294920 | tf_op jit(solution)/shard_map/ppermute | solution.py:214
  83.9 17.5 %collective-permute-start.33 = (bf16[32,1536]{1,0:T(8,128)(2,1)S(1)}, bf16[32,1536]{1,0:T(8,128)(2,1)S(1)}, u32[]{:S(2)}, u32[]{:S(2)}) collective-permute-start(bf16[32,1536]{1,0:T(8,128)(2,1)S(1)} %get-tuple-element.120), channel_id=1, source_target_pairs={{0,5},{1,4},{2,7},{3,6},{4,1},{5,0},{6,3},{7,2},{8,13},{9,12},{10,... | collective-permute-start | bytes 294920 | tf_op jit(solution)/shard_map/ppermute | solution.py:214
  89.5 12.0 %collective-permute-start.34 = (bf16[32,1536]{1,0:T(8,128)(2,1)S(1)}, bf16[32,1536]{1,0:T(8,128)(2,1)S(1)}, u32[]{:S(2)}, u32[]{:S(2)}) collective-permute-start(bf16[32,1536]{1,0:T(8,128)(2,1)S(1)} %get-tuple-element.121), channel_id=1, source_target_pairs={{0,6},{1,7},{2,4},{3,5},{4,2},{5,3},{6,0},{7,1},{8,14},{9,15},{10,... | collective-permute-start | bytes 294920 | tf_op jit(solution)/shard_map/ppermute | solution.py:214
  89.5 12.0 %collective-permute-start.35 = (bf16[32,1536]{1,0:T(8,128)(2,1)S(1)}, bf16[32,1536]{1,0:T(8,128)(2,1)S(1)}, u32[]{:S(2)}, u32[]{:S(2)}) collective-permute-start(bf16[32,1536]{1,0:T(8,128)(2,1)S(1)} %get-tuple-element.122), channel_id=1, source_target_pairs={{0,7},{1,6},{2,5},{3,4},{4,3},{5,2},{6,1},{7,0},{8,15},{9,14},{10,... | collective-permute-start | bytes 294920 | tf_op jit(solution)/shard_map/ppermute | solution.py:214
  99.2 11.5 %collective-permute-start.28 = (bf16[256,1536]{1,0:T(8,128)(2,1)S(1)}, bf16[256,1536]{1,0:T(8,128)(2,1)S(1)}, u32[]{:S(2)}, u32[]{:S(2)}) collective-permute-start(bf16[256,1536]{1,0:T(8,128)(2,1)S(1)} %get-tuple-element.115), channel_id=1, source_target_pairs={{8,0},{16,8},{24,16},{9,1},{17,9},{25,17},{10,2},{18,10},{26,18},{... | collective-permute-start | bytes 2359304 | tf_op jit(solution)/shard_map/ppermute | solution.py:374
  102.7 11.4 %collective-permute-start.40 = (bf16[32,1536]{1,0:T(8,128)(2,1)S(1)}, bf16[32,1536]{1,0:T(8,128)(2,1)S(1)}, u32[]{:S(2)}, u32[]{:S(2)}) collective-permute-start(bf16[32,1536]{1,0:T(8,128)(2,1)S(1)} %get-tuple-element.134), channel_id=1, source_target_pairs={{0,5},{1,4},{2,7},{3,6},{4,1},{5,0},{6,3},{7,2},{8,13},{9,12},{10,... | collective-permute-start | bytes 294920 | tf_op jit(solution)/shard_map/ppermute | solution.py:214
  104.7 11.7 %collective-permute-start.39 = (bf16[32,1536]{1,0:T(8,128)(2,1)S(1)}, bf16[32,1536]{1,0:T(8,128)(2,1)S(1)}, u32[]{:S(2)}, u32[]{:S(2)}) collective-permute-start(bf16[32,1536]{1,0:T(8,128)(2,1)S(1)} %get-tuple-element.131), channel_id=1, source_target_pairs={{0,4},{1,5},{2,6},{3,7},{4,0},{5,1},{6,2},{7,3},{8,12},{9,13},{10,... | collective-permute-start | bytes 294920 | tf_op jit(solution)/shard_map/ppermute | solution.py:214
  114.1 7.7 %collective-permute-start.48 = (bf16[32,1536]{1,0:T(8,128)(2,1)S(1)}, bf16[32,1536]{1,0:T(8,128)(2,1)S(1)}, u32[]{:S(2)}, u32[]{:S(2)}) collective-permute-start(bf16[32,1536]{1,0:T(8,128)(2,1)S(1)} %get-tuple-element.144), channel_id=1, source_target_pairs={{0,6},{1,4},{2,3},{3,2},{4,1},{5,7},{6,0},{7,5},{8,14},{9,12},{10,... | collective-permute-start | bytes 294920 | tf_op jit(solution)/shard_map/ppermute | solution.py:214
  116.5 11.5 %collective-permute-start.49 = (bf16[32,1536]{1,0:T(8,128)(2,1)S(1)}, bf16[32,1536]{1,0:T(8,128)(2,1)S(1)}, u32[]{:S(2)}, u32[]{:S(2)}) collective-permute-start(bf16[32,1536]{1,0:T(8,128)(2,1)S(1)} %get-tuple-element.145), channel_id=1, source_target_pairs={{0,5},{1,3},{2,7},{3,1},{4,6},{5,0},{6,4},{7,2},{8,13},{9,11},{10,... | collective-permute-start | bytes 294920 | tf_op jit(solution)/shard_map/ppermute | solution.py:214
  116.5 11.5 %collective-permute-start.43 = (bf16[32,1536]{1,0:T(8,128)(2,1)S(1)}, bf16[32,1536]{1,0:T(8,128)(2,1)S(1)}, u32[]{:S(2)}, u32[]{:S(2)}) collective-permute-start(bf16[32,1536]{1,0:T(8,128)(2,1)S(1)} %get-tuple-element.139), channel_id=1, source_target_pairs={{0,7},{1,6},{2,5},{3,4},{4,3},{5,2},{6,1},{7,0},{8,15},{9,14},{10,... | collective-permute-start | bytes 294920 | tf_op jit(solution)/shard_map/ppermute | solution.py:214
  118.5 12.3 %collective-permute-start.44 = (bf16[32,1536]{1,0:T(8,128)(2,1)S(1)}, bf16[32,1536]{1,0:T(8,128)(2,1)S(1)}, u32[]{:S(2)}, u32[]{:S(2)}) collective-permute-start(bf16[32,1536]{1,0:T(8,128)(2,1)S(1)} %get-tuple-element.140), channel_id=1, source_target_pairs={{0,1},{1,0},{2,4},{3,7},{4,2},{5,6},{6,5},{7,3},{8,9},{9,8},{10,12... | collective-permute-start | bytes 294920 | tf_op jit(solution)/shard_map/ppermute | solution.py:214
  120.9 12.9 %collective-permute-start.45 = (bf16[32,1536]{1,0:T(8,128)(2,1)S(1)}, bf16[32,1536]{1,0:T(8,128)(2,1)S(1)}, u32[]{:S(2)}, u32[]{:S(2)}) collective-permute-start(bf16[32,1536]{1,0:T(8,128)(2,1)S(1)} %get-tuple-element.141), channel_id=1, source_target_pairs={{0,3},{1,5},{2,6},{3,0},{4,7},{5,1},{6,2},{7,4},{8,11},{9,13},{10,... | collective-permute-start | bytes 294920 | tf_op jit(solution)/shard_map/ppermute | solution.py:214
  121.8 12.7 %collective-permute-start.46 = (bf16[32,1536]{1,0:T(8,128)(2,1)S(1)}, bf16[32,1536]{1,0:T(8,128)(2,1)S(1)}, u32[]{:S(2)}, u32[]{:S(2)}) collective-permute-start(bf16[32,1536]{1,0:T(8,128)(2,1)S(1)} %get-tuple-element.142), channel_id=1, source_target_pairs={{0,4},{1,2},{2,1},{3,5},{4,0},{5,3},{6,7},{7,6},{8,12},{9,10},{10,... | collective-permute-start | bytes 294920 | tf_op jit(solution)/shard_map/ppermute | solution.py:214
  127.9 8.8 %collective-permute-start.47 = (bf16[32,1536]{1,0:T(8,128)(2,1)S(1)}, bf16[32,1536]{1,0:T(8,128)(2,1)S(1)}, u32[]{:S(2)}, u32[]{:S(2)}) collective-permute-start(bf16[32,1536]{1,0:T(8,128)(2,1)S(1)} %get-tuple-element.143), channel_id=1, source_target_pairs={{0,2},{1,7},{2,0},{3,6},{4,5},{5,4},{6,3},{7,1},{8,10},{9,15},{10,... | collective-permute-start | bytes 294920 | tf_op jit(solution)/shard_map/ppermute | solution.py:214
  128.0 12.0 %collective-permute-start.36 = (bf16[32,1536]{1,0:T(8,128)(2,1)S(1)}, bf16[32,1536]{1,0:T(8,128)(2,1)S(1)}, u32[]{:S(2)}, u32[]{:S(2)}) collective-permute-start(bf16[32,1536]{1,0:T(8,128)(2,1)S(1)} %get-tuple-element.127), channel_id=1, source_target_pairs={{0,1},{1,0},{2,3},{3,2},{4,5},{5,4},{6,7},{7,6},{8,9},{9,8},{10,11... | collective-permute-start | bytes 294920 | tf_op jit(solution)/shard_map/ppermute | solution.py:214
  130.9 12.0 %collective-permute-start.37 = (bf16[32,1536]{1,0:T(8,128)(2,1)S(1)}, bf16[32,1536]{1,0:T(8,128)(2,1)S(1)}, u32[]{:S(2)}, u32[]{:S(2)}) collective-permute-start(bf16[32,1536]{1,0:T(8,128)(2,1)S(1)} %get-tuple-element.128), channel_id=1, source_target_pairs={{0,2},{1,3},{2,0},{3,1},{4,6},{5,7},{6,4},{7,5},{8,10},{9,11},{10,... | collective-permute-start | bytes 294920 | tf_op jit(solution)/shard_map/ppermute | solution.py:214
  133.8 9.1 %collective-permute-start.38 = (bf16[32,1536]{1,0:T(8,128)(2,1)S(1)}, bf16[32,1536]{1,0:T(8,128)(2,1)S(1)}, u32[]{:S(2)}, u32[]{:S(2)}) collective-permute-start(bf16[32,1536]{1,0:T(8,128)(2,1)S(1)} %get-tuple-element.129), channel_id=1, source_target_pairs={{0,3},{1,2},{2,1},{3,0},{4,7},{5,6},{6,5},{7,4},{8,11},{9,10},{10,... | collective-permute-start | bytes 294920 | tf_op jit(solution)/shard_map/ppermute | solution.py:214
  134.5 10.8 %collective-permute-start.41 = (bf16[32,1536]{1,0:T(8,128)(2,1)S(1)}, bf16[32,1536]{1,0:T(8,128)(2,1)S(1)}, u32[]{:S(2)}, u32[]{:S(2)}) collective-permute-start(bf16[32,1536]{1,0:T(8,128)(2,1)S(1)} %get-tuple-element.136), channel_id=1, source_target_pairs={{0,6},{1,7},{2,4},{3,5},{4,2},{5,3},{6,0},{7,1},{8,14},{9,15},{10,... | collective-permute-start | bytes 294920 | tf_op jit(solution)/shard_map/ppermute | solution.py:214
  136.7 9.3 %collective-permute-start.42 = (bf16[32,1536]{1,0:T(8,128)(2,1)S(1)}, bf16[32,1536]{1,0:T(8,128)(2,1)S(1)}, u32[]{:S(2)}, u32[]{:S(2)}) collective-permute-start(bf16[32,1536]{1,0:T(8,128)(2,1)S(1)} %get-tuple-element.137), channel_id=1, source_target_pairs={{0,7},{1,6},{2,5},{3,4},{4,3},{5,2},{6,1},{7,0},{8,15},{9,14},{10,... | collective-permute-start | bytes 294920 | tf_op jit(solution)/shard_map/ppermute | solution.py:214
  139.9 13.2 %collective-permute-start.50 = (bf16[32,1536]{1,0:T(8,128)(2,1)S(1)}, bf16[32,1536]{1,0:T(8,128)(2,1)S(1)}, u32[]{:S(2)}, u32[]{:S(2)}) collective-permute-start(bf16[32,1536]{1,0:T(8,128)(2,1)S(1)} %get-tuple-element.147), channel_id=1, source_target_pairs={{0,7},{1,6},{2,5},{3,4},{4,3},{5,2},{6,1},{7,0},{8,15},{9,14},{10,... | collective-permute-start | bytes 294920 | tf_op jit(solution)/shard_map/ppermute | solution.py:214
  142.9 11.8 %collective-permute-start.51 = (bf16[32,1536]{1,0:T(8,128)(2,1)S(1)}, bf16[32,1536]{1,0:T(8,128)(2,1)S(1)}, u32[]{:S(2)}, u32[]{:S(2)}) collective-permute-start(bf16[32,1536]{1,0:T(8,128)(2,1)S(1)} %get-tuple-element.148), channel_id=1, source_target_pairs={{0,1},{1,0},{2,4},{3,7},{4,2},{5,6},{6,5},{7,3},{8,9},{9,8},{10,12... | collective-permute-start | bytes 294920 | tf_op jit(solution)/shard_map/ppermute | solution.py:214
  142.9 13.8 %collective-permute-start.52 = (bf16[32,1536]{1,0:T(8,128)(2,1)S(1)}, bf16[32,1536]{1,0:T(8,128)(2,1)S(1)}, u32[]{:S(2)}, u32[]{:S(2)}) collective-permute-start(bf16[32,1536]{1,0:T(8,128)(2,1)S(1)} %get-tuple-element.149), channel_id=1, source_target_pairs={{0,3},{1,5},{2,6},{3,0},{4,7},{5,1},{6,2},{7,4},{8,11},{9,13},{10,... | collective-permute-start | bytes 294920 | tf_op jit(solution)/shard_map/ppermute | solution.py:214
  145.3 16.7 %collective-permute-start.53 = (bf16[32,1536]{1,0:T(8,128)(2,1)S(1)}, bf16[32,1536]{1,0:T(8,128)(2,1)S(1)}, u32[]{:S(2)}, u32[]{:S(2)}) collective-permute-start(bf16[32,1536]{1,0:T(8,128)(2,1)S(1)} %get-tuple-element.150), channel_id=1, source_target_pairs={{0,4},{1,2},{2,1},{3,5},{4,0},{5,3},{6,7},{7,6},{8,12},{9,10},{10,... | collective-permute-start | bytes 294920 | tf_op jit(solution)/shard_map/ppermute | solution.py:214
  146.0 15.9 %collective-permute-start.54 = (bf16[32,1536]{1,0:T(8,128)(2,1)S(1)}, bf16[32,1536]{1,0:T(8,128)(2,1)S(1)}, u32[]{:S(2)}, u32[]{:S(2)}) collective-permute-start(bf16[32,1536]{1,0:T(8,128)(2,1)S(1)} %get-tuple-element.151), channel_id=1, source_target_pairs={{0,2},{1,7},{2,0},{3,6},{4,5},{5,4},{6,3},{7,1},{8,10},{9,15},{10,... | collective-permute-start | bytes 294920 | tf_op jit(solution)/shard_map/ppermute | solution.py:214
  153.1 8.8 %collective-permute-start.55 = (bf16[32,1536]{1,0:T(8,128)(2,1)S(1)}, bf16[32,1536]{1,0:T(8,128)(2,1)S(1)}, u32[]{:S(2)}, u32[]{:S(2)}) collective-permute-start(bf16[32,1536]{1,0:T(8,128)(2,1)S(1)} %get-tuple-element.152), channel_id=1, source_target_pairs={{0,6},{1,4},{2,3},{3,2},{4,1},{5,7},{6,0},{7,5},{8,14},{9,12},{10,... | collective-permute-start | bytes 294920 | tf_op jit(solution)/shard_map/ppermute | solution.py:214
  154.7 8.7 %collective-permute-start.56 = (bf16[32,1536]{1,0:T(8,128)(2,1)S(1)}, bf16[32,1536]{1,0:T(8,128)(2,1)S(1)}, u32[]{:S(2)}, u32[]{:S(2)}) collective-permute-start(bf16[32,1536]{1,0:T(8,128)(2,1)S(1)} %get-tuple-element.153), channel_id=1, source_target_pairs={{0,5},{1,3},{2,7},{3,1},{4,6},{5,0},{6,4},{7,2},{8,13},{9,11},{10,... | collective-permute-start | bytes 294920 | tf_op jit(solution)/shard_map/ppermute | solution.py:214
  (6 other events, 35.8 us)

commit v6 on v2

--- a/solution.py
+++ b/solution.py
@@ -162,6 +162,14 @@
     spread_slots(outs, dot(m_ref[...], stacked_slots(ins), over))
 
 
+def mix_first_kernel(count, x_ref, gain_ref, w_ref, r_ref, m_ref, *refs):
+    ins, outs, (q_ref, wide_ref) = refs[:count], refs[count : 2 * count], refs[2 * count :]
+    spread_slots([out.at[0] for out in outs], dot(m_ref[...], stacked_slots(ins)))
+    normed = normed_block(pl.program_id(0), x_ref, gain_ref, q_ref, w_ref.shape[1])
+    wide_ref[...] = first_of(normed, w_ref, r_ref)
+    split([out.at[1] for out in outs], wide_ref)
+
+
 def back_kernel(count, w_gate_ref, factor_ref, *refs):
     mixed, (out_ref, wide_ref) = refs[:count], refs[count:]
     gate_grad = (factor_ref[...] * joined(mixed, wide_ref).astype(F32)).astype(BF16)
@@ -245,6 +253,9 @@
     square = pl.BlockSpec((None, rows, rows), lambda j: (0, 0, 0))
     small = pl.BlockSpec((None, size, count * count), lambda j: (0, 0, 0))
     slots = [pl.BlockSpec((size, block), lambda j: (0, j))] * count
+    pairs = [pl.BlockSpec((2, size, block), lambda j: (0, 0, j))] * count
+    upper = [pl.BlockSpec((None, size, block), lambda j: (0, 0, j))] * count
+    lower = [pl.BlockSpec((None, size, block), lambda j: (1, 0, j))] * count
     anywhere = pl.BlockSpec(memory_space=pl.ANY)
     x_at = [
         pl.BlockSpec((None, None, rows, width), lambda j: (0, 0, 0, 0)),
@@ -252,6 +263,7 @@
     ]
 
     slot_shapes = [jax.ShapeDtypeStruct((size, width), BF16)] * count
+    pair_shapes = [jax.ShapeDtypeStruct((2, size, width), BF16)] * count
     plain = jax.ShapeDtypeStruct((rows, width), BF16)
     exact = jax.ShapeDtypeStruct((rows, width), F32)
     output = jax.ShapeDtypeStruct(saved_inputs.shape, BF16)
@@ -309,22 +321,22 @@
         )
         return parts, factor
 
-    def mix(name, parts, transposed):
+    def mix(name, parts, transposed, slots_in=slots):
         return call(
             name,
             functools.partial(mix_kernel, count, transposed),
             (1, 2),
-            [(square_plain, matrix), *zip(slots, parts)],
+            [(square_plain, matrix), *zip(slots_in, parts)],
             slots_out,
             [],
         )
 
-    def back(tick, mixed, factor):
+    def back(tick, mixed, factor, slots_in=slots):
         return call(
             f"back_{tick}",
             functools.partial(back_kernel, count),
             (1, 6),
-            [gate_in, (cut, factor), *zip(slots, mixed)],
+            [gate_in, (cut, factor), *zip(slots_in, mixed)],
             [(cut, exact)],
             [joining],
         )[0]
@@ -361,16 +373,28 @@
     )
     parts, factor_0 = grads(0, [(cut3, arrived_grad)])
     grad_0 = Exchange(parts).send(every)
-    mix_0 = Exchange(mix("mix_0", first_0.all(), False)).send(every)
+    there = Exchange(
+        call(
+            "mixfirst_0",
+            functools.partial(mix_first_kernel, count),
+            (3, 6),
+            [
+                (x_at[1], saved_inputs), gains, value_in, r_in, (square_plain, matrix),
+                *zip(slots, first_0.all()),
+            ],
+            [*zip(pairs, pair_shapes)],
+            [column, wide],
+        )
+    ).send(every)
     fold_0 = Exchange(mix("fold_0", grad_0.all(), True)).send(every)
-    gate_0 = back(0, mix_0.all(), factor_0)
-    first_1 = Exchange(first(1))
-    gate_0, first_1.parts[0] = lax.optimization_barrier((gate_0, first_1.parts[0]))
-    first_1.send(every)
+    gate_0 = back(0, there.all(), factor_0, upper)
+    mix_1 = Exchange(mix("mix_1", there.all(), False, lower))
+    gate_0, mix_1.parts[0] = lax.optimization_barrier((gate_0, mix_1.parts[0]))
+    mix_1.got[0] = mix_1.parts[0]
+    mix_1.send(every)
     stacked, result_0 = result(0, gate_0, fold_0.all(), [(whole3, arrived_grad)], None)
-    result_0 = tied(result_0, [(first_1, slot) for slot in every[: min(3, count // 2)]])
+    result_0 = tied(result_0, [(mix_1, slot) for slot in every[: min(4, count // 2)]])
     passed = lax.ppermute(result_0, "pipe", [(s, s - 1) for s in range(1, pipe)])
-    mix_1 = Exchange(mix("mix_1", first_1.all(), False)).send(every)
     parts, factor_1 = grads(1, [(cut, passed), (cut3, loss_grad)])
     grad_1 = Exchange(parts).send(every)
     fold_1 = Exchange(mix("fold_1", grad_1.all(), True)).send(every)

time: 167 us -> 171 us (1.024)
  waiting for transfers between devices: 13.3 us -> 25.8 us
  starting transfers between devices: 119 us -> 110 us
    ppermute x56 -> x49, starting transfers between devices: 117 us -> 108 us  [send(): self.got[slot] = lax.ppermute(tied(self.parts[slot], after), 'seq', pairs)]
    ppermute x1, waiting for transfers between devices: 2.85 us -> 9.49 us  [local(): lax.ppermute(result_0, 'pipe', [(s, s - 1) for s in range(1, pipe)])]
    ppermute x56 -> x49, waiting for transfers between devices: 10.4 us -> 16.3 us  [send(): self.got[slot] = lax.ppermute(tied(self.parts[slot], after), 'seq', pairs)]
    pallas_call x13 -> x12, Pallas kernels: 32 us -> 32 us  [call(): pl.pallas_call(kernel, grid=(steps or width // block,), in_specs=[spec fo...]
  transfers between devices with their start and end apart: 57 -> 50, of which waited for: 8 -> 9; matrix products, arithmetic and copies ran while one was open for 0% -> 0% of each run, Pallas kernels for 14% -> 11%
where the time goes in v6:
time: 171 us
  starting transfers between devices  110 us (64%)
  Pallas kernels  32 us (19%)
  waiting for transfers between devices  25.8 us (15%)
  local copies, waits for them, and re-layouts  2.45 us (1%)
    ppermute x49, starting transfers between devices, send(): self.got[slot] = lax.ppermute(tied(self.parts[slot], after), 'seq', pairs)  108 us
    pallas_call x12, Pallas kernels, call(): pl.pallas_call(kernel, grid=(steps or width // block,), in_specs=[spec fo...  32 us
    ppermute x49, waiting for transfers between devices, send(): self.got[slot] = lax.ppermute(tied(self.parts[slot], after), 'seq', pairs)  16.3 us
    ppermute x1, waiting for transfers between devices, local(): lax.ppermute(result_0, 'pipe', [(s, s - 1) for s in range(1, pipe)])  9.49 us
  transfers between devices with their start and end apart: 50, of which 9 were waited for; matrix products, arithmetic and copies ran while one was open for 0% of the time, Pallas kernels for 11%

profile of v6, /device:TPU:2, one launch (start us, length us, event | category | flops | bytes accessed | tf_op | source)
XLA Modules:
  0.0 170.7 jit_solution(2911401032466196062)
XLA Ops:
  0.0 5.2 %first_0.1 = (bf16[32,1536]{1,0:T(8,128)(2,1)}, bf16[32,1536]{1,0:T(8,128)(2,1)}, bf16[32,1536]{1,0:T(8,128)(2,1)}, bf16[32,1536]{1,0:T(8,128)(2,1)}, bf16[32,15...) custom-call(bf16[1,2,256,1536]{3,2,1,0:T(8,128)(2,1)} %x_ref.11, ...), custom_call_target="tpu_custom_call" | custom-call | flops 603979776 | bytes 3145728 | tf_op jit(solution)/shard_map/first_0/pallas_call | solution.py:279
  5.2 4.6 %collective-permute-start = (bf16[32,1536]{1,0:T(8,128)(2,1)}, bf16[32,1536]{1,0:T(8,128)(2,1)S(1)}, u32[]{:S(2)}, u32[]{:S(2)}) collective-permute-start(bf16[32,1536]{1,0:T(8,128)(2,1)} %get-tuple-element.74), channel_id=1, source_target_pairs={{0,7},{1,6},{2,5},{3,4},{4,3},{5,2},{6,1},{7,0},{8,15},{9,14},{10,... | collective-permute-start | bytes 294920 | tf_op jit(solution)/shard_map/ppermute | solution.py:222
  9.9 0.5 collective-permute-start.1
  10.4 0.2 collective-permute-start.2
  10.6 1.7 collective-permute-start.3
  12.3 1.3 collective-permute-start.4
  13.6 1.3 copy-done.3
  14.9 1.1 copy-done.5
  16.0 3.3 %grads_0.1 = (bf16[32,1536]{1,0:T(8,128)(2,1)S(1)}, bf16[32,1536]{1,0:T(8,128)(2,1)S(1)}, bf16[32,1536]{1,0:T(8,128)(2,1)S(1)}, bf16[32,1536]{1,0:T(8,128)(2,1)S...) custom-call(bf16[1,2,256,1536]{3,2,1,0:T(8,128)(2,1)S(1)} %copy-done, ...), custom_call_target="tpu_custom_call" | custom-call | flops 603979776 | bytes 6291456 | tf_op jit(solution)/shard_map/grads_0/pallas_call | solution.py:279
  19.3 3.7 %collective-permute-start.5 = (bf16[32,1536]{1,0:T(8,128)(2,1)S(1)}, bf16[32,1536]{1,0:T(8,128)(2,1)S(1)}, u32[]{:S(2)}, u32[]{:S(2)}) collective-permute-start(bf16[32,1536]{1,0:T(8,128)(2,1)S(1)} %copy-done.12), channel_id=1, source_target_pairs={{0,6},{1,4},{2,3},{3,2},{4,1},{5,7},{6,0},{7,5},{8,14},{9,12},{10,... | collective-permute-start | bytes 294920 | tf_op jit(solution)/shard_map/ppermute | solution.py:222
  23.0 2.1 %collective-permute-start.14 = (bf16[32,1536]{1,0:T(8,128)(2,1)S(1)}, bf16[32,1536]{1,0:T(8,128)(2,1)S(1)}, u32[]{:S(2)}, u32[]{:S(2)}) collective-permute-start(bf16[32,1536]{1,0:T(8,128)(2,1)S(1)} %get-tuple-element.92), channel_id=1, source_target_pairs={{0,7},{1,6},{2,5},{3,4},{4,3},{5,2},{6,1},{7,0},{8,15},{9,14},{10,... | collective-permute-start | bytes 294920 | tf_op jit(solution)/shard_map/ppermute | solution.py:222
  25.2 0.2 collective-permute-start.15
  25.4 5.9 %collective-permute-start.16 = (bf16[32,1536]{1,0:T(8,128)(2,1)S(1)}, bf16[32,1536]{1,0:T(8,128)(2,1)S(1)}, u32[]{:S(2)}, u32[]{:S(2)}) collective-permute-start(bf16[32,1536]{1,0:T(8,128)(2,1)S(1)} %get-tuple-element.94), channel_id=1, source_target_pairs={{0,3},{1,5},{2,6},{3,0},{4,7},{5,1},{6,2},{7,4},{8,11},{9,13},{10,... | collective-permute-start | bytes 294920 | tf_op jit(solution)/shard_map/ppermute | solution.py:222
  31.3 0.2 matrix.1.m_ref
  31.5 0.1 collective-permute-start.17
  31.5 3.6 %collective-permute-done.6.refs_7_ = bf16[32,1536]{1,0:T(8,128)(2,1)S(1)} collective-permute-done((bf16[32,1536]{1,0:T(8,128)(2,1)S(1)}, bf16[32,1536]{1,0:T(8,128)(2,1)S(1)}, u32[]{:S(2)}, u32[]{:S(2)}) %collective-permute-start.6) | collective-permute-done | bytes 98336 | tf_op jit(solution)/shard_map/ppermute | solution.py:222
  35.2 0.2 collective-permute-start.18
  35.4 5.3 %collective-permute-start.20 = (bf16[32,1536]{1,0:T(8,128)(2,1)S(1)}, bf16[32,1536]{1,0:T(8,128)(2,1)S(1)}, u32[]{:S(2)}, u32[]{:S(2)}) collective-permute-start(bf16[32,1536]{1,0:T(8,128)(2,1)S(1)} %get-tuple-element.98), channel_id=1, source_target_pairs={{0,5},{1,3},{2,7},{3,1},{4,6},{5,0},{6,4},{7,2},{8,13},{9,11},{10,... | collective-permute-start | bytes 294920 | tf_op jit(solution)/shard_map/ppermute | solution.py:222
  40.7 4.2 %mixfirst_0.1 = (bf16[2,32,1536]{2,1,0:T(8,128)(2,1)S(1)}, bf16[2,32,1536]{2,1,0:T(8,128)(2,1)S(1)}, bf16[2,32,1536]{2,1,0:T(8,128)(2,1)S(1)}, bf16[2,32,1536]{2...) custom-call(bf16[1,2,256,1536]{3,2,1,0:T(8,128)(2,1)S(1)} %copy-done, ...), custom_call_target="tpu_custom_call" | custom-call | flops 905969664 | bytes 4718592 | tf_op jit(solution)/shard_map/mixfirst_0/pallas_call | solution.py:279
  44.9 2.3 %collective-permute-start.10 = (bf16[2,32,1536]{2,1,0:T(8,128)(2,1)S(1)}, bf16[2,32,1536]{2,1,0:T(8,128)(2,1)S(1)}, u32[]{:S(2)}, u32[]{:S(2)}) collective-permute-start(bf16[2,32,1536]{2,1,0:T(8,128)(2,1)S(1)} %get-tuple-element.85), channel_id=1, source_target_pairs={{0,4},{1,2},{2,1},{3,5},{4,0},{5,3},{6,7},{7,6},{8,12},{9,10},{10,... | collective-permute-start | bytes 589832 | tf_op jit(solution)/shard_map/ppermute | solution.py:222
  47.2 1.4 fold_0.1
  48.6 4.5 %collective-permute-start.21 = (bf16[32,1536]{1,0:T(8,128)(2,1)S(1)}, bf16[32,1536]{1,0:T(8,128)(2,1)S(1)}, u32[]{:S(2)}, u32[]{:S(2)}) collective-permute-start(bf16[32,1536]{1,0:T(8,128)(2,1)S(1)} %get-tuple-element.100), channel_id=1, source_target_pairs={{0,7},{1,6},{2,5},{3,4},{4,3},{5,2},{6,1},{7,0},{8,15},{9,14},{10,... | collective-permute-start | bytes 294920 | tf_op jit(solution)/shard_map/ppermute | solution.py:222
  53.2 2.2 %collective-permute-start.12 = (bf16[2,32,1536]{2,1,0:T(8,128)(2,1)S(1)}, bf16[2,32,1536]{2,1,0:T(8,128)(2,1)S(1)}, u32[]{:S(2)}, u32[]{:S(2)}) collective-permute-start(bf16[2,32,1536]{2,1,0:T(8,128)(2,1)S(1)} %get-tuple-element.87), channel_id=1, source_target_pairs={{0,6},{1,4},{2,3},{3,2},{4,1},{5,7},{6,0},{7,5},{8,14},{9,12},{10,... | collective-permute-start | bytes 589832 | tf_op jit(solution)/shard_map/ppermute | solution.py:222
  55.4 3.2 %collective-permute-done.21.refs_1_ = bf16[32,1536]{1,0:T(8,128)(2,1)S(1)} collective-permute-done((bf16[32,1536]{1,0:T(8,128)(2,1)S(1)}, bf16[32,1536]{1,0:T(8,128)(2,1)S(1)}, u32[]{:S(2)}, u32[]{:S(2)}) %collective-permute-start.21) | collective-permute-done | bytes 98336 | tf_op jit(solution)/shard_map/ppermute | solution.py:222
  58.6 3.3 %collective-permute-start.13 = (bf16[2,32,1536]{2,1,0:T(8,128)(2,1)S(1)}, bf16[2,32,1536]{2,1,0:T(8,128)(2,1)S(1)}, u32[]{:S(2)}, u32[]{:S(2)}) collective-permute-start(bf16[2,32,1536]{2,1,0:T(8,128)(2,1)S(1)} %get-tuple-element.88), channel_id=1, source_target_pairs={{0,5},{1,3},{2,7},{3,1},{4,6},{5,0},{6,4},{7,2},{8,13},{9,11},{10,... | collective-permute-start | bytes 589832 | tf_op jit(solution)/shard_map/ppermute | solution.py:222
  61.8 12.1 %collective-permute-start.7 = (bf16[2,32,1536]{2,1,0:T(8,128)(2,1)S(1)}, bf16[2,32,1536]{2,1,0:T(8,128)(2,1)S(1)}, u32[]{:S(2)}, u32[]{:S(2)}) collective-permute-start(bf16[2,32,1536]{2,1,0:T(8,128)(2,1)S(1)} %get-tuple-element.82), channel_id=1, source_target_pairs={{0,7},{1,6},{2,5},{3,4},{4,3},{5,2},{6,1},{7,0},{8,15},{9,14},{10,... | collective-permute-start | bytes 589832 | tf_op jit(solution)/shard_map/ppermute | solution.py:222
  73.9 0.6 collective-permute-start.9
  74.5 2.4 %collective-permute-start.23 = (bf16[32,1536]{1,0:T(8,128)(2,1)S(1)}, bf16[32,1536]{1,0:T(8,128)(2,1)S(1)}, u32[]{:S(2)}, u32[]{:S(2)}) collective-permute-start(bf16[32,1536]{1,0:T(8,128)(2,1)S(1)} %get-tuple-element.102), channel_id=1, source_target_pairs={{0,3},{1,5},{2,6},{3,0},{4,7},{5,1},{6,2},{7,4},{8,11},{9,13},{10,... | collective-permute-start | bytes 294920 | tf_op jit(solution)/shard_map/ppermute | solution.py:222
  76.9 2.9 %collective-permute-done.7.refs_1_ = bf16[2,32,1536]{2,1,0:T(8,128)(2,1)S(1)} collective-permute-done((bf16[2,32,1536]{2,1,0:T(8,128)(2,1)S(1)}, bf16[2,32,1536]{2,1,0:T(8,128)(2,1)S(1)}, u32[]{:S(2)}, u32[]{:S(2)}) %collective-permute-start.7) | collective-permute-done | bytes 196640 | tf_op jit(solution)/shard_map/ppermute | solution.py:222
  79.9 5.2 %collective-permute-start.25 = (bf16[32,1536]{1,0:T(8,128)(2,1)S(1)}, bf16[32,1536]{1,0:T(8,128)(2,1)S(1)}, u32[]{:S(2)}, u32[]{:S(2)}) collective-permute-start(bf16[32,1536]{1,0:T(8,128)(2,1)S(1)} %get-tuple-element.104), channel_id=1, source_target_pairs={{0,2},{1,7},{2,0},{3,6},{4,5},{5,4},{6,3},{7,1},{8,10},{9,15},{10,... | collective-permute-start | bytes 294920 | tf_op jit(solution)/shard_map/ppermute | solution.py:222
  85.1 6.8 %collective-permute-start.26 = (bf16[32,1536]{1,0:T(8,128)(2,1)S(1)}, bf16[32,1536]{1,0:T(8,128)(2,1)S(1)}, u32[]{:S(2)}, u32[]{:S(2)}) collective-permute-start(bf16[32,1536]{1,0:T(8,128)(2,1)S(1)} %get-tuple-element.105), channel_id=1, source_target_pairs={{0,6},{1,4},{2,3},{3,2},{4,1},{5,7},{6,0},{7,5},{8,14},{9,12},{10,... | collective-permute-start | bytes 294920 | tf_op jit(solution)/shard_map/ppermute | solution.py:222
  91.9 2.6 %collective-permute-start.27 = (bf16[32,1536]{1,0:T(8,128)(2,1)S(1)}, bf16[32,1536]{1,0:T(8,128)(2,1)S(1)}, u32[]{:S(2)}, u32[]{:S(2)}) collective-permute-start(bf16[32,1536]{1,0:T(8,128)(2,1)S(1)} %get-tuple-element.106), channel_id=1, source_target_pairs={{0,5},{1,3},{2,7},{3,1},{4,6},{5,0},{6,4},{7,2},{8,13},{9,11},{10,... | collective-permute-start | bytes 294920 | tf_op jit(solution)/shard_map/ppermute | solution.py:222
  94.5 1.2 mix_1.1
  95.8 0.5 collective-permute-start.28
  96.3 4.1 %collective-permute-start.29 = (bf16[32,1536]{1,0:T(8,128)(2,1)S(1)}, bf16[32,1536]{1,0:T(8,128)(2,1)S(1)}, u32[]{:S(2)}, u32[]{:S(2)}) collective-permute-start(bf16[32,1536]{1,0:T(8,128)(2,1)S(1)} %get-tuple-element.109), channel_id=1, source_target_pairs={{0,1},{1,0},{2,4},{3,7},{4,2},{5,6},{6,5},{7,3},{8,9},{9,8},{10,12... | collective-permute-start | bytes 294920 | tf_op jit(solution)/shard_map/ppermute | solution.py:222
  100.4 0.8 collective-permute-start.30
  101.2 1.7 %back_0.1.back_ref = f32[256,1536]{1,0:T(8,128)S(1)} custom-call(bf16[1,384,1536]{2,1,0:T(8,128)(2,1)S(1)} %copy-done.2, f32[256,1536]{1,0:T(8,128)S(1)} %get-tuple-element.72.factor_ref, bf16[2,32,1536]{2,1,0:T(8,128)(2,1)S(1)} %get-tuple-element.81.refs_0_, bf16[2,32,1536]{2,1,0:T(8,128)(2,1)S(1)} %collective-permute-done.7.refs_1_, ...), custom_call_target="tpu_custom_call" | custom-call | flops 301989888 | bytes 4718592 | tf_op jit(solution)/shard_map/back_0/pallas_call | solution.py:279
  103.0 4.1 %result_0.1 = (bf16[1,2,256,1536]{3,2,1,0:T(8,128)(2,1)}, bf16[256,1536]{1,0:T(8,128)(2,1)S(1)}) custom-call(bf16[1,2,256,1536]{3,2,1,0:T(8,128)(2,1)S(1)} %copy-done, f32[1,1536]{1,0:T(1,128)S(1)} %copy-done.8, bf16[1,384,1536]{2,1,0:T(8,128)(2,1)S(1)} %copy-done.1, bf16[1,256,256]{2,1,0:T(8,128)(2,1)S(1)} %copy-done.7, f32[256,1536]{1,0:T(8,128)S(1)} %back_0.1.back_ref, ...), custom_call_target="tpu_custom_call" | custom-call | flops 905969664 | bytes 6291456 | tf_op jit(solution)/shard_map/result_0/pallas_call | solution.py:279
  107.1 1.9 %collective-permute-start.32 = (bf16[256,1536]{1,0:T(8,128)(2,1)S(1)}, bf16[256,1536]{1,0:T(8,128)(2,1)S(1)}, u32[]{:S(2)}, u32[]{:S(2)}) collective-permute-start(bf16[256,1536]{1,0:T(8,128)(2,1)S(1)} %get-tuple-element.112), channel_id=1, source_target_pairs={{8,0},{16,8},{24,16},{9,1},{17,9},{25,17},{10,2},{18,10},{26,18},{... | collective-permute-start | bytes 2359304 | tf_op jit(solution)/shard_map/ppermute | solution.py:397
  109.1 9.5 %collective-permute-done.32.refs_0_.refs_8_ = bf16[256,1536]{1,0:T(8,128)(2,1)S(1)} collective-permute-done((bf16[256,1536]{1,0:T(8,128)(2,1)S(1)}, bf16[256,1536]{1,0:T(8,128)(2,1)S(1)}, u32[]{:S(2)}, u32[]{:S(2)}) %collective-permute-start.32) | collective-permute-done | bytes 786464 | tf_op jit(solution)/shard_map/ppermute | solution.py:397
  118.6 3.4 %grads_1.1 = (bf16[32,1536]{1,0:T(8,128)(2,1)S(1)}, bf16[32,1536]{1,0:T(8,128)(2,1)S(1)}, bf16[32,1536]{1,0:T(8,128)(2,1)S(1)}, bf16[32,1536]{1,0:T(8,128)(2,1)S...) custom-call(bf16[1,2,256,1536]{3,2,1,0:T(8,128)(2,1)S(1)} %copy-done, ...), custom_call_target="tpu_custom_call" | custom-call | flops 603979776 | bytes 6291456 | tf_op jit(solution)/shard_map/grads_1/pallas_call | solution.py:279
  121.9 2.1 %collective-permute-start.36 = (bf16[32,1536]{1,0:T(8,128)(2,1)S(1)}, bf16[32,1536]{1,0:T(8,128)(2,1)S(1)}, u32[]{:S(2)}, u32[]{:S(2)}) collective-permute-start(bf16[32,1536]{1,0:T(8,128)(2,1)S(1)} %get-tuple-element.123), channel_id=1, source_target_pairs={{0,7},{1,6},{2,5},{3,4},{4,3},{5,2},{6,1},{7,0},{8,15},{9,14},{10,... | collective-permute-start | bytes 294920 | tf_op jit(solution)/shard_map/ppermute | solution.py:222
  124.0 1.8 %collective-permute-start.37 = (bf16[32,1536]{1,0:T(8,128)(2,1)S(1)}, bf16[32,1536]{1,0:T(8,128)(2,1)S(1)}, u32[]{:S(2)}, u32[]{:S(2)}) collective-permute-start(bf16[32,1536]{1,0:T(8,128)(2,1)S(1)} %get-tuple-element.124), channel_id=1, source_target_pairs={{0,1},{1,0},{2,4},{3,7},{4,2},{5,6},{6,5},{7,3},{8,9},{9,8},{10,12... | collective-permute-start | bytes 294920 | tf_op jit(solution)/shard_map/ppermute | solution.py:222
  125.9 1.4 collective-permute-start.38
  127.3 2.0 %collective-permute-start.39 = (bf16[32,1536]{1,0:T(8,128)(2,1)S(1)}, bf16[32,1536]{1,0:T(8,128)(2,1)S(1)}, u32[]{:S(2)}, u32[]{:S(2)}) collective-permute-start(bf16[32,1536]{1,0:T(8,128)(2,1)S(1)} %get-tuple-element.126), channel_id=1, source_target_pairs={{0,4},{1,2},{2,1},{3,5},{4,0},{5,3},{6,7},{7,6},{8,12},{9,10},{10,... | collective-permute-start | bytes 294920 | tf_op jit(solution)/shard_map/ppermute | solution.py:222
  129.2 0.1 collective-permute-start.40
  129.3 0.6 collective-permute-done.36.refs_1_
  129.9 2.9 %collective-permute-start.41 = (bf16[32,1536]{1,0:T(8,128)(2,1)S(1)}, bf16[32,1536]{1,0:T(8,128)(2,1)S(1)}, u32[]{:S(2)}, u32[]{:S(2)}) collective-permute-start(bf16[32,1536]{1,0:T(8,128)(2,1)S(1)} %get-tuple-element.128), channel_id=1, source_target_pairs={{0,6},{1,4},{2,3},{3,2},{4,1},{5,7},{6,0},{7,5},{8,14},{9,12},{10,... | collective-permute-start | bytes 294920 | tf_op jit(solution)/shard_map/ppermute | solution.py:222
  132.8 0.8 collective-permute-start.42
  133.5 1.1 collective-permute-done.38.refs_3_
  134.7 7.2 %collective-permute-start.33 = (bf16[32,1536]{1,0:T(8,128)(2,1)S(1)}, bf16[32,1536]{1,0:T(8,128)(2,1)S(1)}, u32[]{:S(2)}, u32[]{:S(2)}) collective-permute-start(bf16[32,1536]{1,0:T(8,128)(2,1)S(1)} %get-tuple-element.119), channel_id=1, source_target_pairs={{0,2},{1,7},{2,0},{3,6},{4,5},{5,4},{6,3},{7,1},{8,10},{9,15},{10,... | collective-permute-start | bytes 294920 | tf_op jit(solution)/shard_map/ppermute | solution.py:222
  141.9 2.1 %collective-permute-start.34 = (bf16[32,1536]{1,0:T(8,128)(2,1)S(1)}, bf16[32,1536]{1,0:T(8,128)(2,1)S(1)}, u32[]{:S(2)}, u32[]{:S(2)}) collective-permute-start(bf16[32,1536]{1,0:T(8,128)(2,1)S(1)} %get-tuple-element.120), channel_id=1, source_target_pairs={{0,6},{1,4},{2,3},{3,2},{4,1},{5,7},{6,0},{7,5},{8,14},{9,12},{10,... | collective-permute-start | bytes 294920 | tf_op jit(solution)/shard_map/ppermute | solution.py:222
  143.9 0.2 collective-permute-start.35
  144.2 1.4 fold_1.1
  145.5 5.1 %collective-permute-start.43 = (bf16[32,1536]{1,0:T(8,128)(2,1)S(1)}, bf16[32,1536]{1,0:T(8,128)(2,1)S(1)}, u32[]{:S(2)}, u32[]{:S(2)}) collective-permute-start(bf16[32,1536]{1,0:T(8,128)(2,1)S(1)} %get-tuple-element.131), channel_id=1, source_target_pairs={{0,7},{1,6},{2,5},{3,4},{4,3},{5,2},{6,1},{7,0},{8,15},{9,14},{10,... | collective-permute-start | bytes 294920 | tf_op jit(solution)/shard_map/ppermute | solution.py:222
  150.6 3.3 %collective-permute-start.44 = (bf16[32,1536]{1,0:T(8,128)(2,1)S(1)}, bf16[32,1536]{1,0:T(8,128)(2,1)S(1)}, u32[]{:S(2)}, u32[]{:S(2)}) collective-permute-start(bf16[32,1536]{1,0:T(8,128)(2,1)S(1)} %get-tuple-element.132), channel_id=1, source_target_pairs={{0,1},{1,0},{2,4},{3,7},{4,2},{5,6},{6,5},{7,3},{8,9},{9,8},{10,12... | collective-permute-start | bytes 294920 | tf_op jit(solution)/shard_map/ppermute | solution.py:222
  154.0 0.5 collective-permute-start.45
  154.5 2.9 %collective-permute-start.46 = (bf16[32,1536]{1,0:T(8,128)(2,1)S(1)}, bf16[32,1536]{1,0:T(8,128)(2,1)S(1)}, u32[]{:S(2)}, u32[]{:S(2)}) collective-permute-start(bf16[32,1536]{1,0:T(8,128)(2,1)S(1)} %get-tuple-element.134), channel_id=1, source_target_pairs={{0,4},{1,2},{2,1},{3,5},{4,0},{5,3},{6,7},{7,6},{8,12},{9,10},{10,... | collective-permute-start | bytes 294920 | tf_op jit(solution)/shard_map/ppermute | solution.py:222
  157.5 2.5 %collective-permute-start.48 = (bf16[32,1536]{1,0:T(8,128)(2,1)S(1)}, bf16[32,1536]{1,0:T(8,128)(2,1)S(1)}, u32[]{:S(2)}, u32[]{:S(2)}) collective-permute-start(bf16[32,1536]{1,0:T(8,128)(2,1)S(1)} %get-tuple-element.136), channel_id=1, source_target_pairs={{0,6},{1,4},{2,3},{3,2},{4,1},{5,7},{6,0},{7,5},{8,14},{9,12},{10,... | collective-permute-start | bytes 294920 | tf_op jit(solution)/shard_map/ppermute | solution.py:222
  160.0 1.7 %back_1.1.back_ref = f32[256,1536]{1,0:T(8,128)S(1)} custom-call(bf16[1,384,1536]{2,1,0:T(8,128)(2,1)S(1)} %copy-done.2, f32[256,1536]{1,0:T(8,128)S(1)} %get-tuple-element.113.factor_ref, bf16[32,1536]{1,0:T(8,128)(2,1)S(1)} %get-tuple-element.114.refs_0_, bf16[32,1536]{1,0:T(8,128)(2,1)S(1)} %collective-permute-done.28.refs_1_, ...), custom_call_target="tpu_custom_call" | custom-call | flops 301989888 | bytes 4718592 | tf_op jit(solution)/shard_map/back_1/pallas_call | solution.py:279
  161.7 0.3 collective-permute-done.47.refs_5_
  162.1 2.0 %collective-permute-done.48.refs_6_ = bf16[32,1536]{1,0:T(8,128)(2,1)S(1)} collective-permute-done((bf16[32,1536]{1,0:T(8,128)(2,1)S(1)}, bf16[32,1536]{1,0:T(8,128)(2,1)S(1)}, u32[]{:S(2)}, u32[]{:S(2)}) %collective-permute-start.48) | collective-permute-done | bytes 98336 | tf_op jit(solution)/shard_map/ppermute | solution.py:222
  164.0 2.5 %collective-permute-done.49.refs_7_ = bf16[32,1536]{1,0:T(8,128)(2,1)S(1)} collective-permute-done((bf16[32,1536]{1,0:T(8,128)(2,1)S(1)}, bf16[32,1536]{1,0:T(8,128)(2,1)S(1)}, u32[]{:S(2)}, u32[]{:S(2)}) %collective-permute-start.49) | collective-permute-done | bytes 98336 | tf_op jit(solution)/shard_map/ppermute | solution.py:222
  166.5 4.1 %result_1.1 = bf16[1,2,256,1536]{3,2,1,0:T(8,128)(2,1)} custom-call(bf16[1,2,256,1536]{3,2,1,0:T(8,128)(2,1)S(1)} %copy-done, f32[1,1536]{1,0:T(1,128)S(1)} %copy-done.8, bf16[1,384,1536]{2,1,0:T(8,128)(2,1)S(1)} %copy-done.1, bf16[1,256,256]{2,1,0:T(8,128)(2,1)S(1)} %copy-done.7, f32[256,1536]{1,0:T(8,128)S(1)} %back_1.1.back_ref, ...), custom_call_target="tpu_custom_call", output_to_operand_aliasing={{}: (15, {})} | custom-call | flops 905969664 | bytes 6291456 | tf_op jit(solution)/shard_map/result_1/pallas_call | solution.py:279
  (74 shorter events, 0.3 us)
Async XLA Ops:
  0.0 13.6 %copy-start.8 = (f32[1,1536]{1,0:T(1,128)S(1)}, f32[1,1536]{1,0:T(1,128)}, u32[]{:S(2)}) copy-start(f32[1,1536]{1,0:T(1,128)} %gain_ref.11) | copy-start | bytes 18436
  0.0 13.6 %copy-start = (bf16[1,2,256,1536]{3,2,1,0:T(8,128)(2,1)S(1)}, bf16[1,2,256,1536]{3,2,1,0:T(8,128)(2,1)}, u32[]{:S(2)}) copy-start(bf16[1,2,256,1536]{3,2,1,0:T(8,128)(2,1)} %x_ref.11) | copy-start | bytes 4718596
  0.0 13.6 %copy-start.2 = (bf16[1,384,1536]{2,1,0:T(8,128)(2,1)S(1)}, bf16[1,384,1536]{2,1,0:T(8,128)(2,1)}, u32[]{:S(2)}) copy-start(bf16[1,384,1536]{2,1,0:T(8,128)(2,1)} %w_gate_ref.7) | copy-start | bytes 3538948
  5.2 14.1 %collective-permute-start = (bf16[32,1536]{1,0:T(8,128)(2,1)}, bf16[32,1536]{1,0:T(8,128)(2,1)S(1)}, u32[]{:S(2)}, u32[]{:S(2)}) collective-permute-start(bf16[32,1536]{1,0:T(8,128)(2,1)} %get-tuple-element.74), channel_id=1, source_target_pairs={{0,7},{1,6},{2,5},{3,4},{4,3},{5,2},{6,1},{7,0},{8,15},{9,14},{10,... | collective-permute-start | bytes 294920 | tf_op jit(solution)/shard_map/ppermute | solution.py:222
  9.9 13.1 %collective-permute-start.1 = (bf16[32,1536]{1,0:T(8,128)(2,1)}, bf16[32,1536]{1,0:T(8,128)(2,1)S(1)}, u32[]{:S(2)}, u32[]{:S(2)}) collective-permute-start(bf16[32,1536]{1,0:T(8,128)(2,1)} %get-tuple-element.75), channel_id=1, source_target_pairs={{0,1},{1,0},{2,4},{3,7},{4,2},{5,6},{6,5},{7,3},{8,9},{9,8},{10,12... | collective-permute-start | bytes 294920 | tf_op jit(solution)/shard_map/ppermute | solution.py:222
  10.4 12.7 %collective-permute-start.2 = (bf16[32,1536]{1,0:T(8,128)(2,1)}, bf16[32,1536]{1,0:T(8,128)(2,1)S(1)}, u32[]{:S(2)}, u32[]{:S(2)}) collective-permute-start(bf16[32,1536]{1,0:T(8,128)(2,1)} %get-tuple-element.76), channel_id=1, source_target_pairs={{0,3},{1,5},{2,6},{3,0},{4,7},{5,1},{6,2},{7,4},{8,11},{9,13},{10,... | collective-permute-start | bytes 294920 | tf_op jit(solution)/shard_map/ppermute | solution.py:222
  10.6 14.6 %collective-permute-start.3 = (bf16[32,1536]{1,0:T(8,128)(2,1)}, bf16[32,1536]{1,0:T(8,128)(2,1)S(1)}, u32[]{:S(2)}, u32[]{:S(2)}) collective-permute-start(bf16[32,1536]{1,0:T(8,128)(2,1)} %get-tuple-element.77), channel_id=1, source_target_pairs={{0,4},{1,2},{2,1},{3,5},{4,0},{5,3},{6,7},{7,6},{8,12},{9,10},{10,... | collective-permute-start | bytes 294920 | tf_op jit(solution)/shard_map/ppermute | solution.py:222
  12.3 28.4 %copy-start.1 = (bf16[1,384,1536]{2,1,0:T(8,128)(2,1)S(1)}, bf16[1,384,1536]{2,1,0:T(8,128)(2,1)}, u32[]{:S(2)}) copy-start(bf16[1,384,1536]{2,1,0:T(8,128)(2,1)} %w_value_ref.3) | copy-start | bytes 3538948
  12.3 13.1 %collective-permute-start.4 = (bf16[32,1536]{1,0:T(8,128)(2,1)}, bf16[32,1536]{1,0:T(8,128)(2,1)S(1)}, u32[]{:S(2)}, u32[]{:S(2)}) collective-permute-start(bf16[32,1536]{1,0:T(8,128)(2,1)} %get-tuple-element.78), channel_id=1, source_target_pairs={{0,2},{1,7},{2,0},{3,6},{4,5},{5,4},{6,3},{7,1},{8,10},{9,15},{10,... | collective-permute-start | bytes 294920 | tf_op jit(solution)/shard_map/ppermute | solution.py:222
  13.6 1.3 copy-start.3
  14.9 1.1 copy-start.5
  16.0 3.3 %copy-start.12 = (bf16[32,1536]{1,0:T(8,128)(2,1)S(1)}, bf16[32,1536]{1,0:T(8,128)(2,1)}, u32[]{:S(2)}) copy-start(bf16[32,1536]{1,0:T(8,128)(2,1)} %get-tuple-element.79) | copy-start | bytes 294916
  16.0 7.0 %copy-start.11 = (bf16[32,1536]{1,0:T(8,128)(2,1)S(1)}, bf16[32,1536]{1,0:T(8,128)(2,1)}, u32[]{:S(2)}) copy-start(bf16[32,1536]{1,0:T(8,128)(2,1)} %get-tuple-element.80) | copy-start | bytes 294916
  16.0 15.3 %copy-start.10 = (bf16[1,32,64]{2,1,0:T(8,128)(2,1)S(1)}, bf16[1,32,64]{2,1,0:T(8,128)(2,1)}, u32[]{:S(2)}) copy-start(bf16[1,32,64]{2,1,0:T(8,128)(2,1)} %l_ref.1) | copy-start | bytes 12292
  16.0 24.7 %copy-start.7 = (bf16[1,256,256]{2,1,0:T(8,128)(2,1)S(1)}, bf16[1,256,256]{2,1,0:T(8,128)(2,1)}, u32[]{:S(2)}) copy-start(bf16[1,256,256]{2,1,0:T(8,128)(2,1)} %r_ref.7) | copy-start | bytes 393220
  16.0 24.6 %copy-start.9 = (bf16[32,1536]{1,0:T(8,128)(2,1)S(1)}, bf16[32,1536]{1,0:T(8,128)(2,1)}, u32[]{:S(2)}) copy-start(bf16[32,1536]{1,0:T(8,128)(2,1)} %get-tuple-element.73.refs_0_) | copy-start | bytes 294916
  19.3 12.1 %collective-permute-start.5 = (bf16[32,1536]{1,0:T(8,128)(2,1)S(1)}, bf16[32,1536]{1,0:T(8,128)(2,1)S(1)}, u32[]{:S(2)}, u32[]{:S(2)}) collective-permute-start(bf16[32,1536]{1,0:T(8,128)(2,1)S(1)} %copy-done.12), channel_id=1, source_target_pairs={{0,6},{1,4},{2,3},{3,2},{4,1},{5,7},{6,0},{7,5},{8,14},{9,12},{10,... | collective-permute-start | bytes 294920 | tf_op jit(solution)/shard_map/ppermute | solution.py:222
  23.0 12.2 %collective-permute-start.6 = (bf16[32,1536]{1,0:T(8,128)(2,1)S(1)}, bf16[32,1536]{1,0:T(8,128)(2,1)S(1)}, u32[]{:S(2)}, u32[]{:S(2)}) collective-permute-start(bf16[32,1536]{1,0:T(8,128)(2,1)S(1)} %copy-done.11), channel_id=1, source_target_pairs={{0,5},{1,3},{2,7},{3,1},{4,6},{5,0},{6,4},{7,2},{8,13},{9,11},{10,... | collective-permute-start | bytes 294920 | tf_op jit(solution)/shard_map/ppermute | solution.py:222
  23.0 12.3 %collective-permute-start.14 = (bf16[32,1536]{1,0:T(8,128)(2,1)S(1)}, bf16[32,1536]{1,0:T(8,128)(2,1)S(1)}, u32[]{:S(2)}, u32[]{:S(2)}) collective-permute-start(bf16[32,1536]{1,0:T(8,128)(2,1)S(1)} %get-tuple-element.92), channel_id=1, source_target_pairs={{0,7},{1,6},{2,5},{3,4},{4,3},{5,2},{6,1},{7,0},{8,15},{9,14},{10,... | collective-permute-start | bytes 294920 | tf_op jit(solution)/shard_map/ppermute | solution.py:222
  25.2 10.2 %collective-permute-start.15 = (bf16[32,1536]{1,0:T(8,128)(2,1)S(1)}, bf16[32,1536]{1,0:T(8,128)(2,1)S(1)}, u32[]{:S(2)}, u32[]{:S(2)}) collective-permute-start(bf16[32,1536]{1,0:T(8,128)(2,1)S(1)} %get-tuple-element.93), channel_id=1, source_target_pairs={{0,1},{1,0},{2,4},{3,7},{4,2},{5,6},{6,5},{7,3},{8,9},{9,8},{10,12... | collective-permute-start | bytes 294920 | tf_op jit(solution)/shard_map/ppermute | solution.py:222
  25.4 19.5 %collective-permute-start.16 = (bf16[32,1536]{1,0:T(8,128)(2,1)S(1)}, bf16[32,1536]{1,0:T(8,128)(2,1)S(1)}, u32[]{:S(2)}, u32[]{:S(2)}) collective-permute-start(bf16[32,1536]{1,0:T(8,128)(2,1)S(1)} %get-tuple-element.94), channel_id=1, source_target_pairs={{0,3},{1,5},{2,6},{3,0},{4,7},{5,1},{6,2},{7,4},{8,11},{9,13},{10,... | collective-permute-start | bytes 294920 | tf_op jit(solution)/shard_map/ppermute | solution.py:222
  31.5 15.8 %collective-permute-start.17 = (bf16[32,1536]{1,0:T(8,128)(2,1)S(1)}, bf16[32,1536]{1,0:T(8,128)(2,1)S(1)}, u32[]{:S(2)}, u32[]{:S(2)}) collective-permute-start(bf16[32,1536]{1,0:T(8,128)(2,1)S(1)} %get-tuple-element.95), channel_id=1, source_target_pairs={{0,4},{1,2},{2,1},{3,5},{4,0},{5,3},{6,7},{7,6},{8,12},{9,10},{10,... | collective-permute-start | bytes 294920 | tf_op jit(solution)/shard_map/ppermute | solution.py:222
  35.2 12.0 %collective-permute-start.18 = (bf16[32,1536]{1,0:T(8,128)(2,1)S(1)}, bf16[32,1536]{1,0:T(8,128)(2,1)S(1)}, u32[]{:S(2)}, u32[]{:S(2)}) collective-permute-start(bf16[32,1536]{1,0:T(8,128)(2,1)S(1)} %get-tuple-element.96), channel_id=1, source_target_pairs={{0,2},{1,7},{2,0},{3,6},{4,5},{5,4},{6,3},{7,1},{8,10},{9,15},{10,... | collective-permute-start | bytes 294920 | tf_op jit(solution)/shard_map/ppermute | solution.py:222
  35.4 11.8 %collective-permute-start.19 = (bf16[32,1536]{1,0:T(8,128)(2,1)S(1)}, bf16[32,1536]{1,0:T(8,128)(2,1)S(1)}, u32[]{:S(2)}, u32[]{:S(2)}) collective-permute-start(bf16[32,1536]{1,0:T(8,128)(2,1)S(1)} %get-tuple-element.97), channel_id=1, source_target_pairs={{0,6},{1,4},{2,3},{3,2},{4,1},{5,7},{6,0},{7,5},{8,14},{9,12},{10,... | collective-permute-start | bytes 294920 | tf_op jit(solution)/shard_map/ppermute | solution.py:222
  35.4 11.8 %collective-permute-start.20 = (bf16[32,1536]{1,0:T(8,128)(2,1)S(1)}, bf16[32,1536]{1,0:T(8,128)(2,1)S(1)}, u32[]{:S(2)}, u32[]{:S(2)}) collective-permute-start(bf16[32,1536]{1,0:T(8,128)(2,1)S(1)} %get-tuple-element.98), channel_id=1, source_target_pairs={{0,5},{1,3},{2,7},{3,1},{4,6},{5,0},{6,4},{7,2},{8,13},{9,11},{10,... | collective-permute-start | bytes 294920 | tf_op jit(solution)/shard_map/ppermute | solution.py:222
  44.9 29.1 %collective-permute-start.10 = (bf16[2,32,1536]{2,1,0:T(8,128)(2,1)S(1)}, bf16[2,32,1536]{2,1,0:T(8,128)(2,1)S(1)}, u32[]{:S(2)}, u32[]{:S(2)}) collective-permute-start(bf16[2,32,1536]{2,1,0:T(8,128)(2,1)S(1)} %get-tuple-element.85), channel_id=1, source_target_pairs={{0,4},{1,2},{2,1},{3,5},{4,0},{5,3},{6,7},{7,6},{8,12},{9,10},{10,... | collective-permute-start | bytes 589832 | tf_op jit(solution)/shard_map/ppermute | solution.py:222
  47.2 26.7 %collective-permute-start.11 = (bf16[2,32,1536]{2,1,0:T(8,128)(2,1)S(1)}, bf16[2,32,1536]{2,1,0:T(8,128)(2,1)S(1)}, u32[]{:S(2)}, u32[]{:S(2)}) collective-permute-start(bf16[2,32,1536]{2,1,0:T(8,128)(2,1)S(1)} %get-tuple-element.86), channel_id=1, source_target_pairs={{0,2},{1,7},{2,0},{3,6},{4,5},{5,4},{6,3},{7,1},{8,10},{9,15},{10,... | collective-permute-start | bytes 589832 | tf_op jit(solution)/shard_map/ppermute | solution.py:222
  48.6 9.9 %collective-permute-start.21 = (bf16[32,1536]{1,0:T(8,128)(2,1)S(1)}, bf16[32,1536]{1,0:T(8,128)(2,1)S(1)}, u32[]{:S(2)}, u32[]{:S(2)}) collective-permute-start(bf16[32,1536]{1,0:T(8,128)(2,1)S(1)} %get-tuple-element.100), channel_id=1, source_target_pairs={{0,7},{1,6},{2,5},{3,4},{4,3},{5,2},{6,1},{7,0},{8,15},{9,14},{10,... | collective-permute-start | bytes 294920 | tf_op jit(solution)/shard_map/ppermute | solution.py:222
  53.2 8.7 %collective-permute-start.22 = (bf16[32,1536]{1,0:T(8,128)(2,1)S(1)}, bf16[32,1536]{1,0:T(8,128)(2,1)S(1)}, u32[]{:S(2)}, u32[]{:S(2)}) collective-permute-start(bf16[32,1536]{1,0:T(8,128)(2,1)S(1)} %get-tuple-element.101), channel_id=1, source_target_pairs={{0,1},{1,0},{2,4},{3,7},{4,2},{5,6},{6,5},{7,3},{8,9},{9,8},{10,12... | collective-permute-start | bytes 294920 | tf_op jit(solution)/shard_map/ppermute | solution.py:222
  53.2 21.3 %collective-permute-start.12 = (bf16[2,32,1536]{2,1,0:T(8,128)(2,1)S(1)}, bf16[2,32,1536]{2,1,0:T(8,128)(2,1)S(1)}, u32[]{:S(2)}, u32[]{:S(2)}) collective-permute-start(bf16[2,32,1536]{2,1,0:T(8,128)(2,1)S(1)} %get-tuple-element.87), channel_id=1, source_target_pairs={{0,6},{1,4},{2,3},{3,2},{4,1},{5,7},{6,0},{7,5},{8,14},{9,12},{10,... | collective-permute-start | bytes 589832 | tf_op jit(solution)/shard_map/ppermute | solution.py:222
  58.6 18.4 %collective-permute-start.13 = (bf16[2,32,1536]{2,1,0:T(8,128)(2,1)S(1)}, bf16[2,32,1536]{2,1,0:T(8,128)(2,1)S(1)}, u32[]{:S(2)}, u32[]{:S(2)}) collective-permute-start(bf16[2,32,1536]{2,1,0:T(8,128)(2,1)S(1)} %get-tuple-element.88), channel_id=1, source_target_pairs={{0,5},{1,3},{2,7},{3,1},{4,6},{5,0},{6,4},{7,2},{8,13},{9,11},{10,... | collective-permute-start | bytes 589832 | tf_op jit(solution)/shard_map/ppermute | solution.py:222
  61.8 18.0 %collective-permute-start.7 = (bf16[2,32,1536]{2,1,0:T(8,128)(2,1)S(1)}, bf16[2,32,1536]{2,1,0:T(8,128)(2,1)S(1)}, u32[]{:S(2)}, u32[]{:S(2)}) collective-permute-start(bf16[2,32,1536]{2,1,0:T(8,128)(2,1)S(1)} %get-tuple-element.82), channel_id=1, source_target_pairs={{0,7},{1,6},{2,5},{3,4},{4,3},{5,2},{6,1},{7,0},{8,15},{9,14},{10,... | collective-permute-start | bytes 589832 | tf_op jit(solution)/shard_map/ppermute | solution.py:222
  73.9 11.2 %collective-permute-start.8 = (bf16[2,32,1536]{2,1,0:T(8,128)(2,1)S(1)}, bf16[2,32,1536]{2,1,0:T(8,128)(2,1)S(1)}, u32[]{:S(2)}, u32[]{:S(2)}) collective-permute-start(bf16[2,32,1536]{2,1,0:T(8,128)(2,1)S(1)} %get-tuple-element.83), channel_id=1, source_target_pairs={{0,1},{1,0},{2,4},{3,7},{4,2},{5,6},{6,5},{7,3},{8,9},{9,8},{10,12... | collective-permute-start | bytes 589832 | tf_op jit(solution)/shard_map/ppermute | solution.py:222
  73.9 18.0 %collective-permute-start.9 = (bf16[2,32,1536]{2,1,0:T(8,128)(2,1)S(1)}, bf16[2,32,1536]{2,1,0:T(8,128)(2,1)S(1)}, u32[]{:S(2)}, u32[]{:S(2)}) collective-permute-start(bf16[2,32,1536]{2,1,0:T(8,128)(2,1)S(1)} %get-tuple-element.84), channel_id=1, source_target_pairs={{0,3},{1,5},{2,6},{3,0},{4,7},{5,1},{6,2},{7,4},{8,11},{9,13},{10,... | collective-permute-start | bytes 589832 | tf_op jit(solution)/shard_map/ppermute | solution.py:222
  74.5 21.3 %collective-permute-start.23 = (bf16[32,1536]{1,0:T(8,128)(2,1)S(1)}, bf16[32,1536]{1,0:T(8,128)(2,1)S(1)}, u32[]{:S(2)}, u32[]{:S(2)}) collective-permute-start(bf16[32,1536]{1,0:T(8,128)(2,1)S(1)} %get-tuple-element.102), channel_id=1, source_target_pairs={{0,3},{1,5},{2,6},{3,0},{4,7},{5,1},{6,2},{7,4},{8,11},{9,13},{10,... | collective-permute-start | bytes 294920 | tf_op jit(solution)/shard_map/ppermute | solution.py:222
  76.9 19.4 %collective-permute-start.24 = (bf16[32,1536]{1,0:T(8,128)(2,1)S(1)}, bf16[32,1536]{1,0:T(8,128)(2,1)S(1)}, u32[]{:S(2)}, u32[]{:S(2)}) collective-permute-start(bf16[32,1536]{1,0:T(8,128)(2,1)S(1)} %get-tuple-element.103), channel_id=1, source_target_pairs={{0,4},{1,2},{2,1},{3,5},{4,0},{5,3},{6,7},{7,6},{8,12},{9,10},{10,... | collective-permute-start | bytes 294920 | tf_op jit(solution)/shard_map/ppermute | solution.py:222
  79.9 20.5 %collective-permute-start.25 = (bf16[32,1536]{1,0:T(8,128)(2,1)S(1)}, bf16[32,1536]{1,0:T(8,128)(2,1)S(1)}, u32[]{:S(2)}, u32[]{:S(2)}) collective-permute-start(bf16[32,1536]{1,0:T(8,128)(2,1)S(1)} %get-tuple-element.104), channel_id=1, source_target_pairs={{0,2},{1,7},{2,0},{3,6},{4,5},{5,4},{6,3},{7,1},{8,10},{9,15},{10,... | collective-permute-start | bytes 294920 | tf_op jit(solution)/shard_map/ppermute | solution.py:222
  85.1 16.0 %collective-permute-start.26 = (bf16[32,1536]{1,0:T(8,128)(2,1)S(1)}, bf16[32,1536]{1,0:T(8,128)(2,1)S(1)}, u32[]{:S(2)}, u32[]{:S(2)}) collective-permute-start(bf16[32,1536]{1,0:T(8,128)(2,1)S(1)} %get-tuple-element.105), channel_id=1, source_target_pairs={{0,6},{1,4},{2,3},{3,2},{4,1},{5,7},{6,0},{7,5},{8,14},{9,12},{10,... | collective-permute-start | bytes 294920 | tf_op jit(solution)/shard_map/ppermute | solution.py:222
  91.9 11.0 %collective-permute-start.27 = (bf16[32,1536]{1,0:T(8,128)(2,1)S(1)}, bf16[32,1536]{1,0:T(8,128)(2,1)S(1)}, u32[]{:S(2)}, u32[]{:S(2)}) collective-permute-start(bf16[32,1536]{1,0:T(8,128)(2,1)S(1)} %get-tuple-element.106), channel_id=1, source_target_pairs={{0,5},{1,3},{2,7},{3,1},{4,6},{5,0},{6,4},{7,2},{8,13},{9,11},{10,... | collective-permute-start | bytes 294920 | tf_op jit(solution)/shard_map/ppermute | solution.py:222
  95.8 11.4 %collective-permute-start.28 = (bf16[32,1536]{1,0:T(8,128)(2,1)S(1)}, bf16[32,1536]{1,0:T(8,128)(2,1)S(1)}, u32[]{:S(2)}, u32[]{:S(2)}) collective-permute-start(bf16[32,1536]{1,0:T(8,128)(2,1)S(1)} %get-tuple-element.108), channel_id=1, source_target_pairs={{0,7},{1,6},{2,5},{3,4},{4,3},{5,2},{6,1},{7,0},{8,15},{9,14},{10,... | collective-permute-start | bytes 294920 | tf_op jit(solution)/shard_map/ppermute | solution.py:222
  96.3 10.8 %collective-permute-start.29 = (bf16[32,1536]{1,0:T(8,128)(2,1)S(1)}, bf16[32,1536]{1,0:T(8,128)(2,1)S(1)}, u32[]{:S(2)}, u32[]{:S(2)}) collective-permute-start(bf16[32,1536]{1,0:T(8,128)(2,1)S(1)} %get-tuple-element.109), channel_id=1, source_target_pairs={{0,1},{1,0},{2,4},{3,7},{4,2},{5,6},{6,5},{7,3},{8,9},{9,8},{10,12... | collective-permute-start | bytes 294920 | tf_op jit(solution)/shard_map/ppermute | solution.py:222
  100.4 6.8 %collective-permute-start.30 = (bf16[32,1536]{1,0:T(8,128)(2,1)S(1)}, bf16[32,1536]{1,0:T(8,128)(2,1)S(1)}, u32[]{:S(2)}, u32[]{:S(2)}) collective-permute-start(bf16[32,1536]{1,0:T(8,128)(2,1)S(1)} %get-tuple-element.110), channel_id=1, source_target_pairs={{0,3},{1,5},{2,6},{3,0},{4,7},{5,1},{6,2},{7,4},{8,11},{9,13},{10,... | collective-permute-start | bytes 294920 | tf_op jit(solution)/shard_map/ppermute | solution.py:222
  101.1 6.0 %collective-permute-start.31 = (bf16[32,1536]{1,0:T(8,128)(2,1)S(1)}, bf16[32,1536]{1,0:T(8,128)(2,1)S(1)}, u32[]{:S(2)}, u32[]{:S(2)}) collective-permute-start(bf16[32,1536]{1,0:T(8,128)(2,1)S(1)} %get-tuple-element.111), channel_id=1, source_target_pairs={{0,4},{1,2},{2,1},{3,5},{4,0},{5,3},{6,7},{7,6},{8,12},{9,10},{10,... | collective-permute-start | bytes 294920 | tf_op jit(solution)/shard_map/ppermute | solution.py:222
  103.0 15.6 %copy-start.4 = (bf16[1,384,1536]{2,1,0:T(8,128)(2,1)S(1)}, bf16[1,384,1536]{2,1,0:T(8,128)(2,1)}, u32[]{:S(2)}) copy-start(bf16[1,384,1536]{2,1,0:T(8,128)(2,1)} %w_out_ref.3) | copy-start | bytes 3538948
  103.0 15.6 %copy-start.6 = (bf16[1,256,1536]{2,1,0:T(8,128)(2,1)S(1)}, bf16[1,256,1536]{2,1,0:T(8,128)(2,1)}, u32[]{:S(2)}) copy-start(bf16[1,256,1536]{2,1,0:T(8,128)(2,1)} %refs_9_.1) | copy-start | bytes 2359300
  107.1 11.4 %collective-permute-start.32 = (bf16[256,1536]{1,0:T(8,128)(2,1)S(1)}, bf16[256,1536]{1,0:T(8,128)(2,1)S(1)}, u32[]{:S(2)}, u32[]{:S(2)}) collective-permute-start(bf16[256,1536]{1,0:T(8,128)(2,1)S(1)} %get-tuple-element.112), channel_id=1, source_target_pairs={{8,0},{16,8},{24,16},{9,1},{17,9},{25,17},{10,2},{18,10},{26,18},{... | collective-permute-start | bytes 2359304 | tf_op jit(solution)/shard_map/ppermute | solution.py:397
  121.9 8.0 %collective-permute-start.36 = (bf16[32,1536]{1,0:T(8,128)(2,1)S(1)}, bf16[32,1536]{1,0:T(8,128)(2,1)S(1)}, u32[]{:S(2)}, u32[]{:S(2)}) collective-permute-start(bf16[32,1536]{1,0:T(8,128)(2,1)S(1)} %get-tuple-element.123), channel_id=1, source_target_pairs={{0,7},{1,6},{2,5},{3,4},{4,3},{5,2},{6,1},{7,0},{8,15},{9,14},{10,... | collective-permute-start | bytes 294920 | tf_op jit(solution)/shard_map/ppermute | solution.py:222
  124.0 8.7 %collective-permute-start.37 = (bf16[32,1536]{1,0:T(8,128)(2,1)S(1)}, bf16[32,1536]{1,0:T(8,128)(2,1)S(1)}, u32[]{:S(2)}, u32[]{:S(2)}) collective-permute-start(bf16[32,1536]{1,0:T(8,128)(2,1)S(1)} %get-tuple-element.124), channel_id=1, source_target_pairs={{0,1},{1,0},{2,4},{3,7},{4,2},{5,6},{6,5},{7,3},{8,9},{9,8},{10,12... | collective-permute-start | bytes 294920 | tf_op jit(solution)/shard_map/ppermute | solution.py:222
  125.9 8.8 %collective-permute-start.38 = (bf16[32,1536]{1,0:T(8,128)(2,1)S(1)}, bf16[32,1536]{1,0:T(8,128)(2,1)S(1)}, u32[]{:S(2)}, u32[]{:S(2)}) collective-permute-start(bf16[32,1536]{1,0:T(8,128)(2,1)S(1)} %get-tuple-element.125), channel_id=1, source_target_pairs={{0,3},{1,5},{2,6},{3,0},{4,7},{5,1},{6,2},{7,4},{8,11},{9,13},{10,... | collective-permute-start | bytes 294920 | tf_op jit(solution)/shard_map/ppermute | solution.py:222
  127.3 14.6 %collective-permute-start.39 = (bf16[32,1536]{1,0:T(8,128)(2,1)S(1)}, bf16[32,1536]{1,0:T(8,128)(2,1)S(1)}, u32[]{:S(2)}, u32[]{:S(2)}) collective-permute-start(bf16[32,1536]{1,0:T(8,128)(2,1)S(1)} %get-tuple-element.126), channel_id=1, source_target_pairs={{0,4},{1,2},{2,1},{3,5},{4,0},{5,3},{6,7},{7,6},{8,12},{9,10},{10,... | collective-permute-start | bytes 294920 | tf_op jit(solution)/shard_map/ppermute | solution.py:222
  129.2 14.7 %collective-permute-start.40 = (bf16[32,1536]{1,0:T(8,128)(2,1)S(1)}, bf16[32,1536]{1,0:T(8,128)(2,1)S(1)}, u32[]{:S(2)}, u32[]{:S(2)}) collective-permute-start(bf16[32,1536]{1,0:T(8,128)(2,1)S(1)} %get-tuple-element.127), channel_id=1, source_target_pairs={{0,2},{1,7},{2,0},{3,6},{4,5},{5,4},{6,3},{7,1},{8,10},{9,15},{10,... | collective-permute-start | bytes 294920 | tf_op jit(solution)/shard_map/ppermute | solution.py:222
  129.9 14.3 %collective-permute-start.41 = (bf16[32,1536]{1,0:T(8,128)(2,1)S(1)}, bf16[32,1536]{1,0:T(8,128)(2,1)S(1)}, u32[]{:S(2)}, u32[]{:S(2)}) collective-permute-start(bf16[32,1536]{1,0:T(8,128)(2,1)S(1)} %get-tuple-element.128), channel_id=1, source_target_pairs={{0,6},{1,4},{2,3},{3,2},{4,1},{5,7},{6,0},{7,5},{8,14},{9,12},{10,... | collective-permute-start | bytes 294920 | tf_op jit(solution)/shard_map/ppermute | solution.py:222
  132.8 11.4 %collective-permute-start.42 = (bf16[32,1536]{1,0:T(8,128)(2,1)S(1)}, bf16[32,1536]{1,0:T(8,128)(2,1)S(1)}, u32[]{:S(2)}, u32[]{:S(2)}) collective-permute-start(bf16[32,1536]{1,0:T(8,128)(2,1)S(1)} %get-tuple-element.129), channel_id=1, source_target_pairs={{0,5},{1,3},{2,7},{3,1},{4,6},{5,0},{6,4},{7,2},{8,13},{9,11},{10,... | collective-permute-start | bytes 294920 | tf_op jit(solution)/shard_map/ppermute | solution.py:222
  134.7 19.3 %collective-permute-start.33 = (bf16[32,1536]{1,0:T(8,128)(2,1)S(1)}, bf16[32,1536]{1,0:T(8,128)(2,1)S(1)}, u32[]{:S(2)}, u32[]{:S(2)}) collective-permute-start(bf16[32,1536]{1,0:T(8,128)(2,1)S(1)} %get-tuple-element.119), channel_id=1, source_target_pairs={{0,2},{1,7},{2,0},{3,6},{4,5},{5,4},{6,3},{7,1},{8,10},{9,15},{10,... | collective-permute-start | bytes 294920 | tf_op jit(solution)/shard_map/ppermute | solution.py:222
  141.9 12.7 %collective-permute-start.34 = (bf16[32,1536]{1,0:T(8,128)(2,1)S(1)}, bf16[32,1536]{1,0:T(8,128)(2,1)S(1)}, u32[]{:S(2)}, u32[]{:S(2)}) collective-permute-start(bf16[32,1536]{1,0:T(8,128)(2,1)S(1)} %get-tuple-element.120), channel_id=1, source_target_pairs={{0,6},{1,4},{2,3},{3,2},{4,1},{5,7},{6,0},{7,5},{8,14},{9,12},{10,... | collective-permute-start | bytes 294920 | tf_op jit(solution)/shard_map/ppermute | solution.py:222
  143.9 13.5 %collective-permute-start.35 = (bf16[32,1536]{1,0:T(8,128)(2,1)S(1)}, bf16[32,1536]{1,0:T(8,128)(2,1)S(1)}, u32[]{:S(2)}, u32[]{:S(2)}) collective-permute-start(bf16[32,1536]{1,0:T(8,128)(2,1)S(1)} %get-tuple-element.121), channel_id=1, source_target_pairs={{0,5},{1,3},{2,7},{3,1},{4,6},{5,0},{6,4},{7,2},{8,13},{9,11},{10,... | collective-permute-start | bytes 294920 | tf_op jit(solution)/shard_map/ppermute | solution.py:222
  145.5 11.9 %collective-permute-start.43 = (bf16[32,1536]{1,0:T(8,128)(2,1)S(1)}, bf16[32,1536]{1,0:T(8,128)(2,1)S(1)}, u32[]{:S(2)}, u32[]{:S(2)}) collective-permute-start(bf16[32,1536]{1,0:T(8,128)(2,1)S(1)} %get-tuple-element.131), channel_id=1, source_target_pairs={{0,7},{1,6},{2,5},{3,4},{4,3},{5,2},{6,1},{7,0},{8,15},{9,14},{10,... | collective-permute-start | bytes 294920 | tf_op jit(solution)/shard_map/ppermute | solution.py:222
  150.6 9.3 %collective-permute-start.44 = (bf16[32,1536]{1,0:T(8,128)(2,1)S(1)}, bf16[32,1536]{1,0:T(8,128)(2,1)S(1)}, u32[]{:S(2)}, u32[]{:S(2)}) collective-permute-start(bf16[32,1536]{1,0:T(8,128)(2,1)S(1)} %get-tuple-element.132), channel_id=1, source_target_pairs={{0,1},{1,0},{2,4},{3,7},{4,2},{5,6},{6,5},{7,3},{8,9},{9,8},{10,12... | collective-permute-start | bytes 294920 | tf_op jit(solution)/shard_map/ppermute | solution.py:222
  154.0 7.7 %collective-permute-start.45 = (bf16[32,1536]{1,0:T(8,128)(2,1)S(1)}, bf16[32,1536]{1,0:T(8,128)(2,1)S(1)}, u32[]{:S(2)}, u32[]{:S(2)}) collective-permute-start(bf16[32,1536]{1,0:T(8,128)(2,1)S(1)} %get-tuple-element.133), channel_id=1, source_target_pairs={{0,3},{1,5},{2,6},{3,0},{4,7},{5,1},{6,2},{7,4},{8,11},{9,13},{10,... | collective-permute-start | bytes 294920 | tf_op jit(solution)/shard_map/ppermute | solution.py:222
  154.5 7.2 %collective-permute-start.46 = (bf16[32,1536]{1,0:T(8,128)(2,1)S(1)}, bf16[32,1536]{1,0:T(8,128)(2,1)S(1)}, u32[]{:S(2)}, u32[]{:S(2)}) collective-permute-start(bf16[32,1536]{1,0:T(8,128)(2,1)S(1)} %get-tuple-element.134), channel_id=1, source_target_pairs={{0,4},{1,2},{2,1},{3,5},{4,0},{5,3},{6,7},{7,6},{8,12},{9,10},{10,... | collective-permute-start | bytes 294920 | tf_op jit(solution)/shard_map/ppermute | solution.py:222
  157.5 4.6 %collective-permute-start.47 = (bf16[32,1536]{1,0:T(8,128)(2,1)S(1)}, bf16[32,1536]{1,0:T(8,128)(2,1)S(1)}, u32[]{:S(2)}, u32[]{:S(2)}) collective-permute-start(bf16[32,1536]{1,0:T(8,128)(2,1)S(1)} %get-tuple-element.135), channel_id=1, source_target_pairs={{0,2},{1,7},{2,0},{3,6},{4,5},{5,4},{6,3},{7,1},{8,10},{9,15},{10,... | collective-permute-start | bytes 294920 | tf_op jit(solution)/shard_map/ppermute | solution.py:222
  157.5 6.6 %collective-permute-start.48 = (bf16[32,1536]{1,0:T(8,128)(2,1)S(1)}, bf16[32,1536]{1,0:T(8,128)(2,1)S(1)}, u32[]{:S(2)}, u32[]{:S(2)}) collective-permute-start(bf16[32,1536]{1,0:T(8,128)(2,1)S(1)} %get-tuple-element.136), channel_id=1, source_target_pairs={{0,6},{1,4},{2,3},{3,2},{4,1},{5,7},{6,0},{7,5},{8,14},{9,12},{10,... | collective-permute-start | bytes 294920 | tf_op jit(solution)/shard_map/ppermute | solution.py:222
  160.0 6.6 %collective-permute-start.49 = (bf16[32,1536]{1,0:T(8,128)(2,1)S(1)}, bf16[32,1536]{1,0:T(8,128)(2,1)S(1)}, u32[]{:S(2)}, u32[]{:S(2)}) collective-permute-start(bf16[32,1536]{1,0:T(8,128)(2,1)S(1)} %get-tuple-element.137), channel_id=1, source_target_pairs={{0,5},{1,3},{2,7},{3,1},{4,6},{5,0},{6,4},{7,2},{8,13},{9,11},{10,... | collective-permute-start | bytes 294920 | tf_op jit(solution)/shard_map/ppermute | solution.py:222
